TPU v7x, 32 devices: a whole 2x2x4 slice. The times are simulated.
32 devices in a mesh: groups: 2 (over y), dp: 4 (over z), mp: 2 (over x), pair: 2 (over core).
Axes of the slice: x: 2, y: 2, z: 4, core: 2. Of those that a mesh axis runs over, the one named last changes fastest.
Arguments:
- hidden: bfloat16 [2, 4096, 4096], P('pair', ('groups', 'dp')), parts along dimension 1, may hold values from -16 to 16
- document_labels: int32 [2, 8, 512], P('pair', ('groups', 'dp')), parts along dimension 1, may hold values from 0 to 63, never falling along the last dimension, each value on 1 to 16 neighbouring positions
- frozen_weight: bfloat16 [4096, 4096], P('dp', 'mp'), may hold values from -0.09375 to 0.09375
- adapter_down: bfloat16 [4096, 16], replicated, may hold values from -0.09375 to 0.09375
- adapter_up: bfloat16 [16, 4096], P(None, 'mp'), may hold values from -1.5 to 1.5
- norm_gain_vector: bfloat16 [4096], P('mp'), may hold values from 0.5 to 1.5
- negative_owner: int32 [2, 256, 4], P('pair', 'groups'), parts along dimension 1, may hold values from 0 to 3, as said below
- negative_pool_row: int32 [2, 256, 4], P('pair', 'groups'), parts along dimension 1, may hold values from 0 to 31
Outputs:
- losses: float32 [2, 256], P('pair', ('groups', 'dp')), parts along dimension 1
- doc_grads: float32 [2, 8, 64, 4096], P('pair', ('groups', 'dp'), None, 'mp'), parts along dimension 1
- lora_a_grad: float32 [8192, 16], P(('groups', 'mp')), parts along dimension 0
- lora_b_grad: float32 [32, 4096], P('groups', 'mp'), parts along dimension 0
- gain_grad: float32 [8192], P(('groups', 'mp')), parts along dimension 0
There are 2 independent parts, one for each index of `groups`. A program takes and returns all parts, laid end to end along the dimension named above; an argument that names none is the same for every part. Nothing has to cross between parts.
Inputs may be any that keep to these rules, and one draw needn't show every extreme that they name: `document_labels`: within a shard and side the ids never fall; every document 0 to 63 has 1 to 16 tokens, and one has exactly that many. `negative_owner`: among the 128 requests of the anchors of one shard (the rows of one device), no owner is named more than 32 times and some owner exactly 32 times; the 4 (owner, row) pairs of one anchor are distinct.
All inputs are finite; a program needn't handle non-finite values.
Results may differ from a plain program's by a relative error of at most 0.009.
Values may be sent and summed in bfloat16 or wider, within the bound.
No kernel may reach another device: no remote copies, remote signals or barrier semaphores. Data moves between devices by JAX's collectives and lax.ppermute only.
A program may use at most 128 MiB of HBM per device.

v0:
```python
import jax
import jax.numpy as jnp
from jax import lax
from jax.sharding import PartitionSpec as P

inverse_temp = 50.0


def body(
    hidden,
    document_labels,
    frozen_weight,
    adapter_down,
    adapter_up,
    norm_gain_vector,
    negative_owner,
    negative_pool_row,
):
    input_tokens = hidden[0]
    width = input_tokens.shape[1]
    column_total = adapter_up.shape[1]
    dp_count = lax.axis_size("dp")
    side_idx = lax.axis_index("pair")
    shard_idx = lax.axis_index("dp")
    column = lax.axis_index("mp")
    other_side = 1 - side_idx
    anchors = negative_owner.shape[1]
    per_shard = anchors // dp_count
    fanout = negative_owner.shape[2]
    slot_cap = min(per_shard, max(fanout, 2 * -(-(per_shard * fanout) // dp_count)))
    requests = per_shard * fanout
    highest_precision = lax.Precision.HIGHEST
    projected_states = jnp.dot(
        input_tokens,
        lax.all_gather(frozen_weight, "dp", axis=0, tiled=True),
        preferred_element_type=jnp.float32,
    )
    adapter_middle = jnp.dot(input_tokens, adapter_down, preferred_element_type=jnp.float32).astype(
        jnp.bfloat16
    )
    own_cols = lax.dynamic_slice_in_dim(input_tokens, column * column_total, column_total, 1)
    hidden_states = (
        own_cols.astype(jnp.float32)
        + projected_states
        + jnp.dot(adapter_middle, adapter_up, preferred_element_type=jnp.float32)
    )
    squares = lax.psum(jnp.sum(hidden_states * hidden_states, axis=1), "mp")
    inverse_root_mean = lax.rsqrt(squares / width + 1e-05)
    gain_f = norm_gain_vector.astype(jnp.float32)
    normed = (hidden_states * inverse_root_mean[:, None] * gain_f).astype(jnp.bfloat16)
    doc_index = document_labels[0, 0]
    doc_count = 2 * per_shard
    member = doc_index[None, :] == jnp.arange(doc_count, dtype=jnp.int32)[:, None]
    member_f = member.astype(jnp.float32)
    token_counts = jnp.sum(member_f, axis=1)
    mean_pooled = (
        jnp.dot(member.astype(jnp.bfloat16), normed, preferred_element_type=jnp.float32)
        / token_counts[:, None]
    ).astype(jnp.bfloat16)
    pooled_f = mean_pooled.astype(jnp.float32)
    doc_sq = lax.psum(jnp.sum(pooled_f * pooled_f, axis=1), "mp")
    document_norm = jnp.sqrt(doc_sq + 1e-06)
    unit_embedding = pooled_f / document_norm[:, None]
    unit_rows = unit_embedding.astype(jnp.bfloat16)
    owner_lists = negative_owner[0].reshape(dp_count, requests)
    row_lists = negative_pool_row[0].reshape(dp_count, requests)
    mine_owner = lax.dynamic_index_in_dim(owner_lists, shard_idx, 0, keepdims=False)
    pool_units = unit_rows[per_shard:]
    matched = owner_lists == shard_idx
    ranking = jnp.cumsum(matched.astype(jnp.int32), axis=1) - 1
    picked = (
        matched[:, :, None, None]
        & (ranking[:, :, None, None] == jnp.arange(slot_cap, dtype=jnp.int32)[None, None, :, None])
        & (
            row_lists[:, :, None, None]
            == jnp.arange(per_shard, dtype=jnp.int32)[None, None, None, :]
        )
    )
    selector = jnp.sum(picked.astype(jnp.float32), axis=1)
    outgoing = jnp.einsum(
        "bcr,rd->bcd", selector.astype(jnp.bfloat16), pool_units, preferred_element_type=jnp.float32
    ).astype(jnp.bfloat16)
    arrived = lax.all_to_all(outgoing, "dp", split_axis=0, concat_axis=0, tiled=True)
    arrived_flat = arrived.reshape(dp_count * slot_cap, column_total)
    request_ids = jnp.arange(requests, dtype=jnp.int32)
    earlier = (mine_owner[None, :] == mine_owner[:, None]) & (
        request_ids[None, :] < request_ids[:, None]
    )
    position = (mine_owner * slot_cap + jnp.sum(earlier.astype(jnp.int32), axis=1)).reshape(
        per_shard, fanout
    )
    gathered = lax.all_gather(unit_rows[:per_shard], ("dp", "pair"), axis=0, tiled=True)
    anchor_blocks = gathered.reshape(dp_count, 2, per_shard, column_total)
    row_units = lax.dynamic_index_in_dim(
        lax.dynamic_index_in_dim(anchor_blocks, shard_idx, 0, keepdims=False),
        other_side,
        0,
        keepdims=False,
    )
    cand_units = lax.dynamic_index_in_dim(anchor_blocks, side_idx, 1, keepdims=False).reshape(
        anchors, column_total
    )
    batch_part = jnp.dot(row_units, cand_units.T, preferred_element_type=jnp.float32)
    neg_part = jnp.dot(row_units, arrived_flat.T, preferred_element_type=jnp.float32)
    batch_sums, neg_sums = lax.psum((batch_part, neg_part), "mp")
    neg_pick = jnp.take_along_axis(neg_sums, position, axis=1)
    logits = inverse_temp * jnp.concatenate([batch_sums, neg_pick], axis=1)
    exp_logits = jnp.exp(logits)
    denominator = jnp.sum(exp_logits, axis=1)
    target_col = shard_idx * per_shard + jnp.arange(per_shard, dtype=jnp.int32)
    target = jnp.arange(anchors + fanout, dtype=jnp.int32)[None, :] == target_col[:, None]
    losses = (jnp.log(denominator) - jnp.sum(jnp.where(target, logits, 0.0), axis=1))[None, :]
    logit_grad = (
        inverse_temp * (exp_logits / denominator[:, None] - target.astype(jnp.float32))
    ).astype(jnp.bfloat16)
    grad_batch = logit_grad[:, :anchors]
    grad_neg = logit_grad[:, anchors:].astype(jnp.float32)
    slot_total = arrived_flat.shape[0]
    slot_hot = position[:, :, None] == jnp.arange(slot_total, dtype=jnp.int32)[None, None, :]
    grad_slots = jnp.sum(jnp.where(slot_hot, grad_neg[:, :, None], 0.0), axis=1).astype(
        jnp.bfloat16
    )
    rows_grad = jnp.dot(grad_batch, cand_units, preferred_element_type=jnp.float32) + jnp.dot(
        grad_slots, arrived_flat, preferred_element_type=jnp.float32
    )
    cand_grad = jnp.dot(grad_batch.T, row_units, preferred_element_type=jnp.float32)
    slot_grad = jnp.dot(grad_slots.T, row_units, preferred_element_type=jnp.float32)
    side_mask = (jnp.arange(2, dtype=jnp.int32) == side_idx)[None, :, None, None]
    scatter_term = jnp.where(
        side_mask, cand_grad.reshape(dp_count, 1, per_shard, column_total), 0.0
    )
    row_mask = (
        (jnp.arange(dp_count, dtype=jnp.int32) == shard_idx)[:, None]
        & (jnp.arange(2, dtype=jnp.int32) == other_side)[None, :]
    )[:, :, None, None]
    scatter_term = scatter_term + jnp.where(row_mask, rows_grad[None, None], 0.0)
    anchor_grad = lax.psum_scatter(
        scatter_term.reshape(dp_count * 2 * per_shard, column_total),
        ("dp", "pair"),
        scatter_dimension=0,
        tiled=True,
    )
    returned = lax.all_to_all(
        slot_grad.reshape(dp_count, slot_cap, column_total).astype(jnp.bfloat16),
        "dp",
        split_axis=0,
        concat_axis=0,
        tiled=True,
    ).astype(jnp.float32)
    pool_grad = jnp.einsum("bcr,bcd->rd", selector, returned, precision=highest_precision)
    doc_grad = jnp.concatenate([anchor_grad, pool_grad], axis=0)
    adapter_up_wide32 = adapter_up.astype(jnp.float32)
    cube = inverse_root_mean * inverse_root_mean * inverse_root_mean
    unit_dots = lax.psum(jnp.sum(unit_embedding * doc_grad, axis=1), "mp")
    per_doc = (doc_grad - unit_embedding * unit_dots[:, None]) / (document_norm * token_counts)[
        :, None
    ]
    tok_grad = jnp.dot(member_f.T, per_doc, precision=highest_precision)
    gained = tok_grad * gain_f
    tok_dots = lax.psum(jnp.sum(gained * hidden_states, axis=1), "mp")
    state_gradient = (
        inverse_root_mean[:, None] * gained - hidden_states * (cube * tok_dots / width)[:, None]
    )
    middle_piece = jnp.dot(state_gradient, adapter_up_wide32.T, precision=highest_precision)
    middle_gradient = lax.psum(middle_piece, "mp").astype(jnp.bfloat16)
    gain_grad = jnp.sum(tok_grad * hidden_states * inverse_root_mean[:, None], axis=0)
    up_map_gradient = jnp.dot(
        adapter_middle.astype(jnp.float32).T, state_gradient, precision=highest_precision
    )
    a_grad = jnp.dot(own_cols.T, middle_gradient, preferred_element_type=jnp.float32)
    a_grad, up_map_gradient, gain_grad = lax.psum(
        (a_grad, up_map_gradient, gain_grad), ("dp", "pair")
    )
    return (losses, doc_grad[None, None], a_grad, up_map_gradient, gain_grad)


def solution(mesh):
    in_specs = (
        P("pair", ("groups", "dp"), None),
        P("pair", ("groups", "dp"), None),
        P("dp", "mp"),
        P(),
        P(None, "mp"),
        P("mp"),
        P("pair", "groups", None),
        P("pair", "groups", None),
    )
    out_specs = (
        P("pair", ("groups", "dp")),
        P("pair", ("groups", "dp"), None, "mp"),
        P(("groups", "mp"), None),
        P("groups", "mp"),
        P(("groups", "mp")),
    )
    return jax.shard_map(body, mesh=mesh, in_specs=in_specs, out_specs=out_specs, check_vma=False)
```

profile of v0, /device:TPU:0, one launch (start us, length us, event | category | flops | bytes accessed | tf_op | source)
XLA Modules:
  0.0 514.0 jit_solution(5223007345118553689)
XLA Ops:
  9.0 3.4 fusion.14
  12.3 2.7 fusion.59
  15.0 284.1 %all-gather.3.cloned.1.call-done = bf16[4096,2048]{1,0:T(8,128)(2,1)} async-done(((bf16[1024,2048]{1,0:T(8,128)(2,1)}), bf16[4096,2048]{1,0:T(8,128)(2,1)}) %all-gather.3.cloned.1.call-update) | async-done | bytes 16777232 | tf_op jit(solution)/shard_map/all_gather | solution.py:35
  299.1 16.7 %multiply_reduce_fusion.2 = (f32[512]{0:T(512)S(1)}, f32[512,2048]{1,0:T(8,128)}) fusion(f32[512,2048]{1,0:T(8,128)} %fusion.59, bf16[4096,2048]{1,0:T(8,128)(2,1)} %all-gather.3.cloned.1.call-done, bf16[1,512,4096]{2,1,0:T(8,128)(2,1)} %param.8, s32[]{:T(128)S(6)} %select_n.58), kind=kOutput, calls=%fused_computation.9 | convolution fusion | flops 8595177472 | bytes 31459332 | tf_op jit(solution)/shard_map/dot_general | solution.py:33
  315.8 4.9 psum.70
  320.7 2.9 multiply_reduce_fusion.4
  323.7 4.9 psum.71
  331.6 3.5 all-to-all-start
  335.9 20.9 %all-gather.5.cloned.1.call-done = bf16[256,2048]{1,0:T(8,128)(2,1)} async-done(((bf16[32,2048]{1,0:T(8,128)(2,1)}), bf16[256,2048]{1,0:T(8,128)(2,1)}) %all-gather.5.cloned.1.call-update) | async-done | bytes 1048592 | tf_op jit(solution)/shard_map/all_gather | solution.py:92
  360.2 8.3 %all-reduce.1 = (f32[32,128]{1,0:T(8,128)S(1)}, f32[32,128]{1,0:T(8,128)S(1)}) all-reduce(f32[32,128]{1,0:T(8,128)S(1)} %fusion.27, f32[32,128]{1,0:T(8,128)S(1)} %fusion.29), channel_id=1, replica_groups=mesh['groups'=2,'dp'=4,'mp'=2,'pair'=2] {'mp'}, use_global_device_ids=true, to_apply=%region_9.10 | all-reduce | flops 8192 | bytes 65536 | tf_op jit(solution)/shard_map/psum | solution.py:105
  372.0 1.7 fusion.8
  375.1 23.3 %all_to_all.10 = bf16[4,32,2048]{2,1,0:T(8,128)(2,1)S(1)} all-to-all(bf16[4,32,2048]{2,1,0:T(8,128)(2,1)S(1)} %convolution_convert_fusion), channel_id=1, replica_groups=mesh['groups'=2,'dp'=4,'mp'=2,'pair'=2] {'dp'}, dimensions={0} | all-to-all | bytes 1048576 | tf_op jit(solution)/shard_map/all_to_all | solution.py:143
  398.8 13.8 %reduce-scatter.2.cloned.1.call-done = f32[32,2048]{1,0:T(8,128)} async-done(((f32[256,2048]{1,0:T(8,128)}), f32[32,2048]{1,0:T(8,128)}) %reduce-scatter.2.cloned.1.call-update) | async-done | bytes 262160 | tf_op jit(solution)/shard_map/reduce_scatter | solution.py:137
  412.5 1.9 multiply_reduce_fusion.3
  414.4 5.1 psum.74
  419.6 6.8 %multiply_reduce_fusion = (f32[2048]{0:T(1024)S(1)}, f32[512]{0:T(512)S(1)}, f32[512,2048]{1,0:T(8,128)}) fusion(f32[512,2048]{1,0:T(8,128)} %get-tuple-element.25, f32[512]{0:T(512)S(1)} %add_rsqrt_fusion, f32[2048]{0:T(1024)S(1)} %convert_element_type.71, f32[32,2048]{1,0:T(8,128)S(1)} %convolution_bitcast_fusion, ...), kind=kOutput, calls=%fused_computation.5 | convolution fusion | flops 812283392 | bytes 9460480 | tf_op jit(solution)/shard_map/dot_general | solution.py:158
  426.4 4.9 psum.75
  431.3 4.1 multiply_subtract_fusion
  435.5 2.0 fusion.60
  437.5 2.2 fusion.61
  439.7 8.0 %psum.76 = bf16[512,16]{0,1:T(8,128)(2,1)S(1)} all-reduce(f32[512,16]{0,1:T(8,128)S(1)} %fusion.60), channel_id=1, replica_groups=mesh['groups'=2,'dp'=4,'mp'=2,'pair'=2] {'mp'}, use_global_device_ids=true, to_apply=%region_18.19 | all-reduce | flops 8192 | bytes 49152 | tf_op jit(solution)/shard_map/psum | solution.py:165
  447.7 2.6 fusion.9
  450.9 14.5 %psum.79 = f32[2048]{0:T(1024)} all-reduce(f32[2048]{0:T(1024)S(1)} %get-tuple-element.5), channel_id=1, replica_groups=mesh['groups'=2,'dp'=4,'mp'=2,'pair'=2] {'dp','pair'}, use_global_device_ids=true, to_apply=%region_22.23 | all-reduce | flops 2048 | bytes 16384 | tf_op jit(solution)/shard_map/psum | solution.py:171
  465.4 39.0 %all-reduce.4.cloned.1.call-done = (f32[2048,16]{0,1:T(8,128)}, f32[16,2048]{1,0:T(8,128)}) async-done(((f32[2048,16]{0,1:T(8,128)}, f32[16,2048]{1,0:T(8,128)}), (f32[2048,16]{0,1:T(8,128)}, f32[16,2048]{1,0:T(8,128)})) %all-reduce.4.cloned.1.call-update) | async-done | bytes 262160 | tf_op jit(solution)/shard_map/psum | solution.py:171
  (78 shorter events, 17.6 us)
Async XLA Ops:
  7.2 1.8 copy-start
  7.2 0.8 copy-start.2
  7.2 0.9 copy-start.3
  7.2 1.4 copy-start.4
  7.2 1.6 copy-start.5
  7.2 5.1 copy-start.1
  7.2 291.9 %all-gather.3.cloned.1.call-start = ((), (), s32[]{:S(2)}) async-start(), calls=%async_computation.3 | async-start | bytes 20971520 | tf_op jit(solution)/shard_map/all_gather | solution.py:35
  8.0 348.8 %all-gather.5.cloned.1.call-start = ((), (), s32[]{:S(2)}) async-start(), calls=%async_computation.4 | async-start | bytes 1179648 | tf_op jit(solution)/shard_map/all_gather | solution.py:92
  331.6 27.4 %all-to-all-start = ((bf16[4,32,2048]{2,1,0:T(8,128)(2,1)}), bf16[4,32,2048]{2,1,0:T(8,128)(2,1)S(1)}, u32[]{:S(2)}, u32[]{:S(2)}) async-start(bf16[4,32,2048]{2,1,0:T(8,128)(2,1)} %convolution_convert_fusion.1), calls=%async_computation | async-start | bytes 1048576 | tf_op jit(solution)/shard_map/all_to_all | solution.py:83
  335.1 77.4 %reduce-scatter.2.cloned.1.call-start = ((), (), s32[]{:S(2)}) async-start(), calls=%async_computation.5 | async-start | bytes 2359296 | tf_op jit(solution)/shard_map/reduce_scatter | solution.py:137
  373.7 130.7 %all-reduce.4.cloned.1.call-start = ((), (), s32[]{:S(2)}) async-start(), calls=%async_computation.6 | async-start | bytes 524288 | tf_op jit(solution)/shard_map/psum | solution.py:171
Sparse Core Ops, SparseCore 0:
  9.6 289.4 all-gather.2
  329.6 27.1 all-gather.4
  373.8 38.6 reduce-scatter.1
  450.5 53.8 all-reduce.3
where the time goes:
time: 515 us; the launch traced here: 514 us
  waiting for transfers between devices  358 us (70%)
  blocking collectives  74.1 us (14%)
  matrix products  45.9 us (9%)
  between operations  14.1 us (3%)
  other arithmetic  10 us (2%)
  local copies, waits for them, and re-layouts  7.8 us (2%)
    all_gather x1, waiting for transfers between devices, body(): lax.all_gather(frozen_weight, 'dp', axis=0, tiled=True)  284 us
    psum x1, waiting for transfers between devices, body(): lax.psum((a_grad, up_map_gradient, gain_grad), ('dp', 'pair'))  39 us
    all_to_all x1, blocking collectives, body(): lax.all_to_all(slot_grad.reshape(dp_count, slot_cap, column_total).astype...  23.3 us
    all_gather x1, waiting for transfers between devices, body(): lax.all_gather(unit_rows[:per_shard], ('dp', 'pair'), axis=0, tiled=True)  20.9 us
    dot_general x1, matrix products, body(): jnp.dot(input_tokens, lax.all_gather(frozen_weight, 'dp', axis=0, tiled=T...  16.7 us
    psum x1, blocking collectives, body(): lax.psum((a_grad, up_map_gradient, gain_grad), ('dp', 'pair'))  14.5 us
    reduce_scatter x1, waiting for transfers between devices, body(): lax.psum_scatter(scatter_term.reshape(dp_count * 2 * per_shard, column_to...  13.8 us
  transfers between devices with their start and end apart: 5, of which 4 were waited for; matrix products, arithmetic and copies ran while one was open for 3% of the time, Pallas kernels for 0%

commit v1 on v0

--- a/solution.py
+++ b/solution.py
@@ -30,9 +30,13 @@
     slot_cap = min(per_shard, max(fanout, 2 * -(-(per_shard * fanout) // dp_count)))
     requests = per_shard * fanout
     highest_precision = lax.Precision.HIGHEST
+    copies = lax.axis_size("groups") * lax.axis_size("pair")
+    copy_rows = frozen_weight.shape[0] // copies
+    copy_idx = lax.axis_index("groups") * lax.axis_size("pair") + side_idx
+    weight_piece = lax.dynamic_slice_in_dim(frozen_weight, copy_idx * copy_rows, copy_rows, 0)
     projected_states = jnp.dot(
         input_tokens,
-        lax.all_gather(frozen_weight, "dp", axis=0, tiled=True),
+        lax.all_gather(weight_piece, ("dp", "groups", "pair"), axis=0, tiled=True),
         preferred_element_type=jnp.float32,
     )
     adapter_middle = jnp.dot(input_tokens, adapter_down, preferred_element_type=jnp.float32).astype(

time: 515 us -> 363 us (0.70)
  waiting for transfers between devices: 358 us -> 190 us
  local copies, waits for them, and re-layouts: 7.8 us -> 16.4 us
  matrix products: 45.9 us -> 53.1 us
    all_gather x1, waiting for transfers between devices: 284 us -> 119 us  [body(): lax.all_gather(weight_piece, ('dp', 'groups', 'pair'), axis=0, tiled=True)]
    dynamic_slice x0 -> x3, local copies, waits for them, and re-layouts: none -> 6.72 us  [the longest x2 4.38 us: body(): lax.dynamic_slice_in_dim(input_tokens, column * column_total, column_tota...]
  transfers between devices with their start and end apart: 5 -> 5, of which waited for: 4 -> 4; matrix products, arithmetic and copies ran while one was open for 3% -> 6% of each run, Pallas kernels for 0% -> 0%
where the time goes in v1:
time: 363 us; the launch traced here: 362 us
  waiting for transfers between devices  190 us (52%)
  blocking collectives  74.9 us (21%)
  matrix products  53.1 us (15%)
  local copies, waits for them, and re-layouts  16.4 us (5%)
  between operations  14.1 us (4%)
  other arithmetic  10.3 us (3%)
  starting transfers between devices  3.64 us (1%)
    all_gather x1, waiting for transfers between devices, body(): lax.all_gather(weight_piece, ('dp', 'groups', 'pair'), axis=0, tiled=True)  119 us
    psum x1, waiting for transfers between devices, body(): lax.psum((a_grad, up_map_gradient, gain_grad), ('dp', 'pair'))  38.7 us
    all_to_all x1, blocking collectives, body(): lax.all_to_all(slot_grad.reshape(dp_count, slot_cap, column_total).astype...  23.9 us
    all_gather x1, waiting for transfers between devices, body(): lax.all_gather(unit_rows[:per_shard], ('dp', 'pair'), axis=0, tiled=True)  19.5 us
    dot_general x1, matrix products, body(): jnp.dot(input_tokens, lax.all_gather(weight_piece, ('dp', 'groups', 'pair...  16.7 us
    psum x1, blocking collectives, body(): lax.psum((a_grad, up_map_gradient, gain_grad), ('dp', 'pair'))  14.6 us
    reduce_scatter x1, waiting for transfers between devices, body(): lax.psum_scatter(scatter_term.reshape(dp_count * 2 * per_shard, column_to...  12.8 us
    psum x1, blocking collectives, body(): batch_sums, neg_sums = lax.psum((batch_part, neg_part), 'mp')  8.95 us
  transfers between devices with their start and end apart: 5, of which 4 were waited for; matrix products, arithmetic and copies ran while one was open for 6% of the time, Pallas kernels for 0%

profile of v1, /device:TPU:0, one launch (start us, length us, event | category | flops | bytes accessed | tf_op | source)
XLA Modules:
  0.0 362.2 jit_solution(1153982941166094891)
XLA Ops:
  7.2 2.3 constant_dynamic-slice_fusion.2
  11.6 2.5 copy.50
  15.0 3.4 fusion.14
  18.4 2.7 fusion.60
  21.1 118.7 %all-gather.3.cloned.1.call-done = bf16[4096,2048]{1,0:T(8,128)(2,1)} async-done(((bf16[256,2048]{1,0:T(8,128)(2,1)}), bf16[4096,2048]{1,0:T(8,128)(2,1)}) %all-gather.3.cloned.1.call-update) | async-done | bytes 16777232 | tf_op jit(solution)/shard_map/all_gather | solution.py:39
  139.8 16.7 %multiply_reduce_fusion.2 = (f32[512]{0:T(512)S(1)}, f32[512,2048]{0,1:T(8,128)}) fusion(f32[512,2048]{0,1:T(8,128)} %fusion.60, bf16[4096,2048]{1,0:T(8,128)(2,1)} %all-gather.3.cloned.1.call-done, bf16[1,512,4096]{2,1,0:T(8,128)(2,1)} %param.8, bf16[1,512,2048]{1,2,0:T(8,128)(2,1)} %copy.50), kind=kOutput, calls=%fused_computation.11 | convolution fusion | flops 8595177472 | bytes 31459328 | tf_op jit(solution)/shard_map/dot_general | solution.py:37
  156.5 4.9 %psum.70 = f32[512]{0:T(512)S(1)} all-reduce(f32[512]{0:T(512)S(1)} %get-tuple-element.24), channel_id=1, replica_groups=mesh['groups'=2,'dp'=4,'mp'=2,'pair'=2] {'mp'}, use_global_device_ids=true, to_apply=%region_1.0 | all-reduce | flops 512 | bytes 4096 | tf_op jit(solution)/shard_map/psum | solution.py:51
  161.4 3.2 multiply_reduce_fusion.4
  164.6 4.9 %psum.71 = f32[64]{0:T(128)S(1)} all-reduce(f32[64]{0:T(128)S(1)} %get-tuple-element.26), channel_id=1, replica_groups=mesh['groups'=2,'dp'=4,'mp'=2,'pair'=2] {'mp'}, use_global_device_ids=true, to_apply=%region_4.0 | all-reduce | flops 64 | bytes 512 | tf_op jit(solution)/shard_map/psum | solution.py:65
  173.1 3.5 all-to-all-start
  179.0 19.5 %all-gather.5.cloned.1.call-done = bf16[256,2048]{1,0:T(8,128)(2,1)} async-done(((bf16[32,2048]{1,0:T(8,128)(2,1)}), bf16[256,2048]{1,0:T(8,128)(2,1)}) %all-gather.5.cloned.1.call-update) | async-done | bytes 1048592 | tf_op jit(solution)/shard_map/all_gather | solution.py:96
  202.7 9.0 %all-reduce.1 = (f32[32,128]{1,0:T(8,128)S(1)}, f32[32,128]{1,0:T(8,128)}) all-reduce(f32[32,128]{1,0:T(8,128)S(1)} %fusion.27, f32[32,128]{1,0:T(8,128)S(1)} %fusion.29), channel_id=1, replica_groups=mesh['groups'=2,'dp'=4,'mp'=2,'pair'=2] {'mp'}, use_global_device_ids=true, to_apply=%region_9.10 | all-reduce | flops 8192 | bytes 65536 | tf_op jit(solution)/shard_map/psum | solution.py:109
  217.3 2.2 fusion.25
  220.9 3.0 fusion.11
  225.2 23.9 %all_to_all.10 = bf16[4,32,2048]{2,1,0:T(8,128)(2,1)S(1)} all-to-all(bf16[4,32,2048]{2,1,0:T(8,128)(2,1)S(1)} %convolution_convert_fusion), channel_id=1, replica_groups=mesh['groups'=2,'dp'=4,'mp'=2,'pair'=2] {'dp'}, dimensions={0} | all-to-all | bytes 1048576 | tf_op jit(solution)/shard_map/all_to_all | solution.py:147
  249.5 12.8 %reduce-scatter.2.cloned.1.call-done = f32[32,2048]{1,0:T(8,128)} async-done(((f32[256,2048]{1,0:T(8,128)}), f32[32,2048]{1,0:T(8,128)}) %reduce-scatter.2.cloned.1.call-update) | async-done | bytes 262160 | tf_op jit(solution)/shard_map/reduce_scatter | solution.py:141
  264.2 4.9 %psum.74 = f32[64]{0:T(128)S(1)} all-reduce(f32[64]{0:T(128)S(1)} %get-tuple-element.17), channel_id=1, replica_groups=mesh['groups'=2,'dp'=4,'mp'=2,'pair'=2] {'mp'}, use_global_device_ids=true, to_apply=%region_15.16 | all-reduce | flops 64 | bytes 512 | tf_op jit(solution)/shard_map/psum | solution.py:158
  269.2 6.9 %multiply_reduce_fusion = (f32[2048]{0:T(1024)S(1)}, f32[512]{0:T(512)S(1)}, f32[512,2048]{0,1:T(8,128)}) fusion(f32[512,2048]{0,1:T(8,128)} %get-tuple-element.25, f32[512]{0:T(512)S(1)} %copy-done.6, f32[2048]{0:T(1024)S(1)} %convert_element_type.71, f32[32,2048]{1,0:T(8,128)S(1)} %convolution_bitcast_fusion, ...), kind=kOutput, calls=%fused_computation.7 | convolution fusion | flops 812283392 | bytes 9460480 | tf_op jit(solution)/shard_map/dot_general | solution.py:162
  276.1 4.9 %psum.75 = f32[512]{0:T(512)S(1)} all-reduce(f32[512]{0:T(512)S(1)} %get-tuple-element.6), channel_id=1, replica_groups=mesh['groups'=2,'dp'=4,'mp'=2,'pair'=2] {'mp'}, use_global_device_ids=true, to_apply=%region_17.18 | all-reduce | flops 512 | bytes 4096 | tf_op jit(solution)/shard_map/psum | solution.py:164
  281.0 6.8 %fusion.31 = f32[16,2048]{1,0:T(8,128)} fusion(bf16[512,16]{0,1:T(8,128)(2,1)S(1)} %fusion.14, f32[512,2048]{0,1:T(8,128)} %get-tuple-element.25, f32[512,2048]{0,1:T(8,128)} %get-tuple-element.28, f32[512]{0:T(512)S(1)} %fusion.48, f32[2048]{0:T(1024)S(1)} %convert_element_type.71, f32[512]{0:T(512)S(1)} %copy-done.6), kind=kOutput, calls=%fused_computation.49 | convolution fusion | flops 205520896 | bytes 8548352 | tf_op jit(solution)/shard_map/dot_general | solution.py:171
  287.9 2.1 fusion.32
  289.9 7.7 %psum.76 = bf16[512,16]{0,1:T(8,128)(2,1)S(1)} all-reduce(f32[512,16]{0,1:T(8,128)S(1)} %fusion.32), channel_id=1, replica_groups=mesh['groups'=2,'dp'=4,'mp'=2,'pair'=2] {'mp'}, use_global_device_ids=true, to_apply=%region_18.19 | all-reduce | flops 8192 | bytes 49152 | tf_op jit(solution)/shard_map/psum | solution.py:169
  299.2 14.6 %psum.79 = f32[2048]{0:T(1024)} all-reduce(f32[2048]{0:T(1024)S(1)} %get-tuple-element.5), channel_id=1, replica_groups=mesh['groups'=2,'dp'=4,'mp'=2,'pair'=2] {'dp','pair'}, use_global_device_ids=true, to_apply=%region_22.23 | all-reduce | flops 2048 | bytes 16384 | tf_op jit(solution)/shard_map/psum | solution.py:175
  313.8 38.7 %all-reduce.4.cloned.1.call-done = (f32[2048,16]{0,1:T(8,128)}, f32[16,2048]{1,0:T(8,128)}) async-done(((f32[2048,16]{0,1:T(8,128)}, f32[16,2048]{1,0:T(8,128)}), (f32[2048,16]{0,1:T(8,128)}, f32[16,2048]{1,0:T(8,128)})) %all-reduce.4.cloned.1.call-update) | async-done | bytes 262160 | tf_op jit(solution)/shard_map/psum | solution.py:175
  (102 shorter events, 28.3 us)
Async XLA Ops:
  7.2 7.9 %copy-start = (bf16[4096,16]{0,1:T(8,128)(2,1)S(1)}, bf16[4096,16]{0,1:T(8,128)(2,1)}, u32[]{:S(2)}) copy-start(bf16[4096,16]{0,1:T(8,128)(2,1)} %param.11) | copy-start | bytes 393220
  7.2 132.6 %all-gather.3.cloned.1.call-start = ((), (), s32[]{:S(2)}) async-start(), calls=%async_computation.3 | async-start | bytes 17825792 | tf_op jit(solution)/shard_map/all_gather | solution.py:39
  9.6 188.9 %all-gather.5.cloned.1.call-start = ((), (), s32[]{:S(2)}) async-start(), calls=%async_computation.4 | async-start | bytes 1179648 | tf_op jit(solution)/shard_map/all_gather | solution.py:96
  9.7 4.4 %copy-start.13 = (bf16[2048]{0:T(1024)(128)(2,1)S(1)}, bf16[2048]{0:T(1024)(128)(2,1)}, u32[]{:S(2)}) copy-start(bf16[2048]{0:T(1024)(128)(2,1)} %param.13) | copy-start | bytes 12292
  9.7 4.4 %copy-start.15 = (s32[1,128,4]{1,2,0:T(4,128)S(1)}, s32[1,128,4]{1,2,0:T(4,128)}, u32[]{:S(2)}) copy-start(s32[1,128,4]{1,2,0:T(4,128)} %param.14) | copy-start | bytes 6148
  9.7 5.0 %copy-start.16 = (s32[1,128,4]{1,2,0:T(4,128)S(1)}, s32[1,128,4]{1,2,0:T(4,128)}, u32[]{:S(2)}) copy-start(s32[1,128,4]{1,2,0:T(4,128)} %param.15) | copy-start | bytes 6148
  9.7 5.2 %copy-start.7 = (s32[1,1,512]{2,1,0:T(1,128)S(1)}, s32[1,1,512]{2,1,0:T(1,128)}, u32[]{:S(2)}) copy-start(s32[1,1,512]{2,1,0:T(1,128)} %param.9) | copy-start | bytes 6148
  11.6 6.8 %copy-start.4 = (bf16[16,2048]{1,0:T(8,128)(2,1)S(1)}, bf16[16,2048]{1,0:T(8,128)(2,1)}, u32[]{:S(2)}) copy-start(bf16[16,2048]{1,0:T(8,128)(2,1)} %param.12) | copy-start | bytes 196612
  161.4 10.0 %copy-start.9 = (f32[512]{0:T(512)}, f32[512]{0:T(512)S(1)}, u32[]{:S(2)}) copy-start(f32[512]{0:T(512)S(1)} %psum.70) | copy-start | bytes 6148
  161.4 8.7 %copy-start.5 = (f32[512]{0:T(512)}, f32[512]{0:T(512)S(1)}, u32[]{:S(2)}) copy-start(f32[512]{0:T(512)S(1)} %add_rsqrt_fusion) | copy-start | bytes 6148
  170.1 1.2 copy-start.11
  173.1 28.5 %all-to-all-start = ((bf16[4,32,2048]{2,1,0:T(8,128)(2,1)}), bf16[4,32,2048]{2,1,0:T(8,128)(2,1)S(1)}, u32[]{:S(2)}, u32[]{:S(2)}) async-start(bf16[4,32,2048]{2,1,0:T(8,128)(2,1)} %convolution_convert_fusion.1), calls=%async_computation | async-start | bytes 1048576 | tf_op jit(solution)/shard_map/all_to_all | solution.py:87
  176.6 85.8 %reduce-scatter.2.cloned.1.call-start = ((), (), s32[]{:S(2)}) async-start(), calls=%async_computation.5 | async-start | bytes 2359296 | tf_op jit(solution)/shard_map/reduce_scatter | solution.py:141
  199.6 0.8 copy-start.3
  220.8 41.5 %copy-start.12 = (f32[64]{0:T(128)S(1)}, f32[64]{0:T(128)}, u32[]{:S(2)}) copy-start(f32[64]{0:T(128)} %copy-done.11) | copy-start | bytes 772
  220.8 48.4 %copy-start.6 = (f32[512]{0:T(512)S(1)}, f32[512]{0:T(512)}, u32[]{:S(2)}) copy-start(f32[512]{0:T(512)} %copy-done.5) | copy-start | bytes 6148
  220.8 48.4 %copy-start.8 = (s32[1,1,512]{2,1,0:T(1,128)S(1)}, s32[1,1,512]{2,1,0:T(1,128)}, u32[]{:S(2)}) copy-start(s32[1,1,512]{2,1,0:T(1,128)} %param.9) | copy-start | bytes 6148
  220.9 48.3 %copy-start.14 = (f32[64]{0:T(128)S(1)}, f32[64]{0:T(128)}, u32[]{:S(2)}) copy-start(f32[64]{0:T(128)} %get-tuple-element.22) | copy-start | bytes 772
  223.9 128.7 %all-reduce.4.cloned.1.call-start = ((), (), s32[]{:S(2)}) async-start(), calls=%async_computation.6 | async-start | bytes 524288 | tf_op jit(solution)/shard_map/psum | solution.py:175
  269.2 11.8 %copy-start.10 = (f32[512]{0:T(512)S(1)}, f32[512]{0:T(512)}, u32[]{:S(2)}) copy-start(f32[512]{0:T(512)} %copy-done.9) | copy-start | bytes 6148
  281.0 6.8 %copy-start.1 = (f32[512,2048]{0,1:T(8,128)S(1)}, f32[512,2048]{0,1:T(8,128)}, u32[]{:S(2)}) copy-start(f32[512,2048]{0,1:T(8,128)} %get-tuple-element.25) | copy-start | bytes 12582916
  281.0 6.8 %copy-start.2 = (f32[512,2048]{0,1:T(8,128)S(1)}, f32[512,2048]{0,1:T(8,128)}, u32[]{:S(2)}) copy-start(f32[512,2048]{0,1:T(8,128)} %get-tuple-element.28) | copy-start | bytes 12582916
Sparse Core Ops, SparseCore 0:
  10.2 129.5 all-gather.2
  171.0 27.4 all-gather.4
  224.0 38.3 reduce-scatter.1
  298.8 53.6 all-reduce.3

commit v2 on v1

v2 whole, which is shorter than its diff:
```python
import jax
import jax.numpy as jnp
from jax import lax
from jax.sharding import PartitionSpec as P

inverse_temp = 50.0
highest = lax.Precision.HIGHEST


def dot_nt(a, b, precision=None):
    return lax.dot_general(
        a, b, (((1,), (1,)), ((), ())), precision=precision, preferred_element_type=jnp.float32
    )


def dot_nn(a, b, precision=None):
    return jnp.dot(a, b, precision=precision, preferred_element_type=jnp.float32)


def swap(x, axis):
    return lax.ppermute(x, axis, [(0, 1), (1, 0)])


def partner(x, axis, flip):
    return lax.ppermute(x, axis, [(i, i ^ flip) for i in range(lax.axis_size(axis))])


def sum_over(x, axis):
    if lax.axis_size(axis) == 2:
        return x + swap(x, axis)
    return lax.psum(x, axis)


def body(
    hidden,
    document_labels,
    frozen_weight,
    adapter_down,
    adapter_up,
    norm_gain_vector,
    negative_owner,
    negative_pool_row,
):
    tokens = hidden[0]
    token_count, width = tokens.shape
    cols = adapter_up.shape[1]
    rank = adapter_up.shape[0]
    dp = lax.axis_size("dp")
    side = lax.axis_index("pair")
    shard = lax.axis_index("dp")
    anchors = negative_owner.shape[1]
    per_shard = anchors // dp
    docs = 2 * per_shard

    block_shard = shard ^ jnp.arange(dp, dtype=jnp.int32)
    list_col = (shard ^ negative_owner[0]) * docs + per_shard + negative_pool_row[0]
    own_list = lax.dynamic_slice_in_dim(list_col, shard * per_shard, per_shard, 0)
    other_own_list = swap(own_list, "pair")
    rel_list = list_col.reshape(dp, per_shard, -1)[block_shard].reshape(anchors, -1)
    col_id = jnp.arange(dp * docs, dtype=jnp.int32)
    anchor_col = (col_id % docs) < per_shard

    def listed(lists):
        hit = lists[:, :, None] == col_id[None, None, :]
        return jnp.any(hit, axis=1) | anchor_col[None, :]

    mask_c = listed(rel_list)
    mask_o = listed(other_own_list)
    rel_row = jnp.arange(anchors, dtype=jnp.int32)
    target_c = col_id[None, :] == (rel_row // per_shard * docs + rel_row % per_shard)[:, None]
    target_o = target_c[:per_shard]

    copies = lax.axis_size("groups") * lax.axis_size("pair")
    copy_rows = frozen_weight.shape[0] // copies
    copy_idx = lax.axis_index("groups") * lax.axis_size("pair") + side
    weight_piece = lax.dynamic_slice_in_dim(frozen_weight, copy_idx * copy_rows, copy_rows, 0)
    weight = lax.all_gather(weight_piece, ("dp", "groups", "pair"), axis=0, tiled=True)
    lora_mid = dot_nn(tokens, adapter_down).astype(jnp.bfloat16)
    own_cols = lax.dynamic_slice_in_dim(tokens, lax.axis_index("mp") * cols, cols, 1)
    states = own_cols.astype(jnp.float32) + dot_nn(tokens, weight) + dot_nn(lora_mid, adapter_up)
    states_b = states.astype(jnp.bfloat16)
    squares = sum_over(jnp.sum(states * states, axis=1), "mp")
    inv_rms = lax.rsqrt(squares / width + 1e-05)

    gain = norm_gain_vector.astype(jnp.float32)
    labels = document_labels[0, 0]
    member = labels[None, :] == jnp.arange(docs, dtype=jnp.int32)[:, None]
    member_f = member.astype(jnp.float32)
    counts = jnp.sum(member_f, axis=1)
    normed = (states * inv_rms[:, None] * gain).astype(jnp.bfloat16)
    doc_sums = dot_nn(member.astype(jnp.bfloat16), normed)
    pooled = (doc_sums / counts[:, None]).astype(jnp.bfloat16)

    own_blocks = [pooled] + [partner(pooled, "dp", j) for j in range(1, dp)]
    other_blocks = [swap(block, "pair") for block in own_blocks]
    docs_own = jnp.concatenate(own_blocks, axis=0)
    docs_oth = jnp.concatenate(other_blocks, axis=0)
    anchors_oth = jnp.concatenate([block[:per_shard] for block in other_blocks], axis=0)
    docs_own_f = docs_own.astype(jnp.float32)
    docs_oth_f = docs_oth.astype(jnp.float32)
    sums = sum_over(
        jnp.concatenate(
            [
                dot_nt(anchors_oth, docs_own),
                dot_nt(pooled[:per_shard], docs_oth),
                jnp.sum(docs_own_f * docs_own_f, axis=1)[None],
                jnp.sum(docs_oth_f * docs_oth_f, axis=1)[None],
            ],
            axis=0,
        ),
        "mp",
    )
    inner_c = sums[:anchors]
    inner_o = sums[anchors : anchors + per_shard]
    inv_own = lax.rsqrt(sums[anchors + per_shard] + 1e-06)
    inv_oth = lax.rsqrt(sums[anchors + per_shard + 1] + 1e-06)
    inv_oth_anchor = inv_oth.reshape(dp, docs)[:, :per_shard].reshape(anchors)
    inv_own_doc = inv_own[:docs]

    def softmax_grad(inner, scale_row, scale_col, mask, target):
        logits = inverse_temp * (inner * scale_row[:, None] * scale_col[None, :])
        exp_logits = jnp.where(mask, jnp.exp(logits), 0.0)
        total = jnp.sum(exp_logits, axis=1)
        hit = jnp.sum(jnp.where(target, logits, 0.0), axis=1)
        grad = inverse_temp * (exp_logits / total[:, None] - target.astype(jnp.float32))
        return jnp.log(total) - hit, grad

    losses_c, grad_c = softmax_grad(inner_c, inv_oth_anchor, inv_own, mask_c, target_c)
    _, grad_o = softmax_grad(inner_o, inv_own_doc[:per_shard], inv_oth, mask_o, target_o)
    losses = losses_c[:per_shard][None]

    grad_ct = grad_c[:, :docs].T.reshape(docs, dp, per_shard)
    inner_ct = inner_c[:, :docs].T.reshape(docs, dp, per_shard)
    zero_pool = jnp.zeros((docs, dp, per_shard), jnp.float32)
    zero_rows = jnp.zeros((docs - per_shard, dp * docs), jnp.float32)
    coef = jnp.concatenate([grad_ct, zero_pool], axis=2).reshape(docs, dp * docs)
    coef = coef + jnp.concatenate([grad_o, zero_rows], axis=0)
    inner = jnp.concatenate(
        [
            inner_o,
            jnp.concatenate([inner_ct, zero_pool], axis=2).reshape(docs, dp * docs)[per_shard:],
        ],
        axis=0,
    )
    coef_b = (coef * inv_oth[None, :]).astype(jnp.bfloat16)
    doc_grad = dot_nn(coef_b, docs_oth)
    unit_dots = jnp.sum(coef_b.astype(jnp.float32) * inner, axis=1) * inv_own_doc
    pooled_f = pooled.astype(jnp.float32)
    per_doc = (doc_grad - pooled_f * (inv_own_doc * unit_dots)[:, None]) * (inv_own_doc / counts)[
        :, None
    ]

    gained = per_doc * gain
    up_f = adapter_up.astype(jnp.float32)
    tok_doc = dot_nt(gained.astype(jnp.bfloat16), states_b)
    tok_dots = jnp.sum(jnp.where(member, tok_doc, 0.0), axis=0)[None]
    up_states = dot_nt(adapter_up, states_b)
    up_gained = dot_nt(up_f, gained, highest)
    small = sum_over(
        jnp.concatenate(
            [
                jnp.concatenate([tok_dots, up_states], axis=0),
                jnp.concatenate([jnp.zeros((1, docs), jnp.float32), up_gained], axis=0),
            ],
            axis=1,
        ),
        "mp",
    )
    alpha = inv_rms * inv_rms * inv_rms * small[0, :token_count] / width
    up_states = small[1:, :token_count]
    up_gained = small[1:, token_count:]
    mid_grad = (
        inv_rms * dot_nn(up_gained, member_f, highest) - alpha * up_states
    ).astype(jnp.bfloat16)
    mid_t = lora_mid.astype(jnp.float32).T
    a_grad = dot_nn(mid_grad, own_cols)
    b_grad = dot_nn(dot_nt(mid_t * inv_rms, member_f, highest), gained, highest) - dot_nn(
        (mid_t * alpha).astype(jnp.bfloat16), states_b
    )
    gain_grad = jnp.sum(per_doc * doc_sums, axis=0) / gain

    grads = jnp.concatenate([a_grad, b_grad, gain_grad[None]], axis=0)
    half = cols // 2
    kept = lax.dynamic_slice_in_dim(grads, side * half, half, 1)
    sent = lax.dynamic_slice_in_dim(grads, (1 - side) * half, half, 1)
    kept = kept + swap(sent, "pair")
    level = [kept] + [partner(kept, "dp", j) for j in range(1, dp)]
    while len(level) > 1:
        level = [level[i] + level[i + 1] for i in range(0, len(level), 2)]
    total = level[0]
    received = swap(total, "pair")
    grads = jnp.concatenate(
        [jnp.where(side == 0, total, received), jnp.where(side == 0, received, total)], axis=1
    )
    return (
        losses,
        doc_grad[None, None],
        grads[:rank].T,
        grads[rank : 2 * rank],
        grads[2 * rank],
    )


def solution(mesh):
    in_specs = (
        P("pair", ("groups", "dp"), None),
        P("pair", ("groups", "dp"), None),
        P("dp", "mp"),
        P(),
        P(None, "mp"),
        P("mp"),
        P("pair", "groups", None),
        P("pair", "groups", None),
    )
    out_specs = (
        P("pair", ("groups", "dp")),
        P("pair", ("groups", "dp"), None, "mp"),
        P(("groups", "mp"), None),
        P("groups", "mp"),
        P(("groups", "mp")),
    )
    return jax.shard_map(body, mesh=mesh, in_specs=in_specs, out_specs=out_specs, check_vma=False)
```

time: 363 us -> 254 us (0.70)
  blocking collectives: 74.9 us -> 0 us
  waiting for transfers between devices: 190 us -> 155 us
  matrix products: 53.1 us -> 32.8 us
  starting transfers between devices: 3.64 us -> 16.8 us
  other arithmetic: 10.3 us -> 14.2 us
    psum x7 -> x0, blocking collectives: 50.9 us -> none  [the longest x1 14.6 us: body(): lax.psum((a_grad, up_map_gradient, gain_grad), ('dp', 'pair'))]
    ppermute x0 -> x16, waiting for transfers between devices: none -> 39.9 us  [the longest x6 28.3 us: partner(): lax.ppermute(x, axis, [(i, i ^ flip) for i in range(lax.axis_size(axis))])]
    psum x1 -> x0, waiting for transfers between devices: 38.7 us -> none  [body(): lax.psum((a_grad, up_map_gradient, gain_grad), ('dp', 'pair'))]
    all_to_all x1 -> x0, blocking collectives: 23.9 us -> none  [body(): lax.all_to_all(slot_grad.reshape(dp_count, slot_cap, column_total).astype...]
    dot_general x16 -> x15, matrix products: 53.1 us -> 32.8 us  [the longest x9 26.7 us: dot_nn(): jnp.dot(a, b, precision=precision, preferred_element_type=jnp.float32)]
    all_gather x1 -> x0, waiting for transfers between devices: 19.5 us -> none  [body(): lax.all_gather(unit_rows[:per_shard], ('dp', 'pair'), axis=0, tiled=True)]
    ppermute x0 -> x16, starting transfers between devices: none -> 16.8 us  [the longest x6 11.1 us: partner(): lax.ppermute(x, axis, [(i, i ^ flip) for i in range(lax.axis_size(axis))])]
    reduce_scatter x1 -> x0, waiting for transfers between devices: 12.8 us -> none  [body(): lax.psum_scatter(scatter_term.reshape(dp_count * 2 * per_shard, column_to...]
  transfers between devices with their start and end apart: 5 -> 17, of which waited for: 4 -> 12; matrix products, arithmetic and copies ran while one was open for 6% -> 13% of each run, Pallas kernels for 0% -> 0%
where the time goes in v2:
time: 254 us; the launch traced here: 253 us
  waiting for transfers between devices  155 us (61%)
  matrix products  32.8 us (13%)
  local copies, waits for them, and re-layouts  19.4 us (8%)
  starting transfers between devices  16.8 us (7%)
  between operations  14.5 us (6%)
  other arithmetic  14.2 us (6%)
    all_gather x1, waiting for transfers between devices, body(): lax.all_gather(weight_piece, ('dp', 'groups', 'pair'), axis=0, tiled=True)  115 us
    ppermute x6, waiting for transfers between devices, partner(): lax.ppermute(x, axis, [(i, i ^ flip) for i in range(lax.axis_size(axis))])  28.3 us
    dot_general x9, matrix products, dot_nn(): jnp.dot(a, b, precision=precision, preferred_element_type=jnp.float32)  26.7 us
    ppermute x10, waiting for transfers between devices, swap(): return lax.ppermute(x, axis, [(0, 1), (1, 0)])  11.6 us
    ppermute x6, starting transfers between devices, partner(): lax.ppermute(x, axis, [(i, i ^ flip) for i in range(lax.axis_size(axis))])  11.1 us
    dot_general x6, matrix products, dot_nt(): lax.dot_general(a, b, (((1,), (1,)), ((), ())), precision=precision, pref...  6.13 us
    ppermute x10, starting transfers between devices, swap(): return lax.ppermute(x, axis, [(0, 1), (1, 0)])  5.71 us
  transfers between devices with their start and end apart: 17, of which 12 were waited for; matrix products, arithmetic and copies ran while one was open for 13% of the time, Pallas kernels for 0%

profile of v2, /device:TPU:0, one launch (start us, length us, event | category | flops | bytes accessed | tf_op | source)
XLA Modules:
  0.0 252.9 jit_solution(1215101329605554401)
XLA Ops:
  7.2 2.3 constant_dynamic-slice_fusion.1
  10.9 1.9 constant_dynamic-slice_fusion.2
  12.8 2.5 %copy.34 = bf16[1,512,2048]{1,2,0:T(8,128)(2,1)} copy(bf16[1,512,2048]{2,1,0:T(8,128)(2,1)S(1)} %constant_dynamic-slice_fusion.2) | data formatting | bytes 4194304 | tf_op jit(solution)/shard_map/dynamic_slice | solution.py:79
  18.2 3.6 %fusion.13 = bf16[512,16]{0,1:T(8,128)(2,1)S(1)} fusion(bf16[4096,16]{0,1:T(8,128)(2,1)S(1)} %copy-done, bf16[1,512,4096]{2,1,0:T(8,128)(2,1)} %param.8), kind=kOutput, calls=%fused_computation.20 | convolution fusion | flops 67117056 | bytes 4341760 | tf_op jit(solution)/shard_map/dot_general | solution.py:17
  21.8 2.7 %fusion.76 = f32[512,2048]{0,1:T(8,128)} fusion(bf16[512,16]{0,1:T(8,128)(2,1)S(1)} %fusion.13, bf16[16,2048]{1,0:T(8,128)(2,1)S(1)} %copy-done.5), kind=kOutput, calls=%fused_computation.141 | convolution fusion | flops 33554432 | bytes 4276224 | tf_op jit(solution)/shard_map/dot_general | solution.py:17
  24.5 115.3 %all-gather.2.cloned.1.call-done = bf16[4096,2048]{1,0:T(8,128)(2,1)} async-done(((bf16[256,2048]{1,0:T(8,128)(2,1)}), bf16[4096,2048]{1,0:T(8,128)(2,1)}) %all-gather.2.cloned.1.call-update) | async-done | bytes 16777232 | tf_op jit(solution)/shard_map/all_gather | solution.py:77
  139.8 15.6 %multiply_reduce_fusion = (f32[512]{0:T(512)S(1)}, f32[512,2048]{0,1:T(8,128)S(1)}) fusion(f32[512,2048]{0,1:T(8,128)} %fusion.76, bf16[4096,2048]{1,0:T(8,128)(2,1)} %all-gather.2.cloned.1.call-done, bf16[1,512,4096]{2,1,0:T(8,128)(2,1)} %param.8, bf16[1,512,2048]{1,2,0:T(8,128)(2,1)} %copy.34), kind=kOutput, calls=%fused_computation.8 | convolution fusion | flops 8595177472 | bytes 31459328 | tf_op jit(solution)/shard_map/dot_general | solution.py:17
  157.1 2.0 collective-permute-done
  159.1 1.7 divide_convert_fusion
  160.8 1.9 collective-permute-start.4
  162.7 2.4 collective-permute-start.6
  166.2 6.7 %collective-permute-done.2 = bf16[64,2048]{1,0:T(8,128)(2,1)S(1)} collective-permute-done((bf16[64,2048]{1,0:T(8,128)(2,1)S(1)}, bf16[64,2048]{1,0:T(8,128)(2,1)S(1)}, u32[]{:S(2)}, u32[]{:S(2)}) %collective-permute-start.2) | collective-permute-done | bytes 262176 | tf_op jit(solution)/shard_map/ppermute | solution.py:25
  172.8 9.3 %collective-permute-done.4 = bf16[64,2048]{1,0:T(8,128)(2,1)S(1)} collective-permute-done((bf16[64,2048]{1,0:T(8,128)(2,1)S(1)}, bf16[64,2048]{1,0:T(8,128)(2,1)S(1)}, u32[]{:S(2)}, u32[]{:S(2)}) %collective-permute-start.4) | collective-permute-done | bytes 262176 | tf_op jit(solution)/shard_map/ppermute | solution.py:25
  187.7 4.2 %collective-permute-done.8 = f32[162,256]{1,0:T(8,128)S(1)} collective-permute-done((f32[162,256]{1,0:T(8,128)S(1)}, f32[162,256]{1,0:T(8,128)S(1)}, u32[]{:S(2)}, u32[]{:S(2)}) %collective-permute-start.8) | collective-permute-done | bytes 165920 | tf_op jit(solution)/shard_map/ppermute | solution.py:21
  193.7 2.6 %fusion.74 = (f32[256]{0:T(256)}, f32[1,256]{1,0:T(1,128)}, f32[1,256]{1,0:T(1,128)}) fusion(f32[]{:T(128)} %broadcast.200, f32[162,256]{1,0:T(8,128)} %copy-done.4), kind=kLoop, calls=%fused_computation.140 | loop fusion | flops 512 | bytes 5124 | tf_op jit(solution)/shard_map/rsqrt | solution.py:116
  200.0 1.7 fusion.73
  203.2 1.6 copy.39
  207.3 1.6 pad_slice_fusion.4
  208.9 1.6 copy.40
  213.6 3.0 %fusion.12 = f32[512]{0:T(512)S(1)} fusion(f32[2048]{0:T(1024)S(1)} %convert_element_type.63, s32[512]{0:T(512)} %bitcast.79, f32[512,2048]{0,1:T(8,128)} %copy-done.1, f32[64,2048]{1,0:T(8,128)S(1)} %get-tuple-element.26, bf16[64,2048]{1,0:T(8,128)(2,1)S(1)} %get-tuple-element.23, f32[64]{0:T(128)S(1)} %get-tuple-element.20, f32[64]{0:T(128)S(1)} %get-tuple-element.19), kind=kOutput, calls=%fused_computation.18 | convolution fusion | flops 136150528 | bytes 4993536 | tf_op jit(solution)/shard_map/dot_general | solution.py:11
  219.2 2.2 collective-permute-done.10
  224.2 4.0 %collective-permute-start.12 = (f32[33,1024]{1,0:T(8,128)S(1)}, f32[33,1024]{1,0:T(8,128)S(1)}, u32[]{:S(2)}, u32[]{:S(2)}) collective-permute-start(f32[33,1024]{1,0:T(8,128)S(1)} %dynamic-slice_add_fusion), channel_id=1, source_target_pairs={{0,4},{4,0},{8,12},{12,8},{1,5},{5,1},{9,13},{13,9},{2,6},{6,2},{1... | collective-permute-start | bytes 405512 | tf_op jit(solution)/shard_map/ppermute | solution.py:25
  230.9 4.7 %collective-permute-done.12 = f32[33,1024]{1,0:T(8,128)S(1)} collective-permute-done((f32[33,1024]{1,0:T(8,128)S(1)}, f32[33,1024]{1,0:T(8,128)S(1)}, u32[]{:S(2)}, u32[]{:S(2)}) %collective-permute-start.12) | collective-permute-done | bytes 135200 | tf_op jit(solution)/shard_map/ppermute | solution.py:25
  235.6 7.6 %collective-permute-done.13 = f32[33,1024]{1,0:T(8,128)S(1)} collective-permute-done((f32[33,1024]{1,0:T(8,128)S(1)}, f32[33,1024]{1,0:T(8,128)S(1)}, u32[]{:S(2)}, u32[]{:S(2)}) %collective-permute-start.13) | collective-permute-done | bytes 135200 | tf_op jit(solution)/shard_map/ppermute | solution.py:25
  (136 shorter events, 35.8 us)
Async XLA Ops:
  7.2 11.0 %copy-start = (bf16[4096,16]{0,1:T(8,128)(2,1)S(1)}, bf16[4096,16]{0,1:T(8,128)(2,1)}, u32[]{:S(2)}) copy-start(bf16[4096,16]{0,1:T(8,128)(2,1)} %param.11) | copy-start | bytes 393220
  7.2 132.6 %all-gather.2.cloned.1.call-start = ((), (), s32[]{:S(2)}) async-start(), calls=%async_computation | async-start | bytes 17825792 | tf_op jit(solution)/shard_map/all_gather | solution.py:77
  10.4 146.6 %collective-permute-start.9 = (s32[32,4]{0,1:T(4,128)S(1)}, s32[32,4]{0,1:T(4,128)S(1)}, u32[]{:S(2)}, u32[]{:S(2)}) collective-permute-start(s32[32,4]{0,1:T(4,128)S(1)} %dynamic-slice_bitcast_fusion), channel_id=1, source_target_pairs={{0,1},{1,0},{2,3},{3,2},{4,5},{5,4},{6,7},{7,6},{8,9},{9,8},{10,11... | collective-permute-start | bytes 1544 | tf_op jit(solution)/shard_map/ppermute | solution.py:21
  16.7 142.4 %copy-start.19 = (f32[64]{0:T(128)}, f32[64]{0:T(128)S(1)}, u32[]{:S(2)}) copy-start(f32[64]{0:T(128)S(1)} %convert_reduce_fusion) | copy-start | bytes 772
  21.8 133.6 %copy-start.8 = (bf16[512,16]{0,1:T(8,128)(2,1)}, bf16[512,16]{0,1:T(8,128)(2,1)S(1)}, u32[]{:S(2)}) copy-start(bf16[512,16]{0,1:T(8,128)(2,1)S(1)} %fusion.13) | copy-start | bytes 49156
  155.4 10.7 %copy-start.1 = (f32[512,2048]{0,1:T(8,128)}, f32[512,2048]{0,1:T(8,128)S(1)}, u32[]{:S(2)}) copy-start(f32[512,2048]{0,1:T(8,128)S(1)} %get-tuple-element.22) | copy-start | bytes 12582916
  155.4 3.7 %collective-permute-start = (f32[512]{0:T(512)S(1)}, f32[512]{0:T(512)S(1)}, u32[]{:S(2)}, u32[]{:S(2)}) collective-permute-start(f32[512]{0:T(512)S(1)} %get-tuple-element.21), channel_id=1, source_target_pairs={{0,2},{2,0},{1,3},{3,1},{4,6},{6,4},{5,7},{7,5},{8,10},{10,8},{9,1... | collective-permute-start | bytes 6152 | tf_op jit(solution)/shard_map/ppermute | solution.py:21
  159.1 27.8 %copy-start.11 = (f32[512]{0:T(512)}, f32[512]{0:T(512)S(1)}, u32[]{:S(2)}) copy-start(f32[512]{0:T(512)S(1)} %add_rsqrt_fusion) | copy-start | bytes 6148
  160.8 12.0 %collective-permute-start.2 = (bf16[64,2048]{1,0:T(8,128)(2,1)S(1)}, bf16[64,2048]{1,0:T(8,128)(2,1)S(1)}, u32[]{:S(2)}, u32[]{:S(2)}) collective-permute-start(bf16[64,2048]{1,0:T(8,128)(2,1)S(1)} %get-tuple-element.23), channel_id=1, source_target_pairs={{0,4},{4,0},{8,12},{12,8},{1,5},{5,1},{9,13},{13,9},{2,6},{6,2},{1... | collective-permute-start | bytes 786440 | tf_op jit(solution)/shard_map/ppermute | solution.py:25
  160.8 21.4 %collective-permute-start.4 = (bf16[64,2048]{1,0:T(8,128)(2,1)S(1)}, bf16[64,2048]{1,0:T(8,128)(2,1)S(1)}, u32[]{:S(2)}, u32[]{:S(2)}) collective-permute-start(bf16[64,2048]{1,0:T(8,128)(2,1)S(1)} %get-tuple-element.23), channel_id=1, source_target_pairs={{0,8},{4,12},{8,0},{12,4},{1,9},{5,13},{9,1},{13,5},{2,10},{6,14},... | collective-permute-start | bytes 786440 | tf_op jit(solution)/shard_map/ppermute | solution.py:25
  162.7 19.4 %collective-permute-start.6 = (bf16[64,2048]{1,0:T(8,128)(2,1)S(1)}, bf16[64,2048]{1,0:T(8,128)(2,1)S(1)}, u32[]{:S(2)}, u32[]{:S(2)}) collective-permute-start(bf16[64,2048]{1,0:T(8,128)(2,1)S(1)} %get-tuple-element.23), channel_id=1, source_target_pairs={{0,12},{4,8},{8,4},{12,0},{1,13},{5,9},{9,5},{13,1},{2,14},{6,10},... | collective-permute-start | bytes 786440 | tf_op jit(solution)/shard_map/ppermute | solution.py:25
  165.2 17.5 %collective-permute-start.1 = (bf16[64,2048]{1,0:T(8,128)(2,1)S(1)}, bf16[64,2048]{1,0:T(8,128)(2,1)S(1)}, u32[]{:S(2)}, u32[]{:S(2)}) collective-permute-start(bf16[64,2048]{1,0:T(8,128)(2,1)S(1)} %get-tuple-element.23), channel_id=1, source_target_pairs={{0,1},{1,0},{2,3},{3,2},{4,5},{5,4},{6,7},{7,6},{8,9},{9,8},{10,11... | collective-permute-start | bytes 786440 | tf_op jit(solution)/shard_map/ppermute | solution.py:21
  172.8 10.2 %collective-permute-start.3 = (bf16[64,2048]{1,0:T(8,128)(2,1)S(1)}, bf16[64,2048]{1,0:T(8,128)(2,1)S(1)}, u32[]{:S(2)}, u32[]{:S(2)}) collective-permute-start(bf16[64,2048]{1,0:T(8,128)(2,1)S(1)} %collective-permute-done.2), channel_id=1, source_target_pairs={{0,1},{1,0},{2,3},{3,2},{4,5},{5,4},{6,7},{7,6},{8,9},{9,8},{10,11... | collective-permute-start | bytes 786440 | tf_op jit(solution)/shard_map/ppermute | solution.py:21
  182.2 1.5 collective-permute-start.5
  182.2 1.9 collective-permute-start.7
  185.4 6.5 %collective-permute-start.8 = (f32[162,256]{1,0:T(8,128)S(1)}, f32[162,256]{1,0:T(8,128)S(1)}, u32[]{:S(2)}, u32[]{:S(2)}) collective-permute-start(f32[162,256]{1,0:T(8,128)S(1)} %pad_maximum_fusion.3), channel_id=1, source_target_pairs={{0,2},{2,0},{1,3},{3,1},{4,6},{6,4},{5,7},{7,5},{8,10},{10,8},{9,1... | collective-permute-start | bytes 497672 | tf_op jit(solution)/shard_map/ppermute | solution.py:21
  217.1 4.3 %collective-permute-start.10 = (f32[17,576]{1,0:T(8,128)S(1)}, f32[17,576]{1,0:T(8,128)S(1)}, u32[]{:S(2)}, u32[]{:S(2)}) collective-permute-start(f32[17,576]{1,0:T(8,128)S(1)} %select_maximum_fusion), channel_id=1, source_target_pairs={{0,2},{2,0},{1,3},{3,1},{4,6},{6,4},{5,7},{7,5},{8,10},{10,8},{9,1... | collective-permute-start | bytes 117512 | tf_op jit(solution)/shard_map/ppermute | solution.py:21
  219.2 11.7 %copy-start.22 = (f32[128]{0:T(128)S(1)}, f32[128]{0:T(128)}, u32[]{:S(2)}) copy-start(f32[128]{0:T(128)} %copy-done.21) | copy-start | bytes 1540
  219.2 11.7 %copy-start.23 = (f32[128]{0:T(128)S(1)}, f32[128]{0:T(128)}, u32[]{:S(2)}) copy-start(f32[128]{0:T(128)} %get-tuple-element.15) | copy-start | bytes 1540
  222.7 1.5 collective-permute-start.11
  224.2 11.4 %collective-permute-start.12 = (f32[33,1024]{1,0:T(8,128)S(1)}, f32[33,1024]{1,0:T(8,128)S(1)}, u32[]{:S(2)}, u32[]{:S(2)}) collective-permute-start(f32[33,1024]{1,0:T(8,128)S(1)} %dynamic-slice_add_fusion), channel_id=1, source_target_pairs={{0,4},{4,0},{8,12},{12,8},{1,5},{5,1},{9,13},{13,9},{2,6},{6,2},{1... | collective-permute-start | bytes 405512 | tf_op jit(solution)/shard_map/ppermute | solution.py:25
  228.2 15.0 %collective-permute-start.13 = (f32[33,1024]{1,0:T(8,128)S(1)}, f32[33,1024]{1,0:T(8,128)S(1)}, u32[]{:S(2)}, u32[]{:S(2)}) collective-permute-start(f32[33,1024]{1,0:T(8,128)S(1)} %dynamic-slice_add_fusion), channel_id=1, source_target_pairs={{0,8},{4,12},{8,0},{12,4},{1,9},{5,13},{9,1},{13,5},{2,10},{6,14},... | collective-permute-start | bytes 405512 | tf_op jit(solution)/shard_map/ppermute | solution.py:25
  229.5 13.7 %collective-permute-start.14 = (f32[33,1024]{1,0:T(8,128)S(1)}, f32[33,1024]{1,0:T(8,128)S(1)}, u32[]{:S(2)}, u32[]{:S(2)}) collective-permute-start(f32[33,1024]{1,0:T(8,128)S(1)} %dynamic-slice_add_fusion), channel_id=1, source_target_pairs={{0,12},{4,8},{8,4},{12,0},{1,13},{5,9},{9,5},{13,1},{2,14},{6,10},... | collective-permute-start | bytes 405512 | tf_op jit(solution)/shard_map/ppermute | solution.py:25
  243.2 1.5 collective-permute-start.15
  (17 other events, 94.9 us)
Sparse Core Ops, SparseCore 0:
  10.2 129.5 all-gather.1

commit v3 on v2

--- a/solution.py
+++ b/solution.py
@@ -5,6 +5,7 @@
 
 inverse_temp = 50.0
 highest = lax.Precision.HIGHEST
+chunk_count = 2
 
 
 def dot_nt(a, b, precision=None):
@@ -70,16 +71,52 @@
     target_c = col_id[None, :] == (rel_row // per_shard * docs + rel_row % per_shard)[:, None]
     target_o = target_c[:per_shard]
 
-    copies = lax.axis_size("groups") * lax.axis_size("pair")
-    copy_rows = frozen_weight.shape[0] // copies
-    copy_idx = lax.axis_index("groups") * lax.axis_size("pair") + side
-    weight_piece = lax.dynamic_slice_in_dim(frozen_weight, copy_idx * copy_rows, copy_rows, 0)
-    weight = lax.all_gather(weight_piece, ("dp", "groups", "pair"), axis=0, tiled=True)
+    group = lax.axis_index("groups")
+    quarter = frozen_weight.shape[0] // 4
+    shard_rows = frozen_weight.shape[0]
+    chunk = cols // chunk_count
+    order = list(range(1, dp, 2)) + list(range(dp - 2 + dp % 2, 0, -2))
+    order = [0] + order
+    hops = [(order[i], order[(i + 1) % dp]) for i in range(dp)]
+    place = jnp.array([order.index(i) for i in range(dp)], jnp.int32)[shard]
+    order_table = jnp.array(order, jnp.int32)
+    quarters = [
+        (group * 2 + side),
+        ((1 - group) * 2 + side),
+        (group * 2 + 1 - side),
+        ((1 - group) * 2 + 1 - side),
+    ]
+    moving = [
+        lax.dynamic_slice(frozen_weight, (quarters[0] * quarter, h * chunk), (quarter, chunk))
+        for h in range(chunk_count)
+    ]
     lora_mid = dot_nn(tokens, adapter_down).astype(jnp.bfloat16)
     own_cols = lax.dynamic_slice_in_dim(tokens, lax.axis_index("mp") * cols, cols, 1)
-    states = own_cols.astype(jnp.float32) + dot_nn(tokens, weight) + dot_nn(lora_mid, adapter_up)
-    states_b = states.astype(jnp.bfloat16)
-    squares = sum_over(jnp.sum(states * states, axis=1), "mp")
+    own_tokens = lax.dynamic_slice_in_dim(tokens, shard * shard_rows, shard_rows, 1)
+    states = []
+    for h in range(chunk_count):
+        part = slice(h * chunk, (h + 1) * chunk)
+        states.append(
+            own_cols[:, part].astype(jnp.float32)
+            + dot_nn(own_tokens, frozen_weight[:, part])
+            + dot_nn(lora_mid, adapter_up[:, part])
+        )
+    for step in range(1, dp):
+        origin = order_table[(place - step) % dp]
+        step_tokens = jnp.concatenate(
+            [
+                lax.dynamic_slice_in_dim(tokens, origin * shard_rows + q * quarter, quarter, 1)
+                for q in quarters
+            ],
+            axis=1,
+        )
+        for h in range(chunk_count):
+            moving[h] = lax.ppermute(moving[h], "dp", hops)
+            across = swap(moving[h], "groups")
+            rows = [moving[h], across, swap(moving[h], "pair"), swap(across, "pair")]
+            states[h] = states[h] + dot_nn(step_tokens, jnp.concatenate(rows, axis=0))
+    states_b = [x.astype(jnp.bfloat16) for x in states]
+    squares = sum_over(sum(jnp.sum(x * x, axis=1) for x in states), "mp")
     inv_rms = lax.rsqrt(squares / width + 1e-05)
 
     gain = norm_gain_vector.astype(jnp.float32)
@@ -87,8 +124,14 @@
     member = labels[None, :] == jnp.arange(docs, dtype=jnp.int32)[:, None]
     member_f = member.astype(jnp.float32)
     counts = jnp.sum(member_f, axis=1)
-    normed = (states * inv_rms[:, None] * gain).astype(jnp.bfloat16)
-    doc_sums = dot_nn(member.astype(jnp.bfloat16), normed)
+    member_b = member.astype(jnp.bfloat16)
+    doc_sums = jnp.concatenate(
+        [
+            dot_nn(member_b, (x * inv_rms[:, None] * g[None, :]).astype(jnp.bfloat16))
+            for x, g in zip(states, jnp.split(gain, chunk_count))
+        ],
+        axis=1,
+    )
     pooled = (doc_sums / counts[:, None]).astype(jnp.bfloat16)
 
     own_blocks = [pooled] + [partner(pooled, "dp", j) for j in range(1, dp)]
@@ -152,9 +195,11 @@
 
     gained = per_doc * gain
     up_f = adapter_up.astype(jnp.float32)
-    tok_doc = dot_nt(gained.astype(jnp.bfloat16), states_b)
+    gained_b = jnp.split(gained.astype(jnp.bfloat16), chunk_count, axis=1)
+    tok_doc = sum(dot_nt(g, x) for g, x in zip(gained_b, states_b))
     tok_dots = jnp.sum(jnp.where(member, tok_doc, 0.0), axis=0)[None]
-    up_states = dot_nt(adapter_up, states_b)
+    up_parts = jnp.split(adapter_up, chunk_count, axis=1)
+    up_states = sum(dot_nt(u, x) for u, x in zip(up_parts, states_b))
     up_gained = dot_nt(up_f, gained, highest)
     small = sum_over(
         jnp.concatenate(
@@ -174,8 +219,9 @@
     ).astype(jnp.bfloat16)
     mid_t = lora_mid.astype(jnp.float32).T
     a_grad = dot_nn(mid_grad, own_cols)
-    b_grad = dot_nn(dot_nt(mid_t * inv_rms, member_f, highest), gained, highest) - dot_nn(
-        (mid_t * alpha).astype(jnp.bfloat16), states_b
+    mid_alpha = (mid_t * alpha).astype(jnp.bfloat16)
+    b_grad = dot_nn(dot_nt(mid_t * inv_rms, member_f, highest), gained, highest) - jnp.concatenate(
+        [dot_nn(mid_alpha, x) for x in states_b], axis=1
     )
     gain_grad = jnp.sum(per_doc * doc_sums, axis=0) / gain
 

time: 254 us -> 199 us (0.78)
  waiting for transfers between devices: 155 us -> 84.9 us
  starting transfers between devices: 16.8 us -> 31.8 us
  between operations: 14.5 us -> 5.37 us
  matrix products: 32.8 us -> 40.4 us
    all_gather x1 -> x0, waiting for transfers between devices: 115 us -> none  [body(): lax.all_gather(weight_piece, ('dp', 'groups', 'pair'), axis=0, tiled=True)]
    ppermute x10 -> x28, waiting for transfers between devices: 11.6 us -> 47 us  [swap(): return lax.ppermute(x, axis, [(0, 1), (1, 0)])]
    dot_general x9 -> x19, matrix products: 26.7 us -> 35.9 us  [dot_nn(): jnp.dot(a, b, precision=precision, preferred_element_type=jnp.float32)]
    ppermute x0 -> x6, waiting for transfers between devices: none -> 8.98 us  [body(): moving[h] = lax.ppermute(moving[h], 'dp', hops)]
    ppermute x10 -> x28, starting transfers between devices: 5.71 us -> 13.9 us  [swap(): return lax.ppermute(x, axis, [(0, 1), (1, 0)])]
    ppermute x0 -> x6, starting transfers between devices: none -> 7.02 us  [body(): moving[h] = lax.ppermute(moving[h], 'dp', hops)]
    dot_general x6 -> x8, matrix products: 6.13 us -> 4.47 us  [dot_nt(): lax.dot_general(a, b, (((1,), (1,)), ((), ())), precision=precision, pref...]
  transfers between devices with their start and end apart: 17 -> 40, of which waited for: 12 -> 21; matrix products, arithmetic and copies ran while one was open for 13% -> 21% of each run, Pallas kernels for 0% -> 0%
where the time goes in v3:
time: 199 us; the launch traced here: 198 us
  waiting for transfers between devices  84.9 us (43%)
  matrix products  40.4 us (20%)
  starting transfers between devices  31.8 us (16%)
  local copies, waits for them, and re-layouts  20.7 us (10%)
  other arithmetic  14.9 us (7%)
  between operations  5.37 us (3%)
    ppermute x28, waiting for transfers between devices, swap(): return lax.ppermute(x, axis, [(0, 1), (1, 0)])  47 us
    dot_general x19, matrix products, dot_nn(): jnp.dot(a, b, precision=precision, preferred_element_type=jnp.float32)  35.9 us
    ppermute x6, waiting for transfers between devices, partner(): lax.ppermute(x, axis, [(i, i ^ flip) for i in range(lax.axis_size(axis))])  29 us
    ppermute x28, starting transfers between devices, swap(): return lax.ppermute(x, axis, [(0, 1), (1, 0)])  13.9 us
    ppermute x6, starting transfers between devices, partner(): lax.ppermute(x, axis, [(i, i ^ flip) for i in range(lax.axis_size(axis))])  10.8 us
    ppermute x6, waiting for transfers between devices, body(): moving[h] = lax.ppermute(moving[h], 'dp', hops)  8.98 us
    ppermute x6, starting transfers between devices, body(): moving[h] = lax.ppermute(moving[h], 'dp', hops)  7.02 us
    dot_general x8, matrix products, dot_nt(): lax.dot_general(a, b, (((1,), (1,)), ((), ())), precision=precision, pref...  4.47 us
  transfers between devices with their start and end apart: 40, of which 21 were waited for; matrix products, arithmetic and copies ran while one was open for 21% of the time, Pallas kernels for 0%

profile of v3, /device:TPU:0, one launch (start us, length us, event | category | flops | bytes accessed | tf_op | source)
XLA Modules:
  0.0 198.0 jit_solution(11532910764892223414)
XLA Ops:
  2.0 3.1 %collective-permute-start = (bf16[256,1024]{1,0:T(8,128)(2,1)S(1)}, bf16[256,1024]{1,0:T(8,128)(2,1)}, u32[]{:S(2)}, u32[]{:S(2)}) collective-permute-start(bf16[256,1024]{1,0:T(8,128)(2,1)S(1)} %get-tuple-element.11), channel_id=1, source_target_pairs={{0,4},{4,12},{12,8},{8,0},{1,5},{5,13},{13,9},{9,1},{2,6},{6,14},{... | collective-permute-start | bytes 1572872 | tf_op jit(solution)/shard_map/ppermute | solution.py:114
  5.1 2.6 %collective-permute-start.12 = (bf16[256,1024]{1,0:T(8,128)(2,1)S(1)}, bf16[256,1024]{1,0:T(8,128)(2,1)}, u32[]{:S(2)}, u32[]{:S(2)}) collective-permute-start(bf16[256,1024]{1,0:T(8,128)(2,1)S(1)} %get-tuple-element.12), channel_id=1, source_target_pairs={{0,4},{4,12},{12,8},{8,0},{1,5},{5,13},{13,9},{9,1},{2,6},{6,14},{... | collective-permute-start | bytes 1572872 | tf_op jit(solution)/shard_map/ppermute | solution.py:114
  13.0 4.7 %fusion.52 = f32[512,1024]{1,0:T(8,128)} fusion(bf16[1024,2048]{1,0:T(8,128)(2,1)} %param.12, bf16[1,512,4096]{2,1,0:T(8,128)(2,1)} %param.10, s32[]{:T(128)S(6)} %select_n.161), kind=kOutput, calls=%fused_computation.62 | convolution fusion | flops 1073741824 | bytes 5242884 | tf_op jit(solution)/shard_map/dot_general | solution.py:18
  17.7 3.8 %fusion.50 = f32[512,1024]{1,0:T(8,128)} fusion(bf16[1024,2048]{1,0:T(8,128)(2,1)S(1)} %copy-done.17, bf16[1,512,4096]{2,1,0:T(8,128)(2,1)} %param.10, s32[]{:T(128)S(6)} %select_n.161), kind=kOutput, calls=%fused_computation.58 | convolution fusion | flops 1073741824 | bytes 5242884 | tf_op jit(solution)/shard_map/dot_general | solution.py:18
  21.5 3.2 %dynamic-slice_bitcast_fusion = bf16[512,2048]{1,0:T(8,128)(2,1)} fusion(bf16[1,512,4096]{2,1,0:T(8,128)(2,1)} %param.10, s32[]{:T(128)S(6)} %select_n.160), kind=kLoop, calls=%fused_computation.64 | loop fusion | bytes 4194308 | tf_op jit(solution)/shard_map/dynamic_slice | solution.py:94
  25.4 3.5 %fusion.61 = bf16[512,16]{0,1:T(8,128)(2,1)S(1)} fusion(bf16[4096,16]{0,1:T(8,128)(2,1)S(1)} %copy-done, bf16[1,512,4096]{2,1,0:T(8,128)(2,1)} %param.10), kind=kOutput, calls=%fused_computation.70 | convolution fusion | flops 67117056 | bytes 4341760 | tf_op jit(solution)/shard_map/dot_general | solution.py:18
  34.8 9.3 %collective-permute-done.1 = bf16[256,1024]{1,0:T(8,128)(2,1)} collective-permute-done((bf16[256,1024]{1,0:T(8,128)(2,1)}, bf16[256,1024]{1,0:T(8,128)(2,1)}, u32[]{:S(2)}, u32[]{:S(2)}) %collective-permute-start.1) | collective-permute-done | bytes 524320 | tf_op jit(solution)/shard_map/ppermute | solution.py:22
  48.2 7.2 %collective-permute-done.13 = bf16[256,1024]{1,0:T(8,128)(2,1)} collective-permute-done((bf16[256,1024]{1,0:T(8,128)(2,1)}, bf16[256,1024]{1,0:T(8,128)(2,1)}, u32[]{:S(2)}, u32[]{:S(2)}) %collective-permute-start.13) | collective-permute-done | bytes 524320 | tf_op jit(solution)/shard_map/ppermute | solution.py:22
  60.0 6.6 %collective-permute-done.5 = bf16[256,1024]{1,0:T(8,128)(2,1)} collective-permute-done((bf16[256,1024]{1,0:T(8,128)(2,1)}, bf16[256,1024]{1,0:T(8,128)(2,1)}, u32[]{:S(2)}, u32[]{:S(2)}) %collective-permute-start.5) | collective-permute-done | bytes 524320 | tf_op jit(solution)/shard_map/ppermute | solution.py:22
  72.8 2.9 %fusion.2 = f32[512,1024]{1,0:T(8,128)S(1)} fusion(bf16[256,1024]{1,0:T(8,128)(2,1)} %collective-permute-done.3, bf16[256,1024]{1,0:T(8,128)(2,1)} %copy-done.35, bf16[256,1024]{1,0:T(8,128)(2,1)} %collective-permute-done.1, bf16[256,1024]{1,0:T(8,128)(2,1)} %collective-permute-done, bf16[512,256]{1,0:T(8,128)(2,1)S(1)} %get-tuple-element.19, ...), kind=kOutput, calls=%fused_computation.4 | convolution fusion | flops 1086324736 | bytes 5242880 | tf_op jit(solution)/shard_map/dot_general | solution.py:18
  77.8 4.3 %collective-permute-done.20 = bf16[256,1024]{1,0:T(8,128)(2,1)} collective-permute-done((bf16[256,1024]{1,0:T(8,128)(2,1)}, bf16[256,1024]{1,0:T(8,128)(2,1)}, u32[]{:S(2)}, u32[]{:S(2)}) %collective-permute-start.20) | collective-permute-done | bytes 524320 | tf_op jit(solution)/shard_map/ppermute | solution.py:114
  83.6 2.8 %fusion.26 = f32[512,1024]{1,0:T(8,128)S(1)} fusion(bf16[256,1024]{1,0:T(8,128)(2,1)} %collective-permute-done.15, bf16[256,1024]{1,0:T(8,128)(2,1)} %collective-permute-done.14, bf16[256,1024]{1,0:T(8,128)(2,1)} %collective-permute-done.13, bf16[256,1024]{1,0:T(8,128)(2,1)} %collective-permute-done.12, bf16[512,256]{1,0:T(8,128)(2,1)S(1)} %get-tuple-element.19, ...), kind=kOutput, calls=%fused_computation.28 | convolution fusion | flops 1086324736 | bytes 5242880 | tf_op jit(solution)/shard_map/dot_general | solution.py:18
  88.9 2.6 %fusion.10 = f32[512,1024]{1,0:T(8,128)S(1)} fusion(bf16[256,1024]{1,0:T(8,128)(2,1)S(1)} %collective-permute-done.7, bf16[256,1024]{1,0:T(8,128)(2,1)} %collective-permute-done.6, bf16[256,1024]{1,0:T(8,128)(2,1)} %collective-permute-done.5, bf16[256,1024]{1,0:T(8,128)(2,1)} %collective-permute-done.4, bf16[512,256]{1,0:T(8,128)(2,1)S(1)} %get-tuple-element.15, ...), kind=kOutput, calls=%fused_computation.12 | convolution fusion | flops 1086324736 | bytes 5242880 | tf_op jit(solution)/shard_map/dot_general | solution.py:18
  92.2 7.6 %collective-permute-done.21 = bf16[256,1024]{1,0:T(8,128)(2,1)S(1)} collective-permute-done((bf16[256,1024]{1,0:T(8,128)(2,1)}, bf16[256,1024]{1,0:T(8,128)(2,1)S(1)}, u32[]{:S(2)}, u32[]{:S(2)}) %collective-permute-start.21) | collective-permute-done | bytes 524320 | tf_op jit(solution)/shard_map/ppermute | solution.py:22
  102.3 2.9 %multiply_reduce_fusion.3 = (f32[512]{0:T(512)S(1)}, f32[512,1024]{1,0:T(8,128)S(1)}) fusion(bf16[256,1024]{1,0:T(8,128)(2,1)S(1)} %collective-permute-done.11, bf16[256,1024]{1,0:T(8,128)(2,1)S(1)} %collective-permute-done.10, bf16[256,1024]{1,0:T(8,128)(2,1)S(1)} %collective-permute-done.9, bf16[256,1024]{1,0:T(8,128)(2,1)} %collective-permute-done.8, ...), kind=kOutput, calls=%fused_computation.60 | convolution fusion | flops 1090518528 | bytes 14682112 | tf_op jit(solution)/shard_map/dot_general | solution.py:18
  105.2 2.7 %multiply_reduce_fusion.2 = (f32[512]{0:T(512)S(1)}, f32[512,1024]{1,0:T(8,128)S(1)}) fusion(bf16[256,1024]{1,0:T(8,128)(2,1)S(1)} %collective-permute-done.23, bf16[256,1024]{1,0:T(8,128)(2,1)S(1)} %collective-permute-done.22, bf16[256,1024]{1,0:T(8,128)(2,1)S(1)} %collective-permute-done.21, bf16[256,1024]{1,0:T(8,128)(2,1)} %collective-permute-done.20, ...), kind=kOutput, calls=%fused_computation.56 | convolution fusion | flops 1090518528 | bytes 14682112 | tf_op jit(solution)/shard_map/dot_general | solution.py:18
  113.2 3.8 %collective-permute-start.30 = (bf16[64,2048]{1,0:T(8,128)(2,1)S(1)}, bf16[64,2048]{1,0:T(8,128)(2,1)S(1)}, u32[]{:S(2)}, u32[]{:S(2)}) collective-permute-start(bf16[64,2048]{1,0:T(8,128)(2,1)S(1)} %divide_convert_fusion), channel_id=1, source_target_pairs={{0,12},{4,8},{8,4},{12,0},{1,13},{5,9},{9,5},{13,1},{2,14},{6,10},... | collective-permute-start | bytes 786440 | tf_op jit(solution)/shard_map/ppermute | solution.py:26
  118.1 6.4 %collective-permute-done.26 = bf16[64,2048]{1,0:T(8,128)(2,1)S(1)} collective-permute-done((bf16[64,2048]{1,0:T(8,128)(2,1)S(1)}, bf16[64,2048]{1,0:T(8,128)(2,1)S(1)}, u32[]{:S(2)}, u32[]{:S(2)}) %collective-permute-start.26) | collective-permute-done | bytes 262176 | tf_op jit(solution)/shard_map/ppermute | solution.py:26
  124.5 10.0 %collective-permute-done.28 = bf16[64,2048]{1,0:T(8,128)(2,1)S(1)} collective-permute-done((bf16[64,2048]{1,0:T(8,128)(2,1)S(1)}, bf16[64,2048]{1,0:T(8,128)(2,1)S(1)}, u32[]{:S(2)}, u32[]{:S(2)}) %collective-permute-start.28) | collective-permute-done | bytes 262176 | tf_op jit(solution)/shard_map/ppermute | solution.py:26
  140.1 4.1 %collective-permute-done.32 = f32[162,256]{1,0:T(8,128)S(1)} collective-permute-done((f32[162,256]{1,0:T(8,128)S(1)}, f32[162,256]{1,0:T(8,128)S(1)}, u32[]{:S(2)}, u32[]{:S(2)}) %collective-permute-start.32) | collective-permute-done | bytes 165920 | tf_op jit(solution)/shard_map/ppermute | solution.py:22
  169.2 2.7 %collective-permute-done.34 = f32[17,576]{1,0:T(8,128)S(1)} collective-permute-done((f32[17,576]{1,0:T(8,128)S(1)}, f32[17,576]{1,0:T(8,128)S(1)}, u32[]{:S(2)}, u32[]{:S(2)}) %collective-permute-start.34) | collective-permute-done | bytes 39200 | tf_op jit(solution)/shard_map/ppermute | solution.py:22
  176.2 3.9 %collective-permute-start.36 = (f32[33,1024]{1,0:T(8,128)S(1)}, f32[33,1024]{1,0:T(8,128)S(1)}, u32[]{:S(2)}, u32[]{:S(2)}) collective-permute-start(f32[33,1024]{1,0:T(8,128)S(1)} %dynamic-slice_add_fusion), channel_id=1, source_target_pairs={{0,4},{4,0},{8,12},{12,8},{1,5},{5,1},{9,13},{13,9},{2,6},{6,2},{1... | collective-permute-start | bytes 405512 | tf_op jit(solution)/shard_map/ppermute | solution.py:26
  182.6 4.3 %collective-permute-done.36 = f32[33,1024]{1,0:T(8,128)S(1)} collective-permute-done((f32[33,1024]{1,0:T(8,128)S(1)}, f32[33,1024]{1,0:T(8,128)S(1)}, u32[]{:S(2)}, u32[]{:S(2)}) %collective-permute-start.36) | collective-permute-done | bytes 135200 | tf_op jit(solution)/shard_map/ppermute | solution.py:26
  186.9 8.2 %collective-permute-done.37 = f32[33,1024]{1,0:T(8,128)S(1)} collective-permute-done((f32[33,1024]{1,0:T(8,128)S(1)}, f32[33,1024]{1,0:T(8,128)S(1)}, u32[]{:S(2)}, u32[]{:S(2)}) %collective-permute-start.37) | collective-permute-done | bytes 135200 | tf_op jit(solution)/shard_map/ppermute | solution.py:26
  (226 shorter events, 79.3 us)
Async XLA Ops:
  2.0 27.0 %collective-permute-start = (bf16[256,1024]{1,0:T(8,128)(2,1)S(1)}, bf16[256,1024]{1,0:T(8,128)(2,1)}, u32[]{:S(2)}, u32[]{:S(2)}) collective-permute-start(bf16[256,1024]{1,0:T(8,128)(2,1)S(1)} %get-tuple-element.11), channel_id=1, source_target_pairs={{0,4},{4,12},{12,8},{8,0},{1,5},{5,13},{13,9},{9,1},{2,6},{6,14},{... | collective-permute-start | bytes 1572872 | tf_op jit(solution)/shard_map/ppermute | solution.py:114
  5.1 27.4 %collective-permute-start.12 = (bf16[256,1024]{1,0:T(8,128)(2,1)S(1)}, bf16[256,1024]{1,0:T(8,128)(2,1)}, u32[]{:S(2)}, u32[]{:S(2)}) collective-permute-start(bf16[256,1024]{1,0:T(8,128)(2,1)S(1)} %get-tuple-element.12), channel_id=1, source_target_pairs={{0,4},{4,12},{12,8},{8,0},{1,5},{5,13},{13,9},{9,1},{2,6},{6,14},{... | collective-permute-start | bytes 1572872 | tf_op jit(solution)/shard_map/ppermute | solution.py:114
  7.8 25.2 %collective-permute-start.33 = (s32[32,4]{0,1:T(4,128)S(1)}, s32[32,4]{0,1:T(4,128)S(1)}, u32[]{:S(2)}, u32[]{:S(2)}) collective-permute-start(s32[32,4]{0,1:T(4,128)S(1)} %fusion.132), channel_id=1, source_target_pairs={{0,1},{1,0},{2,3},{3,2},{4,5},{5,4},{6,7},{7,6},{8,9},{9,8},{10,11... | collective-permute-start | bytes 1544 | tf_op jit(solution)/shard_map/ppermute | solution.py:22
  29.0 15.1 %collective-permute-start.1 = (bf16[256,1024]{1,0:T(8,128)(2,1)}, bf16[256,1024]{1,0:T(8,128)(2,1)}, u32[]{:S(2)}, u32[]{:S(2)}) collective-permute-start(bf16[256,1024]{1,0:T(8,128)(2,1)} %collective-permute-done), channel_id=1, source_target_pairs={{0,16},{16,0},{1,17},{17,1},{2,18},{18,2},{3,19},{19,3},{4,20},{20... | collective-permute-start | bytes 1572872 | tf_op jit(solution)/shard_map/ppermute | solution.py:22
  30.8 15.3 %collective-permute-start.4 = (bf16[256,1024]{1,0:T(8,128)(2,1)}, bf16[256,1024]{1,0:T(8,128)(2,1)}, u32[]{:S(2)}, u32[]{:S(2)}) collective-permute-start(bf16[256,1024]{1,0:T(8,128)(2,1)} %collective-permute-done), channel_id=1, source_target_pairs={{0,4},{4,12},{12,8},{8,0},{1,5},{5,13},{13,9},{9,1},{2,6},{6,14},{... | collective-permute-start | bytes 1572872 | tf_op jit(solution)/shard_map/ppermute | solution.py:114
  32.4 22.9 %collective-permute-start.13 = (bf16[256,1024]{1,0:T(8,128)(2,1)}, bf16[256,1024]{1,0:T(8,128)(2,1)}, u32[]{:S(2)}, u32[]{:S(2)}) collective-permute-start(bf16[256,1024]{1,0:T(8,128)(2,1)} %collective-permute-done.12), channel_id=1, source_target_pairs={{0,16},{16,0},{1,17},{17,1},{2,18},{18,2},{3,19},{19,3},{4,20},{20... | collective-permute-start | bytes 1572872 | tf_op jit(solution)/shard_map/ppermute | solution.py:22
  33.0 22.4 %collective-permute-start.14 = (bf16[256,1024]{1,0:T(8,128)(2,1)}, bf16[256,1024]{1,0:T(8,128)(2,1)}, u32[]{:S(2)}, u32[]{:S(2)}) collective-permute-start(bf16[256,1024]{1,0:T(8,128)(2,1)} %collective-permute-done.12), channel_id=1, source_target_pairs={{0,1},{1,0},{2,3},{3,2},{4,5},{5,4},{6,7},{7,6},{8,9},{9,8},{10,11... | collective-permute-start | bytes 1572872 | tf_op jit(solution)/shard_map/ppermute | solution.py:22
  44.1 14.3 %collective-permute-start.16 = (bf16[256,1024]{1,0:T(8,128)(2,1)}, bf16[256,1024]{1,0:T(8,128)(2,1)}, u32[]{:S(2)}, u32[]{:S(2)}) collective-permute-start(bf16[256,1024]{1,0:T(8,128)(2,1)} %collective-permute-done.12), channel_id=1, source_target_pairs={{0,4},{4,12},{12,8},{8,0},{1,5},{5,13},{13,9},{9,1},{2,6},{6,14},{... | collective-permute-start | bytes 1572872 | tf_op jit(solution)/shard_map/ppermute | solution.py:114
  44.5 15.4 %collective-permute-start.3 = (bf16[256,1024]{1,0:T(8,128)(2,1)}, bf16[256,1024]{1,0:T(8,128)(2,1)}, u32[]{:S(2)}, u32[]{:S(2)}) collective-permute-start(bf16[256,1024]{1,0:T(8,128)(2,1)} %collective-permute-done.1), channel_id=1, source_target_pairs={{0,1},{1,0},{2,3},{3,2},{4,5},{5,4},{6,7},{7,6},{8,9},{9,8},{10,11... | collective-permute-start | bytes 1572872 | tf_op jit(solution)/shard_map/ppermute | solution.py:22
  46.1 20.4 %collective-permute-start.5 = (bf16[256,1024]{1,0:T(8,128)(2,1)}, bf16[256,1024]{1,0:T(8,128)(2,1)}, u32[]{:S(2)}, u32[]{:S(2)}) collective-permute-start(bf16[256,1024]{1,0:T(8,128)(2,1)} %collective-permute-done.4), channel_id=1, source_target_pairs={{0,16},{16,0},{1,17},{17,1},{2,18},{18,2},{3,19},{19,3},{4,20},{20... | collective-permute-start | bytes 1572872 | tf_op jit(solution)/shard_map/ppermute | solution.py:22
  55.3 15.9 %collective-permute-start.8 = (bf16[256,1024]{1,0:T(8,128)(2,1)}, bf16[256,1024]{1,0:T(8,128)(2,1)}, u32[]{:S(2)}, u32[]{:S(2)}) collective-permute-start(bf16[256,1024]{1,0:T(8,128)(2,1)} %collective-permute-done.4), channel_id=1, source_target_pairs={{0,4},{4,12},{12,8},{8,0},{1,5},{5,13},{13,9},{9,1},{2,6},{6,14},{... | collective-permute-start | bytes 1572872 | tf_op jit(solution)/shard_map/ppermute | solution.py:114
  58.4 19.4 %collective-permute-start.17 = (bf16[256,1024]{1,0:T(8,128)(2,1)}, bf16[256,1024]{1,0:T(8,128)(2,1)}, u32[]{:S(2)}, u32[]{:S(2)}) collective-permute-start(bf16[256,1024]{1,0:T(8,128)(2,1)} %collective-permute-done.16), channel_id=1, source_target_pairs={{0,16},{16,0},{1,17},{17,1},{2,18},{18,2},{3,19},{19,3},{4,20},{20... | collective-permute-start | bytes 1572872 | tf_op jit(solution)/shard_map/ppermute | solution.py:22
  60.0 22.2 %collective-permute-start.20 = (bf16[256,1024]{1,0:T(8,128)(2,1)}, bf16[256,1024]{1,0:T(8,128)(2,1)}, u32[]{:S(2)}, u32[]{:S(2)}) collective-permute-start(bf16[256,1024]{1,0:T(8,128)(2,1)} %collective-permute-done.16), channel_id=1, source_target_pairs={{0,4},{4,12},{12,8},{8,0},{1,5},{5,13},{13,9},{9,1},{2,6},{6,14},{... | collective-permute-start | bytes 1572872 | tf_op jit(solution)/shard_map/ppermute | solution.py:114
  68.4 18.0 %collective-permute-start.7 = (bf16[256,1024]{1,0:T(8,128)(2,1)}, bf16[256,1024]{1,0:T(8,128)(2,1)S(1)}, u32[]{:S(2)}, u32[]{:S(2)}) collective-permute-start(bf16[256,1024]{1,0:T(8,128)(2,1)} %collective-permute-done.5), channel_id=1, source_target_pairs={{0,1},{1,0},{2,3},{3,2},{4,5},{5,4},{6,7},{7,6},{8,9},{9,8},{10,11... | collective-permute-start | bytes 1572872 | tf_op jit(solution)/shard_map/ppermute | solution.py:22
  71.3 17.7 %collective-permute-start.9 = (bf16[256,1024]{1,0:T(8,128)(2,1)}, bf16[256,1024]{1,0:T(8,128)(2,1)S(1)}, u32[]{:S(2)}, u32[]{:S(2)}) collective-permute-start(bf16[256,1024]{1,0:T(8,128)(2,1)} %collective-permute-done.8), channel_id=1, source_target_pairs={{0,16},{16,0},{1,17},{17,1},{2,18},{18,2},{3,19},{19,3},{4,20},{20... | collective-permute-start | bytes 1572872 | tf_op jit(solution)/shard_map/ppermute | solution.py:22
  75.7 15.9 %collective-permute-start.18 = (bf16[256,1024]{1,0:T(8,128)(2,1)}, bf16[256,1024]{1,0:T(8,128)(2,1)S(1)}, u32[]{:S(2)}, u32[]{:S(2)}) collective-permute-start(bf16[256,1024]{1,0:T(8,128)(2,1)} %collective-permute-done.16), channel_id=1, source_target_pairs={{0,1},{1,0},{2,3},{3,2},{4,5},{5,4},{6,7},{7,6},{8,9},{9,8},{10,11... | collective-permute-start | bytes 1572872 | tf_op jit(solution)/shard_map/ppermute | solution.py:22
  77.8 22.0 %collective-permute-start.19 = (bf16[256,1024]{1,0:T(8,128)(2,1)}, bf16[256,1024]{1,0:T(8,128)(2,1)S(1)}, u32[]{:S(2)}, u32[]{:S(2)}) collective-permute-start(bf16[256,1024]{1,0:T(8,128)(2,1)} %collective-permute-done.17), channel_id=1, source_target_pairs={{0,1},{1,0},{2,3},{3,2},{4,5},{5,4},{6,7},{7,6},{8,9},{9,8},{10,11... | collective-permute-start | bytes 1572872 | tf_op jit(solution)/shard_map/ppermute | solution.py:22
  82.1 17.6 %collective-permute-start.21 = (bf16[256,1024]{1,0:T(8,128)(2,1)}, bf16[256,1024]{1,0:T(8,128)(2,1)S(1)}, u32[]{:S(2)}, u32[]{:S(2)}) collective-permute-start(bf16[256,1024]{1,0:T(8,128)(2,1)} %collective-permute-done.20), channel_id=1, source_target_pairs={{0,16},{16,0},{1,17},{17,1},{2,18},{18,2},{3,19},{19,3},{4,20},{20... | collective-permute-start | bytes 1572872 | tf_op jit(solution)/shard_map/ppermute | solution.py:22
  86.4 15.8 %collective-permute-start.10 = (bf16[256,1024]{1,0:T(8,128)(2,1)}, bf16[256,1024]{1,0:T(8,128)(2,1)S(1)}, u32[]{:S(2)}, u32[]{:S(2)}) collective-permute-start(bf16[256,1024]{1,0:T(8,128)(2,1)} %collective-permute-done.8), channel_id=1, source_target_pairs={{0,1},{1,0},{2,3},{3,2},{4,5},{5,4},{6,7},{7,6},{8,9},{9,8},{10,11... | collective-permute-start | bytes 1572872 | tf_op jit(solution)/shard_map/ppermute | solution.py:22
  113.1 21.4 %collective-permute-start.28 = (bf16[64,2048]{1,0:T(8,128)(2,1)S(1)}, bf16[64,2048]{1,0:T(8,128)(2,1)S(1)}, u32[]{:S(2)}, u32[]{:S(2)}) collective-permute-start(bf16[64,2048]{1,0:T(8,128)(2,1)S(1)} %divide_convert_fusion), channel_id=1, source_target_pairs={{0,8},{4,12},{8,0},{12,4},{1,9},{5,13},{9,1},{13,5},{2,10},{6,14},... | collective-permute-start | bytes 786440 | tf_op jit(solution)/shard_map/ppermute | solution.py:26
  113.2 21.3 %collective-permute-start.30 = (bf16[64,2048]{1,0:T(8,128)(2,1)S(1)}, bf16[64,2048]{1,0:T(8,128)(2,1)S(1)}, u32[]{:S(2)}, u32[]{:S(2)}) collective-permute-start(bf16[64,2048]{1,0:T(8,128)(2,1)S(1)} %divide_convert_fusion), channel_id=1, source_target_pairs={{0,12},{4,8},{8,4},{12,0},{1,13},{5,9},{9,5},{13,1},{2,14},{6,10},... | collective-permute-start | bytes 786440 | tf_op jit(solution)/shard_map/ppermute | solution.py:26
  117.1 18.0 %collective-permute-start.25 = (bf16[64,2048]{1,0:T(8,128)(2,1)S(1)}, bf16[64,2048]{1,0:T(8,128)(2,1)S(1)}, u32[]{:S(2)}, u32[]{:S(2)}) collective-permute-start(bf16[64,2048]{1,0:T(8,128)(2,1)S(1)} %divide_convert_fusion), channel_id=1, source_target_pairs={{0,1},{1,0},{2,3},{3,2},{4,5},{5,4},{6,7},{7,6},{8,9},{9,8},{10,11... | collective-permute-start | bytes 786440 | tf_op jit(solution)/shard_map/ppermute | solution.py:22
  180.1 15.0 %collective-permute-start.37 = (f32[33,1024]{1,0:T(8,128)S(1)}, f32[33,1024]{1,0:T(8,128)S(1)}, u32[]{:S(2)}, u32[]{:S(2)}) collective-permute-start(f32[33,1024]{1,0:T(8,128)S(1)} %dynamic-slice_add_fusion), channel_id=1, source_target_pairs={{0,8},{4,12},{8,0},{12,4},{1,9},{5,13},{9,1},{13,5},{2,10},{6,14},... | collective-permute-start | bytes 405512 | tf_op jit(solution)/shard_map/ppermute | solution.py:26
  180.1 15.0 %collective-permute-start.38 = (f32[33,1024]{1,0:T(8,128)S(1)}, f32[33,1024]{1,0:T(8,128)S(1)}, u32[]{:S(2)}, u32[]{:S(2)}) collective-permute-start(f32[33,1024]{1,0:T(8,128)S(1)} %dynamic-slice_add_fusion), channel_id=1, source_target_pairs={{0,12},{4,8},{8,4},{12,0},{1,13},{5,9},{9,5},{13,1},{2,14},{6,10},... | collective-permute-start | bytes 405512 | tf_op jit(solution)/shard_map/ppermute | solution.py:26
  (54 other events, 474.8 us)

commit v4 on v3

--- a/solution.py
+++ b/solution.py
@@ -1,6 +1,10 @@
+import functools
+
 import jax
 import jax.numpy as jnp
 from jax import lax
+from jax.experimental import pallas as pl
+from jax.experimental.pallas import tpu as pltpu
 from jax.sharding import PartitionSpec as P
 
 inverse_temp = 50.0
@@ -30,6 +34,157 @@
     if lax.axis_size(axis) == 2:
         return x + swap(x, axis)
     return lax.psum(x, axis)
+
+
+def call(kernel, outs, args, scratch=(), flops=1 << 24):
+    size = sum(a.size * a.dtype.itemsize for a in args)
+    return pl.pallas_call(
+        kernel,
+        out_shape=outs,
+        scratch_shapes=list(scratch),
+        compiler_params=pltpu.CompilerParams(vmem_limit_bytes=48 << 20),
+        cost_estimate=pl.CostEstimate(flops=flops, bytes_accessed=size, transcendentals=0),
+    )(*args)
+
+
+def as_row(column):
+    size = column.shape[0]
+    eye = lax.broadcasted_iota(jnp.int32, (size, size), 0) == lax.broadcasted_iota(
+        jnp.int32, (size, size), 1
+    )
+    return jnp.sum(jnp.where(eye, column, 0.0), axis=0, keepdims=True)
+
+
+def as_column(row):
+    size = row.shape[1]
+    eye = lax.broadcasted_iota(jnp.int32, (size, size), 0) == lax.broadcasted_iota(
+        jnp.int32, (size, size), 1
+    )
+    return jnp.sum(jnp.where(eye, row, 0.0), axis=1, keepdims=True)
+
+
+def gram_kernel(blocks, *refs):
+    own, oth = refs[:blocks], refs[blocks : 2 * blocks]
+    out_ref, sorted_ref, own_ref = refs[2 * blocks :]
+    docs = own[0].shape[0]
+    half = docs // 2
+    anchors = blocks * half
+    for j in range(blocks):
+        own_ref[j * docs : (j + 1) * docs] = own[j][...]
+        sorted_ref[j * half : (j + 1) * half] = oth[j][:half]
+        sorted_ref[anchors + j * half : anchors + (j + 1) * half] = oth[j][half:]
+    rows = blocks * docs
+    out_ref[:rows] = dot_nt(own_ref[...], sorted_ref[:anchors])
+    out_ref[rows : rows + half] = dot_nt(own[0][:half], sorted_ref[anchors:])
+    own_f = own_ref[...].astype(jnp.float32)
+    oth_f = sorted_ref[...].astype(jnp.float32)
+    own_sq = as_row(jnp.sum(own_f * own_f, axis=1, keepdims=True))
+    oth_sq = as_row(jnp.sum(oth_f * oth_f, axis=1, keepdims=True))
+    tail = jnp.concatenate(
+        [
+            own_sq[:, :anchors],
+            own_sq[:, anchors:],
+            oth_sq[:, :anchors],
+            oth_sq[:, anchors:],
+            jnp.zeros((4, anchors), jnp.float32),
+        ],
+        axis=0,
+    )
+    out_ref[rows + half :] = tail
+
+
+def loss_kernel(blocks, sums_count, chunks, *refs):
+    sums_refs = refs[:sums_count]
+    list_c, list_o, pooled_ref, oth_ref, counts_ref, gain_ref, doc_sums_ref, up_ref = refs[
+        sums_count : sums_count + 8
+    ]
+    up_states_ref, labels_ref = refs[sums_count + 8 : sums_count + 10]
+    state_refs = refs[sums_count + 10 : sums_count + 10 + chunks]
+    losses_ref, doc_grad_ref, small_ref, gained_ref, gain_grad_ref = refs[
+        sums_count + 10 + chunks :
+    ]
+    docs = pooled_ref.shape[0]
+    half = docs // 2
+    anchors = blocks * half
+    rows = blocks * docs
+    fanout = list_o.shape[1]
+    sums = sums_refs[0][...]
+    if sums_count == 2:
+        sums = sums + sums_refs[1][...]
+    inner_c = sums[:rows]
+    inner_o = sums[rows : rows + half]
+    scales = lax.rsqrt(sums[rows + half :] + 1e-06)
+    own_scale = as_column(jnp.concatenate([scales[0:1], scales[1:2]], axis=1))
+    oth_scale = scales[2:3]
+    pool_scale = scales[3:4]
+
+    row_id = lax.broadcasted_iota(jnp.int32, (rows, anchors), 0)
+    col_id = lax.broadcasted_iota(jnp.int32, (rows, anchors), 1)
+    mask_c = (row_id % docs) < half
+    for h in range(fanout):
+        mask_c = mask_c | (row_id == list_c[h : h + 1, :])
+    target_c = row_id == (col_id // half) * docs + col_id % half
+    logits_c = inverse_temp * (inner_c * own_scale * oth_scale)
+    exp_all = jnp.exp(logits_c)
+    exp_c = jnp.where(mask_c, exp_all, 0.0)
+    total_c = jnp.sum(exp_c, axis=0, keepdims=True)
+    losses_ref[...] = jnp.log(total_c) - jnp.sum(
+        jnp.where(target_c, logits_c, 0.0), axis=0, keepdims=True
+    )
+    target_own = target_c[:docs].astype(jnp.float32)
+    grad_c = inverse_temp * (exp_c[:docs] / total_c - target_own)
+
+    logits_o = inverse_temp * (inner_o * own_scale[:half] * pool_scale)
+    pool_id = lax.broadcasted_iota(jnp.int32, (half, anchors), 1)
+    mask_o = pool_id == list_o[:, 0:1]
+    for h in range(1, fanout):
+        mask_o = mask_o | (pool_id == list_o[:, h : h + 1])
+    exp_o = jnp.where(mask_o, jnp.exp(logits_o), 0.0)
+    exp_a = exp_all[:half]
+    total_o = jnp.sum(exp_a, axis=1, keepdims=True) + jnp.sum(exp_o, axis=1, keepdims=True)
+    grad_a = inverse_temp * (exp_a / total_o - target_own[:half])
+    grad_o = inverse_temp * (exp_o / total_o)
+
+    zeros = jnp.zeros((docs - half, anchors), jnp.float32)
+    coef = jnp.concatenate(
+        [
+            (grad_c + jnp.concatenate([grad_a, zeros], axis=0)) * oth_scale,
+            jnp.concatenate([grad_o * pool_scale, zeros], axis=0),
+        ],
+        axis=1,
+    ).astype(jnp.bfloat16)
+    inner = jnp.concatenate(
+        [inner_c[:docs], jnp.concatenate([inner_o, zeros], axis=0)], axis=1
+    )
+    doc_grad = dot_nn(coef, oth_ref[...])
+    doc_grad_ref[...] = doc_grad
+    scale = own_scale[:docs]
+    unit_dots = jnp.sum(coef.astype(jnp.float32) * inner, axis=1, keepdims=True) * scale
+    pooled = pooled_ref[...].astype(jnp.float32)
+    per_doc = (doc_grad - pooled * (scale * unit_dots)) * (scale / counts_ref[...])
+    gain = gain_ref[...]
+    gained = per_doc * gain
+    gained_ref[...] = gained
+    gain_grad_ref[...] = jnp.sum(per_doc * doc_sums_ref[...], axis=0, keepdims=True) / gain
+
+    gained_b = gained.astype(jnp.bfloat16)
+    chunk = state_refs[0].shape[1]
+    tok_doc = dot_nt(gained_b[:, :chunk], state_refs[0][...])
+    for i in range(1, chunks):
+        tok_doc = tok_doc + dot_nt(
+            gained_b[:, i * chunk : (i + 1) * chunk], state_refs[i][...]
+        )
+    tokens = tok_doc.shape[1]
+    rank = up_ref.shape[0]
+    doc_id = lax.broadcasted_iota(jnp.int32, (docs, tokens), 0)
+    tok_dots = jnp.sum(
+        jnp.where(doc_id == labels_ref[...], tok_doc, 0.0), axis=0, keepdims=True
+    )
+    up_gained = dot_nt(up_ref[...].astype(jnp.float32), gained, highest)
+    small_ref[...] = jnp.zeros_like(small_ref)
+    small_ref[:rank, :tokens] = up_states_ref[...]
+    small_ref[:rank, tokens : tokens + docs] = up_gained
+    small_ref[rank : rank + 1, :tokens] = tok_dots
 
 
 def body(
@@ -54,22 +209,13 @@
     docs = 2 * per_shard
 
     block_shard = shard ^ jnp.arange(dp, dtype=jnp.int32)
-    list_col = (shard ^ negative_owner[0]) * docs + per_shard + negative_pool_row[0]
-    own_list = lax.dynamic_slice_in_dim(list_col, shard * per_shard, per_shard, 0)
-    other_own_list = swap(own_list, "pair")
-    rel_list = list_col.reshape(dp, per_shard, -1)[block_shard].reshape(anchors, -1)
-    col_id = jnp.arange(dp * docs, dtype=jnp.int32)
-    anchor_col = (col_id % docs) < per_shard
-
-    def listed(lists):
-        hit = lists[:, :, None] == col_id[None, None, :]
-        return jnp.any(hit, axis=1) | anchor_col[None, :]
-
-    mask_c = listed(rel_list)
-    mask_o = listed(other_own_list)
-    rel_row = jnp.arange(anchors, dtype=jnp.int32)
-    target_c = col_id[None, :] == (rel_row // per_shard * docs + rel_row % per_shard)[:, None]
-    target_o = target_c[:per_shard]
+    owner_block = shard ^ negative_owner[0]
+    rel_list = (owner_block * docs + per_shard + negative_pool_row[0]).reshape(dp, per_shard, -1)
+    list_c = rel_list[block_shard].reshape(anchors, -1).T
+    pool_col = owner_block * per_shard + negative_pool_row[0]
+    list_o = swap(
+        lax.dynamic_slice_in_dim(pool_col, shard * per_shard, per_shard, 0), "pair"
+    )
 
     group = lax.axis_index("groups")
     quarter = frozen_weight.shape[0] // 4
@@ -136,84 +282,51 @@
 
     own_blocks = [pooled] + [partner(pooled, "dp", j) for j in range(1, dp)]
     other_blocks = [swap(block, "pair") for block in own_blocks]
-    docs_own = jnp.concatenate(own_blocks, axis=0)
-    docs_oth = jnp.concatenate(other_blocks, axis=0)
-    anchors_oth = jnp.concatenate([block[:per_shard] for block in other_blocks], axis=0)
-    docs_own_f = docs_own.astype(jnp.float32)
-    docs_oth_f = docs_oth.astype(jnp.float32)
-    sums = sum_over(
-        jnp.concatenate(
-            [
-                dot_nt(anchors_oth, docs_own),
-                dot_nt(pooled[:per_shard], docs_oth),
-                jnp.sum(docs_own_f * docs_own_f, axis=1)[None],
-                jnp.sum(docs_oth_f * docs_oth_f, axis=1)[None],
-            ],
-            axis=0,
+    rows = dp * docs
+    sums, sorted_oth = call(
+        functools.partial(gram_kernel, dp),
+        (
+            jax.ShapeDtypeStruct((rows + per_shard + 8, anchors), jnp.float32),
+            jax.ShapeDtypeStruct((rows, cols), jnp.bfloat16),
         ),
-        "mp",
-    )
-    inner_c = sums[:anchors]
-    inner_o = sums[anchors : anchors + per_shard]
-    inv_own = lax.rsqrt(sums[anchors + per_shard] + 1e-06)
-    inv_oth = lax.rsqrt(sums[anchors + per_shard + 1] + 1e-06)
-    inv_oth_anchor = inv_oth.reshape(dp, docs)[:, :per_shard].reshape(anchors)
-    inv_own_doc = inv_own[:docs]
-
-    def softmax_grad(inner, scale_row, scale_col, mask, target):
-        logits = inverse_temp * (inner * scale_row[:, None] * scale_col[None, :])
-        exp_logits = jnp.where(mask, jnp.exp(logits), 0.0)
-        total = jnp.sum(exp_logits, axis=1)
-        hit = jnp.sum(jnp.where(target, logits, 0.0), axis=1)
-        grad = inverse_temp * (exp_logits / total[:, None] - target.astype(jnp.float32))
-        return jnp.log(total) - hit, grad
-
-    losses_c, grad_c = softmax_grad(inner_c, inv_oth_anchor, inv_own, mask_c, target_c)
-    _, grad_o = softmax_grad(inner_o, inv_own_doc[:per_shard], inv_oth, mask_o, target_o)
-    losses = losses_c[:per_shard][None]
-
-    grad_ct = grad_c[:, :docs].T.reshape(docs, dp, per_shard)
-    inner_ct = inner_c[:, :docs].T.reshape(docs, dp, per_shard)
-    zero_pool = jnp.zeros((docs, dp, per_shard), jnp.float32)
-    zero_rows = jnp.zeros((docs - per_shard, dp * docs), jnp.float32)
-    coef = jnp.concatenate([grad_ct, zero_pool], axis=2).reshape(docs, dp * docs)
-    coef = coef + jnp.concatenate([grad_o, zero_rows], axis=0)
-    inner = jnp.concatenate(
-        [
-            inner_o,
-            jnp.concatenate([inner_ct, zero_pool], axis=2).reshape(docs, dp * docs)[per_shard:],
-        ],
-        axis=0,
-    )
-    coef_b = (coef * inv_oth[None, :]).astype(jnp.bfloat16)
-    doc_grad = dot_nn(coef_b, docs_oth)
-    unit_dots = jnp.sum(coef_b.astype(jnp.float32) * inner, axis=1) * inv_own_doc
-    pooled_f = pooled.astype(jnp.float32)
-    per_doc = (doc_grad - pooled_f * (inv_own_doc * unit_dots)[:, None]) * (inv_own_doc / counts)[
-        :, None
-    ]
-
-    gained = per_doc * gain
-    up_f = adapter_up.astype(jnp.float32)
-    gained_b = jnp.split(gained.astype(jnp.bfloat16), chunk_count, axis=1)
-    tok_doc = sum(dot_nt(g, x) for g, x in zip(gained_b, states_b))
-    tok_dots = jnp.sum(jnp.where(member, tok_doc, 0.0), axis=0)[None]
+        own_blocks + other_blocks,
+        [pltpu.VMEM((rows, cols), jnp.bfloat16)],
+    )
     up_parts = jnp.split(adapter_up, chunk_count, axis=1)
     up_states = sum(dot_nt(u, x) for u, x in zip(up_parts, states_b))
-    up_gained = dot_nt(up_f, gained, highest)
-    small = sum_over(
-        jnp.concatenate(
-            [
-                jnp.concatenate([tok_dots, up_states], axis=0),
-                jnp.concatenate([jnp.zeros((1, docs), jnp.float32), up_gained], axis=0),
-            ],
-            axis=1,
+    if lax.axis_size("mp") == 2:
+        sums = [sums, swap(sums, "mp")]
+    else:
+        sums = [lax.psum(sums, "mp")]
+    losses, doc_grad, small, gained, gain_grad = call(
+        functools.partial(loss_kernel, dp, len(sums), chunk_count),
+        (
+            jax.ShapeDtypeStruct((1, anchors), jnp.float32),
+            jax.ShapeDtypeStruct((docs, cols), jnp.float32),
+            jax.ShapeDtypeStruct((rank + 8, token_count + 128), jnp.float32),
+            jax.ShapeDtypeStruct((docs, cols), jnp.float32),
+            jax.ShapeDtypeStruct((1, cols), jnp.float32),
         ),
-        "mp",
-    )
-    alpha = inv_rms * inv_rms * inv_rms * small[0, :token_count] / width
-    up_states = small[1:, :token_count]
-    up_gained = small[1:, token_count:]
+        sums
+        + [
+            list_c,
+            list_o,
+            pooled,
+            sorted_oth,
+            counts[:, None],
+            gain[None],
+            doc_sums,
+            adapter_up,
+            up_states,
+            labels[None],
+        ]
+        + states_b,
+    )
+    losses = losses[:, :per_shard]
+    small = sum_over(small, "mp")
+    alpha = inv_rms * inv_rms * inv_rms * small[rank, :token_count] / width
+    up_states = small[:rank, :token_count]
+    up_gained = small[:rank, token_count : token_count + docs]
     mid_grad = (
         inv_rms * dot_nn(up_gained, member_f, highest) - alpha * up_states
     ).astype(jnp.bfloat16)
@@ -223,9 +336,8 @@
     b_grad = dot_nn(dot_nt(mid_t * inv_rms, member_f, highest), gained, highest) - jnp.concatenate(
         [dot_nn(mid_alpha, x) for x in states_b], axis=1
     )
-    gain_grad = jnp.sum(per_doc * doc_sums, axis=0) / gain
-
-    grads = jnp.concatenate([a_grad, b_grad, gain_grad[None]], axis=0)
+
+    grads = jnp.concatenate([a_grad, b_grad, gain_grad], axis=0)
     half = cols // 2
     kept = lax.dynamic_slice_in_dim(grads, side * half, half, 1)
     sent = lax.dynamic_slice_in_dim(grads, (1 - side) * half, half, 1)

time: 199 us -> 173 us (0.87)
  local copies, waits for them, and re-layouts: 20.7 us -> 4.28 us
  other arithmetic: 14.9 us -> 1.7 us
  matrix products: 40.4 us -> 29 us
  waiting for transfers between devices: 84.9 us -> 91 us
  starting transfers between devices: 31.8 us -> 37.1 us
  Pallas kernels: 0 us -> 4.07 us
    ppermute x6, waiting for transfers between devices: 8.98 us -> 31.8 us  [body(): moving[h] = lax.ppermute(moving[h], 'dp', hops)]
    ppermute x28, waiting for transfers between devices: 47 us -> 30.3 us  [swap(): return lax.ppermute(x, axis, [(0, 1), (1, 0)])]
    dot_general x19 -> x18, matrix products: 35.9 us -> 28.1 us  [dot_nn(): jnp.dot(a, b, precision=precision, preferred_element_type=jnp.float32)]
    slice x9 -> x1, local copies, waits for them, and re-layouts: 5.1 us -> 0.01 us  [body(): alpha = inv_rms * inv_rms * inv_rms * small[rank, :token_count] / width]
    reduce_sum x5 -> x0, other arithmetic: 4.2 us -> none  [the longest x2 2.64 us: softmax_grad(): total = jnp.sum(exp_logits, axis=1)]
    pallas_call x0 -> x2, Pallas kernels: none -> 4.07 us  [call(): pl.pallas_call(kernel, out_shape=outs, scratch_shapes=list(scratch), comp...]
    dot_general x8 -> x3, matrix products: 4.47 us -> 0.88 us  [dot_nt(): lax.dot_general(a, b, (((1,), (1,)), ((), ())), precision=precision, pref...]
    ppermute x6, starting transfers between devices: 7.02 us -> 10.5 us  [body(): moving[h] = lax.ppermute(moving[h], 'dp', hops)]
  transfers between devices with their start and end apart: 40 -> 40, of which waited for: 21 -> 20; matrix products, arithmetic and copies ran while one was open for 21% -> 16% of each run, Pallas kernels for 0% -> 1%
where the time goes in v4:
time: 173 us; the launch traced here: 172 us
  waiting for transfers between devices  91 us (53%)
  starting transfers between devices  37.1 us (21%)
  matrix products  29 us (17%)
  between operations  5.05 us (3%)
  local copies, waits for them, and re-layouts  4.28 us (2%)
  Pallas kernels  4.07 us (2%)
    ppermute x6, waiting for transfers between devices, body(): moving[h] = lax.ppermute(moving[h], 'dp', hops)  31.8 us
    ppermute x28, waiting for transfers between devices, swap(): return lax.ppermute(x, axis, [(0, 1), (1, 0)])  30.3 us
    ppermute x6, waiting for transfers between devices, partner(): lax.ppermute(x, axis, [(i, i ^ flip) for i in range(lax.axis_size(axis))])  28.9 us
    dot_general x18, matrix products, dot_nn(): jnp.dot(a, b, precision=precision, preferred_element_type=jnp.float32)  28.1 us
    ppermute x28, starting transfers between devices, swap(): return lax.ppermute(x, axis, [(0, 1), (1, 0)])  15.6 us
    ppermute x6, starting transfers between devices, partner(): lax.ppermute(x, axis, [(i, i ^ flip) for i in range(lax.axis_size(axis))])  11.1 us
    ppermute x6, starting transfers between devices, body(): moving[h] = lax.ppermute(moving[h], 'dp', hops)  10.5 us
    pallas_call x2, Pallas kernels, call(): pl.pallas_call(kernel, out_shape=outs, scratch_shapes=list(scratch), comp...  4.07 us
  transfers between devices with their start and end apart: 40, of which 20 were waited for; matrix products, arithmetic and copies ran while one was open for 16% of the time, Pallas kernels for 1%

profile of v4, /device:TPU:0, one launch (start us, length us, event | category | flops | bytes accessed | tf_op | source)
XLA Modules:
  0.0 172.2 jit_solution(468893243900548999)
XLA Ops:
  2.0 3.1 %collective-permute-start.12 = (bf16[256,1024]{1,0:T(8,128)(2,1)S(1)}, bf16[256,1024]{1,0:T(8,128)(2,1)}, u32[]{:S(2)}, u32[]{:S(2)}) collective-permute-start(bf16[256,1024]{1,0:T(8,128)(2,1)S(1)} %get-tuple-element.20), channel_id=1, source_target_pairs={{0,4},{4,12},{12,8},{8,0},{1,5},{5,13},{13,9},{9,1},{2,6},{6,14},{... | collective-permute-start | bytes 1572872 | tf_op jit(solution)/shard_map/ppermute | solution.py:260
  5.0 2.6 %collective-permute-start = (bf16[256,1024]{1,0:T(8,128)(2,1)S(1)}, bf16[256,1024]{1,0:T(8,128)(2,1)}, u32[]{:S(2)}, u32[]{:S(2)}) collective-permute-start(bf16[256,1024]{1,0:T(8,128)(2,1)S(1)} %get-tuple-element.19), channel_id=1, source_target_pairs={{0,4},{4,12},{12,8},{8,0},{1,5},{5,13},{13,9},{9,1},{2,6},{6,14},{... | collective-permute-start | bytes 1572872 | tf_op jit(solution)/shard_map/ppermute | solution.py:260
  7.6 3.4 %fusion.59 = bf16[512,16]{0,1:T(8,128)(2,1)S(1)} fusion(bf16[4096,16]{0,1:T(8,128)(2,1)S(1)} %copy-done, bf16[1,512,4096]{2,1,0:T(8,128)(2,1)} %param.10), kind=kOutput, calls=%fused_computation.65 | convolution fusion | flops 67117056 | bytes 4341760 | tf_op jit(solution)/shard_map/dot_general | solution.py:22
  12.9 4.7 %fusion.50 = f32[512,1024]{1,0:T(8,128)} fusion(bf16[1024,2048]{1,0:T(8,128)(2,1)} %param.12, bf16[1,512,4096]{2,1,0:T(8,128)(2,1)} %param.10, s32[]{:T(128)S(6)} %select_n.105), kind=kOutput, calls=%fused_computation.56 | convolution fusion | flops 1073741824 | bytes 5242884 | tf_op jit(solution)/shard_map/dot_general | solution.py:22
  21.5 8.7 %collective-permute-done = bf16[256,1024]{1,0:T(8,128)(2,1)} collective-permute-done((bf16[256,1024]{1,0:T(8,128)(2,1)S(1)}, bf16[256,1024]{1,0:T(8,128)(2,1)}, u32[]{:S(2)}, u32[]{:S(2)}) %collective-permute-start) | collective-permute-done | bytes 524320 | tf_op jit(solution)/shard_map/ppermute | solution.py:260
  38.7 2.6 %collective-permute-done.16 = bf16[256,1024]{1,0:T(8,128)(2,1)S(1)} collective-permute-done((bf16[256,1024]{1,0:T(8,128)(2,1)}, bf16[256,1024]{1,0:T(8,128)(2,1)S(1)}, u32[]{:S(2)}, u32[]{:S(2)}) %collective-permute-start.16) | collective-permute-done | bytes 524320 | tf_op jit(solution)/shard_map/ppermute | solution.py:260
  44.1 8.4 %collective-permute-done.4 = bf16[256,1024]{1,0:T(8,128)(2,1)S(1)} collective-permute-done((bf16[256,1024]{1,0:T(8,128)(2,1)}, bf16[256,1024]{1,0:T(8,128)(2,1)S(1)}, u32[]{:S(2)}, u32[]{:S(2)}) %collective-permute-start.4) | collective-permute-done | bytes 524320 | tf_op jit(solution)/shard_map/ppermute | solution.py:260
  53.0 3.3 %fusion.52 = f32[512,1024]{1,0:T(8,128)S(1)} fusion(bf16[1024,2048]{1,0:T(8,128)(2,1)} %param.12, bf16[1,512,4096]{2,1,0:T(8,128)(2,1)} %param.10, s32[]{:T(128)S(6)} %select_n.105), kind=kOutput, calls=%fused_computation.60 | convolution fusion | flops 1073741824 | bytes 5242884 | tf_op jit(solution)/shard_map/dot_general | solution.py:22
  57.9 5.9 %collective-permute-done.20 = bf16[256,1024]{1,0:T(8,128)(2,1)S(1)} collective-permute-done((bf16[256,1024]{1,0:T(8,128)(2,1)S(1)}, bf16[256,1024]{1,0:T(8,128)(2,1)S(1)}, u32[]{:S(2)}, u32[]{:S(2)}) %collective-permute-start.20) | collective-permute-done | bytes 524320 | tf_op jit(solution)/shard_map/ppermute | solution.py:260
  66.7 2.6 %fusion.26 = f32[512,1024]{1,0:T(8,128)S(1)} fusion(bf16[256,1024]{1,0:T(8,128)(2,1)S(1)} %collective-permute-done.15, bf16[256,1024]{1,0:T(8,128)(2,1)} %collective-permute-done.14, bf16[256,1024]{1,0:T(8,128)(2,1)} %collective-permute-done.13, bf16[256,1024]{1,0:T(8,128)(2,1)} %collective-permute-done.12, bf16[512,256]{1,0:T(8,128)(2,1)S(1)} %get-tuple-element.27, ...), kind=kOutput, calls=%fused_computation.28 | convolution fusion | flops 1086324736 | bytes 5242880 | tf_op jit(solution)/shard_map/dot_general | solution.py:22
  69.4 4.8 %collective-permute-done.8 = bf16[256,1024]{1,0:T(8,128)(2,1)S(1)} collective-permute-done((bf16[256,1024]{1,0:T(8,128)(2,1)S(1)}, bf16[256,1024]{1,0:T(8,128)(2,1)S(1)}, u32[]{:S(2)}, u32[]{:S(2)}) %collective-permute-start.8) | collective-permute-done | bytes 524320 | tf_op jit(solution)/shard_map/ppermute | solution.py:260
  74.2 4.5 %collective-permute-done.5 = bf16[256,1024]{1,0:T(8,128)(2,1)S(1)} collective-permute-done((bf16[256,1024]{1,0:T(8,128)(2,1)S(1)}, bf16[256,1024]{1,0:T(8,128)(2,1)S(1)}, u32[]{:S(2)}, u32[]{:S(2)}) %collective-permute-start.5) | collective-permute-done | bytes 524320 | tf_op jit(solution)/shard_map/ppermute | solution.py:26
  80.5 2.5 %fusion.2 = f32[512,1024]{1,0:T(8,128)S(1)} fusion(bf16[256,1024]{1,0:T(8,128)(2,1)S(1)} %collective-permute-done.3, bf16[256,1024]{1,0:T(8,128)(2,1)S(1)} %collective-permute-done.2, bf16[256,1024]{1,0:T(8,128)(2,1)} %collective-permute-done.1, bf16[256,1024]{1,0:T(8,128)(2,1)} %collective-permute-done, bf16[512,256]{1,0:T(8,128)(2,1)S(1)} %get-tuple-element.27, ...), kind=kOutput, calls=%fused_computation.4 | convolution fusion | flops 1086324736 | bytes 5242880 | tf_op jit(solution)/shard_map/dot_general | solution.py:22
  83.0 6.9 %collective-permute-done.21 = bf16[256,1024]{1,0:T(8,128)(2,1)S(1)} collective-permute-done((bf16[256,1024]{1,0:T(8,128)(2,1)S(1)}, bf16[256,1024]{1,0:T(8,128)(2,1)S(1)}, u32[]{:S(2)}, u32[]{:S(2)}) %collective-permute-start.21) | collective-permute-done | bytes 524320 | tf_op jit(solution)/shard_map/ppermute | solution.py:26
  91.7 6.8 %collective-permute-done.9 = bf16[256,1024]{1,0:T(8,128)(2,1)S(1)} collective-permute-done((bf16[256,1024]{1,0:T(8,128)(2,1)S(1)}, bf16[256,1024]{1,0:T(8,128)(2,1)S(1)}, u32[]{:S(2)}, u32[]{:S(2)}) %collective-permute-start.9) | collective-permute-done | bytes 524320 | tf_op jit(solution)/shard_map/ppermute | solution.py:26
  101.5 2.9 %fusion.114 = (bf16[512,1024]{1,0:T(8,128)(2,1)S(1)}, f32[512]{0:T(512)S(1)}, f32[512,1024]{1,0:T(8,128)S(1)}) fusion(bf16[256,1024]{1,0:T(8,128)(2,1)S(1)} %collective-permute-done.11, bf16[256,1024]{1,0:T(8,128)(2,1)S(1)} %collective-permute-done.10, bf16[256,1024]{1,0:T(8,128)(2,1)S(1)} %collective-permute-done.9, ...), kind=kOutput, calls=%fused_computation.157 | convolution fusion | flops 1091042816 | bytes 15730688 | tf_op jit(solution)/shard_map/dot_general | solution.py:22
  105.9 2.2 %collective-permute-done.24 = f32[512]{0:T(512)S(1)} collective-permute-done((f32[512]{0:T(512)S(1)}, f32[512]{0:T(512)S(1)}, u32[]{:S(2)}, u32[]{:S(2)}) %collective-permute-start.24) | collective-permute-done | bytes 2080 | tf_op jit(solution)/shard_map/ppermute | solution.py:26
  109.7 3.4 %collective-permute-start.26 = (bf16[64,2048]{1,0:T(8,128)(2,1)S(1)}, bf16[64,2048]{1,0:T(8,128)(2,1)}, u32[]{:S(2)}, u32[]{:S(2)}) collective-permute-start(bf16[64,2048]{1,0:T(8,128)(2,1)S(1)} %get-tuple-element.38.refs_0_.refs_4_), channel_id=1, source_target_pairs={{0,8},{4,12},{8,0},{12,4},{1,9},{5,13},{9,1},{13,5},{2,10},{6,14},... | collective-permute-start | bytes 786440 | tf_op jit(solution)/shard_map/ppermute | solution.py:30
  114.3 7.2 %collective-permute-done.25.refs_1_ = bf16[64,2048]{1,0:T(8,128)(2,1)S(1)} collective-permute-done((bf16[64,2048]{1,0:T(8,128)(2,1)S(1)}, bf16[64,2048]{1,0:T(8,128)(2,1)S(1)}, u32[]{:S(2)}, u32[]{:S(2)}) %collective-permute-start.25) | collective-permute-done | bytes 262176 | tf_op jit(solution)/shard_map/ppermute | solution.py:30
  121.4 10.2 %collective-permute-done.26.refs_2_ = bf16[64,2048]{1,0:T(8,128)(2,1)} collective-permute-done((bf16[64,2048]{1,0:T(8,128)(2,1)S(1)}, bf16[64,2048]{1,0:T(8,128)(2,1)}, u32[]{:S(2)}, u32[]{:S(2)}) %collective-permute-start.26) | collective-permute-done | bytes 262176 | tf_op jit(solution)/shard_map/ppermute | solution.py:30
  137.9 4.1 %collective-permute-done.32.refs_1_ = f32[296,128]{1,0:T(8,128)S(1)} collective-permute-done((f32[296,128]{1,0:T(8,128)S(1)}, f32[296,128]{1,0:T(8,128)S(1)}, u32[]{:S(2)}, u32[]{:S(2)}) %collective-permute-start.32) | collective-permute-done | bytes 151584 | tf_op jit(solution)/shard_map/ppermute | solution.py:26
  145.6 2.6 %collective-permute-done.34 = f32[24,640]{1,0:T(8,128)S(1)} collective-permute-done((f32[24,640]{1,0:T(8,128)S(1)}, f32[24,640]{1,0:T(8,128)S(1)}, u32[]{:S(2)}, u32[]{:S(2)}) %collective-permute-start.34) | collective-permute-done | bytes 61472 | tf_op jit(solution)/shard_map/ppermute | solution.py:26
  151.3 5.2 %collective-permute-start.37 = (f32[33,1024]{1,0:T(8,128)S(1)}, f32[33,1024]{1,0:T(8,128)S(1)}, u32[]{:S(2)}, u32[]{:S(2)}) collective-permute-start(f32[33,1024]{1,0:T(8,128)S(1)} %dynamic-slice_add_fusion), channel_id=1, source_target_pairs={{0,8},{4,12},{8,0},{12,4},{1,9},{5,13},{9,1},{13,5},{2,10},{6,14},... | collective-permute-start | bytes 405512 | tf_op jit(solution)/shard_map/ppermute | solution.py:30
  157.9 10.7 %collective-permute-done.37 = f32[33,1024]{1,0:T(8,128)S(1)} collective-permute-done((f32[33,1024]{1,0:T(8,128)S(1)}, f32[33,1024]{1,0:T(8,128)S(1)}, u32[]{:S(2)}, u32[]{:S(2)}) %collective-permute-start.37) | collective-permute-done | bytes 135200 | tf_op jit(solution)/shard_map/ppermute | solution.py:30
  (137 shorter events, 48.0 us)
Async XLA Ops:
  2.0 16.9 %collective-permute-start.12 = (bf16[256,1024]{1,0:T(8,128)(2,1)S(1)}, bf16[256,1024]{1,0:T(8,128)(2,1)}, u32[]{:S(2)}, u32[]{:S(2)}) collective-permute-start(bf16[256,1024]{1,0:T(8,128)(2,1)S(1)} %get-tuple-element.20), channel_id=1, source_target_pairs={{0,4},{4,12},{12,8},{8,0},{1,5},{5,13},{13,9},{9,1},{2,6},{6,14},{... | collective-permute-start | bytes 1572872 | tf_op jit(solution)/shard_map/ppermute | solution.py:260
  5.0 25.1 %collective-permute-start = (bf16[256,1024]{1,0:T(8,128)(2,1)S(1)}, bf16[256,1024]{1,0:T(8,128)(2,1)}, u32[]{:S(2)}, u32[]{:S(2)}) collective-permute-start(bf16[256,1024]{1,0:T(8,128)(2,1)S(1)} %get-tuple-element.19), channel_id=1, source_target_pairs={{0,4},{4,12},{12,8},{8,0},{1,5},{5,13},{13,9},{9,1},{2,6},{6,14},{... | collective-permute-start | bytes 1572872 | tf_op jit(solution)/shard_map/ppermute | solution.py:260
  18.9 22.4 %collective-permute-start.16 = (bf16[256,1024]{1,0:T(8,128)(2,1)}, bf16[256,1024]{1,0:T(8,128)(2,1)S(1)}, u32[]{:S(2)}, u32[]{:S(2)}) collective-permute-start(bf16[256,1024]{1,0:T(8,128)(2,1)} %collective-permute-done.12), channel_id=1, source_target_pairs={{0,4},{4,12},{12,8},{8,0},{1,5},{5,13},{13,9},{9,1},{2,6},{6,14},{... | collective-permute-start | bytes 1572872 | tf_op jit(solution)/shard_map/ppermute | solution.py:260
  20.0 21.3 %collective-permute-start.13 = (bf16[256,1024]{1,0:T(8,128)(2,1)}, bf16[256,1024]{1,0:T(8,128)(2,1)}, u32[]{:S(2)}, u32[]{:S(2)}) collective-permute-start(bf16[256,1024]{1,0:T(8,128)(2,1)} %collective-permute-done.12), channel_id=1, source_target_pairs={{0,16},{16,0},{1,17},{17,1},{2,18},{18,2},{3,19},{19,3},{4,20},{20... | collective-permute-start | bytes 1572872 | tf_op jit(solution)/shard_map/ppermute | solution.py:26
  21.5 21.1 %collective-permute-start.14 = (bf16[256,1024]{1,0:T(8,128)(2,1)}, bf16[256,1024]{1,0:T(8,128)(2,1)}, u32[]{:S(2)}, u32[]{:S(2)}) collective-permute-start(bf16[256,1024]{1,0:T(8,128)(2,1)} %collective-permute-done.12), channel_id=1, source_target_pairs={{0,1},{1,0},{2,3},{3,2},{4,5},{5,4},{6,7},{7,6},{8,9},{9,8},{10,11... | collective-permute-start | bytes 1572872 | tf_op jit(solution)/shard_map/ppermute | solution.py:26
  30.2 22.4 %collective-permute-start.4 = (bf16[256,1024]{1,0:T(8,128)(2,1)}, bf16[256,1024]{1,0:T(8,128)(2,1)S(1)}, u32[]{:S(2)}, u32[]{:S(2)}) collective-permute-start(bf16[256,1024]{1,0:T(8,128)(2,1)} %collective-permute-done), channel_id=1, source_target_pairs={{0,4},{4,12},{12,8},{8,0},{1,5},{5,13},{13,9},{9,1},{2,6},{6,14},{... | collective-permute-start | bytes 1572872 | tf_op jit(solution)/shard_map/ppermute | solution.py:260
  31.2 21.3 %collective-permute-start.1 = (bf16[256,1024]{1,0:T(8,128)(2,1)}, bf16[256,1024]{1,0:T(8,128)(2,1)}, u32[]{:S(2)}, u32[]{:S(2)}) collective-permute-start(bf16[256,1024]{1,0:T(8,128)(2,1)} %collective-permute-done), channel_id=1, source_target_pairs={{0,16},{16,0},{1,17},{17,1},{2,18},{18,2},{3,19},{19,3},{4,20},{20... | collective-permute-start | bytes 1572872 | tf_op jit(solution)/shard_map/ppermute | solution.py:26
  41.3 15.1 %collective-permute-start.2 = (bf16[256,1024]{1,0:T(8,128)(2,1)}, bf16[256,1024]{1,0:T(8,128)(2,1)S(1)}, u32[]{:S(2)}, u32[]{:S(2)}) collective-permute-start(bf16[256,1024]{1,0:T(8,128)(2,1)} %collective-permute-done), channel_id=1, source_target_pairs={{0,1},{1,0},{2,3},{3,2},{4,5},{5,4},{6,7},{7,6},{8,9},{9,8},{10,11... | collective-permute-start | bytes 1572872 | tf_op jit(solution)/shard_map/ppermute | solution.py:26
  41.3 22.5 %collective-permute-start.20 = (bf16[256,1024]{1,0:T(8,128)(2,1)S(1)}, bf16[256,1024]{1,0:T(8,128)(2,1)S(1)}, u32[]{:S(2)}, u32[]{:S(2)}) collective-permute-start(bf16[256,1024]{1,0:T(8,128)(2,1)S(1)} %collective-permute-done.16), channel_id=1, source_target_pairs={{0,4},{4,12},{12,8},{8,0},{1,5},{5,13},{13,9},{9,1},{2,6},{6,14},{... | collective-permute-start | bytes 1572872 | tf_op jit(solution)/shard_map/ppermute | solution.py:260
  42.6 23.1 %collective-permute-start.17 = (bf16[256,1024]{1,0:T(8,128)(2,1)S(1)}, bf16[256,1024]{1,0:T(8,128)(2,1)S(1)}, u32[]{:S(2)}, u32[]{:S(2)}) collective-permute-start(bf16[256,1024]{1,0:T(8,128)(2,1)S(1)} %collective-permute-done.16), channel_id=1, source_target_pairs={{0,16},{16,0},{1,17},{17,1},{2,18},{18,2},{3,19},{19,3},{4,20},{20... | collective-permute-start | bytes 1572872 | tf_op jit(solution)/shard_map/ppermute | solution.py:26
  52.5 13.8 %collective-permute-start.15 = (bf16[256,1024]{1,0:T(8,128)(2,1)}, bf16[256,1024]{1,0:T(8,128)(2,1)S(1)}, u32[]{:S(2)}, u32[]{:S(2)}) collective-permute-start(bf16[256,1024]{1,0:T(8,128)(2,1)} %collective-permute-done.13), channel_id=1, source_target_pairs={{0,1},{1,0},{2,3},{3,2},{4,5},{5,4},{6,7},{7,6},{8,9},{9,8},{10,11... | collective-permute-start | bytes 1572872 | tf_op jit(solution)/shard_map/ppermute | solution.py:26
  56.4 17.8 %collective-permute-start.8 = (bf16[256,1024]{1,0:T(8,128)(2,1)S(1)}, bf16[256,1024]{1,0:T(8,128)(2,1)S(1)}, u32[]{:S(2)}, u32[]{:S(2)}) collective-permute-start(bf16[256,1024]{1,0:T(8,128)(2,1)S(1)} %collective-permute-done.4), channel_id=1, source_target_pairs={{0,4},{4,12},{12,8},{8,0},{1,5},{5,13},{13,9},{9,1},{2,6},{6,14},{... | collective-permute-start | bytes 1572872 | tf_op jit(solution)/shard_map/ppermute | solution.py:260
  63.8 14.9 %collective-permute-start.5 = (bf16[256,1024]{1,0:T(8,128)(2,1)S(1)}, bf16[256,1024]{1,0:T(8,128)(2,1)S(1)}, u32[]{:S(2)}, u32[]{:S(2)}) collective-permute-start(bf16[256,1024]{1,0:T(8,128)(2,1)S(1)} %collective-permute-done.4), channel_id=1, source_target_pairs={{0,16},{16,0},{1,17},{17,1},{2,18},{18,2},{3,19},{19,3},{4,20},{20... | collective-permute-start | bytes 1572872 | tf_op jit(solution)/shard_map/ppermute | solution.py:26
  65.6 14.9 %collective-permute-start.3 = (bf16[256,1024]{1,0:T(8,128)(2,1)}, bf16[256,1024]{1,0:T(8,128)(2,1)S(1)}, u32[]{:S(2)}, u32[]{:S(2)}) collective-permute-start(bf16[256,1024]{1,0:T(8,128)(2,1)} %collective-permute-done.1), channel_id=1, source_target_pairs={{0,1},{1,0},{2,3},{3,2},{4,5},{5,4},{6,7},{7,6},{8,9},{9,8},{10,11... | collective-permute-start | bytes 1572872 | tf_op jit(solution)/shard_map/ppermute | solution.py:26
  66.1 23.7 %collective-permute-start.21 = (bf16[256,1024]{1,0:T(8,128)(2,1)S(1)}, bf16[256,1024]{1,0:T(8,128)(2,1)S(1)}, u32[]{:S(2)}, u32[]{:S(2)}) collective-permute-start(bf16[256,1024]{1,0:T(8,128)(2,1)S(1)} %collective-permute-done.20), channel_id=1, source_target_pairs={{0,16},{16,0},{1,17},{17,1},{2,18},{18,2},{3,19},{19,3},{4,20},{20... | collective-permute-start | bytes 1572872 | tf_op jit(solution)/shard_map/ppermute | solution.py:26
  66.3 23.5 %collective-permute-start.19 = (bf16[256,1024]{1,0:T(8,128)(2,1)S(1)}, bf16[256,1024]{1,0:T(8,128)(2,1)S(1)}, u32[]{:S(2)}, u32[]{:S(2)}) collective-permute-start(bf16[256,1024]{1,0:T(8,128)(2,1)S(1)} %collective-permute-done.17), channel_id=1, source_target_pairs={{0,1},{1,0},{2,3},{3,2},{4,5},{5,4},{6,7},{7,6},{8,9},{9,8},{10,11... | collective-permute-start | bytes 1572872 | tf_op jit(solution)/shard_map/ppermute | solution.py:26
  74.2 17.5 %collective-permute-start.6 = (bf16[256,1024]{1,0:T(8,128)(2,1)S(1)}, bf16[256,1024]{1,0:T(8,128)(2,1)S(1)}, u32[]{:S(2)}, u32[]{:S(2)}) collective-permute-start(bf16[256,1024]{1,0:T(8,128)(2,1)S(1)} %collective-permute-done.4), channel_id=1, source_target_pairs={{0,1},{1,0},{2,3},{3,2},{4,5},{5,4},{6,7},{7,6},{8,9},{9,8},{10,11... | collective-permute-start | bytes 1572872 | tf_op jit(solution)/shard_map/ppermute | solution.py:26
  78.6 19.9 %collective-permute-start.9 = (bf16[256,1024]{1,0:T(8,128)(2,1)S(1)}, bf16[256,1024]{1,0:T(8,128)(2,1)S(1)}, u32[]{:S(2)}, u32[]{:S(2)}) collective-permute-start(bf16[256,1024]{1,0:T(8,128)(2,1)S(1)} %collective-permute-done.8), channel_id=1, source_target_pairs={{0,16},{16,0},{1,17},{17,1},{2,18},{18,2},{3,19},{19,3},{4,20},{20... | collective-permute-start | bytes 1572872 | tf_op jit(solution)/shard_map/ppermute | solution.py:26
  80.5 18.0 %collective-permute-start.7 = (bf16[256,1024]{1,0:T(8,128)(2,1)S(1)}, bf16[256,1024]{1,0:T(8,128)(2,1)S(1)}, u32[]{:S(2)}, u32[]{:S(2)}) collective-permute-start(bf16[256,1024]{1,0:T(8,128)(2,1)S(1)} %collective-permute-done.5), channel_id=1, source_target_pairs={{0,1},{1,0},{2,3},{3,2},{4,5},{5,4},{6,7},{7,6},{8,9},{9,8},{10,11... | collective-permute-start | bytes 1572872 | tf_op jit(solution)/shard_map/ppermute | solution.py:26
  109.7 21.9 %collective-permute-start.26 = (bf16[64,2048]{1,0:T(8,128)(2,1)S(1)}, bf16[64,2048]{1,0:T(8,128)(2,1)}, u32[]{:S(2)}, u32[]{:S(2)}) collective-permute-start(bf16[64,2048]{1,0:T(8,128)(2,1)S(1)} %get-tuple-element.38.refs_0_.refs_4_), channel_id=1, source_target_pairs={{0,8},{4,12},{8,0},{12,4},{1,9},{5,13},{9,1},{13,5},{2,10},{6,14},... | collective-permute-start | bytes 786440 | tf_op jit(solution)/shard_map/ppermute | solution.py:30
  113.1 18.6 %collective-permute-start.27 = (bf16[64,2048]{1,0:T(8,128)(2,1)S(1)}, bf16[64,2048]{1,0:T(8,128)(2,1)}, u32[]{:S(2)}, u32[]{:S(2)}) collective-permute-start(bf16[64,2048]{1,0:T(8,128)(2,1)S(1)} %get-tuple-element.38.refs_0_.refs_4_), channel_id=1, source_target_pairs={{0,12},{4,8},{8,4},{12,0},{1,13},{5,9},{9,5},{13,1},{2,14},{6,10},... | collective-permute-start | bytes 786440 | tf_op jit(solution)/shard_map/ppermute | solution.py:30
  113.7 24.2 %collective-permute-start.33 = (s32[32,4]{1,0:T(8,128)S(1)}, s32[32,4]{1,0:T(8,128)S(1)}, u32[]{:S(2)}, u32[]{:S(2)}) collective-permute-start(s32[32,4]{1,0:T(8,128)S(1)} %copy.26), channel_id=1, source_target_pairs={{0,1},{1,0},{2,3},{3,2},{4,5},{5,4},{6,7},{7,6},{8,9},{9,8},{10,11... | collective-permute-start | bytes 1544 | tf_op jit(solution)/shard_map/ppermute | solution.py:26
  113.8 19.6 %collective-permute-start.28 = (bf16[64,2048]{1,0:T(8,128)(2,1)S(1)}, bf16[64,2048]{1,0:T(8,128)(2,1)}, u32[]{:S(2)}, u32[]{:S(2)}) collective-permute-start(bf16[64,2048]{1,0:T(8,128)(2,1)S(1)} %get-tuple-element.38.refs_0_.refs_4_), channel_id=1, source_target_pairs={{0,1},{1,0},{2,3},{3,2},{4,5},{5,4},{6,7},{7,6},{8,9},{9,8},{10,11... | collective-permute-start | bytes 786440 | tf_op jit(solution)/shard_map/ppermute | solution.py:26
  151.3 17.3 %collective-permute-start.37 = (f32[33,1024]{1,0:T(8,128)S(1)}, f32[33,1024]{1,0:T(8,128)S(1)}, u32[]{:S(2)}, u32[]{:S(2)}) collective-permute-start(f32[33,1024]{1,0:T(8,128)S(1)} %dynamic-slice_add_fusion), channel_id=1, source_target_pairs={{0,8},{4,12},{8,0},{12,4},{1,9},{5,13},{9,1},{13,5},{2,10},{6,14},... | collective-permute-start | bytes 405512 | tf_op jit(solution)/shard_map/ppermute | solution.py:30
  (29 other events, 287.1 us)

commit v5 on v4

--- a/solution.py
+++ b/solution.py
@@ -208,8 +208,14 @@
     per_shard = anchors // dp
     docs = 2 * per_shard
 
-    block_shard = shard ^ jnp.arange(dp, dtype=jnp.int32)
-    owner_block = shard ^ negative_owner[0]
+    order = [0] + list(range(1, dp, 2)) + list(range(dp - 2 + dp % 2, 0, -2))
+    hops = [(order[i], order[(i + 1) % dp]) for i in range(dp)]
+    order_table = jnp.array(order, jnp.int32)
+    place_table = jnp.array([order.index(i) for i in range(dp)], jnp.int32)
+    place = place_table[shard]
+
+    block_shard = order_table[(place - jnp.arange(dp, dtype=jnp.int32)) % dp]
+    owner_block = (place - place_table[negative_owner[0]]) % dp
     rel_list = (owner_block * docs + per_shard + negative_pool_row[0]).reshape(dp, per_shard, -1)
     list_c = rel_list[block_shard].reshape(anchors, -1).T
     pool_col = owner_block * per_shard + negative_pool_row[0]
@@ -221,11 +227,6 @@
     quarter = frozen_weight.shape[0] // 4
     shard_rows = frozen_weight.shape[0]
     chunk = cols // chunk_count
-    order = list(range(1, dp, 2)) + list(range(dp - 2 + dp % 2, 0, -2))
-    order = [0] + order
-    hops = [(order[i], order[(i + 1) % dp]) for i in range(dp)]
-    place = jnp.array([order.index(i) for i in range(dp)], jnp.int32)[shard]
-    order_table = jnp.array(order, jnp.int32)
     quarters = [
         (group * 2 + side),
         ((1 - group) * 2 + side),
@@ -239,14 +240,7 @@
     lora_mid = dot_nn(tokens, adapter_down).astype(jnp.bfloat16)
     own_cols = lax.dynamic_slice_in_dim(tokens, lax.axis_index("mp") * cols, cols, 1)
     own_tokens = lax.dynamic_slice_in_dim(tokens, shard * shard_rows, shard_rows, 1)
-    states = []
-    for h in range(chunk_count):
-        part = slice(h * chunk, (h + 1) * chunk)
-        states.append(
-            own_cols[:, part].astype(jnp.float32)
-            + dot_nn(own_tokens, frozen_weight[:, part])
-            + dot_nn(lora_mid, adapter_up[:, part])
-        )
+    states = [None] * chunk_count
     for step in range(1, dp):
         origin = order_table[(place - step) % dp]
         step_tokens = jnp.concatenate(
@@ -257,7 +251,15 @@
             axis=1,
         )
         for h in range(chunk_count):
+            part = slice(h * chunk, (h + 1) * chunk)
             moving[h] = lax.ppermute(moving[h], "dp", hops)
+            if step == 1:
+                own_first, mid_first, _ = lax.optimization_barrier((own_tokens, lora_mid, moving[h]))
+                states[h] = (
+                    own_cols[:, part].astype(jnp.float32)
+                    + dot_nn(own_first, frozen_weight[:, part])
+                    + dot_nn(mid_first, adapter_up[:, part])
+                )
             across = swap(moving[h], "groups")
             rows = [moving[h], across, swap(moving[h], "pair"), swap(across, "pair")]
             states[h] = states[h] + dot_nn(step_tokens, jnp.concatenate(rows, axis=0))
@@ -280,7 +282,9 @@
     )
     pooled = (doc_sums / counts[:, None]).astype(jnp.bfloat16)
 
-    own_blocks = [pooled] + [partner(pooled, "dp", j) for j in range(1, dp)]
+    own_blocks = [pooled]
+    for _ in range(1, dp):
+        own_blocks.append(lax.ppermute(own_blocks[-1], "dp", hops))
     other_blocks = [swap(block, "pair") for block in own_blocks]
     rows = dp * docs
     sums, sorted_oth = call(
@@ -342,10 +346,23 @@
     kept = lax.dynamic_slice_in_dim(grads, side * half, half, 1)
     sent = lax.dynamic_slice_in_dim(grads, (1 - side) * half, half, 1)
     kept = kept + swap(sent, "pair")
-    level = [kept] + [partner(kept, "dp", j) for j in range(1, dp)]
-    while len(level) > 1:
-        level = [level[i] + level[i + 1] for i in range(0, len(level), 2)]
-    total = level[0]
+    piece = half // dp
+    parts = kept.reshape(-1, dp, piece)
+
+    def part_of(owner):
+        return lax.dynamic_index_in_dim(parts, owner, 1, keepdims=False)
+
+    total = part_of(shard)
+    for j in range(1, dp):
+        total = total + partner(part_of(shard ^ j), "dp", j)
+    gathered = jnp.stack([total] + [partner(total, "dp", j) for j in range(1, dp)], axis=1)
+    total = jnp.concatenate(
+        [
+            lax.dynamic_index_in_dim(gathered, shard ^ j, 1, keepdims=False)
+            for j in range(dp)
+        ],
+        axis=1,
+    )
     received = swap(total, "pair")
     grads = jnp.concatenate(
         [jnp.where(side == 0, total, received), jnp.where(side == 0, received, total)], axis=1

time: 173 us -> 167 us (0.965)
  waiting for transfers between devices: 91 us -> 76.9 us
  local copies, waits for them, and re-layouts: 4.28 us -> 10.4 us
    ppermute x6, waiting for transfers between devices: 28.9 us -> 7.82 us  [partner(): lax.ppermute(x, axis, [(i, i ^ flip) for i in range(lax.axis_size(axis))])]
    ppermute x0 -> x3, waiting for transfers between devices: none -> 19.6 us  [body(): own_blocks.append(lax.ppermute(own_blocks[-1], 'dp', hops))]
    ppermute x28, waiting for transfers between devices: 30.3 us -> 18.6 us  [swap(): return lax.ppermute(x, axis, [(0, 1), (1, 0)])]
    ppermute x28, starting transfers between devices: 15.6 us -> 18.6 us  [swap(): return lax.ppermute(x, axis, [(0, 1), (1, 0)])]
    ppermute x6, starting transfers between devices: 11.1 us -> 8.9 us  [partner(): lax.ppermute(x, axis, [(i, i ^ flip) for i in range(lax.axis_size(axis))])]
    dynamic_slice x1, local copies, waits for them, and re-layouts: 0.14 us -> 1.88 us  [body(): lax.dynamic_slice_in_dim(tokens, lax.axis_index('mp') * cols, cols, 1)]
  transfers between devices with their start and end apart: 40 -> 43, of which waited for: 20 -> 21; matrix products, arithmetic and copies ran while one was open for 16% -> 18% of each run, Pallas kernels for 1% -> 1%
where the time goes in v5:
time: 167 us; the launch traced here: 166 us
  waiting for transfers between devices  76.9 us (46%)
  starting transfers between devices  37.4 us (22%)
  matrix products  28.7 us (17%)
  local copies, waits for them, and re-layouts  10.4 us (6%)
  between operations  5.37 us (3%)
  Pallas kernels  4.1 us (2%)
  other arithmetic  3.09 us (2%)
    ppermute x6, waiting for transfers between devices, body(): moving[h] = lax.ppermute(moving[h], 'dp', hops)  30.9 us
    dot_general x18, matrix products, dot_nn(): jnp.dot(a, b, precision=precision, preferred_element_type=jnp.float32)  27.8 us
    ppermute x3, waiting for transfers between devices, body(): own_blocks.append(lax.ppermute(own_blocks[-1], 'dp', hops))  19.6 us
    ppermute x28, waiting for transfers between devices, swap(): return lax.ppermute(x, axis, [(0, 1), (1, 0)])  18.6 us
    ppermute x28, starting transfers between devices, swap(): return lax.ppermute(x, axis, [(0, 1), (1, 0)])  18.6 us
    ppermute x6, starting transfers between devices, partner(): lax.ppermute(x, axis, [(i, i ^ flip) for i in range(lax.axis_size(axis))])  8.9 us
    ppermute x6, starting transfers between devices, body(): moving[h] = lax.ppermute(moving[h], 'dp', hops)  8.86 us
    ppermute x6, waiting for transfers between devices, partner(): lax.ppermute(x, axis, [(i, i ^ flip) for i in range(lax.axis_size(axis))])  7.82 us
  transfers between devices with their start and end apart: 43, of which 21 were waited for; matrix products, arithmetic and copies ran while one was open for 18% of the time, Pallas kernels for 1%

profile of v5, /device:TPU:0, one launch (start us, length us, event | category | flops | bytes accessed | tf_op | source)
XLA Modules:
  0.0 166.0 jit_solution(11751376586481978360)
XLA Ops:
  2.8 3.0 %collective-permute-start = (bf16[256,1024]{1,0:T(8,128)(2,1)S(1)}, bf16[256,1024]{1,0:T(8,128)(2,1)}, u32[]{:S(2)}, u32[]{:S(2)}) collective-permute-start(bf16[256,1024]{1,0:T(8,128)(2,1)S(1)} %get-tuple-element.29), channel_id=1, source_target_pairs={{0,4},{4,12},{12,8},{8,0},{1,5},{5,13},{13,9},{9,1},{2,6},{6,14},{... | collective-permute-start | bytes 1572872 | tf_op jit(solution)/shard_map/ppermute | solution.py:255
  5.8 2.6 %collective-permute-start.12 = (bf16[256,1024]{1,0:T(8,128)(2,1)}, bf16[256,1024]{1,0:T(8,128)(2,1)}, u32[]{:S(2)}, u32[]{:S(2)}) collective-permute-start(bf16[256,1024]{1,0:T(8,128)(2,1)} %get-tuple-element.30), channel_id=1, source_target_pairs={{0,4},{4,12},{12,8},{8,0},{1,5},{5,13},{13,9},{9,1},{2,6},{6,14},{... | collective-permute-start | bytes 1572872 | tf_op jit(solution)/shard_map/ppermute | solution.py:255
  8.4 3.4 %fusion.59 = bf16[512,16]{0,1:T(8,128)(2,1)S(1)} fusion(bf16[4096,16]{0,1:T(8,128)(2,1)S(1)} %copy-done, bf16[1,512,4096]{2,1,0:T(8,128)(2,1)} %param.10), kind=kOutput, calls=%fused_computation.66 | convolution fusion | flops 67117056 | bytes 4341760 | tf_op jit(solution)/shard_map/dot_general | solution.py:22
  25.2 5.6 %collective-permute-done.12 = bf16[256,1024]{1,0:T(8,128)(2,1)} collective-permute-done((bf16[256,1024]{1,0:T(8,128)(2,1)}, bf16[256,1024]{1,0:T(8,128)(2,1)}, u32[]{:S(2)}, u32[]{:S(2)}) %collective-permute-start.12) | collective-permute-done | bytes 524320 | tf_op jit(solution)/shard_map/ppermute | solution.py:255
  32.8 2.9 %fusion.52 = f32[512,1024]{1,0:T(8,128)S(1)} fusion(bf16[512,1024]{1,0:T(8,128)(2,1)S(1)} %dynamic-slice_bitcast_fusion.1, bf16[1024,2048]{1,0:T(8,128)(2,1)} %param.12), kind=kOutput, calls=%fused_computation.61 | convolution fusion | flops 1073741824 | bytes 5242880 | tf_op jit(solution)/shard_map/dot_general | solution.py:22
  36.7 5.4 %collective-permute-done.4 = bf16[256,1024]{1,0:T(8,128)(2,1)} collective-permute-done((bf16[256,1024]{1,0:T(8,128)(2,1)}, bf16[256,1024]{1,0:T(8,128)(2,1)}, u32[]{:S(2)}, u32[]{:S(2)}) %collective-permute-start.4) | collective-permute-done | bytes 524320 | tf_op jit(solution)/shard_map/ppermute | solution.py:255
  46.7 6.5 %collective-permute-done.16 = bf16[256,1024]{1,0:T(8,128)(2,1)S(1)} collective-permute-done((bf16[256,1024]{1,0:T(8,128)(2,1)}, bf16[256,1024]{1,0:T(8,128)(2,1)S(1)}, u32[]{:S(2)}, u32[]{:S(2)}) %collective-permute-start.16) | collective-permute-done | bytes 524320 | tf_op jit(solution)/shard_map/ppermute | solution.py:255
  57.1 7.4 %collective-permute-done.8 = bf16[256,1024]{1,0:T(8,128)(2,1)S(1)} collective-permute-done((bf16[256,1024]{1,0:T(8,128)(2,1)}, bf16[256,1024]{1,0:T(8,128)(2,1)S(1)}, u32[]{:S(2)}, u32[]{:S(2)}) %collective-permute-start.8) | collective-permute-done | bytes 524320 | tf_op jit(solution)/shard_map/ppermute | solution.py:255
  66.4 2.6 %fusion.2 = f32[512,1024]{1,0:T(8,128)S(1)} fusion(bf16[256,1024]{1,0:T(8,128)(2,1)S(1)} %collective-permute-done.3, bf16[256,1024]{1,0:T(8,128)(2,1)} %collective-permute-done.2, bf16[256,1024]{1,0:T(8,128)(2,1)} %collective-permute-done.1, bf16[256,1024]{1,0:T(8,128)(2,1)} %collective-permute-done, bf16[512,256]{1,0:T(8,128)(2,1)S(1)} %copy-done.16, ...), kind=kOutput, calls=%fused_computation.5 | convolution fusion | flops 1086324736 | bytes 5242880 | tf_op jit(solution)/shard_map/dot_general | solution.py:22
  69.7 5.2 %collective-permute-done.20 = bf16[256,1024]{1,0:T(8,128)(2,1)S(1)} collective-permute-done((bf16[256,1024]{1,0:T(8,128)(2,1)S(1)}, bf16[256,1024]{1,0:T(8,128)(2,1)S(1)}, u32[]{:S(2)}, u32[]{:S(2)}) %collective-permute-start.20) | collective-permute-done | bytes 524320 | tf_op jit(solution)/shard_map/ppermute | solution.py:255
  76.5 2.3 %fusion.26 = f32[512,1024]{1,0:T(8,128)S(1)} fusion(bf16[256,1024]{1,0:T(8,128)(2,1)S(1)} %collective-permute-done.15, bf16[256,1024]{1,0:T(8,128)(2,1)S(1)} %collective-permute-done.14, bf16[256,1024]{1,0:T(8,128)(2,1)S(1)} %collective-permute-done.13, bf16[256,1024]{1,0:T(8,128)(2,1)} %collective-permute-done.12, bf16[512,256]{1,0:T(8,128)(2,1)S(1)} %copy-done.16, ...), kind=kOutput, calls=%fused_computation.29 | convolution fusion | flops 1086324736 | bytes 5242880 | tf_op jit(solution)/shard_map/dot_general | solution.py:22
  79.4 2.3 %fusion.10 = f32[512,1024]{1,0:T(8,128)S(1)} fusion(bf16[256,1024]{1,0:T(8,128)(2,1)S(1)} %collective-permute-done.7, bf16[256,1024]{1,0:T(8,128)(2,1)S(1)} %collective-permute-done.6, bf16[256,1024]{1,0:T(8,128)(2,1)S(1)} %collective-permute-done.5, bf16[256,1024]{1,0:T(8,128)(2,1)} %collective-permute-done.4, bf16[512,256]{1,0:T(8,128)(2,1)S(1)} %copy-done.12, ...), kind=kOutput, calls=%fused_computation.13 | convolution fusion | flops 1086324736 | bytes 5242880 | tf_op jit(solution)/shard_map/dot_general | solution.py:22
  81.9 6.6 %collective-permute-done.21 = bf16[256,1024]{1,0:T(8,128)(2,1)S(1)} collective-permute-done((bf16[256,1024]{1,0:T(8,128)(2,1)S(1)}, bf16[256,1024]{1,0:T(8,128)(2,1)S(1)}, u32[]{:S(2)}, u32[]{:S(2)}) %collective-permute-start.21) | collective-permute-done | bytes 524320 | tf_op jit(solution)/shard_map/ppermute | solution.py:26
  89.8 3.0 %fusion.119 = (bf16[512,1024]{1,0:T(8,128)(2,1)S(1)}, f32[512]{0:T(512)S(1)}, f32[512,1024]{1,0:T(8,128)}) fusion(bf16[256,1024]{1,0:T(8,128)(2,1)S(1)} %collective-permute-done.11, bf16[256,1024]{1,0:T(8,128)(2,1)S(1)} %collective-permute-done.10, bf16[256,1024]{1,0:T(8,128)(2,1)S(1)} %collective-permute-done.9, ...), kind=kOutput, calls=%fused_computation.188 | convolution fusion | flops 1091042816 | bytes 15730688 | tf_op jit(solution)/shard_map/dot_general | solution.py:22
  92.8 4.2 %fusion.118 = (bf16[512,1024]{1,0:T(8,128)(2,1)S(1)}, f32[512]{0:T(512)S(1)}, f32[512,1024]{1,0:T(8,128)}) fusion(bf16[256,1024]{1,0:T(8,128)(2,1)S(1)} %collective-permute-done.23, bf16[256,1024]{1,0:T(8,128)(2,1)S(1)} %collective-permute-done.22, bf16[256,1024]{1,0:T(8,128)(2,1)S(1)} %collective-permute-done.21, ...), kind=kOutput, calls=%fused_computation.187 | convolution fusion | flops 1091042816 | bytes 15730688 | tf_op jit(solution)/shard_map/dot_general | solution.py:22
  104.5 7.2 %collective-permute-done.25.refs_1_ = bf16[64,2048]{1,0:T(8,128)(2,1)S(1)} collective-permute-done((bf16[64,2048]{1,0:T(8,128)(2,1)S(1)}, bf16[64,2048]{1,0:T(8,128)(2,1)S(1)}, u32[]{:S(2)}, u32[]{:S(2)}) %collective-permute-start.25) | collective-permute-done | bytes 262176 | tf_op jit(solution)/shard_map/ppermute | solution.py:287
  113.4 5.9 %collective-permute-done.26.refs_2_ = bf16[64,2048]{1,0:T(8,128)(2,1)} collective-permute-done((bf16[64,2048]{1,0:T(8,128)(2,1)S(1)}, bf16[64,2048]{1,0:T(8,128)(2,1)}, u32[]{:S(2)}, u32[]{:S(2)}) %collective-permute-start.26) | collective-permute-done | bytes 262176 | tf_op jit(solution)/shard_map/ppermute | solution.py:287
  120.4 6.5 %collective-permute-done.27.refs_3_ = bf16[64,2048]{1,0:T(8,128)(2,1)} collective-permute-done((bf16[64,2048]{1,0:T(8,128)(2,1)}, bf16[64,2048]{1,0:T(8,128)(2,1)}, u32[]{:S(2)}, u32[]{:S(2)}) %collective-permute-start.27) | collective-permute-done | bytes 262176 | tf_op jit(solution)/shard_map/ppermute | solution.py:287
  132.8 4.1 %collective-permute-done.32.refs_1_ = f32[296,128]{1,0:T(8,128)S(1)} collective-permute-done((f32[296,128]{1,0:T(8,128)S(1)}, f32[296,128]{1,0:T(8,128)S(1)}, u32[]{:S(2)}, u32[]{:S(2)}) %collective-permute-start.32) | collective-permute-done | bytes 151584 | tf_op jit(solution)/shard_map/ppermute | solution.py:26
  140.6 2.6 %collective-permute-done.34 = f32[24,640]{1,0:T(8,128)S(1)} collective-permute-done((f32[24,640]{1,0:T(8,128)S(1)}, f32[24,640]{1,0:T(8,128)S(1)}, u32[]{:S(2)}, u32[]{:S(2)}) %collective-permute-start.34) | collective-permute-done | bytes 61472 | tf_op jit(solution)/shard_map/ppermute | solution.py:26
  146.8 3.4 %collective-permute-start.37 = (f32[33,256]{1,0:T(8,128)S(1)}, f32[33,256]{1,0:T(8,128)S(1)}, u32[]{:S(2)}, u32[]{:S(2)}) collective-permute-start(f32[33,256]{1,0:T(8,128)S(1)} %bitcast.128), channel_id=1, source_target_pairs={{0,8},{4,12},{8,0},{12,4},{1,9},{5,13},{9,1},{13,5},{2,10},{6,14},... | collective-permute-start | bytes 101384 | tf_op jit(solution)/shard_map/ppermute | solution.py:30
  150.8 2.2 %collective-permute-done.37 = f32[33,256]{1,0:T(8,128)S(1)} collective-permute-done((f32[33,256]{1,0:T(8,128)S(1)}, f32[33,256]{1,0:T(8,128)S(1)}, u32[]{:S(2)}, u32[]{:S(2)}) %collective-permute-start.37) | collective-permute-done | bytes 33824 | tf_op jit(solution)/shard_map/ppermute | solution.py:30
  153.0 3.0 %collective-permute-done.38 = f32[33,256]{1,0:T(8,128)S(1)} collective-permute-done((f32[33,256]{1,0:T(8,128)S(1)}, f32[33,256]{1,0:T(8,128)S(1)}, u32[]{:S(2)}, u32[]{:S(2)}) %collective-permute-start.38) | collective-permute-done | bytes 33824 | tf_op jit(solution)/shard_map/ppermute | solution.py:30
  157.3 3.1 %collective-permute-start.41 = (f32[33,256]{1,0:T(8,128)S(1)}, f32[33,256]{1,0:T(8,128)S(1)}, u32[]{:S(2)}, u32[]{:S(2)}) collective-permute-start(f32[33,256]{1,0:T(8,128)S(1)} %fusion.79), channel_id=1, source_target_pairs={{0,12},{4,8},{8,4},{12,0},{1,13},{5,9},{9,5},{13,1},{2,14},{6,10},... | collective-permute-start | bytes 101384 | tf_op jit(solution)/shard_map/ppermute | solution.py:30
  (180 shorter events, 59.7 us)
Async XLA Ops:
  2.8 16.9 %collective-permute-start = (bf16[256,1024]{1,0:T(8,128)(2,1)S(1)}, bf16[256,1024]{1,0:T(8,128)(2,1)}, u32[]{:S(2)}, u32[]{:S(2)}) collective-permute-start(bf16[256,1024]{1,0:T(8,128)(2,1)S(1)} %get-tuple-element.29), channel_id=1, source_target_pairs={{0,4},{4,12},{12,8},{8,0},{1,5},{5,13},{13,9},{9,1},{2,6},{6,14},{... | collective-permute-start | bytes 1572872 | tf_op jit(solution)/shard_map/ppermute | solution.py:255
  5.8 25.1 %collective-permute-start.12 = (bf16[256,1024]{1,0:T(8,128)(2,1)}, bf16[256,1024]{1,0:T(8,128)(2,1)}, u32[]{:S(2)}, u32[]{:S(2)}) collective-permute-start(bf16[256,1024]{1,0:T(8,128)(2,1)} %get-tuple-element.30), channel_id=1, source_target_pairs={{0,4},{4,12},{12,8},{8,0},{1,5},{5,13},{13,9},{9,1},{2,6},{6,14},{... | collective-permute-start | bytes 1572872 | tf_op jit(solution)/shard_map/ppermute | solution.py:255
  19.6 16.0 %collective-permute-start.1 = (bf16[256,1024]{1,0:T(8,128)(2,1)}, bf16[256,1024]{1,0:T(8,128)(2,1)}, u32[]{:S(2)}, u32[]{:S(2)}) collective-permute-start(bf16[256,1024]{1,0:T(8,128)(2,1)} %collective-permute-done), channel_id=1, source_target_pairs={{0,16},{16,0},{1,17},{17,1},{2,18},{18,2},{3,19},{19,3},{4,20},{20... | collective-permute-start | bytes 1572872 | tf_op jit(solution)/shard_map/ppermute | solution.py:26
  21.5 15.0 %collective-permute-start.2 = (bf16[256,1024]{1,0:T(8,128)(2,1)}, bf16[256,1024]{1,0:T(8,128)(2,1)}, u32[]{:S(2)}, u32[]{:S(2)}) collective-permute-start(bf16[256,1024]{1,0:T(8,128)(2,1)} %collective-permute-done), channel_id=1, source_target_pairs={{0,1},{1,0},{2,3},{3,2},{4,5},{5,4},{6,7},{7,6},{8,9},{9,8},{10,11... | collective-permute-start | bytes 1572872 | tf_op jit(solution)/shard_map/ppermute | solution.py:26
  21.5 20.6 %collective-permute-start.4 = (bf16[256,1024]{1,0:T(8,128)(2,1)}, bf16[256,1024]{1,0:T(8,128)(2,1)}, u32[]{:S(2)}, u32[]{:S(2)}) collective-permute-start(bf16[256,1024]{1,0:T(8,128)(2,1)} %collective-permute-done), channel_id=1, source_target_pairs={{0,4},{4,12},{12,8},{8,0},{1,5},{5,13},{13,9},{9,1},{2,6},{6,14},{... | collective-permute-start | bytes 1572872 | tf_op jit(solution)/shard_map/ppermute | solution.py:255
  30.9 14.4 %collective-permute-start.13 = (bf16[256,1024]{1,0:T(8,128)(2,1)}, bf16[256,1024]{1,0:T(8,128)(2,1)S(1)}, u32[]{:S(2)}, u32[]{:S(2)}) collective-permute-start(bf16[256,1024]{1,0:T(8,128)(2,1)} %collective-permute-done.12), channel_id=1, source_target_pairs={{0,16},{16,0},{1,17},{17,1},{2,18},{18,2},{3,19},{19,3},{4,20},{20... | collective-permute-start | bytes 1572872 | tf_op jit(solution)/shard_map/ppermute | solution.py:26
  32.8 12.6 %collective-permute-start.14 = (bf16[256,1024]{1,0:T(8,128)(2,1)}, bf16[256,1024]{1,0:T(8,128)(2,1)S(1)}, u32[]{:S(2)}, u32[]{:S(2)}) collective-permute-start(bf16[256,1024]{1,0:T(8,128)(2,1)} %collective-permute-done.12), channel_id=1, source_target_pairs={{0,1},{1,0},{2,3},{3,2},{4,5},{5,4},{6,7},{7,6},{8,9},{9,8},{10,11... | collective-permute-start | bytes 1572872 | tf_op jit(solution)/shard_map/ppermute | solution.py:26
  35.7 17.6 %collective-permute-start.16 = (bf16[256,1024]{1,0:T(8,128)(2,1)}, bf16[256,1024]{1,0:T(8,128)(2,1)S(1)}, u32[]{:S(2)}, u32[]{:S(2)}) collective-permute-start(bf16[256,1024]{1,0:T(8,128)(2,1)} %collective-permute-done.12), channel_id=1, source_target_pairs={{0,4},{4,12},{12,8},{8,0},{1,5},{5,13},{13,9},{9,1},{2,6},{6,14},{... | collective-permute-start | bytes 1572872 | tf_op jit(solution)/shard_map/ppermute | solution.py:255
  36.5 18.6 %collective-permute-start.3 = (bf16[256,1024]{1,0:T(8,128)(2,1)}, bf16[256,1024]{1,0:T(8,128)(2,1)S(1)}, u32[]{:S(2)}, u32[]{:S(2)}) collective-permute-start(bf16[256,1024]{1,0:T(8,128)(2,1)} %collective-permute-done.1), channel_id=1, source_target_pairs={{0,1},{1,0},{2,3},{3,2},{4,5},{5,4},{6,7},{7,6},{8,9},{9,8},{10,11... | collective-permute-start | bytes 1572872 | tf_op jit(solution)/shard_map/ppermute | solution.py:26
  42.1 13.9 %collective-permute-start.5 = (bf16[256,1024]{1,0:T(8,128)(2,1)}, bf16[256,1024]{1,0:T(8,128)(2,1)S(1)}, u32[]{:S(2)}, u32[]{:S(2)}) collective-permute-start(bf16[256,1024]{1,0:T(8,128)(2,1)} %collective-permute-done.4), channel_id=1, source_target_pairs={{0,16},{16,0},{1,17},{17,1},{2,18},{18,2},{3,19},{19,3},{4,20},{20... | collective-permute-start | bytes 1572872 | tf_op jit(solution)/shard_map/ppermute | solution.py:26
  45.3 11.2 %collective-permute-start.6 = (bf16[256,1024]{1,0:T(8,128)(2,1)}, bf16[256,1024]{1,0:T(8,128)(2,1)S(1)}, u32[]{:S(2)}, u32[]{:S(2)}) collective-permute-start(bf16[256,1024]{1,0:T(8,128)(2,1)} %collective-permute-done.4), channel_id=1, source_target_pairs={{0,1},{1,0},{2,3},{3,2},{4,5},{5,4},{6,7},{7,6},{8,9},{9,8},{10,11... | collective-permute-start | bytes 1572872 | tf_op jit(solution)/shard_map/ppermute | solution.py:26
  45.4 19.1 %collective-permute-start.8 = (bf16[256,1024]{1,0:T(8,128)(2,1)}, bf16[256,1024]{1,0:T(8,128)(2,1)S(1)}, u32[]{:S(2)}, u32[]{:S(2)}) collective-permute-start(bf16[256,1024]{1,0:T(8,128)(2,1)} %collective-permute-done.4), channel_id=1, source_target_pairs={{0,4},{4,12},{12,8},{8,0},{1,5},{5,13},{13,9},{9,1},{2,6},{6,14},{... | collective-permute-start | bytes 1572872 | tf_op jit(solution)/shard_map/ppermute | solution.py:255
  53.3 15.9 %collective-permute-start.17 = (bf16[256,1024]{1,0:T(8,128)(2,1)S(1)}, bf16[256,1024]{1,0:T(8,128)(2,1)S(1)}, u32[]{:S(2)}, u32[]{:S(2)}) collective-permute-start(bf16[256,1024]{1,0:T(8,128)(2,1)S(1)} %collective-permute-done.16), channel_id=1, source_target_pairs={{0,16},{16,0},{1,17},{17,1},{2,18},{18,2},{3,19},{19,3},{4,20},{20... | collective-permute-start | bytes 1572872 | tf_op jit(solution)/shard_map/ppermute | solution.py:26
  55.1 19.7 %collective-permute-start.20 = (bf16[256,1024]{1,0:T(8,128)(2,1)S(1)}, bf16[256,1024]{1,0:T(8,128)(2,1)S(1)}, u32[]{:S(2)}, u32[]{:S(2)}) collective-permute-start(bf16[256,1024]{1,0:T(8,128)(2,1)S(1)} %collective-permute-done.16), channel_id=1, source_target_pairs={{0,4},{4,12},{12,8},{8,0},{1,5},{5,13},{13,9},{9,1},{2,6},{6,14},{... | collective-permute-start | bytes 1572872 | tf_op jit(solution)/shard_map/ppermute | solution.py:255
  56.0 13.0 %collective-permute-start.15 = (bf16[256,1024]{1,0:T(8,128)(2,1)S(1)}, bf16[256,1024]{1,0:T(8,128)(2,1)S(1)}, u32[]{:S(2)}, u32[]{:S(2)}) collective-permute-start(bf16[256,1024]{1,0:T(8,128)(2,1)S(1)} %collective-permute-done.13), channel_id=1, source_target_pairs={{0,1},{1,0},{2,3},{3,2},{4,5},{5,4},{6,7},{7,6},{8,9},{9,8},{10,11... | collective-permute-start | bytes 1572872 | tf_op jit(solution)/shard_map/ppermute | solution.py:26
  56.5 22.3 %collective-permute-start.7 = (bf16[256,1024]{1,0:T(8,128)(2,1)S(1)}, bf16[256,1024]{1,0:T(8,128)(2,1)S(1)}, u32[]{:S(2)}, u32[]{:S(2)}) collective-permute-start(bf16[256,1024]{1,0:T(8,128)(2,1)S(1)} %collective-permute-done.5), channel_id=1, source_target_pairs={{0,1},{1,0},{2,3},{3,2},{4,5},{5,4},{6,7},{7,6},{8,9},{9,8},{10,11... | collective-permute-start | bytes 1572872 | tf_op jit(solution)/shard_map/ppermute | solution.py:26
  64.5 14.4 %collective-permute-start.9 = (bf16[256,1024]{1,0:T(8,128)(2,1)S(1)}, bf16[256,1024]{1,0:T(8,128)(2,1)S(1)}, u32[]{:S(2)}, u32[]{:S(2)}) collective-permute-start(bf16[256,1024]{1,0:T(8,128)(2,1)S(1)} %collective-permute-done.8), channel_id=1, source_target_pairs={{0,16},{16,0},{1,17},{17,1},{2,18},{18,2},{3,19},{19,3},{4,20},{20... | collective-permute-start | bytes 1572872 | tf_op jit(solution)/shard_map/ppermute | solution.py:26
  69.1 12.7 %collective-permute-start.18 = (bf16[256,1024]{1,0:T(8,128)(2,1)S(1)}, bf16[256,1024]{1,0:T(8,128)(2,1)S(1)}, u32[]{:S(2)}, u32[]{:S(2)}) collective-permute-start(bf16[256,1024]{1,0:T(8,128)(2,1)S(1)} %collective-permute-done.16), channel_id=1, source_target_pairs={{0,1},{1,0},{2,3},{3,2},{4,5},{5,4},{6,7},{7,6},{8,9},{9,8},{10,11... | collective-permute-start | bytes 1572872 | tf_op jit(solution)/shard_map/ppermute | solution.py:26
  69.2 19.3 %collective-permute-start.19 = (bf16[256,1024]{1,0:T(8,128)(2,1)S(1)}, bf16[256,1024]{1,0:T(8,128)(2,1)S(1)}, u32[]{:S(2)}, u32[]{:S(2)}) collective-permute-start(bf16[256,1024]{1,0:T(8,128)(2,1)S(1)} %collective-permute-done.17), channel_id=1, source_target_pairs={{0,1},{1,0},{2,3},{3,2},{4,5},{5,4},{6,7},{7,6},{8,9},{9,8},{10,11... | collective-permute-start | bytes 1572872 | tf_op jit(solution)/shard_map/ppermute | solution.py:26
  74.9 13.6 %collective-permute-start.21 = (bf16[256,1024]{1,0:T(8,128)(2,1)S(1)}, bf16[256,1024]{1,0:T(8,128)(2,1)S(1)}, u32[]{:S(2)}, u32[]{:S(2)}) collective-permute-start(bf16[256,1024]{1,0:T(8,128)(2,1)S(1)} %collective-permute-done.20), channel_id=1, source_target_pairs={{0,16},{16,0},{1,17},{17,1},{2,18},{18,2},{3,19},{19,3},{4,20},{20... | collective-permute-start | bytes 1572872 | tf_op jit(solution)/shard_map/ppermute | solution.py:26
  78.8 11.0 %collective-permute-start.10 = (bf16[256,1024]{1,0:T(8,128)(2,1)S(1)}, bf16[256,1024]{1,0:T(8,128)(2,1)S(1)}, u32[]{:S(2)}, u32[]{:S(2)}) collective-permute-start(bf16[256,1024]{1,0:T(8,128)(2,1)S(1)} %collective-permute-done.8), channel_id=1, source_target_pairs={{0,1},{1,0},{2,3},{3,2},{4,5},{5,4},{6,7},{7,6},{8,9},{9,8},{10,11... | collective-permute-start | bytes 1572872 | tf_op jit(solution)/shard_map/ppermute | solution.py:26
  78.9 10.9 %collective-permute-start.11 = (bf16[256,1024]{1,0:T(8,128)(2,1)S(1)}, bf16[256,1024]{1,0:T(8,128)(2,1)S(1)}, u32[]{:S(2)}, u32[]{:S(2)}) collective-permute-start(bf16[256,1024]{1,0:T(8,128)(2,1)S(1)} %collective-permute-done.9), channel_id=1, source_target_pairs={{0,1},{1,0},{2,3},{3,2},{4,5},{5,4},{6,7},{7,6},{8,9},{9,8},{10,11... | collective-permute-start | bytes 1572872 | tf_op jit(solution)/shard_map/ppermute | solution.py:26
  81.7 11.1 %collective-permute-start.22 = (bf16[256,1024]{1,0:T(8,128)(2,1)S(1)}, bf16[256,1024]{1,0:T(8,128)(2,1)S(1)}, u32[]{:S(2)}, u32[]{:S(2)}) collective-permute-start(bf16[256,1024]{1,0:T(8,128)(2,1)S(1)} %collective-permute-done.20), channel_id=1, source_target_pairs={{0,1},{1,0},{2,3},{3,2},{4,5},{5,4},{6,7},{7,6},{8,9},{9,8},{10,11... | collective-permute-start | bytes 1572872 | tf_op jit(solution)/shard_map/ppermute | solution.py:26
  112.0 20.8 %collective-permute-start.33 = (s32[32,4]{1,0:T(8,128)S(1)}, s32[32,4]{1,0:T(8,128)S(1)}, u32[]{:S(2)}, u32[]{:S(2)}) collective-permute-start(s32[32,4]{1,0:T(8,128)S(1)} %fusion.91), channel_id=1, source_target_pairs={{0,1},{1,0},{2,3},{3,2},{4,5},{5,4},{6,7},{7,6},{8,9},{9,8},{10,11... | collective-permute-start | bytes 1544 | tf_op jit(solution)/shard_map/ppermute | solution.py:26
  (43 other events, 405.4 us)

commit v6 on v5

--- a/solution.py
+++ b/solution.py
@@ -36,13 +36,31 @@
     return lax.psum(x, axis)
 
 
-def call(kernel, outs, args, scratch=(), flops=1 << 24):
+def widths(cols):
+    tiles = cols // 128
+    base, more = divmod(tiles, chunk_count)
+    return [128 * (base + (i >= chunk_count - more)) for i in range(chunk_count)]
+
+
+def spans(cols):
+    out, at = [], 0
+    for width in widths(cols):
+        out.append((at, at + width))
+        at += width
+    return out
+
+
+def after(x, *deps):
+    return lax.optimization_barrier((x, *deps))[0]
+
+
+def call(kernel, outs, args, scratch=(), flops=1 << 24, vmem=16):
     size = sum(a.size * a.dtype.itemsize for a in args)
     return pl.pallas_call(
         kernel,
         out_shape=outs,
         scratch_shapes=list(scratch),
-        compiler_params=pltpu.CompilerParams(vmem_limit_bytes=48 << 20),
+        compiler_params=pltpu.CompilerParams(vmem_limit_bytes=vmem << 20),
         cost_estimate=pl.CostEstimate(flops=flops, bytes_accessed=size, transcendentals=0),
     )(*args)
 
@@ -64,18 +82,19 @@
 
 
 def gram_kernel(blocks, *refs):
-    own, oth = refs[:blocks], refs[blocks : 2 * blocks]
-    out_ref, sorted_ref, own_ref = refs[2 * blocks :]
-    docs = own[0].shape[0]
-    half = docs // 2
+    own, oth = refs[: 2 * blocks], refs[2 * blocks : 4 * blocks]
+    out_ref, sorted_ref, own_ref = refs[4 * blocks :]
+    half = own[0].shape[0]
+    docs = 2 * half
     anchors = blocks * half
     for j in range(blocks):
-        own_ref[j * docs : (j + 1) * docs] = own[j][...]
-        sorted_ref[j * half : (j + 1) * half] = oth[j][:half]
-        sorted_ref[anchors + j * half : anchors + (j + 1) * half] = oth[j][half:]
+        own_ref[j * docs : j * docs + half] = own[j][...]
+        own_ref[j * docs + half : (j + 1) * docs] = own[blocks + j][...]
+        sorted_ref[j * half : (j + 1) * half] = oth[j][...]
+        sorted_ref[anchors + j * half : anchors + (j + 1) * half] = oth[blocks + j][...]
     rows = blocks * docs
     out_ref[:rows] = dot_nt(own_ref[...], sorted_ref[:anchors])
-    out_ref[rows : rows + half] = dot_nt(own[0][:half], sorted_ref[anchors:])
+    out_ref[rows : rows + half] = dot_nt(own[0][...], sorted_ref[anchors:])
     own_f = own_ref[...].astype(jnp.float32)
     oth_f = sorted_ref[...].astype(jnp.float32)
     own_sq = as_row(jnp.sum(own_f * own_f, axis=1, keepdims=True))
@@ -168,12 +187,9 @@
     gain_grad_ref[...] = jnp.sum(per_doc * doc_sums_ref[...], axis=0, keepdims=True) / gain
 
     gained_b = gained.astype(jnp.bfloat16)
-    chunk = state_refs[0].shape[1]
-    tok_doc = dot_nt(gained_b[:, :chunk], state_refs[0][...])
-    for i in range(1, chunks):
-        tok_doc = tok_doc + dot_nt(
-            gained_b[:, i * chunk : (i + 1) * chunk], state_refs[i][...]
-        )
+    tok_doc = 0.0
+    for (low, high), state_ref in zip(spans(gained_b.shape[1]), state_refs):
+        tok_doc = tok_doc + dot_nt(gained_b[:, low:high], state_ref[...])
     tokens = tok_doc.shape[1]
     rank = up_ref.shape[0]
     doc_id = lax.broadcasted_iota(jnp.int32, (docs, tokens), 0)
@@ -226,21 +242,26 @@
     group = lax.axis_index("groups")
     quarter = frozen_weight.shape[0] // 4
     shard_rows = frozen_weight.shape[0]
-    chunk = cols // chunk_count
+    parts = spans(cols)
     quarters = [
         (group * 2 + side),
         ((1 - group) * 2 + side),
         (group * 2 + 1 - side),
         ((1 - group) * 2 + 1 - side),
     ]
-    moving = [
-        lax.dynamic_slice(frozen_weight, (quarters[0] * quarter, h * chunk), (quarter, chunk))
-        for h in range(chunk_count)
-    ]
+    moving = []
+    for low, high in parts:
+        corner = quarters[0] * quarter
+        moving.append(lax.dynamic_slice(frozen_weight, (corner, low), (quarter, high - low)))
     lora_mid = dot_nn(tokens, adapter_down).astype(jnp.bfloat16)
     own_cols = lax.dynamic_slice_in_dim(tokens, lax.axis_index("mp") * cols, cols, 1)
     own_tokens = lax.dynamic_slice_in_dim(tokens, shard * shard_rows, shard_rows, 1)
     states = [None] * chunk_count
+    ringed = []
+    for step in range(1, dp):
+        for h in range(chunk_count):
+            ringed.append(lax.ppermute(ringed[-chunk_count] if step > 1 else moving[h], "dp", hops))
+    event = 0
     for step in range(1, dp):
         origin = order_table[(place - step) % dp]
         step_tokens = jnp.concatenate(
@@ -250,19 +271,21 @@
             ],
             axis=1,
         )
-        for h in range(chunk_count):
-            part = slice(h * chunk, (h + 1) * chunk)
-            moving[h] = lax.ppermute(moving[h], "dp", hops)
+        for h, (low, high) in enumerate(parts):
+            moved = ringed[event]
             if step == 1:
-                own_first, mid_first, _ = lax.optimization_barrier((own_tokens, lora_mid, moving[h]))
+                own_first, mid_first = own_tokens, lora_mid
+                own_first, mid_first = after((own_first, mid_first), moved)
                 states[h] = (
-                    own_cols[:, part].astype(jnp.float32)
-                    + dot_nn(own_first, frozen_weight[:, part])
-                    + dot_nn(mid_first, adapter_up[:, part])
+                    own_cols[:, low:high].astype(jnp.float32)
+                    + dot_nn(own_first, frozen_weight[:, low:high])
+                    + dot_nn(mid_first, adapter_up[:, low:high])
                 )
-            across = swap(moving[h], "groups")
-            rows = [moving[h], across, swap(moving[h], "pair"), swap(across, "pair")]
-            states[h] = states[h] + dot_nn(step_tokens, jnp.concatenate(rows, axis=0))
+            across = swap(moved, "groups")
+            lhs = step_tokens
+            rows = [moved, across, swap(moved, "pair"), swap(across, "pair")]
+            states[h] = states[h] + dot_nn(lhs, jnp.concatenate(rows, axis=0))
+            event += 1
     states_b = [x.astype(jnp.bfloat16) for x in states]
     squares = sum_over(sum(jnp.sum(x * x, axis=1) for x in states), "mp")
     inv_rms = lax.rsqrt(squares / width + 1e-05)
@@ -276,15 +299,17 @@
     doc_sums = jnp.concatenate(
         [
             dot_nn(member_b, (x * inv_rms[:, None] * g[None, :]).astype(jnp.bfloat16))
-            for x, g in zip(states, jnp.split(gain, chunk_count))
+            for x, g in zip(states, [gain[low:high] for low, high in parts])
         ],
         axis=1,
     )
     pooled = (doc_sums / counts[:, None]).astype(jnp.bfloat16)
 
-    own_blocks = [pooled]
+    own_anchors, own_pools = [pooled[:per_shard]], [pooled[per_shard:]]
     for _ in range(1, dp):
-        own_blocks.append(lax.ppermute(own_blocks[-1], "dp", hops))
+        own_anchors.append(lax.ppermute(own_anchors[-1], "dp", hops))
+        own_pools.append(lax.ppermute(own_pools[-1], "dp", hops))
+    own_blocks = own_anchors + own_pools
     other_blocks = [swap(block, "pair") for block in own_blocks]
     rows = dp * docs
     sums, sorted_oth = call(
@@ -295,8 +320,9 @@
         ),
         own_blocks + other_blocks,
         [pltpu.VMEM((rows, cols), jnp.bfloat16)],
-    )
-    up_parts = jnp.split(adapter_up, chunk_count, axis=1)
+        vmem=16 if dp <= 4 else 48,
+    )
+    up_parts = [adapter_up[:, low:high] for low, high in parts]
     up_states = sum(dot_nt(u, x) for u, x in zip(up_parts, states_b))
     if lax.axis_size("mp") == 2:
         sums = [sums, swap(sums, "mp")]
@@ -325,6 +351,7 @@
             labels[None],
         ]
         + states_b,
+        vmem=16 if dp <= 4 else 48,
     )
     losses = losses[:, :per_shard]
     small = sum_over(small, "mp")
@@ -346,23 +373,12 @@
     kept = lax.dynamic_slice_in_dim(grads, side * half, half, 1)
     sent = lax.dynamic_slice_in_dim(grads, (1 - side) * half, half, 1)
     kept = kept + swap(sent, "pair")
-    piece = half // dp
-    parts = kept.reshape(-1, dp, piece)
-
-    def part_of(owner):
-        return lax.dynamic_index_in_dim(parts, owner, 1, keepdims=False)
-
-    total = part_of(shard)
-    for j in range(1, dp):
-        total = total + partner(part_of(shard ^ j), "dp", j)
-    gathered = jnp.stack([total] + [partner(total, "dp", j) for j in range(1, dp)], axis=1)
-    total = jnp.concatenate(
-        [
-            lax.dynamic_index_in_dim(gathered, shard ^ j, 1, keepdims=False)
-            for j in range(dp)
-        ],
-        axis=1,
-    )
+    kept = kept.astype(jnp.bfloat16)
+    level = [kept] + [partner(kept, "dp", j) for j in range(1, dp)]
+    level = [x.astype(jnp.float32) for x in level]
+    while len(level) > 1:
+        level = [level[i] + level[i + 1] for i in range(0, len(level), 2)]
+    total = level[0]
     received = swap(total, "pair")
     grads = jnp.concatenate(
         [jnp.where(side == 0, total, received), jnp.where(side == 0, received, total)], axis=1

time: 167 us -> 163 us (0.976)
  starting transfers between devices: 37.4 us -> 31.6 us
  other arithmetic: 3.09 us -> 5.11 us
    ppermute x28 -> x32, waiting for transfers between devices: 18.6 us -> 34.6 us  [swap(): return lax.ppermute(x, axis, [(0, 1), (1, 0)])]
    ppermute x9 -> x12, waiting for transfers between devices: 50.5 us -> 35.8 us  [the longest x6 17.7 us: body(): lax.ppermute(ringed[-chunk_count] if step > 1 else moving[h], 'dp', hops)]
    ppermute x6 -> x3, starting transfers between devices: 8.9 us -> 4.44 us  [partner(): lax.ppermute(x, axis, [(i, i ^ flip) for i in range(lax.axis_size(axis))])]
    ppermute x6 -> x3, waiting for transfers between devices: 7.82 us -> 5.43 us  [partner(): lax.ppermute(x, axis, [(i, i ^ flip) for i in range(lax.axis_size(axis))])]
    ppermute x28 -> x32, starting transfers between devices: 18.6 us -> 17.4 us  [swap(): return lax.ppermute(x, axis, [(0, 1), (1, 0)])]
    ppermute x9 -> x12, starting transfers between devices: 9.94 us -> 9.83 us  [the longest x6 9 us: body(): lax.ppermute(ringed[-chunk_count] if step > 1 else moving[h], 'dp', hops)]
  transfers between devices with their start and end apart: 43 -> 47, of which waited for: 21 -> 25; matrix products, arithmetic and copies ran while one was open for 18% -> 20% of each run, Pallas kernels for 1% -> 1%
where the time goes in v6:
time: 163 us; the launch traced here: 162 us
  waiting for transfers between devices  75.8 us (47%)
  starting transfers between devices  31.6 us (19%)
  matrix products  28.9 us (18%)
  local copies, waits for them, and re-layouts  11.5 us (7%)
  between operations  5.26 us (3%)
  other arithmetic  5.11 us (3%)
  Pallas kernels  4.01 us (2%)
    ppermute x32, waiting for transfers between devices, swap(): return lax.ppermute(x, axis, [(0, 1), (1, 0)])  34.6 us
    dot_general x18, matrix products, dot_nn(): jnp.dot(a, b, precision=precision, preferred_element_type=jnp.float32)  28 us
    ppermute x6, waiting for transfers between devices, body(): lax.ppermute(ringed[-chunk_count] if step > 1 else moving[h], 'dp', hops)  17.7 us
    ppermute x32, starting transfers between devices, swap(): return lax.ppermute(x, axis, [(0, 1), (1, 0)])  17.4 us
    ppermute x3, waiting for transfers between devices, body(): own_anchors.append(lax.ppermute(own_anchors[-1], 'dp', hops))  10.6 us
    ppermute x6, starting transfers between devices, body(): lax.ppermute(ringed[-chunk_count] if step > 1 else moving[h], 'dp', hops)  9 us
    ppermute x3, waiting for transfers between devices, body(): own_pools.append(lax.ppermute(own_pools[-1], 'dp', hops))  7.55 us
    ppermute x3, waiting for transfers between devices, partner(): lax.ppermute(x, axis, [(i, i ^ flip) for i in range(lax.axis_size(axis))])  5.43 us
  transfers between devices with their start and end apart: 47, of which 25 were waited for; matrix products, arithmetic and copies ran while one was open for 20% of the time, Pallas kernels for 1%

profile of v6, /device:TPU:0, one launch (start us, length us, event | category | flops | bytes accessed | tf_op | source)
XLA Modules:
  0.0 162.3 jit_solution(1271650828509074949)
XLA Ops:
  2.8 3.0 %collective-permute-start = (bf16[256,1024]{1,0:T(8,128)(2,1)S(1)}, bf16[256,1024]{1,0:T(8,128)(2,1)}, u32[]{:S(2)}, u32[]{:S(2)}) collective-permute-start(bf16[256,1024]{1,0:T(8,128)(2,1)S(1)} %get-tuple-element.29), channel_id=1, source_target_pairs={{0,4},{4,12},{12,8},{8,0},{1,5},{5,13},{13,9},{9,1},{2,6},{6,14},{... | collective-permute-start | bytes 1572872 | tf_op jit(solution)/shard_map/ppermute | solution.py:263
  5.8 2.6 %collective-permute-start.12 = (bf16[256,1024]{1,0:T(8,128)(2,1)}, bf16[256,1024]{1,0:T(8,128)(2,1)}, u32[]{:S(2)}, u32[]{:S(2)}) collective-permute-start(bf16[256,1024]{1,0:T(8,128)(2,1)} %get-tuple-element.30), channel_id=1, source_target_pairs={{0,4},{4,12},{12,8},{8,0},{1,5},{5,13},{13,9},{9,1},{2,6},{6,14},{... | collective-permute-start | bytes 1572872 | tf_op jit(solution)/shard_map/ppermute | solution.py:263
  15.0 3.5 %fusion.59 = bf16[512,16]{0,1:T(8,128)(2,1)S(1)} fusion(bf16[4096,16]{0,1:T(8,128)(2,1)S(1)} %copy-done, bf16[1,512,4096]{2,1,0:T(8,128)(2,1)} %param.10), kind=kOutput, calls=%fused_computation.66 | convolution fusion | flops 67117056 | bytes 4341760 | tf_op jit(solution)/shard_map/dot_general | solution.py:22
  26.9 4.0 %collective-permute-done.12 = bf16[256,1024]{1,0:T(8,128)(2,1)} collective-permute-done((bf16[256,1024]{1,0:T(8,128)(2,1)}, bf16[256,1024]{1,0:T(8,128)(2,1)}, u32[]{:S(2)}, u32[]{:S(2)}) %collective-permute-start.12) | collective-permute-done | bytes 524320 | tf_op jit(solution)/shard_map/ppermute | solution.py:263
  32.8 2.9 %fusion.52 = f32[512,1024]{1,0:T(8,128)S(1)} fusion(bf16[512,1024]{1,0:T(8,128)(2,1)S(1)} %dynamic-slice_bitcast_fusion.1, bf16[1024,2048]{1,0:T(8,128)(2,1)} %param.12), kind=kOutput, calls=%fused_computation.61 | convolution fusion | flops 1073741824 | bytes 5242880 | tf_op jit(solution)/shard_map/dot_general | solution.py:22
  35.7 2.4 %collective-permute-done.1 = bf16[256,1024]{1,0:T(8,128)(2,1)} collective-permute-done((bf16[256,1024]{1,0:T(8,128)(2,1)}, bf16[256,1024]{1,0:T(8,128)(2,1)}, u32[]{:S(2)}, u32[]{:S(2)}) %collective-permute-start.1) | collective-permute-done | bytes 524320 | tf_op jit(solution)/shard_map/ppermute | solution.py:26
  38.6 3.6 %collective-permute-done.4 = bf16[256,1024]{1,0:T(8,128)(2,1)} collective-permute-done((bf16[256,1024]{1,0:T(8,128)(2,1)}, bf16[256,1024]{1,0:T(8,128)(2,1)}, u32[]{:S(2)}, u32[]{:S(2)}) %collective-permute-start.4) | collective-permute-done | bytes 524320 | tf_op jit(solution)/shard_map/ppermute | solution.py:263
  45.3 3.9 %collective-permute-done.13 = bf16[256,1024]{1,0:T(8,128)(2,1)S(1)} collective-permute-done((bf16[256,1024]{1,0:T(8,128)(2,1)}, bf16[256,1024]{1,0:T(8,128)(2,1)S(1)}, u32[]{:S(2)}, u32[]{:S(2)}) %collective-permute-start.13) | collective-permute-done | bytes 524320 | tf_op jit(solution)/shard_map/ppermute | solution.py:26
  56.1 4.4 %collective-permute-done.5 = bf16[256,1024]{1,0:T(8,128)(2,1)S(1)} collective-permute-done((bf16[256,1024]{1,0:T(8,128)(2,1)}, bf16[256,1024]{1,0:T(8,128)(2,1)S(1)}, u32[]{:S(2)}, u32[]{:S(2)}) %collective-permute-start.5) | collective-permute-done | bytes 524320 | tf_op jit(solution)/shard_map/ppermute | solution.py:26
  61.5 3.6 %collective-permute-done.8 = bf16[256,1024]{1,0:T(8,128)(2,1)S(1)} collective-permute-done((bf16[256,1024]{1,0:T(8,128)(2,1)}, bf16[256,1024]{1,0:T(8,128)(2,1)S(1)}, u32[]{:S(2)}, u32[]{:S(2)}) %collective-permute-start.8) | collective-permute-done | bytes 524320 | tf_op jit(solution)/shard_map/ppermute | solution.py:263
  66.6 2.6 %fusion.2 = f32[512,1024]{1,0:T(8,128)S(1)} fusion(bf16[256,1024]{1,0:T(8,128)(2,1)S(1)} %collective-permute-done.3, bf16[256,1024]{1,0:T(8,128)(2,1)} %collective-permute-done.2, bf16[256,1024]{1,0:T(8,128)(2,1)} %collective-permute-done.1, bf16[256,1024]{1,0:T(8,128)(2,1)} %collective-permute-done, bf16[512,256]{1,0:T(8,128)(2,1)S(1)} %copy-done.18, ...), kind=kOutput, calls=%fused_computation.5 | convolution fusion | flops 1086324736 | bytes 5242880 | tf_op jit(solution)/shard_map/dot_general | solution.py:22
  71.7 4.2 %collective-permute-done.20 = bf16[256,1024]{1,0:T(8,128)(2,1)S(1)} collective-permute-done((bf16[256,1024]{1,0:T(8,128)(2,1)S(1)}, bf16[256,1024]{1,0:T(8,128)(2,1)S(1)}, u32[]{:S(2)}, u32[]{:S(2)}) %collective-permute-start.20) | collective-permute-done | bytes 524320 | tf_op jit(solution)/shard_map/ppermute | solution.py:263
  79.9 3.1 %collective-permute-done.9 = bf16[256,1024]{1,0:T(8,128)(2,1)S(1)} collective-permute-done((bf16[256,1024]{1,0:T(8,128)(2,1)S(1)}, bf16[256,1024]{1,0:T(8,128)(2,1)S(1)}, u32[]{:S(2)}, u32[]{:S(2)}) %collective-permute-start.9) | collective-permute-done | bytes 524320 | tf_op jit(solution)/shard_map/ppermute | solution.py:26
  85.9 6.5 %collective-permute-done.21 = bf16[256,1024]{1,0:T(8,128)(2,1)S(1)} collective-permute-done((bf16[256,1024]{1,0:T(8,128)(2,1)S(1)}, bf16[256,1024]{1,0:T(8,128)(2,1)S(1)}, u32[]{:S(2)}, u32[]{:S(2)}) %collective-permute-start.21) | collective-permute-done | bytes 524320 | tf_op jit(solution)/shard_map/ppermute | solution.py:26
  93.8 3.0 %fusion.117 = (bf16[512,1024]{1,0:T(8,128)(2,1)S(1)}, f32[512]{0:T(512)S(1)}, f32[512,1024]{1,0:T(8,128)}) fusion(bf16[256,1024]{1,0:T(8,128)(2,1)S(1)} %collective-permute-done.11, bf16[256,1024]{1,0:T(8,128)(2,1)S(1)} %collective-permute-done.10, bf16[256,1024]{1,0:T(8,128)(2,1)S(1)} %collective-permute-done.9, ...), kind=kOutput, calls=%fused_computation.173 | convolution fusion | flops 1091042816 | bytes 15730688 | tf_op jit(solution)/shard_map/dot_general | solution.py:22
  96.8 4.2 %fusion.116 = (bf16[512,1024]{1,0:T(8,128)(2,1)S(1)}, f32[512]{0:T(512)S(1)}, f32[512,1024]{1,0:T(8,128)}) fusion(bf16[256,1024]{1,0:T(8,128)(2,1)S(1)} %collective-permute-done.23, bf16[256,1024]{1,0:T(8,128)(2,1)S(1)} %collective-permute-done.22, bf16[256,1024]{1,0:T(8,128)(2,1)S(1)} %collective-permute-done.21, ...), kind=kOutput, calls=%fused_computation.172 | convolution fusion | flops 1091042816 | bytes 15730688 | tf_op jit(solution)/shard_map/dot_general | solution.py:22
  108.0 6.5 %collective-permute-done.25.refs_1_ = bf16[32,2048]{1,0:T(8,128)(2,1)S(1)} collective-permute-done((bf16[32,2048]{1,0:T(8,128)(2,1)S(1)}, bf16[32,2048]{1,0:T(8,128)(2,1)S(1)}, u32[]{:S(2)}, u32[]{:S(2)}) %collective-permute-start.25) | collective-permute-done | bytes 131104 | tf_op jit(solution)/shard_map/ppermute | solution.py:310
  117.4 3.6 %collective-permute-done.26.refs_2_ = bf16[32,2048]{1,0:T(8,128)(2,1)} collective-permute-done((bf16[32,2048]{1,0:T(8,128)(2,1)S(1)}, bf16[32,2048]{1,0:T(8,128)(2,1)}, u32[]{:S(2)}, u32[]{:S(2)}) %collective-permute-start.26) | collective-permute-done | bytes 131104 | tf_op jit(solution)/shard_map/ppermute | solution.py:310
  120.9 2.7 %collective-permute-done.29.refs_6_ = bf16[32,2048]{1,0:T(8,128)(2,1)} collective-permute-done((bf16[32,2048]{1,0:T(8,128)(2,1)S(1)}, bf16[32,2048]{1,0:T(8,128)(2,1)}, u32[]{:S(2)}, u32[]{:S(2)}) %collective-permute-start.29) | collective-permute-done | bytes 131104 | tf_op jit(solution)/shard_map/ppermute | solution.py:311
  127.1 2.7 %collective-permute-done.30.refs_7_ = bf16[32,2048]{1,0:T(8,128)(2,1)} collective-permute-done((bf16[32,2048]{1,0:T(8,128)(2,1)}, bf16[32,2048]{1,0:T(8,128)(2,1)}, u32[]{:S(2)}, u32[]{:S(2)}) %collective-permute-start.30) | collective-permute-done | bytes 131104 | tf_op jit(solution)/shard_map/ppermute | solution.py:311
  136.0 4.3 %collective-permute-done.39.refs_1_ = f32[296,128]{1,0:T(8,128)S(1)} collective-permute-done((f32[296,128]{1,0:T(8,128)S(1)}, f32[296,128]{1,0:T(8,128)S(1)}, u32[]{:S(2)}, u32[]{:S(2)}) %collective-permute-start.39) | collective-permute-done | bytes 151584 | tf_op jit(solution)/shard_map/ppermute | solution.py:26
  143.7 2.8 %collective-permute-done.41 = f32[24,640]{1,0:T(8,128)S(1)} collective-permute-done((f32[24,640]{1,0:T(8,128)S(1)}, f32[24,640]{1,0:T(8,128)S(1)}, u32[]{:S(2)}, u32[]{:S(2)}) %collective-permute-start.41) | collective-permute-done | bytes 61472 | tf_op jit(solution)/shard_map/ppermute | solution.py:26
  150.3 3.7 %collective-permute-start.45 = (bf16[33,1024]{1,0:T(8,128)(2,1)S(1)}, bf16[33,1024]{1,0:T(8,128)(2,1)S(1)}, u32[]{:S(2)}, u32[]{:S(2)}) collective-permute-start(bf16[33,1024]{1,0:T(8,128)(2,1)S(1)} %add_convert_fusion), channel_id=1, source_target_pairs={{0,12},{4,8},{8,4},{12,0},{1,13},{5,9},{9,5},{13,1},{2,14},{6,10},... | collective-permute-start | bytes 202760 | tf_op jit(solution)/shard_map/ppermute | solution.py:30
  155.2 4.3 %collective-permute-done.44 = bf16[33,1024]{1,0:T(8,128)(2,1)S(1)} collective-permute-done((bf16[33,1024]{1,0:T(8,128)(2,1)S(1)}, bf16[33,1024]{1,0:T(8,128)(2,1)S(1)}, u32[]{:S(2)}, u32[]{:S(2)}) %collective-permute-start.44) | collective-permute-done | bytes 67616 | tf_op jit(solution)/shard_map/ppermute | solution.py:30
  (185 shorter events, 69.0 us)
Async XLA Ops:
  2.8 20.1 %collective-permute-start = (bf16[256,1024]{1,0:T(8,128)(2,1)S(1)}, bf16[256,1024]{1,0:T(8,128)(2,1)}, u32[]{:S(2)}, u32[]{:S(2)}) collective-permute-start(bf16[256,1024]{1,0:T(8,128)(2,1)S(1)} %get-tuple-element.29), channel_id=1, source_target_pairs={{0,4},{4,12},{12,8},{8,0},{1,5},{5,13},{13,9},{9,1},{2,6},{6,14},{... | collective-permute-start | bytes 1572872 | tf_op jit(solution)/shard_map/ppermute | solution.py:263
  5.8 25.1 %collective-permute-start.12 = (bf16[256,1024]{1,0:T(8,128)(2,1)}, bf16[256,1024]{1,0:T(8,128)(2,1)}, u32[]{:S(2)}, u32[]{:S(2)}) collective-permute-start(bf16[256,1024]{1,0:T(8,128)(2,1)} %get-tuple-element.30), channel_id=1, source_target_pairs={{0,4},{4,12},{12,8},{8,0},{1,5},{5,13},{13,9},{9,1},{2,6},{6,14},{... | collective-permute-start | bytes 1572872 | tf_op jit(solution)/shard_map/ppermute | solution.py:263
  22.9 15.2 %collective-permute-start.1 = (bf16[256,1024]{1,0:T(8,128)(2,1)}, bf16[256,1024]{1,0:T(8,128)(2,1)}, u32[]{:S(2)}, u32[]{:S(2)}) collective-permute-start(bf16[256,1024]{1,0:T(8,128)(2,1)} %collective-permute-done), channel_id=1, source_target_pairs={{0,16},{16,0},{1,17},{17,1},{2,18},{18,2},{3,19},{19,3},{4,20},{20... | collective-permute-start | bytes 1572872 | tf_op jit(solution)/shard_map/ppermute | solution.py:26
  24.5 14.1 %collective-permute-start.2 = (bf16[256,1024]{1,0:T(8,128)(2,1)}, bf16[256,1024]{1,0:T(8,128)(2,1)}, u32[]{:S(2)}, u32[]{:S(2)}) collective-permute-start(bf16[256,1024]{1,0:T(8,128)(2,1)} %collective-permute-done), channel_id=1, source_target_pairs={{0,1},{1,0},{2,3},{3,2},{4,5},{5,4},{6,7},{7,6},{8,9},{9,8},{10,11... | collective-permute-start | bytes 1572872 | tf_op jit(solution)/shard_map/ppermute | solution.py:26
  24.5 17.7 %collective-permute-start.4 = (bf16[256,1024]{1,0:T(8,128)(2,1)}, bf16[256,1024]{1,0:T(8,128)(2,1)}, u32[]{:S(2)}, u32[]{:S(2)}) collective-permute-start(bf16[256,1024]{1,0:T(8,128)(2,1)} %collective-permute-done), channel_id=1, source_target_pairs={{0,4},{4,12},{12,8},{8,0},{1,5},{5,13},{13,9},{9,1},{2,6},{6,14},{... | collective-permute-start | bytes 1572872 | tf_op jit(solution)/shard_map/ppermute | solution.py:263
  30.9 18.3 %collective-permute-start.13 = (bf16[256,1024]{1,0:T(8,128)(2,1)}, bf16[256,1024]{1,0:T(8,128)(2,1)S(1)}, u32[]{:S(2)}, u32[]{:S(2)}) collective-permute-start(bf16[256,1024]{1,0:T(8,128)(2,1)} %collective-permute-done.12), channel_id=1, source_target_pairs={{0,16},{16,0},{1,17},{17,1},{2,18},{18,2},{3,19},{19,3},{4,20},{20... | collective-permute-start | bytes 1572872 | tf_op jit(solution)/shard_map/ppermute | solution.py:26
  32.8 16.4 %collective-permute-start.14 = (bf16[256,1024]{1,0:T(8,128)(2,1)}, bf16[256,1024]{1,0:T(8,128)(2,1)S(1)}, u32[]{:S(2)}, u32[]{:S(2)}) collective-permute-start(bf16[256,1024]{1,0:T(8,128)(2,1)} %collective-permute-done.12), channel_id=1, source_target_pairs={{0,1},{1,0},{2,3},{3,2},{4,5},{5,4},{6,7},{7,6},{8,9},{9,8},{10,11... | collective-permute-start | bytes 1572872 | tf_op jit(solution)/shard_map/ppermute | solution.py:26
  38.1 14.3 %collective-permute-start.16 = (bf16[256,1024]{1,0:T(8,128)(2,1)}, bf16[256,1024]{1,0:T(8,128)(2,1)S(1)}, u32[]{:S(2)}, u32[]{:S(2)}) collective-permute-start(bf16[256,1024]{1,0:T(8,128)(2,1)} %collective-permute-done.12), channel_id=1, source_target_pairs={{0,4},{4,12},{12,8},{8,0},{1,5},{5,13},{13,9},{9,1},{2,6},{6,14},{... | collective-permute-start | bytes 1572872 | tf_op jit(solution)/shard_map/ppermute | solution.py:263
  38.6 15.5 %collective-permute-start.3 = (bf16[256,1024]{1,0:T(8,128)(2,1)}, bf16[256,1024]{1,0:T(8,128)(2,1)S(1)}, u32[]{:S(2)}, u32[]{:S(2)}) collective-permute-start(bf16[256,1024]{1,0:T(8,128)(2,1)} %collective-permute-done.1), channel_id=1, source_target_pairs={{0,1},{1,0},{2,3},{3,2},{4,5},{5,4},{6,7},{7,6},{8,9},{9,8},{10,11... | collective-permute-start | bytes 1572872 | tf_op jit(solution)/shard_map/ppermute | solution.py:26
  42.2 18.3 %collective-permute-start.5 = (bf16[256,1024]{1,0:T(8,128)(2,1)}, bf16[256,1024]{1,0:T(8,128)(2,1)S(1)}, u32[]{:S(2)}, u32[]{:S(2)}) collective-permute-start(bf16[256,1024]{1,0:T(8,128)(2,1)} %collective-permute-done.4), channel_id=1, source_target_pairs={{0,16},{16,0},{1,17},{17,1},{2,18},{18,2},{3,19},{19,3},{4,20},{20... | collective-permute-start | bytes 1572872 | tf_op jit(solution)/shard_map/ppermute | solution.py:26
  49.3 11.7 %collective-permute-start.6 = (bf16[256,1024]{1,0:T(8,128)(2,1)}, bf16[256,1024]{1,0:T(8,128)(2,1)S(1)}, u32[]{:S(2)}, u32[]{:S(2)}) collective-permute-start(bf16[256,1024]{1,0:T(8,128)(2,1)} %collective-permute-done.4), channel_id=1, source_target_pairs={{0,1},{1,0},{2,3},{3,2},{4,5},{5,4},{6,7},{7,6},{8,9},{9,8},{10,11... | collective-permute-start | bytes 1572872 | tf_op jit(solution)/shard_map/ppermute | solution.py:26
  49.3 15.8 %collective-permute-start.8 = (bf16[256,1024]{1,0:T(8,128)(2,1)}, bf16[256,1024]{1,0:T(8,128)(2,1)S(1)}, u32[]{:S(2)}, u32[]{:S(2)}) collective-permute-start(bf16[256,1024]{1,0:T(8,128)(2,1)} %collective-permute-done.4), channel_id=1, source_target_pairs={{0,4},{4,12},{12,8},{8,0},{1,5},{5,13},{13,9},{9,1},{2,6},{6,14},{... | collective-permute-start | bytes 1572872 | tf_op jit(solution)/shard_map/ppermute | solution.py:263
  52.5 19.3 %collective-permute-start.17 = (bf16[256,1024]{1,0:T(8,128)(2,1)S(1)}, bf16[256,1024]{1,0:T(8,128)(2,1)S(1)}, u32[]{:S(2)}, u32[]{:S(2)}) collective-permute-start(bf16[256,1024]{1,0:T(8,128)(2,1)S(1)} %collective-permute-done.16), channel_id=1, source_target_pairs={{0,16},{16,0},{1,17},{17,1},{2,18},{18,2},{3,19},{19,3},{4,20},{20... | collective-permute-start | bytes 1572872 | tf_op jit(solution)/shard_map/ppermute | solution.py:26
  54.0 21.9 %collective-permute-start.20 = (bf16[256,1024]{1,0:T(8,128)(2,1)S(1)}, bf16[256,1024]{1,0:T(8,128)(2,1)S(1)}, u32[]{:S(2)}, u32[]{:S(2)}) collective-permute-start(bf16[256,1024]{1,0:T(8,128)(2,1)S(1)} %collective-permute-done.16), channel_id=1, source_target_pairs={{0,4},{4,12},{12,8},{8,0},{1,5},{5,13},{13,9},{9,1},{2,6},{6,14},{... | collective-permute-start | bytes 1572872 | tf_op jit(solution)/shard_map/ppermute | solution.py:263
  61.0 18.8 %collective-permute-start.7 = (bf16[256,1024]{1,0:T(8,128)(2,1)S(1)}, bf16[256,1024]{1,0:T(8,128)(2,1)S(1)}, u32[]{:S(2)}, u32[]{:S(2)}) collective-permute-start(bf16[256,1024]{1,0:T(8,128)(2,1)S(1)} %collective-permute-done.5), channel_id=1, source_target_pairs={{0,1},{1,0},{2,3},{3,2},{4,5},{5,4},{6,7},{7,6},{8,9},{9,8},{10,11... | collective-permute-start | bytes 1572872 | tf_op jit(solution)/shard_map/ppermute | solution.py:26
  65.1 17.9 %collective-permute-start.9 = (bf16[256,1024]{1,0:T(8,128)(2,1)S(1)}, bf16[256,1024]{1,0:T(8,128)(2,1)S(1)}, u32[]{:S(2)}, u32[]{:S(2)}) collective-permute-start(bf16[256,1024]{1,0:T(8,128)(2,1)S(1)} %collective-permute-done.8), channel_id=1, source_target_pairs={{0,16},{16,0},{1,17},{17,1},{2,18},{18,2},{3,19},{19,3},{4,20},{20... | collective-permute-start | bytes 1572872 | tf_op jit(solution)/shard_map/ppermute | solution.py:26
  69.3 16.0 %collective-permute-start.18 = (bf16[256,1024]{1,0:T(8,128)(2,1)S(1)}, bf16[256,1024]{1,0:T(8,128)(2,1)S(1)}, u32[]{:S(2)}, u32[]{:S(2)}) collective-permute-start(bf16[256,1024]{1,0:T(8,128)(2,1)S(1)} %collective-permute-done.16), channel_id=1, source_target_pairs={{0,1},{1,0},{2,3},{3,2},{4,5},{5,4},{6,7},{7,6},{8,9},{9,8},{10,11... | collective-permute-start | bytes 1572872 | tf_op jit(solution)/shard_map/ppermute | solution.py:26
  71.7 20.7 %collective-permute-start.19 = (bf16[256,1024]{1,0:T(8,128)(2,1)S(1)}, bf16[256,1024]{1,0:T(8,128)(2,1)S(1)}, u32[]{:S(2)}, u32[]{:S(2)}) collective-permute-start(bf16[256,1024]{1,0:T(8,128)(2,1)S(1)} %collective-permute-done.17), channel_id=1, source_target_pairs={{0,1},{1,0},{2,3},{3,2},{4,5},{5,4},{6,7},{7,6},{8,9},{9,8},{10,11... | collective-permute-start | bytes 1572872 | tf_op jit(solution)/shard_map/ppermute | solution.py:26
  75.9 16.5 %collective-permute-start.21 = (bf16[256,1024]{1,0:T(8,128)(2,1)S(1)}, bf16[256,1024]{1,0:T(8,128)(2,1)S(1)}, u32[]{:S(2)}, u32[]{:S(2)}) collective-permute-start(bf16[256,1024]{1,0:T(8,128)(2,1)S(1)} %collective-permute-done.20), channel_id=1, source_target_pairs={{0,16},{16,0},{1,17},{17,1},{2,18},{18,2},{3,19},{19,3},{4,20},{20... | collective-permute-start | bytes 1572872 | tf_op jit(solution)/shard_map/ppermute | solution.py:26
  79.8 13.9 %collective-permute-start.10 = (bf16[256,1024]{1,0:T(8,128)(2,1)S(1)}, bf16[256,1024]{1,0:T(8,128)(2,1)S(1)}, u32[]{:S(2)}, u32[]{:S(2)}) collective-permute-start(bf16[256,1024]{1,0:T(8,128)(2,1)S(1)} %collective-permute-done.8), channel_id=1, source_target_pairs={{0,1},{1,0},{2,3},{3,2},{4,5},{5,4},{6,7},{7,6},{8,9},{9,8},{10,11... | collective-permute-start | bytes 1572872 | tf_op jit(solution)/shard_map/ppermute | solution.py:26
  83.0 10.7 %collective-permute-start.11 = (bf16[256,1024]{1,0:T(8,128)(2,1)S(1)}, bf16[256,1024]{1,0:T(8,128)(2,1)S(1)}, u32[]{:S(2)}, u32[]{:S(2)}) collective-permute-start(bf16[256,1024]{1,0:T(8,128)(2,1)S(1)} %collective-permute-done.9), channel_id=1, source_target_pairs={{0,1},{1,0},{2,3},{3,2},{4,5},{5,4},{6,7},{7,6},{8,9},{9,8},{10,11... | collective-permute-start | bytes 1572872 | tf_op jit(solution)/shard_map/ppermute | solution.py:26
  85.3 11.4 %collective-permute-start.22 = (bf16[256,1024]{1,0:T(8,128)(2,1)S(1)}, bf16[256,1024]{1,0:T(8,128)(2,1)S(1)}, u32[]{:S(2)}, u32[]{:S(2)}) collective-permute-start(bf16[256,1024]{1,0:T(8,128)(2,1)S(1)} %collective-permute-done.20), channel_id=1, source_target_pairs={{0,1},{1,0},{2,3},{3,2},{4,5},{5,4},{6,7},{7,6},{8,9},{9,8},{10,11... | collective-permute-start | bytes 1572872 | tf_op jit(solution)/shard_map/ppermute | solution.py:26
  117.3 9.2 %collective-permute-start.32 = (bf16[32,2048]{1,0:T(8,128)(2,1)S(1)}, bf16[32,2048]{1,0:T(8,128)(2,1)}, u32[]{:S(2)}, u32[]{:S(2)}) collective-permute-start(bf16[32,2048]{1,0:T(8,128)(2,1)S(1)} %collective-permute-done.25.refs_1_), channel_id=1, source_target_pairs={{0,1},{1,0},{2,3},{3,2},{4,5},{5,4},{6,7},{7,6},{8,9},{9,8},{10,11... | collective-permute-start | bytes 393224 | tf_op jit(solution)/shard_map/ppermute | solution.py:26
  149.6 9.8 %collective-permute-start.44 = (bf16[33,1024]{1,0:T(8,128)(2,1)S(1)}, bf16[33,1024]{1,0:T(8,128)(2,1)S(1)}, u32[]{:S(2)}, u32[]{:S(2)}) collective-permute-start(bf16[33,1024]{1,0:T(8,128)(2,1)S(1)} %add_convert_fusion), channel_id=1, source_target_pairs={{0,8},{4,12},{8,0},{12,4},{1,9},{5,13},{9,1},{13,5},{2,10},{6,14},... | collective-permute-start | bytes 202760 | tf_op jit(solution)/shard_map/ppermute | solution.py:30
  (49 other events, 477.5 us)

commit v7 on v6

--- a/solution.py
+++ b/solution.py
@@ -82,19 +82,18 @@
 
 
 def gram_kernel(blocks, *refs):
-    own, oth = refs[: 2 * blocks], refs[2 * blocks : 4 * blocks]
-    out_ref, sorted_ref, own_ref = refs[4 * blocks :]
-    half = own[0].shape[0]
-    docs = 2 * half
+    own, oth = refs[:blocks], refs[blocks : 2 * blocks]
+    out_ref, sorted_ref, own_ref = refs[2 * blocks :]
+    docs = own[0].shape[0]
+    half = docs // 2
     anchors = blocks * half
     for j in range(blocks):
-        own_ref[j * docs : j * docs + half] = own[j][...]
-        own_ref[j * docs + half : (j + 1) * docs] = own[blocks + j][...]
-        sorted_ref[j * half : (j + 1) * half] = oth[j][...]
-        sorted_ref[anchors + j * half : anchors + (j + 1) * half] = oth[blocks + j][...]
+        own_ref[j * docs : (j + 1) * docs] = own[j][...]
+        sorted_ref[j * half : (j + 1) * half] = oth[j][:half]
+        sorted_ref[anchors + j * half : anchors + (j + 1) * half] = oth[j][half:]
     rows = blocks * docs
     out_ref[:rows] = dot_nt(own_ref[...], sorted_ref[:anchors])
-    out_ref[rows : rows + half] = dot_nt(own[0][...], sorted_ref[anchors:])
+    out_ref[rows : rows + half] = dot_nt(own[0][:half], sorted_ref[anchors:])
     own_f = own_ref[...].astype(jnp.float32)
     oth_f = sorted_ref[...].astype(jnp.float32)
     own_sq = as_row(jnp.sum(own_f * own_f, axis=1, keepdims=True))
@@ -226,12 +225,20 @@
 
     order = [0] + list(range(1, dp, 2)) + list(range(dp - 2 + dp % 2, 0, -2))
     hops = [(order[i], order[(i + 1) % dp]) for i in range(dp)]
-    order_table = jnp.array(order, jnp.int32)
-    place_table = jnp.array([order.index(i) for i in range(dp)], jnp.int32)
-    place = place_table[shard]
-
-    block_shard = order_table[(place - jnp.arange(dp, dtype=jnp.int32)) % dp]
-    owner_block = (place - place_table[negative_owner[0]]) % dp
+    back_hops = [(b, a) for a, b in hops]
+
+    def place_of(index):
+        return jnp.where(index % 2 == 1, (index + 1) // 2, (dp - index // 2) % dp)
+
+    def shard_at(position):
+        return jnp.where(
+            position == 0, 0, jnp.where(position <= dp // 2, 2 * position - 1, 2 * (dp - position))
+        )
+
+    place = place_of(shard)
+
+    block_shard = shard_at((place - jnp.arange(dp, dtype=jnp.int32)) % dp)
+    owner_block = (place - place_of(negative_owner[0])) % dp
     rel_list = (owner_block * docs + per_shard + negative_pool_row[0]).reshape(dp, per_shard, -1)
     list_c = rel_list[block_shard].reshape(anchors, -1).T
     pool_col = owner_block * per_shard + negative_pool_row[0]
@@ -263,7 +270,7 @@
             ringed.append(lax.ppermute(ringed[-chunk_count] if step > 1 else moving[h], "dp", hops))
     event = 0
     for step in range(1, dp):
-        origin = order_table[(place - step) % dp]
+        origin = shard_at((place - step) % dp)
         step_tokens = jnp.concatenate(
             [
                 lax.dynamic_slice_in_dim(tokens, origin * shard_rows + q * quarter, quarter, 1)
@@ -305,11 +312,14 @@
     )
     pooled = (doc_sums / counts[:, None]).astype(jnp.bfloat16)
 
-    own_anchors, own_pools = [pooled[:per_shard]], [pooled[per_shard:]]
-    for _ in range(1, dp):
-        own_anchors.append(lax.ppermute(own_anchors[-1], "dp", hops))
-        own_pools.append(lax.ppermute(own_pools[-1], "dp", hops))
-    own_blocks = own_anchors + own_pools
+    own_blocks = [pooled] * dp
+    for j in range(1, dp):
+        if j <= dp // 2:
+            own_blocks[j] = lax.ppermute(own_blocks[j - 1], "dp", hops)
+        else:
+            own_blocks[dp + dp // 2 - j] = lax.ppermute(
+                own_blocks[(dp + dp // 2 - j + 1) % dp], "dp", back_hops
+            )
     other_blocks = [swap(block, "pair") for block in own_blocks]
     rows = dp * docs
     sums, sorted_oth = call(

time: 163 us -> 158 us (0.969)
  starting transfers between devices: 31.6 us -> 40.3 us
  between operations: 5.26 us -> 1.41 us
  waiting for transfers between devices: 75.8 us -> 72.4 us
  local copies, waits for them, and re-layouts: 11.5 us -> 8.29 us
  other arithmetic: 5.11 us -> 1.95 us
    ppermute x6, waiting for transfers between devices: 17.7 us -> 35.7 us  [body(): lax.ppermute(ringed[-chunk_count] if step > 1 else moving[h], 'dp', hops)]
    ppermute x32 -> x28, waiting for transfers between devices: 34.6 us -> 19 us  [swap(): return lax.ppermute(x, axis, [(0, 1), (1, 0)])]
    ppermute x6 -> x3, starting transfers between devices: 0.83 us -> 8.45 us  [the longest x2 6 us: body(): own_blocks[j] = lax.ppermute(own_blocks[j - 1], 'dp', hops)]
    ppermute x6 -> x3, waiting for transfers between devices: 18.1 us -> 11 us  [the longest x2 11 us: body(): own_blocks[j] = lax.ppermute(own_blocks[j - 1], 'dp', hops)]
    rem x2, other arithmetic: 1.97 us -> 0.17 us  [body(): owner_block = (place - place_of(negative_owner[0])) % dp]
    ppermute x32 -> x28, starting transfers between devices: 17.4 us -> 18 us  [swap(): return lax.ppermute(x, axis, [(0, 1), (1, 0)])]
  transfers between devices with their start and end apart: 47 -> 40, of which waited for: 25 -> 16; matrix products, arithmetic and copies ran while one was open for 20% -> 17% of each run, Pallas kernels for 1% -> 1%
where the time goes in v7:
time: 158 us; the launch traced here: 157 us
  waiting for transfers between devices  72.4 us (46%)
  starting transfers between devices  40.3 us (26%)
  matrix products  28.7 us (18%)
  local copies, waits for them, and re-layouts  8.29 us (5%)
  Pallas kernels  4.06 us (3%)
  other arithmetic  1.95 us (1%)
    ppermute x6, waiting for transfers between devices, body(): lax.ppermute(ringed[-chunk_count] if step > 1 else moving[h], 'dp', hops)  35.7 us
    dot_general x18, matrix products, dot_nn(): jnp.dot(a, b, precision=precision, preferred_element_type=jnp.float32)  27.8 us
    ppermute x28, waiting for transfers between devices, swap(): return lax.ppermute(x, axis, [(0, 1), (1, 0)])  19 us
    ppermute x28, starting transfers between devices, swap(): return lax.ppermute(x, axis, [(0, 1), (1, 0)])  18 us
    ppermute x2, waiting for transfers between devices, body(): own_blocks[j] = lax.ppermute(own_blocks[j - 1], 'dp', hops)  11 us
    ppermute x6, starting transfers between devices, body(): lax.ppermute(ringed[-chunk_count] if step > 1 else moving[h], 'dp', hops)  8.86 us
    ppermute x3, waiting for transfers between devices, partner(): lax.ppermute(x, axis, [(i, i ^ flip) for i in range(lax.axis_size(axis))])  6.6 us
    ppermute x2, starting transfers between devices, body(): own_blocks[j] = lax.ppermute(own_blocks[j - 1], 'dp', hops)  6 us
  transfers between devices with their start and end apart: 40, of which 16 were waited for; matrix products, arithmetic and copies ran while one was open for 17% of the time, Pallas kernels for 1%

profile of v7, /device:TPU:0, one launch (start us, length us, event | category | flops | bytes accessed | tf_op | source)
XLA Modules:
  0.0 157.2 jit_solution(15380029090454709592)
XLA Ops:
  2.8 3.0 %collective-permute-start = (bf16[256,1024]{1,0:T(8,128)(2,1)S(1)}, bf16[256,1024]{1,0:T(8,128)(2,1)}, u32[]{:S(2)}, u32[]{:S(2)}) collective-permute-start(bf16[256,1024]{1,0:T(8,128)(2,1)S(1)} %get-tuple-element.29), channel_id=1, source_target_pairs={{0,4},{4,12},{12,8},{8,0},{1,5},{5,13},{13,9},{9,1},{2,6},{6,14},{... | collective-permute-start | bytes 1572872 | tf_op jit(solution)/shard_map/ppermute | solution.py:270
  5.8 2.6 %collective-permute-start.12 = (bf16[256,1024]{1,0:T(8,128)(2,1)}, bf16[256,1024]{1,0:T(8,128)(2,1)}, u32[]{:S(2)}, u32[]{:S(2)}) collective-permute-start(bf16[256,1024]{1,0:T(8,128)(2,1)} %get-tuple-element.30), channel_id=1, source_target_pairs={{0,4},{4,12},{12,8},{8,0},{1,5},{5,13},{13,9},{9,1},{2,6},{6,14},{... | collective-permute-start | bytes 1572872 | tf_op jit(solution)/shard_map/ppermute | solution.py:270
  8.5 3.4 %fusion.59 = bf16[512,16]{0,1:T(8,128)(2,1)S(1)} fusion(bf16[4096,16]{0,1:T(8,128)(2,1)S(1)} %copy-done, bf16[1,512,4096]{2,1,0:T(8,128)(2,1)} %param.8), kind=kOutput, calls=%fused_computation.65 | convolution fusion | flops 67117056 | bytes 4341760 | tf_op jit(solution)/shard_map/dot_general | solution.py:22
  14.1 5.5 %collective-permute-done = bf16[256,1024]{1,0:T(8,128)(2,1)} collective-permute-done((bf16[256,1024]{1,0:T(8,128)(2,1)S(1)}, bf16[256,1024]{1,0:T(8,128)(2,1)}, u32[]{:S(2)}, u32[]{:S(2)}) %collective-permute-start) | collective-permute-done | bytes 524320 | tf_op jit(solution)/shard_map/ppermute | solution.py:270
  25.3 5.6 %collective-permute-done.12 = bf16[256,1024]{1,0:T(8,128)(2,1)} collective-permute-done((bf16[256,1024]{1,0:T(8,128)(2,1)}, bf16[256,1024]{1,0:T(8,128)(2,1)}, u32[]{:S(2)}, u32[]{:S(2)}) %collective-permute-start.12) | collective-permute-done | bytes 524320 | tf_op jit(solution)/shard_map/ppermute | solution.py:270
  32.8 2.8 %fusion.52 = f32[512,1024]{1,0:T(8,128)S(1)} fusion(bf16[512,1024]{1,0:T(8,128)(2,1)S(1)} %dynamic-slice_bitcast_fusion.1, bf16[1024,2048]{1,0:T(8,128)(2,1)} %param.10), kind=kOutput, calls=%fused_computation.60 | convolution fusion | flops 1073741824 | bytes 5242880 | tf_op jit(solution)/shard_map/dot_general | solution.py:22
  36.7 5.4 %collective-permute-done.4 = bf16[256,1024]{1,0:T(8,128)(2,1)} collective-permute-done((bf16[256,1024]{1,0:T(8,128)(2,1)}, bf16[256,1024]{1,0:T(8,128)(2,1)}, u32[]{:S(2)}, u32[]{:S(2)}) %collective-permute-start.4) | collective-permute-done | bytes 524320 | tf_op jit(solution)/shard_map/ppermute | solution.py:270
  46.7 6.5 %collective-permute-done.16 = bf16[256,1024]{1,0:T(8,128)(2,1)S(1)} collective-permute-done((bf16[256,1024]{1,0:T(8,128)(2,1)}, bf16[256,1024]{1,0:T(8,128)(2,1)S(1)}, u32[]{:S(2)}, u32[]{:S(2)}) %collective-permute-start.16) | collective-permute-done | bytes 524320 | tf_op jit(solution)/shard_map/ppermute | solution.py:270
  57.1 7.4 %collective-permute-done.8 = bf16[256,1024]{1,0:T(8,128)(2,1)S(1)} collective-permute-done((bf16[256,1024]{1,0:T(8,128)(2,1)}, bf16[256,1024]{1,0:T(8,128)(2,1)S(1)}, u32[]{:S(2)}, u32[]{:S(2)}) %collective-permute-start.8) | collective-permute-done | bytes 524320 | tf_op jit(solution)/shard_map/ppermute | solution.py:270
  66.4 2.6 %fusion.2 = f32[512,1024]{1,0:T(8,128)S(1)} fusion(bf16[256,1024]{1,0:T(8,128)(2,1)S(1)} %collective-permute-done.3, bf16[256,1024]{1,0:T(8,128)(2,1)} %collective-permute-done.2, bf16[256,1024]{1,0:T(8,128)(2,1)} %collective-permute-done.1, bf16[256,1024]{1,0:T(8,128)(2,1)} %collective-permute-done, bf16[512,256]{1,0:T(8,128)(2,1)S(1)} %copy-done.15, ...), kind=kOutput, calls=%fused_computation.4 | convolution fusion | flops 1086324736 | bytes 5242880 | tf_op jit(solution)/shard_map/dot_general | solution.py:22
  69.6 5.3 %collective-permute-done.20 = bf16[256,1024]{1,0:T(8,128)(2,1)S(1)} collective-permute-done((bf16[256,1024]{1,0:T(8,128)(2,1)S(1)}, bf16[256,1024]{1,0:T(8,128)(2,1)S(1)}, u32[]{:S(2)}, u32[]{:S(2)}) %collective-permute-start.20) | collective-permute-done | bytes 524320 | tf_op jit(solution)/shard_map/ppermute | solution.py:270
  76.5 2.3 %fusion.26 = f32[512,1024]{1,0:T(8,128)S(1)} fusion(bf16[256,1024]{1,0:T(8,128)(2,1)S(1)} %collective-permute-done.15, bf16[256,1024]{1,0:T(8,128)(2,1)S(1)} %collective-permute-done.14, bf16[256,1024]{1,0:T(8,128)(2,1)S(1)} %collective-permute-done.13, bf16[256,1024]{1,0:T(8,128)(2,1)} %collective-permute-done.12, bf16[512,256]{1,0:T(8,128)(2,1)S(1)} %copy-done.15, ...), kind=kOutput, calls=%fused_computation.28 | convolution fusion | flops 1086324736 | bytes 5242880 | tf_op jit(solution)/shard_map/dot_general | solution.py:22
  79.4 2.3 %fusion.10 = f32[512,1024]{1,0:T(8,128)S(1)} fusion(bf16[256,1024]{1,0:T(8,128)(2,1)S(1)} %collective-permute-done.7, bf16[256,1024]{1,0:T(8,128)(2,1)S(1)} %collective-permute-done.6, bf16[256,1024]{1,0:T(8,128)(2,1)S(1)} %collective-permute-done.5, bf16[256,1024]{1,0:T(8,128)(2,1)} %collective-permute-done.4, bf16[512,256]{1,0:T(8,128)(2,1)S(1)} %copy-done.11, ...), kind=kOutput, calls=%fused_computation.12 | convolution fusion | flops 1086324736 | bytes 5242880 | tf_op jit(solution)/shard_map/dot_general | solution.py:22
  81.9 6.4 %collective-permute-done.21 = bf16[256,1024]{1,0:T(8,128)(2,1)S(1)} collective-permute-done((bf16[256,1024]{1,0:T(8,128)(2,1)S(1)}, bf16[256,1024]{1,0:T(8,128)(2,1)S(1)}, u32[]{:S(2)}, u32[]{:S(2)}) %collective-permute-start.21) | collective-permute-done | bytes 524320 | tf_op jit(solution)/shard_map/ppermute | solution.py:26
  89.7 3.0 %fusion.137 = (bf16[512,1024]{1,0:T(8,128)(2,1)S(1)}, f32[512]{0:T(512)S(1)}, f32[512,1024]{1,0:T(8,128)}) fusion(bf16[256,1024]{1,0:T(8,128)(2,1)S(1)} %collective-permute-done.11, bf16[256,1024]{1,0:T(8,128)(2,1)S(1)} %collective-permute-done.10, bf16[256,1024]{1,0:T(8,128)(2,1)S(1)} %collective-permute-done.9, ...), kind=kOutput, calls=%fused_computation.220 | convolution fusion | flops 1091042816 | bytes 15730688 | tf_op jit(solution)/shard_map/dot_general | solution.py:22
  92.6 4.2 %fusion.136 = (bf16[512,1024]{1,0:T(8,128)(2,1)S(1)}, f32[512]{0:T(512)S(1)}, f32[512,1024]{1,0:T(8,128)}) fusion(bf16[256,1024]{1,0:T(8,128)(2,1)S(1)} %collective-permute-done.23, bf16[256,1024]{1,0:T(8,128)(2,1)S(1)} %collective-permute-done.22, bf16[256,1024]{1,0:T(8,128)(2,1)S(1)} %collective-permute-done.21, ...), kind=kOutput, calls=%fused_computation.219 | convolution fusion | flops 1091042816 | bytes 15730688 | tf_op jit(solution)/shard_map/dot_general | solution.py:22
  103.7 2.4 %collective-permute-start.27 = (bf16[64,2048]{1,0:T(8,128)(2,1)S(1)}, bf16[64,2048]{1,0:T(8,128)(2,1)}, u32[]{:S(2)}, u32[]{:S(2)}) collective-permute-start(bf16[64,2048]{1,0:T(8,128)(2,1)S(1)} %get-tuple-element.48.refs_0_.refs_4_), channel_id=1, source_target_pairs={{4,0},{12,4},{8,12},{0,8},{5,1},{13,5},{9,13},{1,9},{6,2},{14,6},{... | collective-permute-start | bytes 786440 | tf_op jit(solution)/shard_map/ppermute | solution.py:320
  106.1 6.1 %collective-permute-done.25.refs_1_ = bf16[64,2048]{1,0:T(8,128)(2,1)S(1)} collective-permute-done((bf16[64,2048]{1,0:T(8,128)(2,1)S(1)}, bf16[64,2048]{1,0:T(8,128)(2,1)S(1)}, u32[]{:S(2)}, u32[]{:S(2)}) %collective-permute-start.25) | collective-permute-done | bytes 262176 | tf_op jit(solution)/shard_map/ppermute | solution.py:318
  112.3 5.4 %collective-permute-start.26 = (bf16[64,2048]{1,0:T(8,128)(2,1)S(1)}, bf16[64,2048]{1,0:T(8,128)(2,1)}, u32[]{:S(2)}, u32[]{:S(2)}) collective-permute-start(bf16[64,2048]{1,0:T(8,128)(2,1)S(1)} %collective-permute-done.25.refs_1_), channel_id=1, source_target_pairs={{0,4},{4,12},{12,8},{8,0},{1,5},{5,13},{13,9},{9,1},{2,6},{6,14},{... | collective-permute-start | bytes 786440 | tf_op jit(solution)/shard_map/ppermute | solution.py:318
  118.6 4.9 %collective-permute-done.26.refs_2_ = bf16[64,2048]{1,0:T(8,128)(2,1)} collective-permute-done((bf16[64,2048]{1,0:T(8,128)(2,1)S(1)}, bf16[64,2048]{1,0:T(8,128)(2,1)}, u32[]{:S(2)}, u32[]{:S(2)}) %collective-permute-start.26) | collective-permute-done | bytes 262176 | tf_op jit(solution)/shard_map/ppermute | solution.py:318
  129.2 4.3 %collective-permute-done.32.refs_1_ = f32[296,128]{1,0:T(8,128)S(1)} collective-permute-done((f32[296,128]{1,0:T(8,128)S(1)}, f32[296,128]{1,0:T(8,128)S(1)}, u32[]{:S(2)}, u32[]{:S(2)}) %collective-permute-start.32) | collective-permute-done | bytes 151584 | tf_op jit(solution)/shard_map/ppermute | solution.py:26
  136.9 2.7 %collective-permute-done.34 = f32[24,640]{1,0:T(8,128)S(1)} collective-permute-done((f32[24,640]{1,0:T(8,128)S(1)}, f32[24,640]{1,0:T(8,128)S(1)}, u32[]{:S(2)}, u32[]{:S(2)}) %collective-permute-start.34) | collective-permute-done | bytes 61472 | tf_op jit(solution)/shard_map/ppermute | solution.py:26
  144.2 3.5 %collective-permute-start.37 = (bf16[33,1024]{1,0:T(8,128)(2,1)S(1)}, bf16[33,1024]{1,0:T(8,128)(2,1)S(1)}, u32[]{:S(2)}, u32[]{:S(2)}) collective-permute-start(bf16[33,1024]{1,0:T(8,128)(2,1)S(1)} %add_convert_fusion), channel_id=1, source_target_pairs={{0,8},{4,12},{8,0},{12,4},{1,9},{5,13},{9,1},{13,5},{2,10},{6,14},... | collective-permute-start | bytes 202760 | tf_op jit(solution)/shard_map/ppermute | solution.py:30
  147.7 6.6 %collective-permute-done.37 = bf16[33,1024]{1,0:T(8,128)(2,1)S(1)} collective-permute-done((bf16[33,1024]{1,0:T(8,128)(2,1)S(1)}, bf16[33,1024]{1,0:T(8,128)(2,1)S(1)}, u32[]{:S(2)}, u32[]{:S(2)}) %collective-permute-start.37) | collective-permute-done | bytes 67616 | tf_op jit(solution)/shard_map/ppermute | solution.py:30
  (159 shorter events, 51.4 us)
Async XLA Ops:
  2.8 16.9 %collective-permute-start = (bf16[256,1024]{1,0:T(8,128)(2,1)S(1)}, bf16[256,1024]{1,0:T(8,128)(2,1)}, u32[]{:S(2)}, u32[]{:S(2)}) collective-permute-start(bf16[256,1024]{1,0:T(8,128)(2,1)S(1)} %get-tuple-element.29), channel_id=1, source_target_pairs={{0,4},{4,12},{12,8},{8,0},{1,5},{5,13},{13,9},{9,1},{2,6},{6,14},{... | collective-permute-start | bytes 1572872 | tf_op jit(solution)/shard_map/ppermute | solution.py:270
  5.8 25.1 %collective-permute-start.12 = (bf16[256,1024]{1,0:T(8,128)(2,1)}, bf16[256,1024]{1,0:T(8,128)(2,1)}, u32[]{:S(2)}, u32[]{:S(2)}) collective-permute-start(bf16[256,1024]{1,0:T(8,128)(2,1)} %get-tuple-element.30), channel_id=1, source_target_pairs={{0,4},{4,12},{12,8},{8,0},{1,5},{5,13},{13,9},{9,1},{2,6},{6,14},{... | collective-permute-start | bytes 1572872 | tf_op jit(solution)/shard_map/ppermute | solution.py:270
  19.7 16.0 %collective-permute-start.1 = (bf16[256,1024]{1,0:T(8,128)(2,1)}, bf16[256,1024]{1,0:T(8,128)(2,1)}, u32[]{:S(2)}, u32[]{:S(2)}) collective-permute-start(bf16[256,1024]{1,0:T(8,128)(2,1)} %collective-permute-done), channel_id=1, source_target_pairs={{0,16},{16,0},{1,17},{17,1},{2,18},{18,2},{3,19},{19,3},{4,20},{20... | collective-permute-start | bytes 1572872 | tf_op jit(solution)/shard_map/ppermute | solution.py:26
  21.5 14.9 %collective-permute-start.2 = (bf16[256,1024]{1,0:T(8,128)(2,1)}, bf16[256,1024]{1,0:T(8,128)(2,1)}, u32[]{:S(2)}, u32[]{:S(2)}) collective-permute-start(bf16[256,1024]{1,0:T(8,128)(2,1)} %collective-permute-done), channel_id=1, source_target_pairs={{0,1},{1,0},{2,3},{3,2},{4,5},{5,4},{6,7},{7,6},{8,9},{9,8},{10,11... | collective-permute-start | bytes 1572872 | tf_op jit(solution)/shard_map/ppermute | solution.py:26
  21.6 20.6 %collective-permute-start.4 = (bf16[256,1024]{1,0:T(8,128)(2,1)}, bf16[256,1024]{1,0:T(8,128)(2,1)}, u32[]{:S(2)}, u32[]{:S(2)}) collective-permute-start(bf16[256,1024]{1,0:T(8,128)(2,1)} %collective-permute-done), channel_id=1, source_target_pairs={{0,4},{4,12},{12,8},{8,0},{1,5},{5,13},{13,9},{9,1},{2,6},{6,14},{... | collective-permute-start | bytes 1572872 | tf_op jit(solution)/shard_map/ppermute | solution.py:270
  30.9 14.5 %collective-permute-start.13 = (bf16[256,1024]{1,0:T(8,128)(2,1)}, bf16[256,1024]{1,0:T(8,128)(2,1)S(1)}, u32[]{:S(2)}, u32[]{:S(2)}) collective-permute-start(bf16[256,1024]{1,0:T(8,128)(2,1)} %collective-permute-done.12), channel_id=1, source_target_pairs={{0,16},{16,0},{1,17},{17,1},{2,18},{18,2},{3,19},{19,3},{4,20},{20... | collective-permute-start | bytes 1572872 | tf_op jit(solution)/shard_map/ppermute | solution.py:26
  32.8 12.7 %collective-permute-start.14 = (bf16[256,1024]{1,0:T(8,128)(2,1)}, bf16[256,1024]{1,0:T(8,128)(2,1)S(1)}, u32[]{:S(2)}, u32[]{:S(2)}) collective-permute-start(bf16[256,1024]{1,0:T(8,128)(2,1)} %collective-permute-done.12), channel_id=1, source_target_pairs={{0,1},{1,0},{2,3},{3,2},{4,5},{5,4},{6,7},{7,6},{8,9},{9,8},{10,11... | collective-permute-start | bytes 1572872 | tf_op jit(solution)/shard_map/ppermute | solution.py:26
  35.7 17.6 %collective-permute-start.16 = (bf16[256,1024]{1,0:T(8,128)(2,1)}, bf16[256,1024]{1,0:T(8,128)(2,1)S(1)}, u32[]{:S(2)}, u32[]{:S(2)}) collective-permute-start(bf16[256,1024]{1,0:T(8,128)(2,1)} %collective-permute-done.12), channel_id=1, source_target_pairs={{0,4},{4,12},{12,8},{8,0},{1,5},{5,13},{13,9},{9,1},{2,6},{6,14},{... | collective-permute-start | bytes 1572872 | tf_op jit(solution)/shard_map/ppermute | solution.py:270
  36.5 18.7 %collective-permute-start.3 = (bf16[256,1024]{1,0:T(8,128)(2,1)}, bf16[256,1024]{1,0:T(8,128)(2,1)S(1)}, u32[]{:S(2)}, u32[]{:S(2)}) collective-permute-start(bf16[256,1024]{1,0:T(8,128)(2,1)} %collective-permute-done.1), channel_id=1, source_target_pairs={{0,1},{1,0},{2,3},{3,2},{4,5},{5,4},{6,7},{7,6},{8,9},{9,8},{10,11... | collective-permute-start | bytes 1572872 | tf_op jit(solution)/shard_map/ppermute | solution.py:26
  42.1 13.9 %collective-permute-start.5 = (bf16[256,1024]{1,0:T(8,128)(2,1)}, bf16[256,1024]{1,0:T(8,128)(2,1)S(1)}, u32[]{:S(2)}, u32[]{:S(2)}) collective-permute-start(bf16[256,1024]{1,0:T(8,128)(2,1)} %collective-permute-done.4), channel_id=1, source_target_pairs={{0,16},{16,0},{1,17},{17,1},{2,18},{18,2},{3,19},{19,3},{4,20},{20... | collective-permute-start | bytes 1572872 | tf_op jit(solution)/shard_map/ppermute | solution.py:26
  45.4 11.1 %collective-permute-start.6 = (bf16[256,1024]{1,0:T(8,128)(2,1)}, bf16[256,1024]{1,0:T(8,128)(2,1)S(1)}, u32[]{:S(2)}, u32[]{:S(2)}) collective-permute-start(bf16[256,1024]{1,0:T(8,128)(2,1)} %collective-permute-done.4), channel_id=1, source_target_pairs={{0,1},{1,0},{2,3},{3,2},{4,5},{5,4},{6,7},{7,6},{8,9},{9,8},{10,11... | collective-permute-start | bytes 1572872 | tf_op jit(solution)/shard_map/ppermute | solution.py:26
  45.4 19.0 %collective-permute-start.8 = (bf16[256,1024]{1,0:T(8,128)(2,1)}, bf16[256,1024]{1,0:T(8,128)(2,1)S(1)}, u32[]{:S(2)}, u32[]{:S(2)}) collective-permute-start(bf16[256,1024]{1,0:T(8,128)(2,1)} %collective-permute-done.4), channel_id=1, source_target_pairs={{0,4},{4,12},{12,8},{8,0},{1,5},{5,13},{13,9},{9,1},{2,6},{6,14},{... | collective-permute-start | bytes 1572872 | tf_op jit(solution)/shard_map/ppermute | solution.py:270
  53.3 15.9 %collective-permute-start.17 = (bf16[256,1024]{1,0:T(8,128)(2,1)S(1)}, bf16[256,1024]{1,0:T(8,128)(2,1)S(1)}, u32[]{:S(2)}, u32[]{:S(2)}) collective-permute-start(bf16[256,1024]{1,0:T(8,128)(2,1)S(1)} %collective-permute-done.16), channel_id=1, source_target_pairs={{0,16},{16,0},{1,17},{17,1},{2,18},{18,2},{3,19},{19,3},{4,20},{20... | collective-permute-start | bytes 1572872 | tf_op jit(solution)/shard_map/ppermute | solution.py:26
  55.2 19.7 %collective-permute-start.20 = (bf16[256,1024]{1,0:T(8,128)(2,1)S(1)}, bf16[256,1024]{1,0:T(8,128)(2,1)S(1)}, u32[]{:S(2)}, u32[]{:S(2)}) collective-permute-start(bf16[256,1024]{1,0:T(8,128)(2,1)S(1)} %collective-permute-done.16), channel_id=1, source_target_pairs={{0,4},{4,12},{12,8},{8,0},{1,5},{5,13},{13,9},{9,1},{2,6},{6,14},{... | collective-permute-start | bytes 1572872 | tf_op jit(solution)/shard_map/ppermute | solution.py:270
  56.0 13.0 %collective-permute-start.15 = (bf16[256,1024]{1,0:T(8,128)(2,1)S(1)}, bf16[256,1024]{1,0:T(8,128)(2,1)S(1)}, u32[]{:S(2)}, u32[]{:S(2)}) collective-permute-start(bf16[256,1024]{1,0:T(8,128)(2,1)S(1)} %collective-permute-done.13), channel_id=1, source_target_pairs={{0,1},{1,0},{2,3},{3,2},{4,5},{5,4},{6,7},{7,6},{8,9},{9,8},{10,11... | collective-permute-start | bytes 1572872 | tf_op jit(solution)/shard_map/ppermute | solution.py:26
  56.5 22.3 %collective-permute-start.7 = (bf16[256,1024]{1,0:T(8,128)(2,1)S(1)}, bf16[256,1024]{1,0:T(8,128)(2,1)S(1)}, u32[]{:S(2)}, u32[]{:S(2)}) collective-permute-start(bf16[256,1024]{1,0:T(8,128)(2,1)S(1)} %collective-permute-done.5), channel_id=1, source_target_pairs={{0,1},{1,0},{2,3},{3,2},{4,5},{5,4},{6,7},{7,6},{8,9},{9,8},{10,11... | collective-permute-start | bytes 1572872 | tf_op jit(solution)/shard_map/ppermute | solution.py:26
  64.5 14.4 %collective-permute-start.9 = (bf16[256,1024]{1,0:T(8,128)(2,1)S(1)}, bf16[256,1024]{1,0:T(8,128)(2,1)S(1)}, u32[]{:S(2)}, u32[]{:S(2)}) collective-permute-start(bf16[256,1024]{1,0:T(8,128)(2,1)S(1)} %collective-permute-done.8), channel_id=1, source_target_pairs={{0,16},{16,0},{1,17},{17,1},{2,18},{18,2},{3,19},{19,3},{4,20},{20... | collective-permute-start | bytes 1572872 | tf_op jit(solution)/shard_map/ppermute | solution.py:26
  69.1 12.7 %collective-permute-start.18 = (bf16[256,1024]{1,0:T(8,128)(2,1)S(1)}, bf16[256,1024]{1,0:T(8,128)(2,1)S(1)}, u32[]{:S(2)}, u32[]{:S(2)}) collective-permute-start(bf16[256,1024]{1,0:T(8,128)(2,1)S(1)} %collective-permute-done.16), channel_id=1, source_target_pairs={{0,1},{1,0},{2,3},{3,2},{4,5},{5,4},{6,7},{7,6},{8,9},{9,8},{10,11... | collective-permute-start | bytes 1572872 | tf_op jit(solution)/shard_map/ppermute | solution.py:26
  69.2 19.2 %collective-permute-start.19 = (bf16[256,1024]{1,0:T(8,128)(2,1)S(1)}, bf16[256,1024]{1,0:T(8,128)(2,1)S(1)}, u32[]{:S(2)}, u32[]{:S(2)}) collective-permute-start(bf16[256,1024]{1,0:T(8,128)(2,1)S(1)} %collective-permute-done.17), channel_id=1, source_target_pairs={{0,1},{1,0},{2,3},{3,2},{4,5},{5,4},{6,7},{7,6},{8,9},{9,8},{10,11... | collective-permute-start | bytes 1572872 | tf_op jit(solution)/shard_map/ppermute | solution.py:26
  74.9 13.4 %collective-permute-start.21 = (bf16[256,1024]{1,0:T(8,128)(2,1)S(1)}, bf16[256,1024]{1,0:T(8,128)(2,1)S(1)}, u32[]{:S(2)}, u32[]{:S(2)}) collective-permute-start(bf16[256,1024]{1,0:T(8,128)(2,1)S(1)} %collective-permute-done.20), channel_id=1, source_target_pairs={{0,16},{16,0},{1,17},{17,1},{2,18},{18,2},{3,19},{19,3},{4,20},{20... | collective-permute-start | bytes 1572872 | tf_op jit(solution)/shard_map/ppermute | solution.py:26
  81.7 10.9 %collective-permute-start.22 = (bf16[256,1024]{1,0:T(8,128)(2,1)S(1)}, bf16[256,1024]{1,0:T(8,128)(2,1)S(1)}, u32[]{:S(2)}, u32[]{:S(2)}) collective-permute-start(bf16[256,1024]{1,0:T(8,128)(2,1)S(1)} %collective-permute-done.20), channel_id=1, source_target_pairs={{0,1},{1,0},{2,3},{3,2},{4,5},{5,4},{6,7},{7,6},{8,9},{9,8},{10,11... | collective-permute-start | bytes 1572872 | tf_op jit(solution)/shard_map/ppermute | solution.py:26
  103.6 25.6 %collective-permute-start.33 = (s32[32,4]{1,0:T(8,128)S(1)}, s32[32,4]{1,0:T(8,128)S(1)}, u32[]{:S(2)}, u32[]{:S(2)}) collective-permute-start(s32[32,4]{1,0:T(8,128)S(1)} %fusion.100), channel_id=1, source_target_pairs={{0,1},{1,0},{2,3},{3,2},{4,5},{5,4},{6,7},{7,6},{8,9},{9,8},{10,11... | collective-permute-start | bytes 1544 | tf_op jit(solution)/shard_map/ppermute | solution.py:26
  103.7 14.8 %collective-permute-start.27 = (bf16[64,2048]{1,0:T(8,128)(2,1)S(1)}, bf16[64,2048]{1,0:T(8,128)(2,1)}, u32[]{:S(2)}, u32[]{:S(2)}) collective-permute-start(bf16[64,2048]{1,0:T(8,128)(2,1)S(1)} %get-tuple-element.48.refs_0_.refs_4_), channel_id=1, source_target_pairs={{4,0},{12,4},{8,12},{0,8},{5,1},{13,5},{9,13},{1,9},{6,2},{14,6},{... | collective-permute-start | bytes 786440 | tf_op jit(solution)/shard_map/ppermute | solution.py:320
  112.3 11.2 %collective-permute-start.26 = (bf16[64,2048]{1,0:T(8,128)(2,1)S(1)}, bf16[64,2048]{1,0:T(8,128)(2,1)}, u32[]{:S(2)}, u32[]{:S(2)}) collective-permute-start(bf16[64,2048]{1,0:T(8,128)(2,1)S(1)} %collective-permute-done.25.refs_1_), channel_id=1, source_target_pairs={{0,4},{4,12},{12,8},{8,0},{1,5},{5,13},{13,9},{9,1},{2,6},{6,14},{... | collective-permute-start | bytes 786440 | tf_op jit(solution)/shard_map/ppermute | solution.py:318
  (39 other events, 405.0 us)

commit v8 on v7

--- a/solution.py
+++ b/solution.py
@@ -259,6 +259,8 @@
     moving = []
     for low, high in parts:
         corner = quarters[0] * quarter
+        if moving:
+            corner = after(corner, moving[0])
         moving.append(lax.dynamic_slice(frozen_weight, (corner, low), (quarter, high - low)))
     lora_mid = dot_nn(tokens, adapter_down).astype(jnp.bfloat16)
     own_cols = lax.dynamic_slice_in_dim(tokens, lax.axis_index("mp") * cols, cols, 1)
@@ -282,16 +284,21 @@
             moved = ringed[event]
             if step == 1:
                 own_first, mid_first = own_tokens, lora_mid
-                own_first, mid_first = after((own_first, mid_first), moved)
                 states[h] = (
                     own_cols[:, low:high].astype(jnp.float32)
                     + dot_nn(own_first, frozen_weight[:, low:high])
                     + dot_nn(mid_first, adapter_up[:, low:high])
                 )
+                states[h] = lax.optimization_barrier(states[h])
             across = swap(moved, "groups")
             lhs = step_tokens
-            rows = [moved, across, swap(moved, "pair"), swap(across, "pair")]
-            states[h] = states[h] + dot_nn(lhs, jnp.concatenate(rows, axis=0))
+            late = across
+            if step == dp - 1 and h == chunk_count - 1:
+                late = after(across, *states)
+            rows = [moved, across, swap(moved, "pair"), swap(late, "pair")]
+            states[h] = lax.optimization_barrier(
+                states[h] + dot_nn(lhs, jnp.concatenate(rows, axis=0))
+            )
             event += 1
     states_b = [x.astype(jnp.bfloat16) for x in states]
     squares = sum_over(sum(jnp.sum(x * x, axis=1) for x in states), "mp")

time: 158 us -> 157 us (level)
  waiting for transfers between devices: 72.4 us -> 66.6 us
  starting transfers between devices: 40.3 us -> 44.5 us
    ppermute x6, waiting for transfers between devices: 35.7 us -> 32.9 us  [body(): lax.ppermute(ringed[-chunk_count] if step > 1 else moving[h], 'dp', hops)]
    unnamed x48 -> x30, local copies, waits for them, and re-layouts: 0.33 us -> 2.94 us
    ppermute x2, waiting for transfers between devices: 11 us -> 8.78 us  [body(): own_blocks[j] = lax.ppermute(own_blocks[j - 1], 'dp', hops)]
    ppermute x2, starting transfers between devices: 6 us -> 8.08 us  [body(): own_blocks[j] = lax.ppermute(own_blocks[j - 1], 'dp', hops)]
    dynamic_slice x1, local copies, waits for them, and re-layouts: 1.88 us -> 0.25 us  [body(): lax.dynamic_slice_in_dim(tokens, lax.axis_index('mp') * cols, cols, 1)]
  transfers between devices with their start and end apart: 40 -> 40, of which waited for: 16 -> 17; matrix products, arithmetic and copies ran while one was open for 17% -> 17% of each run, Pallas kernels for 1% -> 1%
where the time goes in v8:
time: 157 us; the launch traced here: 156 us
  waiting for transfers between devices  66.6 us (42%)
  starting transfers between devices  44.5 us (28%)
  matrix products  28.8 us (18%)
  local copies, waits for them, and re-layouts  8.66 us (6%)
  Pallas kernels  4.06 us (3%)
  other arithmetic  2.55 us (2%)
    ppermute x6, waiting for transfers between devices, body(): lax.ppermute(ringed[-chunk_count] if step > 1 else moving[h], 'dp', hops)  32.9 us
    dot_general x18, matrix products, dot_nn(): jnp.dot(a, b, precision=precision, preferred_element_type=jnp.float32)  28 us
    ppermute x28, starting transfers between devices, swap(): return lax.ppermute(x, axis, [(0, 1), (1, 0)])  18.8 us
    ppermute x28, waiting for transfers between devices, swap(): return lax.ppermute(x, axis, [(0, 1), (1, 0)])  18.4 us
    ppermute x6, starting transfers between devices, body(): lax.ppermute(ringed[-chunk_count] if step > 1 else moving[h], 'dp', hops)  8.85 us
    ppermute x2, waiting for transfers between devices, body(): own_blocks[j] = lax.ppermute(own_blocks[j - 1], 'dp', hops)  8.78 us
    ppermute x2, starting transfers between devices, body(): own_blocks[j] = lax.ppermute(own_blocks[j - 1], 'dp', hops)  8.08 us
    ppermute x3, waiting for transfers between devices, partner(): lax.ppermute(x, axis, [(i, i ^ flip) for i in range(lax.axis_size(axis))])  6.6 us
  transfers between devices with their start and end apart: 40, of which 17 were waited for; matrix products, arithmetic and copies ran while one was open for 17% of the time, Pallas kernels for 1%

profile of v8, /device:TPU:0, one launch (start us, length us, event | category | flops | bytes accessed | tf_op | source)
XLA Modules:
  0.0 156.4 jit_solution(8777826084765133741)
XLA Ops:
  1.8 3.1 %collective-permute-start = (bf16[256,1024]{1,0:T(8,128)(2,1)S(1)}, bf16[256,1024]{1,0:T(8,128)(2,1)}, u32[]{:S(2)}, u32[]{:S(2)}) collective-permute-start(bf16[256,1024]{1,0:T(8,128)(2,1)S(1)} %constant_dynamic-slice_fusion.1), channel_id=1, source_target_pairs={{0,4},{4,12},{12,8},{8,0},{1,5},{5,13},{13,9},{9,1},{2,6},{6,14},{... | collective-permute-start | bytes 1572872 | tf_op jit(solution)/shard_map/ppermute | solution.py:272
  6.0 2.6 %collective-permute-start.12 = (bf16[256,1024]{1,0:T(8,128)(2,1)S(1)}, bf16[256,1024]{1,0:T(8,128)(2,1)}, u32[]{:S(2)}, u32[]{:S(2)}) collective-permute-start(bf16[256,1024]{1,0:T(8,128)(2,1)S(1)} %constant_dynamic-slice_fusion.2), channel_id=1, source_target_pairs={{0,4},{4,12},{12,8},{8,0},{1,5},{5,13},{13,9},{9,1},{2,6},{6,14},{... | collective-permute-start | bytes 1572872 | tf_op jit(solution)/shard_map/ppermute | solution.py:272
  8.7 3.5 %fusion.73 = bf16[512,16]{0,1:T(8,128)(2,1)S(1)} fusion(bf16[4096,16]{0,1:T(8,128)(2,1)S(1)} %copy-done, bf16[1,512,4096]{2,1,0:T(8,128)(2,1)} %param.8), kind=kOutput, calls=%fused_computation.71 | convolution fusion | flops 67117056 | bytes 4341760 | tf_op jit(solution)/shard_map/dot_general | solution.py:22
  15.7 3.0 %collective-permute-done = bf16[256,1024]{1,0:T(8,128)(2,1)} collective-permute-done((bf16[256,1024]{1,0:T(8,128)(2,1)S(1)}, bf16[256,1024]{1,0:T(8,128)(2,1)}, u32[]{:S(2)}, u32[]{:S(2)}) %collective-permute-start) | collective-permute-done | bytes 524320 | tf_op jit(solution)/shard_map/ppermute | solution.py:272
  24.5 5.5 %collective-permute-done.12 = bf16[256,1024]{1,0:T(8,128)(2,1)} collective-permute-done((bf16[256,1024]{1,0:T(8,128)(2,1)S(1)}, bf16[256,1024]{1,0:T(8,128)(2,1)}, u32[]{:S(2)}, u32[]{:S(2)}) %collective-permute-start.12) | collective-permute-done | bytes 524320 | tf_op jit(solution)/shard_map/ppermute | solution.py:272
  35.9 5.3 %collective-permute-done.4 = bf16[256,1024]{1,0:T(8,128)(2,1)} collective-permute-done((bf16[256,1024]{1,0:T(8,128)(2,1)}, bf16[256,1024]{1,0:T(8,128)(2,1)}, u32[]{:S(2)}, u32[]{:S(2)}) %collective-permute-start.4) | collective-permute-done | bytes 524320 | tf_op jit(solution)/shard_map/ppermute | solution.py:272
  43.6 2.8 %fusion.69 = f32[512,1024]{1,0:T(8,128)S(1)} fusion(f32[512,1024]{1,0:T(8,128)S(1)} %copy-done.9, bf16[256,1024]{1,0:T(8,128)(2,1)} %collective-permute-done.3, bf16[256,1024]{1,0:T(8,128)(2,1)} %collective-permute-done.2, bf16[256,1024]{1,0:T(8,128)(2,1)} %collective-permute-done.1, bf16[256,1024]{1,0:T(8,128)(2,1)} %collective-permute-done, ...), kind=kOutput, calls=%fused_computation.68 | convolution fusion | flops 1086849024 | bytes 7340032 | tf_op jit(solution)/shard_map/dot_general | solution.py:22
  47.2 5.1 %collective-permute-done.16 = bf16[256,1024]{1,0:T(8,128)(2,1)S(1)} collective-permute-done((bf16[256,1024]{1,0:T(8,128)(2,1)}, bf16[256,1024]{1,0:T(8,128)(2,1)S(1)}, u32[]{:S(2)}, u32[]{:S(2)}) %collective-permute-start.16) | collective-permute-done | bytes 524320 | tf_op jit(solution)/shard_map/ppermute | solution.py:272
  55.1 2.5 %fusion.60 = f32[512,1024]{1,0:T(8,128)S(1)} fusion(f32[512,1024]{1,0:T(8,128)S(1)} %add_add_fusion, bf16[256,1024]{1,0:T(8,128)(2,1)S(1)} %collective-permute-done.15, bf16[256,1024]{1,0:T(8,128)(2,1)S(1)} %collective-permute-done.14, bf16[256,1024]{1,0:T(8,128)(2,1)} %collective-permute-done.13, bf16[256,1024]{1,0:T(8,128)(2,1)} %collective-permute-done.12, ...), kind=kOutput, calls=%fused_computation.65 | convolution fusion | flops 1086849024 | bytes 7340032 | tf_op jit(solution)/shard_map/dot_general | solution.py:22
  58.2 5.4 %collective-permute-done.8 = bf16[256,1024]{1,0:T(8,128)(2,1)S(1)} collective-permute-done((bf16[256,1024]{1,0:T(8,128)(2,1)}, bf16[256,1024]{1,0:T(8,128)(2,1)S(1)}, u32[]{:S(2)}, u32[]{:S(2)}) %collective-permute-start.8) | collective-permute-done | bytes 524320 | tf_op jit(solution)/shard_map/ppermute | solution.py:272
  65.5 8.6 %collective-permute-done.20 = bf16[256,1024]{1,0:T(8,128)(2,1)} collective-permute-done((bf16[256,1024]{1,0:T(8,128)(2,1)S(1)}, bf16[256,1024]{1,0:T(8,128)(2,1)}, u32[]{:S(2)}, u32[]{:S(2)}) %collective-permute-start.20) | collective-permute-done | bytes 524320 | tf_op jit(solution)/shard_map/ppermute | solution.py:272
  75.6 2.3 %fusion.66 = f32[512,1024]{1,0:T(8,128)S(1)} fusion(f32[512,1024]{1,0:T(8,128)S(1)} %fusion.69, bf16[256,1024]{1,0:T(8,128)(2,1)S(1)} %collective-permute-done.7, bf16[256,1024]{1,0:T(8,128)(2,1)S(1)} %collective-permute-done.6, bf16[256,1024]{1,0:T(8,128)(2,1)S(1)} %collective-permute-done.5, bf16[256,1024]{1,0:T(8,128)(2,1)} %collective-permute-done.4, ...), kind=kOutput, calls=%fused_computation.67 | convolution fusion | flops 1086849024 | bytes 7340032 | tf_op jit(solution)/shard_map/dot_general | solution.py:22
  78.5 2.6 %fusion.57 = f32[512,1024]{1,0:T(8,128)} fusion(f32[512,1024]{1,0:T(8,128)S(1)} %fusion.60, bf16[256,1024]{1,0:T(8,128)(2,1)S(1)} %collective-permute-done.19, bf16[256,1024]{1,0:T(8,128)(2,1)S(1)} %collective-permute-done.18, bf16[256,1024]{1,0:T(8,128)(2,1)S(1)} %collective-permute-done.17, bf16[256,1024]{1,0:T(8,128)(2,1)S(1)} %collective-permute-done.16, ...), kind=kOutput, calls=%fused_computation.64 | convolution fusion | flops 1086849024 | bytes 7340032 | tf_op jit(solution)/shard_map/dot_general | solution.py:22
  81.2 2.6 %fusion.63 = f32[512,1024]{1,0:T(8,128)} fusion(f32[512,1024]{1,0:T(8,128)S(1)} %fusion.66, bf16[256,1024]{1,0:T(8,128)(2,1)S(1)} %collective-permute-done.11, bf16[256,1024]{1,0:T(8,128)(2,1)S(1)} %collective-permute-done.10, bf16[256,1024]{1,0:T(8,128)(2,1)S(1)} %collective-permute-done.9, bf16[256,1024]{1,0:T(8,128)(2,1)S(1)} %collective-permute-done.8, ...), kind=kOutput, calls=%fused_computation.66 | convolution fusion | flops 1086849024 | bytes 7340032 | tf_op jit(solution)/shard_map/dot_general | solution.py:22
  83.8 4.8 %collective-permute-done.21 = bf16[256,1024]{1,0:T(8,128)(2,1)S(1)} collective-permute-done((bf16[256,1024]{1,0:T(8,128)(2,1)}, bf16[256,1024]{1,0:T(8,128)(2,1)S(1)}, u32[]{:S(2)}, u32[]{:S(2)}) %collective-permute-start.21) | collective-permute-done | bytes 524320 | tf_op jit(solution)/shard_map/ppermute | solution.py:26
  90.5 3.0 %fusion.54 = f32[512,1024]{1,0:T(8,128)S(1)} fusion(f32[512,1024]{1,0:T(8,128)} %fusion.57, bf16[256,1024]{1,0:T(8,128)(2,1)S(1)} %collective-permute-done.23, bf16[256,1024]{1,0:T(8,128)(2,1)S(1)} %collective-permute-done.22, bf16[256,1024]{1,0:T(8,128)(2,1)S(1)} %collective-permute-done.21, bf16[256,1024]{1,0:T(8,128)(2,1)} %collective-permute-done.20, ...), kind=kOutput, calls=%fused_computation.63 | convolution fusion | flops 1086849024 | bytes 7340032 | tf_op jit(solution)/shard_map/dot_general | solution.py:22
  104.2 5.3 %collective-permute-done.25.refs_1_ = bf16[64,2048]{1,0:T(8,128)(2,1)S(1)} collective-permute-done((bf16[64,2048]{1,0:T(8,128)(2,1)S(1)}, bf16[64,2048]{1,0:T(8,128)(2,1)S(1)}, u32[]{:S(2)}, u32[]{:S(2)}) %collective-permute-start.25) | collective-permute-done | bytes 262176 | tf_op jit(solution)/shard_map/ppermute | solution.py:325
  109.6 7.3 %collective-permute-start.26 = (bf16[64,2048]{1,0:T(8,128)(2,1)S(1)}, bf16[64,2048]{1,0:T(8,128)(2,1)}, u32[]{:S(2)}, u32[]{:S(2)}) collective-permute-start(bf16[64,2048]{1,0:T(8,128)(2,1)S(1)} %collective-permute-done.25.refs_1_), channel_id=1, source_target_pairs={{0,4},{4,12},{12,8},{8,0},{1,5},{5,13},{13,9},{9,1},{2,6},{6,14},{... | collective-permute-start | bytes 786440 | tf_op jit(solution)/shard_map/ppermute | solution.py:325
  117.8 3.4 %collective-permute-done.26.refs_2_ = bf16[64,2048]{1,0:T(8,128)(2,1)} collective-permute-done((bf16[64,2048]{1,0:T(8,128)(2,1)S(1)}, bf16[64,2048]{1,0:T(8,128)(2,1)}, u32[]{:S(2)}, u32[]{:S(2)}) %collective-permute-start.26) | collective-permute-done | bytes 262176 | tf_op jit(solution)/shard_map/ppermute | solution.py:325
  127.1 4.1 %collective-permute-done.32.refs_1_ = f32[296,128]{1,0:T(8,128)S(1)} collective-permute-done((f32[296,128]{1,0:T(8,128)S(1)}, f32[296,128]{1,0:T(8,128)S(1)}, u32[]{:S(2)}, u32[]{:S(2)}) %collective-permute-start.32) | collective-permute-done | bytes 151584 | tf_op jit(solution)/shard_map/ppermute | solution.py:26
  134.8 2.6 %collective-permute-done.34 = f32[24,640]{1,0:T(8,128)S(1)} collective-permute-done((f32[24,640]{1,0:T(8,128)S(1)}, f32[24,640]{1,0:T(8,128)S(1)}, u32[]{:S(2)}, u32[]{:S(2)}) %collective-permute-start.34) | collective-permute-done | bytes 61472 | tf_op jit(solution)/shard_map/ppermute | solution.py:26
  140.4 3.0 %collective-permute-start.36 = (bf16[33,1024]{1,0:T(8,128)(2,1)S(1)}, bf16[33,1024]{1,0:T(8,128)(2,1)S(1)}, u32[]{:S(2)}, u32[]{:S(2)}) collective-permute-start(bf16[33,1024]{1,0:T(8,128)(2,1)S(1)} %add_convert_fusion), channel_id=1, source_target_pairs={{0,4},{4,0},{8,12},{12,8},{1,5},{5,1},{9,13},{13,9},{2,6},{6,2},{1... | collective-permute-start | bytes 202760 | tf_op jit(solution)/shard_map/ppermute | solution.py:30
  143.4 3.5 %collective-permute-start.37 = (bf16[33,1024]{1,0:T(8,128)(2,1)S(1)}, bf16[33,1024]{1,0:T(8,128)(2,1)S(1)}, u32[]{:S(2)}, u32[]{:S(2)}) collective-permute-start(bf16[33,1024]{1,0:T(8,128)(2,1)S(1)} %add_convert_fusion), channel_id=1, source_target_pairs={{0,8},{4,12},{8,0},{12,4},{1,9},{5,13},{9,1},{13,5},{2,10},{6,14},... | collective-permute-start | bytes 202760 | tf_op jit(solution)/shard_map/ppermute | solution.py:30
  146.9 6.6 %collective-permute-done.37 = bf16[33,1024]{1,0:T(8,128)(2,1)S(1)} collective-permute-done((bf16[33,1024]{1,0:T(8,128)(2,1)S(1)}, bf16[33,1024]{1,0:T(8,128)(2,1)S(1)}, u32[]{:S(2)}, u32[]{:S(2)}) %collective-permute-start.37) | collective-permute-done | bytes 67616 | tf_op jit(solution)/shard_map/ppermute | solution.py:30
  (142 shorter events, 56.7 us)
Async XLA Ops:
  1.8 16.9 %collective-permute-start = (bf16[256,1024]{1,0:T(8,128)(2,1)S(1)}, bf16[256,1024]{1,0:T(8,128)(2,1)}, u32[]{:S(2)}, u32[]{:S(2)}) collective-permute-start(bf16[256,1024]{1,0:T(8,128)(2,1)S(1)} %constant_dynamic-slice_fusion.1), channel_id=1, source_target_pairs={{0,4},{4,12},{12,8},{8,0},{1,5},{5,13},{13,9},{9,1},{2,6},{6,14},{... | collective-permute-start | bytes 1572872 | tf_op jit(solution)/shard_map/ppermute | solution.py:272
  6.0 23.9 %collective-permute-start.12 = (bf16[256,1024]{1,0:T(8,128)(2,1)S(1)}, bf16[256,1024]{1,0:T(8,128)(2,1)}, u32[]{:S(2)}, u32[]{:S(2)}) collective-permute-start(bf16[256,1024]{1,0:T(8,128)(2,1)S(1)} %constant_dynamic-slice_fusion.2), channel_id=1, source_target_pairs={{0,4},{4,12},{12,8},{8,0},{1,5},{5,13},{13,9},{9,1},{2,6},{6,14},{... | collective-permute-start | bytes 1572872 | tf_op jit(solution)/shard_map/ppermute | solution.py:272
  18.7 13.1 %collective-permute-start.1 = (bf16[256,1024]{1,0:T(8,128)(2,1)}, bf16[256,1024]{1,0:T(8,128)(2,1)}, u32[]{:S(2)}, u32[]{:S(2)}) collective-permute-start(bf16[256,1024]{1,0:T(8,128)(2,1)} %collective-permute-done), channel_id=1, source_target_pairs={{0,16},{16,0},{1,17},{17,1},{2,18},{18,2},{3,19},{19,3},{4,20},{20... | collective-permute-start | bytes 1572872 | tf_op jit(solution)/shard_map/ppermute | solution.py:26
  23.7 11.5 %collective-permute-start.2 = (bf16[256,1024]{1,0:T(8,128)(2,1)}, bf16[256,1024]{1,0:T(8,128)(2,1)}, u32[]{:S(2)}, u32[]{:S(2)}) collective-permute-start(bf16[256,1024]{1,0:T(8,128)(2,1)} %collective-permute-done), channel_id=1, source_target_pairs={{0,1},{1,0},{2,3},{3,2},{4,5},{5,4},{6,7},{7,6},{8,9},{9,8},{10,11... | collective-permute-start | bytes 1572872 | tf_op jit(solution)/shard_map/ppermute | solution.py:26
  23.8 17.4 %collective-permute-start.4 = (bf16[256,1024]{1,0:T(8,128)(2,1)}, bf16[256,1024]{1,0:T(8,128)(2,1)}, u32[]{:S(2)}, u32[]{:S(2)}) collective-permute-start(bf16[256,1024]{1,0:T(8,128)(2,1)} %collective-permute-done), channel_id=1, source_target_pairs={{0,4},{4,12},{12,8},{8,0},{1,5},{5,13},{13,9},{9,1},{2,6},{6,14},{... | collective-permute-start | bytes 1572872 | tf_op jit(solution)/shard_map/ppermute | solution.py:272
  30.0 13.1 %collective-permute-start.13 = (bf16[256,1024]{1,0:T(8,128)(2,1)}, bf16[256,1024]{1,0:T(8,128)(2,1)}, u32[]{:S(2)}, u32[]{:S(2)}) collective-permute-start(bf16[256,1024]{1,0:T(8,128)(2,1)} %collective-permute-done.12), channel_id=1, source_target_pairs={{0,16},{16,0},{1,17},{17,1},{2,18},{18,2},{3,19},{19,3},{4,20},{20... | collective-permute-start | bytes 1572872 | tf_op jit(solution)/shard_map/ppermute | solution.py:26
  31.8 11.2 %collective-permute-start.3 = (bf16[256,1024]{1,0:T(8,128)(2,1)}, bf16[256,1024]{1,0:T(8,128)(2,1)}, u32[]{:S(2)}, u32[]{:S(2)}) collective-permute-start(bf16[256,1024]{1,0:T(8,128)(2,1)} %collective-permute-done.1), channel_id=1, source_target_pairs={{0,1},{1,0},{2,3},{3,2},{4,5},{5,4},{6,7},{7,6},{8,9},{9,8},{10,11... | collective-permute-start | bytes 1572872 | tf_op jit(solution)/shard_map/ppermute | solution.py:26
  34.6 11.8 %collective-permute-start.14 = (bf16[256,1024]{1,0:T(8,128)(2,1)}, bf16[256,1024]{1,0:T(8,128)(2,1)S(1)}, u32[]{:S(2)}, u32[]{:S(2)}) collective-permute-start(bf16[256,1024]{1,0:T(8,128)(2,1)} %collective-permute-done.12), channel_id=1, source_target_pairs={{0,1},{1,0},{2,3},{3,2},{4,5},{5,4},{6,7},{7,6},{8,9},{9,8},{10,11... | collective-permute-start | bytes 1572872 | tf_op jit(solution)/shard_map/ppermute | solution.py:26
  35.2 17.1 %collective-permute-start.16 = (bf16[256,1024]{1,0:T(8,128)(2,1)}, bf16[256,1024]{1,0:T(8,128)(2,1)S(1)}, u32[]{:S(2)}, u32[]{:S(2)}) collective-permute-start(bf16[256,1024]{1,0:T(8,128)(2,1)} %collective-permute-done.12), channel_id=1, source_target_pairs={{0,4},{4,12},{12,8},{8,0},{1,5},{5,13},{13,9},{9,1},{2,6},{6,14},{... | collective-permute-start | bytes 1572872 | tf_op jit(solution)/shard_map/ppermute | solution.py:272
  41.2 13.0 %collective-permute-start.5 = (bf16[256,1024]{1,0:T(8,128)(2,1)}, bf16[256,1024]{1,0:T(8,128)(2,1)S(1)}, u32[]{:S(2)}, u32[]{:S(2)}) collective-permute-start(bf16[256,1024]{1,0:T(8,128)(2,1)} %collective-permute-done.4), channel_id=1, source_target_pairs={{0,16},{16,0},{1,17},{17,1},{2,18},{18,2},{3,19},{19,3},{4,20},{20... | collective-permute-start | bytes 1572872 | tf_op jit(solution)/shard_map/ppermute | solution.py:26
  43.1 14.5 %collective-permute-start.6 = (bf16[256,1024]{1,0:T(8,128)(2,1)}, bf16[256,1024]{1,0:T(8,128)(2,1)S(1)}, u32[]{:S(2)}, u32[]{:S(2)}) collective-permute-start(bf16[256,1024]{1,0:T(8,128)(2,1)} %collective-permute-done.4), channel_id=1, source_target_pairs={{0,1},{1,0},{2,3},{3,2},{4,5},{5,4},{6,7},{7,6},{8,9},{9,8},{10,11... | collective-permute-start | bytes 1572872 | tf_op jit(solution)/shard_map/ppermute | solution.py:26
  43.1 12.0 %collective-permute-start.15 = (bf16[256,1024]{1,0:T(8,128)(2,1)}, bf16[256,1024]{1,0:T(8,128)(2,1)S(1)}, u32[]{:S(2)}, u32[]{:S(2)}) collective-permute-start(bf16[256,1024]{1,0:T(8,128)(2,1)} %collective-permute-done.13), channel_id=1, source_target_pairs={{0,1},{1,0},{2,3},{3,2},{4,5},{5,4},{6,7},{7,6},{8,9},{9,8},{10,11... | collective-permute-start | bytes 1572872 | tf_op jit(solution)/shard_map/ppermute | solution.py:26
  46.4 17.1 %collective-permute-start.8 = (bf16[256,1024]{1,0:T(8,128)(2,1)}, bf16[256,1024]{1,0:T(8,128)(2,1)S(1)}, u32[]{:S(2)}, u32[]{:S(2)}) collective-permute-start(bf16[256,1024]{1,0:T(8,128)(2,1)} %collective-permute-done.4), channel_id=1, source_target_pairs={{0,4},{4,12},{12,8},{8,0},{1,5},{5,13},{13,9},{9,1},{2,6},{6,14},{... | collective-permute-start | bytes 1572872 | tf_op jit(solution)/shard_map/ppermute | solution.py:272
  52.3 13.1 %collective-permute-start.17 = (bf16[256,1024]{1,0:T(8,128)(2,1)S(1)}, bf16[256,1024]{1,0:T(8,128)(2,1)S(1)}, u32[]{:S(2)}, u32[]{:S(2)}) collective-permute-start(bf16[256,1024]{1,0:T(8,128)(2,1)S(1)} %collective-permute-done.16), channel_id=1, source_target_pairs={{0,16},{16,0},{1,17},{17,1},{2,18},{18,2},{3,19},{19,3},{4,20},{20... | collective-permute-start | bytes 1572872 | tf_op jit(solution)/shard_map/ppermute | solution.py:26
  54.2 19.9 %collective-permute-start.20 = (bf16[256,1024]{1,0:T(8,128)(2,1)S(1)}, bf16[256,1024]{1,0:T(8,128)(2,1)}, u32[]{:S(2)}, u32[]{:S(2)}) collective-permute-start(bf16[256,1024]{1,0:T(8,128)(2,1)S(1)} %collective-permute-done.16), channel_id=1, source_target_pairs={{0,4},{4,12},{12,8},{8,0},{1,5},{5,13},{13,9},{9,1},{2,6},{6,14},{... | collective-permute-start | bytes 1572872 | tf_op jit(solution)/shard_map/ppermute | solution.py:272
  55.1 19.0 %collective-permute-start.7 = (bf16[256,1024]{1,0:T(8,128)(2,1)S(1)}, bf16[256,1024]{1,0:T(8,128)(2,1)S(1)}, u32[]{:S(2)}, u32[]{:S(2)}) collective-permute-start(bf16[256,1024]{1,0:T(8,128)(2,1)S(1)} %collective-permute-done.5), channel_id=1, source_target_pairs={{0,1},{1,0},{2,3},{3,2},{4,5},{5,4},{6,7},{7,6},{8,9},{9,8},{10,11... | collective-permute-start | bytes 1572872 | tf_op jit(solution)/shard_map/ppermute | solution.py:26
  57.6 20.4 %collective-permute-start.18 = (bf16[256,1024]{1,0:T(8,128)(2,1)S(1)}, bf16[256,1024]{1,0:T(8,128)(2,1)S(1)}, u32[]{:S(2)}, u32[]{:S(2)}) collective-permute-start(bf16[256,1024]{1,0:T(8,128)(2,1)S(1)} %collective-permute-done.16), channel_id=1, source_target_pairs={{0,1},{1,0},{2,3},{3,2},{4,5},{5,4},{6,7},{7,6},{8,9},{9,8},{10,11... | collective-permute-start | bytes 1572872 | tf_op jit(solution)/shard_map/ppermute | solution.py:26
  63.6 14.7 %collective-permute-start.9 = (bf16[256,1024]{1,0:T(8,128)(2,1)S(1)}, bf16[256,1024]{1,0:T(8,128)(2,1)S(1)}, u32[]{:S(2)}, u32[]{:S(2)}) collective-permute-start(bf16[256,1024]{1,0:T(8,128)(2,1)S(1)} %collective-permute-done.8), channel_id=1, source_target_pairs={{0,16},{16,0},{1,17},{17,1},{2,18},{18,2},{3,19},{19,3},{4,20},{20... | collective-permute-start | bytes 1572872 | tf_op jit(solution)/shard_map/ppermute | solution.py:26
  65.4 15.7 %collective-permute-start.10 = (bf16[256,1024]{1,0:T(8,128)(2,1)S(1)}, bf16[256,1024]{1,0:T(8,128)(2,1)S(1)}, u32[]{:S(2)}, u32[]{:S(2)}) collective-permute-start(bf16[256,1024]{1,0:T(8,128)(2,1)S(1)} %collective-permute-done.8), channel_id=1, source_target_pairs={{0,1},{1,0},{2,3},{3,2},{4,5},{5,4},{6,7},{7,6},{8,9},{9,8},{10,11... | collective-permute-start | bytes 1572872 | tf_op jit(solution)/shard_map/ppermute | solution.py:26
  74.1 14.5 %collective-permute-start.21 = (bf16[256,1024]{1,0:T(8,128)(2,1)}, bf16[256,1024]{1,0:T(8,128)(2,1)S(1)}, u32[]{:S(2)}, u32[]{:S(2)}) collective-permute-start(bf16[256,1024]{1,0:T(8,128)(2,1)} %collective-permute-done.20), channel_id=1, source_target_pairs={{0,16},{16,0},{1,17},{17,1},{2,18},{18,2},{3,19},{19,3},{4,20},{20... | collective-permute-start | bytes 1572872 | tf_op jit(solution)/shard_map/ppermute | solution.py:26
  78.0 11.0 %collective-permute-start.22 = (bf16[256,1024]{1,0:T(8,128)(2,1)}, bf16[256,1024]{1,0:T(8,128)(2,1)S(1)}, u32[]{:S(2)}, u32[]{:S(2)}) collective-permute-start(bf16[256,1024]{1,0:T(8,128)(2,1)} %collective-permute-done.20), channel_id=1, source_target_pairs={{0,1},{1,0},{2,3},{3,2},{4,5},{5,4},{6,7},{7,6},{8,9},{9,8},{10,11... | collective-permute-start | bytes 1572872 | tf_op jit(solution)/shard_map/ppermute | solution.py:26
  101.9 25.2 %collective-permute-start.33 = (s32[32,4]{1,0:T(8,128)S(1)}, s32[32,4]{1,0:T(8,128)S(1)}, u32[]{:S(2)}, u32[]{:S(2)}) collective-permute-start(s32[32,4]{1,0:T(8,128)S(1)} %fusion.116), channel_id=1, source_target_pairs={{0,1},{1,0},{2,3},{3,2},{4,5},{5,4},{6,7},{7,6},{8,9},{9,8},{10,11... | collective-permute-start | bytes 1544 | tf_op jit(solution)/shard_map/ppermute | solution.py:26
  102.0 15.7 %collective-permute-start.27 = (bf16[64,2048]{1,0:T(8,128)(2,1)S(1)}, bf16[64,2048]{1,0:T(8,128)(2,1)}, u32[]{:S(2)}, u32[]{:S(2)}) collective-permute-start(bf16[64,2048]{1,0:T(8,128)(2,1)S(1)} %get-tuple-element.42.refs_0_.refs_4_), channel_id=1, source_target_pairs={{4,0},{12,4},{8,12},{0,8},{5,1},{13,5},{9,13},{1,9},{6,2},{14,6},{... | collective-permute-start | bytes 786440 | tf_op jit(solution)/shard_map/ppermute | solution.py:327
  109.6 11.6 %collective-permute-start.26 = (bf16[64,2048]{1,0:T(8,128)(2,1)S(1)}, bf16[64,2048]{1,0:T(8,128)(2,1)}, u32[]{:S(2)}, u32[]{:S(2)}) collective-permute-start(bf16[64,2048]{1,0:T(8,128)(2,1)S(1)} %collective-permute-done.25.refs_1_), channel_id=1, source_target_pairs={{0,4},{4,12},{12,8},{8,0},{1,5},{5,13},{13,9},{9,1},{2,6},{6,14},{... | collective-permute-start | bytes 786440 | tf_op jit(solution)/shard_map/ppermute | solution.py:325
  (30 other events, 159.1 us)

commit v9 on v8

--- a/solution.py
+++ b/solution.py
@@ -109,6 +109,31 @@
         axis=0,
     )
     out_ref[rows + half :] = tail
+
+
+def pool_kernel(squares_count, chunks, width, *refs):
+    squares = refs[0][...]
+    for ref in refs[1:squares_count]:
+        squares = squares + ref[...]
+    state_refs = refs[squares_count : squares_count + chunks]
+    labels_ref, gain_ref, counts_ref, sums_ref, pooled_ref, inv_rms_ref = refs[
+        squares_count + chunks :
+    ]
+    inv_rms = lax.rsqrt(squares / width + 1e-05)
+    inv_rms_ref[...] = inv_rms
+    scale = as_column(inv_rms)
+    docs, tokens = counts_ref.shape[0], squares.shape[1]
+    doc_id = lax.broadcasted_iota(jnp.int32, (docs, tokens), 0)
+    member = jnp.where(doc_id == labels_ref[...], 1.0, 0.0).astype(jnp.bfloat16)
+    counts = counts_ref[...]
+    for (low, high), state_ref in zip(spans(gain_ref.shape[1]), state_refs):
+        tile = 256 if (high - low) % 256 == 0 else 128
+        for at in range(0, high - low, tile):
+            part = slice(low + at, low + at + tile)
+            normed = (state_ref[:, at : at + tile] * scale * gain_ref[:, part]).astype(jnp.bfloat16)
+            sums = dot_nn(member, normed)
+            sums_ref[:, part] = sums
+            pooled_ref[:, part] = (sums / counts).astype(jnp.bfloat16)
 
 
 def loss_kernel(blocks, sums_count, chunks, *refs):
@@ -301,23 +326,27 @@
             )
             event += 1
     states_b = [x.astype(jnp.bfloat16) for x in states]
-    squares = sum_over(sum(jnp.sum(x * x, axis=1) for x in states), "mp")
-    inv_rms = lax.rsqrt(squares / width + 1e-05)
+    squares = sum(jnp.sum(x * x, axis=1) for x in states)
 
     gain = norm_gain_vector.astype(jnp.float32)
     labels = document_labels[0, 0]
     member = labels[None, :] == jnp.arange(docs, dtype=jnp.int32)[:, None]
     member_f = member.astype(jnp.float32)
     counts = jnp.sum(member_f, axis=1)
-    member_b = member.astype(jnp.bfloat16)
-    doc_sums = jnp.concatenate(
-        [
-            dot_nn(member_b, (x * inv_rms[:, None] * g[None, :]).astype(jnp.bfloat16))
-            for x, g in zip(states, [gain[low:high] for low, high in parts])
-        ],
-        axis=1,
-    )
-    pooled = (doc_sums / counts[:, None]).astype(jnp.bfloat16)
+    if lax.axis_size("mp") == 2:
+        squares = [squares, swap(squares, "mp")]
+    else:
+        squares = [lax.psum(squares, "mp")]
+    doc_sums, pooled, inv_rms = call(
+        functools.partial(pool_kernel, len(squares), chunk_count, width),
+        (
+            jax.ShapeDtypeStruct((docs, cols), jnp.float32),
+            jax.ShapeDtypeStruct((docs, cols), jnp.bfloat16),
+            jax.ShapeDtypeStruct((1, token_count), jnp.float32),
+        ),
+        [x[None] for x in squares] + states + [labels[None], gain[None], counts[:, None]],
+    )
+    inv_rms = inv_rms[0]
 
     own_blocks = [pooled] * dp
     for j in range(1, dp):

time: 157 us -> 159 us (1.013)
  local copies, waits for them, and re-layouts: 8.66 us -> 13.2 us
  waiting for transfers between devices: 66.6 us -> 63.5 us
  matrix products: 28.8 us -> 26.5 us
    unnamed x30 -> x32, local copies, waits for them, and re-layouts: 2.94 us -> 6.1 us
    ppermute x2, waiting for transfers between devices: 8.78 us -> 6.18 us  [body(): own_blocks[j] = lax.ppermute(own_blocks[j - 1], 'dp', hops)]
    dot_general x18 -> x16, matrix products: 28 us -> 25.6 us  [dot_nn(): jnp.dot(a, b, precision=precision, preferred_element_type=jnp.float32)]
    pallas_call x2 -> x3, Pallas kernels: 4.06 us -> 4.73 us  [call(): pl.pallas_call(kernel, out_shape=outs, scratch_shapes=list(scratch), comp...]
  transfers between devices with their start and end apart: 40 -> 40, of which waited for: 17 -> 17; matrix products, arithmetic and copies ran while one was open for 17% -> 19% of each run, Pallas kernels for 1% -> 1%
where the time goes in v9:
time: 159 us; the launch traced here: 158 us
  waiting for transfers between devices  63.5 us (40%)
  starting transfers between devices  45.7 us (29%)
  matrix products  26.5 us (17%)
  local copies, waits for them, and re-layouts  13.2 us (8%)
  Pallas kernels  4.73 us (3%)
  other arithmetic  3.73 us (2%)
    ppermute x6, waiting for transfers between devices, body(): lax.ppermute(ringed[-chunk_count] if step > 1 else moving[h], 'dp', hops)  32.9 us
    dot_general x16, matrix products, dot_nn(): jnp.dot(a, b, precision=precision, preferred_element_type=jnp.float32)  25.6 us
    ppermute x28, starting transfers between devices, swap(): return lax.ppermute(x, axis, [(0, 1), (1, 0)])  18.8 us
    ppermute x28, waiting for transfers between devices, swap(): return lax.ppermute(x, axis, [(0, 1), (1, 0)])  17.8 us
    ppermute x2, starting transfers between devices, body(): own_blocks[j] = lax.ppermute(own_blocks[j - 1], 'dp', hops)  8.97 us
    ppermute x6, starting transfers between devices, body(): lax.ppermute(ringed[-chunk_count] if step > 1 else moving[h], 'dp', hops)  8.85 us
    ppermute x3, starting transfers between devices, partner(): lax.ppermute(x, axis, [(i, i ^ flip) for i in range(lax.axis_size(axis))])  6.8 us
    ppermute x3, waiting for transfers between devices, partner(): lax.ppermute(x, axis, [(i, i ^ flip) for i in range(lax.axis_size(axis))])  6.6 us
  transfers between devices with their start and end apart: 40, of which 17 were waited for; matrix products, arithmetic and copies ran while one was open for 19% of the time, Pallas kernels for 1%

profile of v9, /device:TPU:0, one launch (start us, length us, event | category | flops | bytes accessed | tf_op | source)
XLA Modules:
  0.0 158.4 jit_solution(5869067378721044343)
XLA Ops:
  1.8 3.1 %collective-permute-start = (bf16[256,1024]{1,0:T(8,128)(2,1)S(1)}, bf16[256,1024]{1,0:T(8,128)(2,1)}, u32[]{:S(2)}, u32[]{:S(2)}) collective-permute-start(bf16[256,1024]{1,0:T(8,128)(2,1)S(1)} %constant_dynamic-slice_fusion.1), channel_id=1, source_target_pairs={{0,4},{4,12},{12,8},{8,0},{1,5},{5,13},{13,9},{9,1},{2,6},{6,14},{... | collective-permute-start | bytes 1572872 | tf_op jit(solution)/shard_map/ppermute | solution.py:297
  6.0 2.6 %collective-permute-start.12 = (bf16[256,1024]{1,0:T(8,128)(2,1)S(1)}, bf16[256,1024]{1,0:T(8,128)(2,1)}, u32[]{:S(2)}, u32[]{:S(2)}) collective-permute-start(bf16[256,1024]{1,0:T(8,128)(2,1)S(1)} %constant_dynamic-slice_fusion.2), channel_id=1, source_target_pairs={{0,4},{4,12},{12,8},{8,0},{1,5},{5,13},{13,9},{9,1},{2,6},{6,14},{... | collective-permute-start | bytes 1572872 | tf_op jit(solution)/shard_map/ppermute | solution.py:297
  8.7 3.5 %fusion.73 = bf16[512,16]{0,1:T(8,128)(2,1)S(1)} fusion(bf16[4096,16]{0,1:T(8,128)(2,1)S(1)} %copy-done, bf16[1,512,4096]{2,1,0:T(8,128)(2,1)} %param.8), kind=kOutput, calls=%fused_computation.69 | convolution fusion | flops 67117056 | bytes 4341760 | tf_op jit(solution)/shard_map/dot_general | solution.py:22
  15.7 3.0 %collective-permute-done = bf16[256,1024]{1,0:T(8,128)(2,1)} collective-permute-done((bf16[256,1024]{1,0:T(8,128)(2,1)S(1)}, bf16[256,1024]{1,0:T(8,128)(2,1)}, u32[]{:S(2)}, u32[]{:S(2)}) %collective-permute-start) | collective-permute-done | bytes 524320 | tf_op jit(solution)/shard_map/ppermute | solution.py:297
  24.5 5.5 %collective-permute-done.12 = bf16[256,1024]{1,0:T(8,128)(2,1)} collective-permute-done((bf16[256,1024]{1,0:T(8,128)(2,1)S(1)}, bf16[256,1024]{1,0:T(8,128)(2,1)}, u32[]{:S(2)}, u32[]{:S(2)}) %collective-permute-start.12) | collective-permute-done | bytes 524320 | tf_op jit(solution)/shard_map/ppermute | solution.py:297
  35.9 5.3 %collective-permute-done.4 = bf16[256,1024]{1,0:T(8,128)(2,1)} collective-permute-done((bf16[256,1024]{1,0:T(8,128)(2,1)}, bf16[256,1024]{1,0:T(8,128)(2,1)}, u32[]{:S(2)}, u32[]{:S(2)}) %collective-permute-start.4) | collective-permute-done | bytes 524320 | tf_op jit(solution)/shard_map/ppermute | solution.py:297
  43.6 2.8 %fusion.69 = f32[512,1024]{1,0:T(8,128)S(1)} fusion(f32[512,1024]{1,0:T(8,128)S(1)} %copy-done.10, bf16[256,1024]{1,0:T(8,128)(2,1)} %collective-permute-done.3, bf16[256,1024]{1,0:T(8,128)(2,1)} %collective-permute-done.2, bf16[256,1024]{1,0:T(8,128)(2,1)} %collective-permute-done.1, bf16[256,1024]{1,0:T(8,128)(2,1)} %collective-permute-done, ...), kind=kOutput, calls=%fused_computation.66 | convolution fusion | flops 1086849024 | bytes 7340032 | tf_op jit(solution)/shard_map/dot_general | solution.py:22
  47.2 5.1 %collective-permute-done.16 = bf16[256,1024]{1,0:T(8,128)(2,1)S(1)} collective-permute-done((bf16[256,1024]{1,0:T(8,128)(2,1)}, bf16[256,1024]{1,0:T(8,128)(2,1)S(1)}, u32[]{:S(2)}, u32[]{:S(2)}) %collective-permute-start.16) | collective-permute-done | bytes 524320 | tf_op jit(solution)/shard_map/ppermute | solution.py:297
  55.1 2.5 %fusion.60 = f32[512,1024]{1,0:T(8,128)S(1)} fusion(f32[512,1024]{1,0:T(8,128)S(1)} %add_add_fusion, bf16[256,1024]{1,0:T(8,128)(2,1)S(1)} %collective-permute-done.15, bf16[256,1024]{1,0:T(8,128)(2,1)S(1)} %collective-permute-done.14, bf16[256,1024]{1,0:T(8,128)(2,1)} %collective-permute-done.13, bf16[256,1024]{1,0:T(8,128)(2,1)} %collective-permute-done.12, ...), kind=kOutput, calls=%fused_computation.63 | convolution fusion | flops 1086849024 | bytes 7340032 | tf_op jit(solution)/shard_map/dot_general | solution.py:22
  58.2 5.4 %collective-permute-done.8 = bf16[256,1024]{1,0:T(8,128)(2,1)S(1)} collective-permute-done((bf16[256,1024]{1,0:T(8,128)(2,1)}, bf16[256,1024]{1,0:T(8,128)(2,1)S(1)}, u32[]{:S(2)}, u32[]{:S(2)}) %collective-permute-start.8) | collective-permute-done | bytes 524320 | tf_op jit(solution)/shard_map/ppermute | solution.py:297
  65.5 8.6 %collective-permute-done.20 = bf16[256,1024]{1,0:T(8,128)(2,1)} collective-permute-done((bf16[256,1024]{1,0:T(8,128)(2,1)S(1)}, bf16[256,1024]{1,0:T(8,128)(2,1)}, u32[]{:S(2)}, u32[]{:S(2)}) %collective-permute-start.20) | collective-permute-done | bytes 524320 | tf_op jit(solution)/shard_map/ppermute | solution.py:297
  75.6 2.3 %fusion.66 = f32[512,1024]{1,0:T(8,128)S(1)} fusion(f32[512,1024]{1,0:T(8,128)S(1)} %fusion.69, bf16[256,1024]{1,0:T(8,128)(2,1)S(1)} %collective-permute-done.7, bf16[256,1024]{1,0:T(8,128)(2,1)S(1)} %collective-permute-done.6, bf16[256,1024]{1,0:T(8,128)(2,1)S(1)} %collective-permute-done.5, bf16[256,1024]{1,0:T(8,128)(2,1)} %collective-permute-done.4, ...), kind=kOutput, calls=%fused_computation.65 | convolution fusion | flops 1086849024 | bytes 7340032 | tf_op jit(solution)/shard_map/dot_general | solution.py:22
  78.5 2.6 %fusion.57 = f32[512,1024]{1,0:T(8,128)} fusion(f32[512,1024]{1,0:T(8,128)S(1)} %fusion.60, bf16[256,1024]{1,0:T(8,128)(2,1)S(1)} %collective-permute-done.19, bf16[256,1024]{1,0:T(8,128)(2,1)S(1)} %collective-permute-done.18, bf16[256,1024]{1,0:T(8,128)(2,1)S(1)} %collective-permute-done.17, bf16[256,1024]{1,0:T(8,128)(2,1)S(1)} %collective-permute-done.16, ...), kind=kOutput, calls=%fused_computation.62 | convolution fusion | flops 1086849024 | bytes 7340032 | tf_op jit(solution)/shard_map/dot_general | solution.py:22
  81.2 2.6 %fusion.63.refs_2_ = f32[512,1024]{1,0:T(8,128)} fusion(f32[512,1024]{1,0:T(8,128)S(1)} %fusion.66, bf16[256,1024]{1,0:T(8,128)(2,1)S(1)} %collective-permute-done.11, bf16[256,1024]{1,0:T(8,128)(2,1)S(1)} %collective-permute-done.10, bf16[256,1024]{1,0:T(8,128)(2,1)S(1)} %collective-permute-done.9, bf16[256,1024]{1,0:T(8,128)(2,1)S(1)} %collective-permute-done.8, ...), kind=kOutput, calls=%fused_computation.64 | convolution fusion | flops 1086849024 | bytes 7340032 | tf_op jit(solution)/shard_map/dot_general | solution.py:22
  83.8 4.8 %collective-permute-done.21 = bf16[256,1024]{1,0:T(8,128)(2,1)S(1)} collective-permute-done((bf16[256,1024]{1,0:T(8,128)(2,1)}, bf16[256,1024]{1,0:T(8,128)(2,1)S(1)}, u32[]{:S(2)}, u32[]{:S(2)}) %collective-permute-start.21) | collective-permute-done | bytes 524320 | tf_op jit(solution)/shard_map/ppermute | solution.py:26
  90.5 3.0 %fusion.54.refs_3_ = f32[512,1024]{1,0:T(8,128)S(1)} fusion(f32[512,1024]{1,0:T(8,128)} %fusion.57, bf16[256,1024]{1,0:T(8,128)(2,1)S(1)} %collective-permute-done.23, bf16[256,1024]{1,0:T(8,128)(2,1)S(1)} %collective-permute-done.22, bf16[256,1024]{1,0:T(8,128)(2,1)S(1)} %collective-permute-done.21, bf16[256,1024]{1,0:T(8,128)(2,1)} %collective-permute-done.20, ...), kind=kOutput, calls=%fused_computation.61 | convolution fusion | flops 1086849024 | bytes 7340032 | tf_op jit(solution)/shard_map/dot_general | solution.py:22
  104.0 2.2 %collective-permute-start.27 = (bf16[64,2048]{1,0:T(8,128)(2,1)S(1)}, bf16[64,2048]{1,0:T(8,128)(2,1)}, u32[]{:S(2)}, u32[]{:S(2)}) collective-permute-start(bf16[64,2048]{1,0:T(8,128)(2,1)S(1)} %get-tuple-element.19.refs_0_.refs_4_), channel_id=1, source_target_pairs={{4,0},{12,4},{8,12},{0,8},{5,1},{13,5},{9,13},{1,9},{6,2},{14,6},{... | collective-permute-start | bytes 786440 | tf_op jit(solution)/shard_map/ppermute | solution.py:356
  106.2 4.4 %collective-permute-done.25.refs_1_ = bf16[64,2048]{1,0:T(8,128)(2,1)S(1)} collective-permute-done((bf16[64,2048]{1,0:T(8,128)(2,1)S(1)}, bf16[64,2048]{1,0:T(8,128)(2,1)S(1)}, u32[]{:S(2)}, u32[]{:S(2)}) %collective-permute-start.25) | collective-permute-done | bytes 262176 | tf_op jit(solution)/shard_map/ppermute | solution.py:354
  110.7 8.2 %collective-permute-start.26 = (bf16[64,2048]{1,0:T(8,128)(2,1)S(1)}, bf16[64,2048]{1,0:T(8,128)(2,1)}, u32[]{:S(2)}, u32[]{:S(2)}) collective-permute-start(bf16[64,2048]{1,0:T(8,128)(2,1)S(1)} %collective-permute-done.25.refs_1_), channel_id=1, source_target_pairs={{0,4},{4,12},{12,8},{8,0},{1,5},{5,13},{13,9},{9,1},{2,6},{6,14},{... | collective-permute-start | bytes 786440 | tf_op jit(solution)/shard_map/ppermute | solution.py:354
  128.8 4.1 %collective-permute-done.32.refs_1_ = f32[296,128]{1,0:T(8,128)S(1)} collective-permute-done((f32[296,128]{1,0:T(8,128)S(1)}, f32[296,128]{1,0:T(8,128)S(1)}, u32[]{:S(2)}, u32[]{:S(2)}) %collective-permute-start.32) | collective-permute-done | bytes 151584 | tf_op jit(solution)/shard_map/ppermute | solution.py:26
  136.5 2.6 %collective-permute-done.34 = f32[24,640]{1,0:T(8,128)S(1)} collective-permute-done((f32[24,640]{1,0:T(8,128)S(1)}, f32[24,640]{1,0:T(8,128)S(1)}, u32[]{:S(2)}, u32[]{:S(2)}) %collective-permute-start.34) | collective-permute-done | bytes 61472 | tf_op jit(solution)/shard_map/ppermute | solution.py:26
  142.1 3.3 %collective-permute-start.36 = (bf16[33,1024]{1,0:T(8,128)(2,1)S(1)}, bf16[33,1024]{1,0:T(8,128)(2,1)S(1)}, u32[]{:S(2)}, u32[]{:S(2)}) collective-permute-start(bf16[33,1024]{1,0:T(8,128)(2,1)S(1)} %add_convert_fusion), channel_id=1, source_target_pairs={{0,4},{4,0},{8,12},{12,8},{1,5},{5,1},{9,13},{13,9},{2,6},{6,2},{1... | collective-permute-start | bytes 202760 | tf_op jit(solution)/shard_map/ppermute | solution.py:30
  145.4 3.5 %collective-permute-start.37 = (bf16[33,1024]{1,0:T(8,128)(2,1)S(1)}, bf16[33,1024]{1,0:T(8,128)(2,1)S(1)}, u32[]{:S(2)}, u32[]{:S(2)}) collective-permute-start(bf16[33,1024]{1,0:T(8,128)(2,1)S(1)} %add_convert_fusion), channel_id=1, source_target_pairs={{0,8},{4,12},{8,0},{12,4},{1,9},{5,13},{9,1},{13,5},{2,10},{6,14},... | collective-permute-start | bytes 202760 | tf_op jit(solution)/shard_map/ppermute | solution.py:30
  148.9 6.6 %collective-permute-done.37 = bf16[33,1024]{1,0:T(8,128)(2,1)S(1)} collective-permute-done((bf16[33,1024]{1,0:T(8,128)(2,1)S(1)}, bf16[33,1024]{1,0:T(8,128)(2,1)S(1)}, u32[]{:S(2)}, u32[]{:S(2)}) %collective-permute-start.37) | collective-permute-done | bytes 67616 | tf_op jit(solution)/shard_map/ppermute | solution.py:30
  (139 shorter events, 59.6 us)
Async XLA Ops:
  1.8 16.9 %collective-permute-start = (bf16[256,1024]{1,0:T(8,128)(2,1)S(1)}, bf16[256,1024]{1,0:T(8,128)(2,1)}, u32[]{:S(2)}, u32[]{:S(2)}) collective-permute-start(bf16[256,1024]{1,0:T(8,128)(2,1)S(1)} %constant_dynamic-slice_fusion.1), channel_id=1, source_target_pairs={{0,4},{4,12},{12,8},{8,0},{1,5},{5,13},{13,9},{9,1},{2,6},{6,14},{... | collective-permute-start | bytes 1572872 | tf_op jit(solution)/shard_map/ppermute | solution.py:297
  6.0 23.9 %collective-permute-start.12 = (bf16[256,1024]{1,0:T(8,128)(2,1)S(1)}, bf16[256,1024]{1,0:T(8,128)(2,1)}, u32[]{:S(2)}, u32[]{:S(2)}) collective-permute-start(bf16[256,1024]{1,0:T(8,128)(2,1)S(1)} %constant_dynamic-slice_fusion.2), channel_id=1, source_target_pairs={{0,4},{4,12},{12,8},{8,0},{1,5},{5,13},{13,9},{9,1},{2,6},{6,14},{... | collective-permute-start | bytes 1572872 | tf_op jit(solution)/shard_map/ppermute | solution.py:297
  18.7 13.1 %collective-permute-start.1 = (bf16[256,1024]{1,0:T(8,128)(2,1)}, bf16[256,1024]{1,0:T(8,128)(2,1)}, u32[]{:S(2)}, u32[]{:S(2)}) collective-permute-start(bf16[256,1024]{1,0:T(8,128)(2,1)} %collective-permute-done), channel_id=1, source_target_pairs={{0,16},{16,0},{1,17},{17,1},{2,18},{18,2},{3,19},{19,3},{4,20},{20... | collective-permute-start | bytes 1572872 | tf_op jit(solution)/shard_map/ppermute | solution.py:26
  23.7 11.5 %collective-permute-start.2 = (bf16[256,1024]{1,0:T(8,128)(2,1)}, bf16[256,1024]{1,0:T(8,128)(2,1)}, u32[]{:S(2)}, u32[]{:S(2)}) collective-permute-start(bf16[256,1024]{1,0:T(8,128)(2,1)} %collective-permute-done), channel_id=1, source_target_pairs={{0,1},{1,0},{2,3},{3,2},{4,5},{5,4},{6,7},{7,6},{8,9},{9,8},{10,11... | collective-permute-start | bytes 1572872 | tf_op jit(solution)/shard_map/ppermute | solution.py:26
  23.8 17.4 %collective-permute-start.4 = (bf16[256,1024]{1,0:T(8,128)(2,1)}, bf16[256,1024]{1,0:T(8,128)(2,1)}, u32[]{:S(2)}, u32[]{:S(2)}) collective-permute-start(bf16[256,1024]{1,0:T(8,128)(2,1)} %collective-permute-done), channel_id=1, source_target_pairs={{0,4},{4,12},{12,8},{8,0},{1,5},{5,13},{13,9},{9,1},{2,6},{6,14},{... | collective-permute-start | bytes 1572872 | tf_op jit(solution)/shard_map/ppermute | solution.py:297
  30.0 13.1 %collective-permute-start.13 = (bf16[256,1024]{1,0:T(8,128)(2,1)}, bf16[256,1024]{1,0:T(8,128)(2,1)}, u32[]{:S(2)}, u32[]{:S(2)}) collective-permute-start(bf16[256,1024]{1,0:T(8,128)(2,1)} %collective-permute-done.12), channel_id=1, source_target_pairs={{0,16},{16,0},{1,17},{17,1},{2,18},{18,2},{3,19},{19,3},{4,20},{20... | collective-permute-start | bytes 1572872 | tf_op jit(solution)/shard_map/ppermute | solution.py:26
  31.8 11.2 %collective-permute-start.3 = (bf16[256,1024]{1,0:T(8,128)(2,1)}, bf16[256,1024]{1,0:T(8,128)(2,1)}, u32[]{:S(2)}, u32[]{:S(2)}) collective-permute-start(bf16[256,1024]{1,0:T(8,128)(2,1)} %collective-permute-done.1), channel_id=1, source_target_pairs={{0,1},{1,0},{2,3},{3,2},{4,5},{5,4},{6,7},{7,6},{8,9},{9,8},{10,11... | collective-permute-start | bytes 1572872 | tf_op jit(solution)/shard_map/ppermute | solution.py:26
  34.6 11.7 %collective-permute-start.14 = (bf16[256,1024]{1,0:T(8,128)(2,1)}, bf16[256,1024]{1,0:T(8,128)(2,1)S(1)}, u32[]{:S(2)}, u32[]{:S(2)}) collective-permute-start(bf16[256,1024]{1,0:T(8,128)(2,1)} %collective-permute-done.12), channel_id=1, source_target_pairs={{0,1},{1,0},{2,3},{3,2},{4,5},{5,4},{6,7},{7,6},{8,9},{9,8},{10,11... | collective-permute-start | bytes 1572872 | tf_op jit(solution)/shard_map/ppermute | solution.py:26
  35.2 17.1 %collective-permute-start.16 = (bf16[256,1024]{1,0:T(8,128)(2,1)}, bf16[256,1024]{1,0:T(8,128)(2,1)S(1)}, u32[]{:S(2)}, u32[]{:S(2)}) collective-permute-start(bf16[256,1024]{1,0:T(8,128)(2,1)} %collective-permute-done.12), channel_id=1, source_target_pairs={{0,4},{4,12},{12,8},{8,0},{1,5},{5,13},{13,9},{9,1},{2,6},{6,14},{... | collective-permute-start | bytes 1572872 | tf_op jit(solution)/shard_map/ppermute | solution.py:297
  41.2 13.0 %collective-permute-start.5 = (bf16[256,1024]{1,0:T(8,128)(2,1)}, bf16[256,1024]{1,0:T(8,128)(2,1)S(1)}, u32[]{:S(2)}, u32[]{:S(2)}) collective-permute-start(bf16[256,1024]{1,0:T(8,128)(2,1)} %collective-permute-done.4), channel_id=1, source_target_pairs={{0,16},{16,0},{1,17},{17,1},{2,18},{18,2},{3,19},{19,3},{4,20},{20... | collective-permute-start | bytes 1572872 | tf_op jit(solution)/shard_map/ppermute | solution.py:26
  43.1 14.5 %collective-permute-start.6 = (bf16[256,1024]{1,0:T(8,128)(2,1)}, bf16[256,1024]{1,0:T(8,128)(2,1)S(1)}, u32[]{:S(2)}, u32[]{:S(2)}) collective-permute-start(bf16[256,1024]{1,0:T(8,128)(2,1)} %collective-permute-done.4), channel_id=1, source_target_pairs={{0,1},{1,0},{2,3},{3,2},{4,5},{5,4},{6,7},{7,6},{8,9},{9,8},{10,11... | collective-permute-start | bytes 1572872 | tf_op jit(solution)/shard_map/ppermute | solution.py:26
  43.1 12.0 %collective-permute-start.15 = (bf16[256,1024]{1,0:T(8,128)(2,1)}, bf16[256,1024]{1,0:T(8,128)(2,1)S(1)}, u32[]{:S(2)}, u32[]{:S(2)}) collective-permute-start(bf16[256,1024]{1,0:T(8,128)(2,1)} %collective-permute-done.13), channel_id=1, source_target_pairs={{0,1},{1,0},{2,3},{3,2},{4,5},{5,4},{6,7},{7,6},{8,9},{9,8},{10,11... | collective-permute-start | bytes 1572872 | tf_op jit(solution)/shard_map/ppermute | solution.py:26
  46.4 17.1 %collective-permute-start.8 = (bf16[256,1024]{1,0:T(8,128)(2,1)}, bf16[256,1024]{1,0:T(8,128)(2,1)S(1)}, u32[]{:S(2)}, u32[]{:S(2)}) collective-permute-start(bf16[256,1024]{1,0:T(8,128)(2,1)} %collective-permute-done.4), channel_id=1, source_target_pairs={{0,4},{4,12},{12,8},{8,0},{1,5},{5,13},{13,9},{9,1},{2,6},{6,14},{... | collective-permute-start | bytes 1572872 | tf_op jit(solution)/shard_map/ppermute | solution.py:297
  52.3 13.1 %collective-permute-start.17 = (bf16[256,1024]{1,0:T(8,128)(2,1)S(1)}, bf16[256,1024]{1,0:T(8,128)(2,1)S(1)}, u32[]{:S(2)}, u32[]{:S(2)}) collective-permute-start(bf16[256,1024]{1,0:T(8,128)(2,1)S(1)} %collective-permute-done.16), channel_id=1, source_target_pairs={{0,16},{16,0},{1,17},{17,1},{2,18},{18,2},{3,19},{19,3},{4,20},{20... | collective-permute-start | bytes 1572872 | tf_op jit(solution)/shard_map/ppermute | solution.py:26
  54.2 19.9 %collective-permute-start.20 = (bf16[256,1024]{1,0:T(8,128)(2,1)S(1)}, bf16[256,1024]{1,0:T(8,128)(2,1)}, u32[]{:S(2)}, u32[]{:S(2)}) collective-permute-start(bf16[256,1024]{1,0:T(8,128)(2,1)S(1)} %collective-permute-done.16), channel_id=1, source_target_pairs={{0,4},{4,12},{12,8},{8,0},{1,5},{5,13},{13,9},{9,1},{2,6},{6,14},{... | collective-permute-start | bytes 1572872 | tf_op jit(solution)/shard_map/ppermute | solution.py:297
  55.1 19.0 %collective-permute-start.7 = (bf16[256,1024]{1,0:T(8,128)(2,1)S(1)}, bf16[256,1024]{1,0:T(8,128)(2,1)S(1)}, u32[]{:S(2)}, u32[]{:S(2)}) collective-permute-start(bf16[256,1024]{1,0:T(8,128)(2,1)S(1)} %collective-permute-done.5), channel_id=1, source_target_pairs={{0,1},{1,0},{2,3},{3,2},{4,5},{5,4},{6,7},{7,6},{8,9},{9,8},{10,11... | collective-permute-start | bytes 1572872 | tf_op jit(solution)/shard_map/ppermute | solution.py:26
  57.6 20.4 %collective-permute-start.18 = (bf16[256,1024]{1,0:T(8,128)(2,1)S(1)}, bf16[256,1024]{1,0:T(8,128)(2,1)S(1)}, u32[]{:S(2)}, u32[]{:S(2)}) collective-permute-start(bf16[256,1024]{1,0:T(8,128)(2,1)S(1)} %collective-permute-done.16), channel_id=1, source_target_pairs={{0,1},{1,0},{2,3},{3,2},{4,5},{5,4},{6,7},{7,6},{8,9},{9,8},{10,11... | collective-permute-start | bytes 1572872 | tf_op jit(solution)/shard_map/ppermute | solution.py:26
  63.6 14.7 %collective-permute-start.9 = (bf16[256,1024]{1,0:T(8,128)(2,1)S(1)}, bf16[256,1024]{1,0:T(8,128)(2,1)S(1)}, u32[]{:S(2)}, u32[]{:S(2)}) collective-permute-start(bf16[256,1024]{1,0:T(8,128)(2,1)S(1)} %collective-permute-done.8), channel_id=1, source_target_pairs={{0,16},{16,0},{1,17},{17,1},{2,18},{18,2},{3,19},{19,3},{4,20},{20... | collective-permute-start | bytes 1572872 | tf_op jit(solution)/shard_map/ppermute | solution.py:26
  65.4 15.7 %collective-permute-start.10 = (bf16[256,1024]{1,0:T(8,128)(2,1)S(1)}, bf16[256,1024]{1,0:T(8,128)(2,1)S(1)}, u32[]{:S(2)}, u32[]{:S(2)}) collective-permute-start(bf16[256,1024]{1,0:T(8,128)(2,1)S(1)} %collective-permute-done.8), channel_id=1, source_target_pairs={{0,1},{1,0},{2,3},{3,2},{4,5},{5,4},{6,7},{7,6},{8,9},{9,8},{10,11... | collective-permute-start | bytes 1572872 | tf_op jit(solution)/shard_map/ppermute | solution.py:26
  74.1 14.5 %collective-permute-start.21 = (bf16[256,1024]{1,0:T(8,128)(2,1)}, bf16[256,1024]{1,0:T(8,128)(2,1)S(1)}, u32[]{:S(2)}, u32[]{:S(2)}) collective-permute-start(bf16[256,1024]{1,0:T(8,128)(2,1)} %collective-permute-done.20), channel_id=1, source_target_pairs={{0,16},{16,0},{1,17},{17,1},{2,18},{18,2},{3,19},{19,3},{4,20},{20... | collective-permute-start | bytes 1572872 | tf_op jit(solution)/shard_map/ppermute | solution.py:26
  78.0 11.5 %collective-permute-start.22 = (bf16[256,1024]{1,0:T(8,128)(2,1)}, bf16[256,1024]{1,0:T(8,128)(2,1)S(1)}, u32[]{:S(2)}, u32[]{:S(2)}) collective-permute-start(bf16[256,1024]{1,0:T(8,128)(2,1)} %collective-permute-done.20), channel_id=1, source_target_pairs={{0,1},{1,0},{2,3},{3,2},{4,5},{5,4},{6,7},{7,6},{8,9},{9,8},{10,11... | collective-permute-start | bytes 1572872 | tf_op jit(solution)/shard_map/ppermute | solution.py:26
  103.9 24.9 %collective-permute-start.33 = (s32[32,4]{1,0:T(8,128)S(1)}, s32[32,4]{1,0:T(8,128)S(1)}, u32[]{:S(2)}, u32[]{:S(2)}) collective-permute-start(s32[32,4]{1,0:T(8,128)S(1)} %fusion.108), channel_id=1, source_target_pairs={{0,1},{1,0},{2,3},{3,2},{4,5},{5,4},{6,7},{7,6},{8,9},{9,8},{10,11... | collective-permute-start | bytes 1544 | tf_op jit(solution)/shard_map/ppermute | solution.py:26
  104.0 17.0 %collective-permute-start.27 = (bf16[64,2048]{1,0:T(8,128)(2,1)S(1)}, bf16[64,2048]{1,0:T(8,128)(2,1)}, u32[]{:S(2)}, u32[]{:S(2)}) collective-permute-start(bf16[64,2048]{1,0:T(8,128)(2,1)S(1)} %get-tuple-element.19.refs_0_.refs_4_), channel_id=1, source_target_pairs={{4,0},{12,4},{8,12},{0,8},{5,1},{13,5},{9,13},{1,9},{6,2},{14,6},{... | collective-permute-start | bytes 786440 | tf_op jit(solution)/shard_map/ppermute | solution.py:356
  110.7 12.2 %collective-permute-start.26 = (bf16[64,2048]{1,0:T(8,128)(2,1)S(1)}, bf16[64,2048]{1,0:T(8,128)(2,1)}, u32[]{:S(2)}, u32[]{:S(2)}) collective-permute-start(bf16[64,2048]{1,0:T(8,128)(2,1)S(1)} %collective-permute-done.25.refs_1_), channel_id=1, source_target_pairs={{0,4},{4,12},{12,8},{8,0},{1,5},{5,13},{13,9},{9,1},{2,6},{6,14},{... | collective-permute-start | bytes 786440 | tf_op jit(solution)/shard_map/ppermute | solution.py:354
  (31 other events, 148.3 us)

commit v10 on v9

--- a/solution.py
+++ b/solution.py
@@ -130,7 +130,8 @@
         tile = 256 if (high - low) % 256 == 0 else 128
         for at in range(0, high - low, tile):
             part = slice(low + at, low + at + tile)
-            normed = (state_ref[:, at : at + tile] * scale * gain_ref[:, part]).astype(jnp.bfloat16)
+            states = state_ref[:, at : at + tile].astype(jnp.float32)
+            normed = (states * scale * gain_ref[:, part]).astype(jnp.bfloat16)
             sums = dot_nn(member, normed)
             sums_ref[:, part] = sums
             pooled_ref[:, part] = (sums / counts).astype(jnp.bfloat16)
@@ -344,7 +345,7 @@
             jax.ShapeDtypeStruct((docs, cols), jnp.bfloat16),
             jax.ShapeDtypeStruct((1, token_count), jnp.float32),
         ),
-        [x[None] for x in squares] + states + [labels[None], gain[None], counts[:, None]],
+        [x[None] for x in squares] + states_b + [labels[None], gain[None], counts[:, None]],
     )
     inv_rms = inv_rms[0]
 

time: 159 us -> 155 us (0.975)
  local copies, waits for them, and re-layouts: 13.2 us -> 9.3 us
    unnamed x32 -> x26, local copies, waits for them, and re-layouts: 6.1 us -> 2.22 us
where the time goes in v10:
time: 155 us
  waiting for transfers between devices  63.5 us (41%)
  starting transfers between devices  45.8 us (30%)
  matrix products  26.4 us (17%)
  local copies, waits for them, and re-layouts  9.3 us (6%)
  Pallas kernels  4.87 us (3%)
  other arithmetic  3.73 us (2%)
    ppermute x6, waiting for transfers between devices, body(): lax.ppermute(ringed[-chunk_count] if step > 1 else moving[h], 'dp', hops)  32.9 us
    dot_general x16, matrix products, dot_nn(): jnp.dot(a, b, precision=precision, preferred_element_type=jnp.float32)  25.5 us
    ppermute x28, starting transfers between devices, swap(): return lax.ppermute(x, axis, [(0, 1), (1, 0)])  18.9 us
    ppermute x28, waiting for transfers between devices, swap(): return lax.ppermute(x, axis, [(0, 1), (1, 0)])  17.8 us
    ppermute x2, starting transfers between devices, body(): own_blocks[j] = lax.ppermute(own_blocks[j - 1], 'dp', hops)  8.97 us
    ppermute x6, starting transfers between devices, body(): lax.ppermute(ringed[-chunk_count] if step > 1 else moving[h], 'dp', hops)  8.85 us
    ppermute x3, starting transfers between devices, partner(): lax.ppermute(x, axis, [(i, i ^ flip) for i in range(lax.axis_size(axis))])  6.8 us
    ppermute x3, waiting for transfers between devices, partner(): lax.ppermute(x, axis, [(i, i ^ flip) for i in range(lax.axis_size(axis))])  6.6 us
  transfers between devices with their start and end apart: 40, of which 17 were waited for; matrix products, arithmetic and copies ran while one was open for 19% of the time, Pallas kernels for 1%

profile of v10, /device:TPU:0, one launch (start us, length us, event | category | flops | bytes accessed | tf_op | source)
XLA Modules:
  0.0 154.7 jit_solution(7138000922379927172)
XLA Ops:
  1.8 3.1 %collective-permute-start = (bf16[256,1024]{1,0:T(8,128)(2,1)S(1)}, bf16[256,1024]{1,0:T(8,128)(2,1)}, u32[]{:S(2)}, u32[]{:S(2)}) collective-permute-start(bf16[256,1024]{1,0:T(8,128)(2,1)S(1)} %constant_dynamic-slice_fusion.1), channel_id=1, source_target_pairs={{0,4},{4,12},{12,8},{8,0},{1,5},{5,13},{13,9},{9,1},{2,6},{6,14},{... | collective-permute-start | bytes 1572872 | tf_op jit(solution)/shard_map/ppermute | solution.py:298
  6.0 2.6 %collective-permute-start.12 = (bf16[256,1024]{1,0:T(8,128)(2,1)S(1)}, bf16[256,1024]{1,0:T(8,128)(2,1)}, u32[]{:S(2)}, u32[]{:S(2)}) collective-permute-start(bf16[256,1024]{1,0:T(8,128)(2,1)S(1)} %constant_dynamic-slice_fusion.2), channel_id=1, source_target_pairs={{0,4},{4,12},{12,8},{8,0},{1,5},{5,13},{13,9},{9,1},{2,6},{6,14},{... | collective-permute-start | bytes 1572872 | tf_op jit(solution)/shard_map/ppermute | solution.py:298
  8.7 3.5 %fusion.73 = bf16[512,16]{0,1:T(8,128)(2,1)S(1)} fusion(bf16[4096,16]{0,1:T(8,128)(2,1)S(1)} %copy-done, bf16[1,512,4096]{2,1,0:T(8,128)(2,1)} %param.8), kind=kOutput, calls=%fused_computation.69 | convolution fusion | flops 67117056 | bytes 4341760 | tf_op jit(solution)/shard_map/dot_general | solution.py:22
  15.7 3.0 %collective-permute-done = bf16[256,1024]{1,0:T(8,128)(2,1)} collective-permute-done((bf16[256,1024]{1,0:T(8,128)(2,1)S(1)}, bf16[256,1024]{1,0:T(8,128)(2,1)}, u32[]{:S(2)}, u32[]{:S(2)}) %collective-permute-start) | collective-permute-done | bytes 524320 | tf_op jit(solution)/shard_map/ppermute | solution.py:298
  24.5 5.5 %collective-permute-done.12 = bf16[256,1024]{1,0:T(8,128)(2,1)} collective-permute-done((bf16[256,1024]{1,0:T(8,128)(2,1)S(1)}, bf16[256,1024]{1,0:T(8,128)(2,1)}, u32[]{:S(2)}, u32[]{:S(2)}) %collective-permute-start.12) | collective-permute-done | bytes 524320 | tf_op jit(solution)/shard_map/ppermute | solution.py:298
  35.9 5.3 %collective-permute-done.4 = bf16[256,1024]{1,0:T(8,128)(2,1)} collective-permute-done((bf16[256,1024]{1,0:T(8,128)(2,1)}, bf16[256,1024]{1,0:T(8,128)(2,1)}, u32[]{:S(2)}, u32[]{:S(2)}) %collective-permute-start.4) | collective-permute-done | bytes 524320 | tf_op jit(solution)/shard_map/ppermute | solution.py:298
  43.6 2.8 %fusion.69 = f32[512,1024]{1,0:T(8,128)S(1)} fusion(f32[512,1024]{1,0:T(8,128)S(1)} %copy-done.6, bf16[256,1024]{1,0:T(8,128)(2,1)} %collective-permute-done.3, bf16[256,1024]{1,0:T(8,128)(2,1)} %collective-permute-done.2, bf16[256,1024]{1,0:T(8,128)(2,1)} %collective-permute-done.1, bf16[256,1024]{1,0:T(8,128)(2,1)} %collective-permute-done, ...), kind=kOutput, calls=%fused_computation.66 | convolution fusion | flops 1086849024 | bytes 7340032 | tf_op jit(solution)/shard_map/dot_general | solution.py:22
  47.2 5.1 %collective-permute-done.16 = bf16[256,1024]{1,0:T(8,128)(2,1)S(1)} collective-permute-done((bf16[256,1024]{1,0:T(8,128)(2,1)}, bf16[256,1024]{1,0:T(8,128)(2,1)S(1)}, u32[]{:S(2)}, u32[]{:S(2)}) %collective-permute-start.16) | collective-permute-done | bytes 524320 | tf_op jit(solution)/shard_map/ppermute | solution.py:298
  55.1 2.5 %fusion.60 = f32[512,1024]{1,0:T(8,128)S(1)} fusion(f32[512,1024]{1,0:T(8,128)S(1)} %add_add_fusion, bf16[256,1024]{1,0:T(8,128)(2,1)S(1)} %collective-permute-done.15, bf16[256,1024]{1,0:T(8,128)(2,1)S(1)} %collective-permute-done.14, bf16[256,1024]{1,0:T(8,128)(2,1)} %collective-permute-done.13, bf16[256,1024]{1,0:T(8,128)(2,1)} %collective-permute-done.12, ...), kind=kOutput, calls=%fused_computation.63 | convolution fusion | flops 1086849024 | bytes 7340032 | tf_op jit(solution)/shard_map/dot_general | solution.py:22
  58.2 5.4 %collective-permute-done.8 = bf16[256,1024]{1,0:T(8,128)(2,1)S(1)} collective-permute-done((bf16[256,1024]{1,0:T(8,128)(2,1)}, bf16[256,1024]{1,0:T(8,128)(2,1)S(1)}, u32[]{:S(2)}, u32[]{:S(2)}) %collective-permute-start.8) | collective-permute-done | bytes 524320 | tf_op jit(solution)/shard_map/ppermute | solution.py:298
  65.5 8.6 %collective-permute-done.20 = bf16[256,1024]{1,0:T(8,128)(2,1)} collective-permute-done((bf16[256,1024]{1,0:T(8,128)(2,1)S(1)}, bf16[256,1024]{1,0:T(8,128)(2,1)}, u32[]{:S(2)}, u32[]{:S(2)}) %collective-permute-start.20) | collective-permute-done | bytes 524320 | tf_op jit(solution)/shard_map/ppermute | solution.py:298
  75.6 2.3 %fusion.66 = f32[512,1024]{1,0:T(8,128)S(1)} fusion(f32[512,1024]{1,0:T(8,128)S(1)} %fusion.69, bf16[256,1024]{1,0:T(8,128)(2,1)S(1)} %collective-permute-done.7, bf16[256,1024]{1,0:T(8,128)(2,1)S(1)} %collective-permute-done.6, bf16[256,1024]{1,0:T(8,128)(2,1)S(1)} %collective-permute-done.5, bf16[256,1024]{1,0:T(8,128)(2,1)} %collective-permute-done.4, ...), kind=kOutput, calls=%fused_computation.65 | convolution fusion | flops 1086849024 | bytes 7340032 | tf_op jit(solution)/shard_map/dot_general | solution.py:22
  78.5 2.6 %fusion.57 = f32[512,1024]{1,0:T(8,128)} fusion(f32[512,1024]{1,0:T(8,128)S(1)} %fusion.60, bf16[256,1024]{1,0:T(8,128)(2,1)S(1)} %collective-permute-done.19, bf16[256,1024]{1,0:T(8,128)(2,1)S(1)} %collective-permute-done.18, bf16[256,1024]{1,0:T(8,128)(2,1)S(1)} %collective-permute-done.17, bf16[256,1024]{1,0:T(8,128)(2,1)S(1)} %collective-permute-done.16, ...), kind=kOutput, calls=%fused_computation.62 | convolution fusion | flops 1086849024 | bytes 7340032 | tf_op jit(solution)/shard_map/dot_general | solution.py:22
  81.1 2.6 %fusion.63 = f32[512,1024]{1,0:T(8,128)} fusion(f32[512,1024]{1,0:T(8,128)S(1)} %fusion.66, bf16[256,1024]{1,0:T(8,128)(2,1)S(1)} %collective-permute-done.11, bf16[256,1024]{1,0:T(8,128)(2,1)S(1)} %collective-permute-done.10, bf16[256,1024]{1,0:T(8,128)(2,1)S(1)} %collective-permute-done.9, bf16[256,1024]{1,0:T(8,128)(2,1)S(1)} %collective-permute-done.8, ...), kind=kOutput, calls=%fused_computation.64 | convolution fusion | flops 1086849024 | bytes 7340032 | tf_op jit(solution)/shard_map/dot_general | solution.py:22
  83.8 4.8 %collective-permute-done.21 = bf16[256,1024]{1,0:T(8,128)(2,1)S(1)} collective-permute-done((bf16[256,1024]{1,0:T(8,128)(2,1)}, bf16[256,1024]{1,0:T(8,128)(2,1)S(1)}, u32[]{:S(2)}, u32[]{:S(2)}) %collective-permute-start.21) | collective-permute-done | bytes 524320 | tf_op jit(solution)/shard_map/ppermute | solution.py:26
  90.5 3.0 %fusion.54 = f32[512,1024]{1,0:T(8,128)S(1)} fusion(f32[512,1024]{1,0:T(8,128)} %fusion.57, bf16[256,1024]{1,0:T(8,128)(2,1)S(1)} %collective-permute-done.23, bf16[256,1024]{1,0:T(8,128)(2,1)S(1)} %collective-permute-done.22, bf16[256,1024]{1,0:T(8,128)(2,1)S(1)} %collective-permute-done.21, bf16[256,1024]{1,0:T(8,128)(2,1)} %collective-permute-done.20, ...), kind=kOutput, calls=%fused_computation.61 | convolution fusion | flops 1086849024 | bytes 7340032 | tf_op jit(solution)/shard_map/dot_general | solution.py:22
  100.3 2.2 %collective-permute-start.27 = (bf16[64,2048]{1,0:T(8,128)(2,1)S(1)}, bf16[64,2048]{1,0:T(8,128)(2,1)}, u32[]{:S(2)}, u32[]{:S(2)}) collective-permute-start(bf16[64,2048]{1,0:T(8,128)(2,1)S(1)} %get-tuple-element.19.refs_0_.refs_4_), channel_id=1, source_target_pairs={{4,0},{12,4},{8,12},{0,8},{5,1},{13,5},{9,13},{1,9},{6,2},{14,6},{... | collective-permute-start | bytes 786440 | tf_op jit(solution)/shard_map/ppermute | solution.py:357
  102.5 4.4 %collective-permute-done.25.refs_1_ = bf16[64,2048]{1,0:T(8,128)(2,1)S(1)} collective-permute-done((bf16[64,2048]{1,0:T(8,128)(2,1)S(1)}, bf16[64,2048]{1,0:T(8,128)(2,1)S(1)}, u32[]{:S(2)}, u32[]{:S(2)}) %collective-permute-start.25) | collective-permute-done | bytes 262176 | tf_op jit(solution)/shard_map/ppermute | solution.py:355
  107.0 8.2 %collective-permute-start.26 = (bf16[64,2048]{1,0:T(8,128)(2,1)S(1)}, bf16[64,2048]{1,0:T(8,128)(2,1)}, u32[]{:S(2)}, u32[]{:S(2)}) collective-permute-start(bf16[64,2048]{1,0:T(8,128)(2,1)S(1)} %collective-permute-done.25.refs_1_), channel_id=1, source_target_pairs={{0,4},{4,12},{12,8},{8,0},{1,5},{5,13},{13,9},{9,1},{2,6},{6,14},{... | collective-permute-start | bytes 786440 | tf_op jit(solution)/shard_map/ppermute | solution.py:355
  125.1 4.1 %collective-permute-done.32.refs_1_ = f32[296,128]{1,0:T(8,128)S(1)} collective-permute-done((f32[296,128]{1,0:T(8,128)S(1)}, f32[296,128]{1,0:T(8,128)S(1)}, u32[]{:S(2)}, u32[]{:S(2)}) %collective-permute-start.32) | collective-permute-done | bytes 151584 | tf_op jit(solution)/shard_map/ppermute | solution.py:26
  132.8 2.6 %collective-permute-done.34 = f32[24,640]{1,0:T(8,128)S(1)} collective-permute-done((f32[24,640]{1,0:T(8,128)S(1)}, f32[24,640]{1,0:T(8,128)S(1)}, u32[]{:S(2)}, u32[]{:S(2)}) %collective-permute-start.34) | collective-permute-done | bytes 61472 | tf_op jit(solution)/shard_map/ppermute | solution.py:26
  138.4 3.3 %collective-permute-start.36 = (bf16[33,1024]{1,0:T(8,128)(2,1)S(1)}, bf16[33,1024]{1,0:T(8,128)(2,1)S(1)}, u32[]{:S(2)}, u32[]{:S(2)}) collective-permute-start(bf16[33,1024]{1,0:T(8,128)(2,1)S(1)} %add_convert_fusion), channel_id=1, source_target_pairs={{0,4},{4,0},{8,12},{12,8},{1,5},{5,1},{9,13},{13,9},{2,6},{6,2},{1... | collective-permute-start | bytes 202760 | tf_op jit(solution)/shard_map/ppermute | solution.py:30
  141.7 3.5 %collective-permute-start.37 = (bf16[33,1024]{1,0:T(8,128)(2,1)S(1)}, bf16[33,1024]{1,0:T(8,128)(2,1)S(1)}, u32[]{:S(2)}, u32[]{:S(2)}) collective-permute-start(bf16[33,1024]{1,0:T(8,128)(2,1)S(1)} %add_convert_fusion), channel_id=1, source_target_pairs={{0,8},{4,12},{8,0},{12,4},{1,9},{5,13},{9,1},{13,5},{2,10},{6,14},... | collective-permute-start | bytes 202760 | tf_op jit(solution)/shard_map/ppermute | solution.py:30
  145.2 6.6 %collective-permute-done.37 = bf16[33,1024]{1,0:T(8,128)(2,1)S(1)} collective-permute-done((bf16[33,1024]{1,0:T(8,128)(2,1)S(1)}, bf16[33,1024]{1,0:T(8,128)(2,1)S(1)}, u32[]{:S(2)}, u32[]{:S(2)}) %collective-permute-start.37) | collective-permute-done | bytes 67616 | tf_op jit(solution)/shard_map/ppermute | solution.py:30
  (133 shorter events, 55.9 us)
Async XLA Ops:
  1.8 16.9 %collective-permute-start = (bf16[256,1024]{1,0:T(8,128)(2,1)S(1)}, bf16[256,1024]{1,0:T(8,128)(2,1)}, u32[]{:S(2)}, u32[]{:S(2)}) collective-permute-start(bf16[256,1024]{1,0:T(8,128)(2,1)S(1)} %constant_dynamic-slice_fusion.1), channel_id=1, source_target_pairs={{0,4},{4,12},{12,8},{8,0},{1,5},{5,13},{13,9},{9,1},{2,6},{6,14},{... | collective-permute-start | bytes 1572872 | tf_op jit(solution)/shard_map/ppermute | solution.py:298
  6.0 23.9 %collective-permute-start.12 = (bf16[256,1024]{1,0:T(8,128)(2,1)S(1)}, bf16[256,1024]{1,0:T(8,128)(2,1)}, u32[]{:S(2)}, u32[]{:S(2)}) collective-permute-start(bf16[256,1024]{1,0:T(8,128)(2,1)S(1)} %constant_dynamic-slice_fusion.2), channel_id=1, source_target_pairs={{0,4},{4,12},{12,8},{8,0},{1,5},{5,13},{13,9},{9,1},{2,6},{6,14},{... | collective-permute-start | bytes 1572872 | tf_op jit(solution)/shard_map/ppermute | solution.py:298
  18.7 13.1 %collective-permute-start.1 = (bf16[256,1024]{1,0:T(8,128)(2,1)}, bf16[256,1024]{1,0:T(8,128)(2,1)}, u32[]{:S(2)}, u32[]{:S(2)}) collective-permute-start(bf16[256,1024]{1,0:T(8,128)(2,1)} %collective-permute-done), channel_id=1, source_target_pairs={{0,16},{16,0},{1,17},{17,1},{2,18},{18,2},{3,19},{19,3},{4,20},{20... | collective-permute-start | bytes 1572872 | tf_op jit(solution)/shard_map/ppermute | solution.py:26
  23.7 11.6 %collective-permute-start.2 = (bf16[256,1024]{1,0:T(8,128)(2,1)}, bf16[256,1024]{1,0:T(8,128)(2,1)}, u32[]{:S(2)}, u32[]{:S(2)}) collective-permute-start(bf16[256,1024]{1,0:T(8,128)(2,1)} %collective-permute-done), channel_id=1, source_target_pairs={{0,1},{1,0},{2,3},{3,2},{4,5},{5,4},{6,7},{7,6},{8,9},{9,8},{10,11... | collective-permute-start | bytes 1572872 | tf_op jit(solution)/shard_map/ppermute | solution.py:26
  23.8 17.4 %collective-permute-start.4 = (bf16[256,1024]{1,0:T(8,128)(2,1)}, bf16[256,1024]{1,0:T(8,128)(2,1)}, u32[]{:S(2)}, u32[]{:S(2)}) collective-permute-start(bf16[256,1024]{1,0:T(8,128)(2,1)} %collective-permute-done), channel_id=1, source_target_pairs={{0,4},{4,12},{12,8},{8,0},{1,5},{5,13},{13,9},{9,1},{2,6},{6,14},{... | collective-permute-start | bytes 1572872 | tf_op jit(solution)/shard_map/ppermute | solution.py:298
  30.0 13.1 %collective-permute-start.13 = (bf16[256,1024]{1,0:T(8,128)(2,1)}, bf16[256,1024]{1,0:T(8,128)(2,1)}, u32[]{:S(2)}, u32[]{:S(2)}) collective-permute-start(bf16[256,1024]{1,0:T(8,128)(2,1)} %collective-permute-done.12), channel_id=1, source_target_pairs={{0,16},{16,0},{1,17},{17,1},{2,18},{18,2},{3,19},{19,3},{4,20},{20... | collective-permute-start | bytes 1572872 | tf_op jit(solution)/shard_map/ppermute | solution.py:26
  31.8 11.2 %collective-permute-start.3 = (bf16[256,1024]{1,0:T(8,128)(2,1)}, bf16[256,1024]{1,0:T(8,128)(2,1)}, u32[]{:S(2)}, u32[]{:S(2)}) collective-permute-start(bf16[256,1024]{1,0:T(8,128)(2,1)} %collective-permute-done.1), channel_id=1, source_target_pairs={{0,1},{1,0},{2,3},{3,2},{4,5},{5,4},{6,7},{7,6},{8,9},{9,8},{10,11... | collective-permute-start | bytes 1572872 | tf_op jit(solution)/shard_map/ppermute | solution.py:26
  34.6 11.7 %collective-permute-start.14 = (bf16[256,1024]{1,0:T(8,128)(2,1)}, bf16[256,1024]{1,0:T(8,128)(2,1)S(1)}, u32[]{:S(2)}, u32[]{:S(2)}) collective-permute-start(bf16[256,1024]{1,0:T(8,128)(2,1)} %collective-permute-done.12), channel_id=1, source_target_pairs={{0,1},{1,0},{2,3},{3,2},{4,5},{5,4},{6,7},{7,6},{8,9},{9,8},{10,11... | collective-permute-start | bytes 1572872 | tf_op jit(solution)/shard_map/ppermute | solution.py:26
  35.2 17.1 %collective-permute-start.16 = (bf16[256,1024]{1,0:T(8,128)(2,1)}, bf16[256,1024]{1,0:T(8,128)(2,1)S(1)}, u32[]{:S(2)}, u32[]{:S(2)}) collective-permute-start(bf16[256,1024]{1,0:T(8,128)(2,1)} %collective-permute-done.12), channel_id=1, source_target_pairs={{0,4},{4,12},{12,8},{8,0},{1,5},{5,13},{13,9},{9,1},{2,6},{6,14},{... | collective-permute-start | bytes 1572872 | tf_op jit(solution)/shard_map/ppermute | solution.py:298
  41.2 13.0 %collective-permute-start.5 = (bf16[256,1024]{1,0:T(8,128)(2,1)}, bf16[256,1024]{1,0:T(8,128)(2,1)S(1)}, u32[]{:S(2)}, u32[]{:S(2)}) collective-permute-start(bf16[256,1024]{1,0:T(8,128)(2,1)} %collective-permute-done.4), channel_id=1, source_target_pairs={{0,16},{16,0},{1,17},{17,1},{2,18},{18,2},{3,19},{19,3},{4,20},{20... | collective-permute-start | bytes 1572872 | tf_op jit(solution)/shard_map/ppermute | solution.py:26
  43.1 14.5 %collective-permute-start.6 = (bf16[256,1024]{1,0:T(8,128)(2,1)}, bf16[256,1024]{1,0:T(8,128)(2,1)S(1)}, u32[]{:S(2)}, u32[]{:S(2)}) collective-permute-start(bf16[256,1024]{1,0:T(8,128)(2,1)} %collective-permute-done.4), channel_id=1, source_target_pairs={{0,1},{1,0},{2,3},{3,2},{4,5},{5,4},{6,7},{7,6},{8,9},{9,8},{10,11... | collective-permute-start | bytes 1572872 | tf_op jit(solution)/shard_map/ppermute | solution.py:26
  43.1 12.0 %collective-permute-start.15 = (bf16[256,1024]{1,0:T(8,128)(2,1)}, bf16[256,1024]{1,0:T(8,128)(2,1)S(1)}, u32[]{:S(2)}, u32[]{:S(2)}) collective-permute-start(bf16[256,1024]{1,0:T(8,128)(2,1)} %collective-permute-done.13), channel_id=1, source_target_pairs={{0,1},{1,0},{2,3},{3,2},{4,5},{5,4},{6,7},{7,6},{8,9},{9,8},{10,11... | collective-permute-start | bytes 1572872 | tf_op jit(solution)/shard_map/ppermute | solution.py:26
  46.4 17.1 %collective-permute-start.8 = (bf16[256,1024]{1,0:T(8,128)(2,1)}, bf16[256,1024]{1,0:T(8,128)(2,1)S(1)}, u32[]{:S(2)}, u32[]{:S(2)}) collective-permute-start(bf16[256,1024]{1,0:T(8,128)(2,1)} %collective-permute-done.4), channel_id=1, source_target_pairs={{0,4},{4,12},{12,8},{8,0},{1,5},{5,13},{13,9},{9,1},{2,6},{6,14},{... | collective-permute-start | bytes 1572872 | tf_op jit(solution)/shard_map/ppermute | solution.py:298
  52.3 13.1 %collective-permute-start.17 = (bf16[256,1024]{1,0:T(8,128)(2,1)S(1)}, bf16[256,1024]{1,0:T(8,128)(2,1)S(1)}, u32[]{:S(2)}, u32[]{:S(2)}) collective-permute-start(bf16[256,1024]{1,0:T(8,128)(2,1)S(1)} %collective-permute-done.16), channel_id=1, source_target_pairs={{0,16},{16,0},{1,17},{17,1},{2,18},{18,2},{3,19},{19,3},{4,20},{20... | collective-permute-start | bytes 1572872 | tf_op jit(solution)/shard_map/ppermute | solution.py:26
  54.2 19.9 %collective-permute-start.20 = (bf16[256,1024]{1,0:T(8,128)(2,1)S(1)}, bf16[256,1024]{1,0:T(8,128)(2,1)}, u32[]{:S(2)}, u32[]{:S(2)}) collective-permute-start(bf16[256,1024]{1,0:T(8,128)(2,1)S(1)} %collective-permute-done.16), channel_id=1, source_target_pairs={{0,4},{4,12},{12,8},{8,0},{1,5},{5,13},{13,9},{9,1},{2,6},{6,14},{... | collective-permute-start | bytes 1572872 | tf_op jit(solution)/shard_map/ppermute | solution.py:298
  55.1 19.0 %collective-permute-start.7 = (bf16[256,1024]{1,0:T(8,128)(2,1)S(1)}, bf16[256,1024]{1,0:T(8,128)(2,1)S(1)}, u32[]{:S(2)}, u32[]{:S(2)}) collective-permute-start(bf16[256,1024]{1,0:T(8,128)(2,1)S(1)} %collective-permute-done.5), channel_id=1, source_target_pairs={{0,1},{1,0},{2,3},{3,2},{4,5},{5,4},{6,7},{7,6},{8,9},{9,8},{10,11... | collective-permute-start | bytes 1572872 | tf_op jit(solution)/shard_map/ppermute | solution.py:26
  57.6 20.4 %collective-permute-start.18 = (bf16[256,1024]{1,0:T(8,128)(2,1)S(1)}, bf16[256,1024]{1,0:T(8,128)(2,1)S(1)}, u32[]{:S(2)}, u32[]{:S(2)}) collective-permute-start(bf16[256,1024]{1,0:T(8,128)(2,1)S(1)} %collective-permute-done.16), channel_id=1, source_target_pairs={{0,1},{1,0},{2,3},{3,2},{4,5},{5,4},{6,7},{7,6},{8,9},{9,8},{10,11... | collective-permute-start | bytes 1572872 | tf_op jit(solution)/shard_map/ppermute | solution.py:26
  63.6 14.7 %collective-permute-start.9 = (bf16[256,1024]{1,0:T(8,128)(2,1)S(1)}, bf16[256,1024]{1,0:T(8,128)(2,1)S(1)}, u32[]{:S(2)}, u32[]{:S(2)}) collective-permute-start(bf16[256,1024]{1,0:T(8,128)(2,1)S(1)} %collective-permute-done.8), channel_id=1, source_target_pairs={{0,16},{16,0},{1,17},{17,1},{2,18},{18,2},{3,19},{19,3},{4,20},{20... | collective-permute-start | bytes 1572872 | tf_op jit(solution)/shard_map/ppermute | solution.py:26
  65.4 15.7 %collective-permute-start.10 = (bf16[256,1024]{1,0:T(8,128)(2,1)S(1)}, bf16[256,1024]{1,0:T(8,128)(2,1)S(1)}, u32[]{:S(2)}, u32[]{:S(2)}) collective-permute-start(bf16[256,1024]{1,0:T(8,128)(2,1)S(1)} %collective-permute-done.8), channel_id=1, source_target_pairs={{0,1},{1,0},{2,3},{3,2},{4,5},{5,4},{6,7},{7,6},{8,9},{9,8},{10,11... | collective-permute-start | bytes 1572872 | tf_op jit(solution)/shard_map/ppermute | solution.py:26
  74.1 14.5 %collective-permute-start.21 = (bf16[256,1024]{1,0:T(8,128)(2,1)}, bf16[256,1024]{1,0:T(8,128)(2,1)S(1)}, u32[]{:S(2)}, u32[]{:S(2)}) collective-permute-start(bf16[256,1024]{1,0:T(8,128)(2,1)} %collective-permute-done.20), channel_id=1, source_target_pairs={{0,16},{16,0},{1,17},{17,1},{2,18},{18,2},{3,19},{19,3},{4,20},{20... | collective-permute-start | bytes 1572872 | tf_op jit(solution)/shard_map/ppermute | solution.py:26
  78.0 11.5 %collective-permute-start.22 = (bf16[256,1024]{1,0:T(8,128)(2,1)}, bf16[256,1024]{1,0:T(8,128)(2,1)S(1)}, u32[]{:S(2)}, u32[]{:S(2)}) collective-permute-start(bf16[256,1024]{1,0:T(8,128)(2,1)} %collective-permute-done.20), channel_id=1, source_target_pairs={{0,1},{1,0},{2,3},{3,2},{4,5},{5,4},{6,7},{7,6},{8,9},{9,8},{10,11... | collective-permute-start | bytes 1572872 | tf_op jit(solution)/shard_map/ppermute | solution.py:26
  100.2 24.9 %collective-permute-start.33 = (s32[32,4]{1,0:T(8,128)S(1)}, s32[32,4]{1,0:T(8,128)S(1)}, u32[]{:S(2)}, u32[]{:S(2)}) collective-permute-start(s32[32,4]{1,0:T(8,128)S(1)} %fusion.108), channel_id=1, source_target_pairs={{0,1},{1,0},{2,3},{3,2},{4,5},{5,4},{6,7},{7,6},{8,9},{9,8},{10,11... | collective-permute-start | bytes 1544 | tf_op jit(solution)/shard_map/ppermute | solution.py:26
  100.3 17.0 %collective-permute-start.27 = (bf16[64,2048]{1,0:T(8,128)(2,1)S(1)}, bf16[64,2048]{1,0:T(8,128)(2,1)}, u32[]{:S(2)}, u32[]{:S(2)}) collective-permute-start(bf16[64,2048]{1,0:T(8,128)(2,1)S(1)} %get-tuple-element.19.refs_0_.refs_4_), channel_id=1, source_target_pairs={{4,0},{12,4},{8,12},{0,8},{5,1},{13,5},{9,13},{1,9},{6,2},{14,6},{... | collective-permute-start | bytes 786440 | tf_op jit(solution)/shard_map/ppermute | solution.py:357
  107.0 12.2 %collective-permute-start.26 = (bf16[64,2048]{1,0:T(8,128)(2,1)S(1)}, bf16[64,2048]{1,0:T(8,128)(2,1)}, u32[]{:S(2)}, u32[]{:S(2)}) collective-permute-start(bf16[64,2048]{1,0:T(8,128)(2,1)S(1)} %collective-permute-done.25.refs_1_), channel_id=1, source_target_pairs={{0,4},{4,12},{12,8},{8,0},{1,5},{5,13},{13,9},{9,1},{2,6},{6,14},{... | collective-permute-start | bytes 786440 | tf_op jit(solution)/shard_map/ppermute | solution.py:355
  (28 other events, 141.9 us)

commit v11 on v10

--- a/solution.py
+++ b/solution.py
@@ -83,32 +83,29 @@
 
 def gram_kernel(blocks, *refs):
     own, oth = refs[:blocks], refs[blocks : 2 * blocks]
-    out_ref, sorted_ref, own_ref = refs[2 * blocks :]
+    list_ref, out_ref, sorted_ref, own_ref = refs[2 * blocks :]
     docs = own[0].shape[0]
     half = docs // 2
     anchors = blocks * half
-    for j in range(blocks):
-        own_ref[j * docs : (j + 1) * docs] = own[j][...]
-        sorted_ref[j * half : (j + 1) * half] = oth[j][:half]
-        sorted_ref[anchors + j * half : anchors + (j + 1) * half] = oth[j][half:]
-    rows = blocks * docs
-    out_ref[:rows] = dot_nt(own_ref[...], sorted_ref[:anchors])
-    out_ref[rows : rows + half] = dot_nt(own[0][:half], sorted_ref[anchors:])
-    own_f = own_ref[...].astype(jnp.float32)
-    oth_f = sorted_ref[...].astype(jnp.float32)
-    own_sq = as_row(jnp.sum(own_f * own_f, axis=1, keepdims=True))
-    oth_sq = as_row(jnp.sum(oth_f * oth_f, axis=1, keepdims=True))
-    tail = jnp.concatenate(
-        [
-            own_sq[:, :anchors],
-            own_sq[:, anchors:],
-            oth_sq[:, :anchors],
-            oth_sq[:, anchors:],
-            jnp.zeros((4, anchors), jnp.float32),
-        ],
-        axis=0,
-    )
-    out_ref[rows + half :] = tail
+    for blocks_of, ref in ((own, own_ref), (oth, sorted_ref)):
+        for j in range(blocks):
+            ref[j * half : (j + 1) * half] = blocks_of[j][:half]
+            ref[anchors + j * half : anchors + (j + 1) * half] = blocks_of[j][half:]
+    out_ref[:anchors] = dot_nt(own_ref[:anchors], sorted_ref[:anchors])
+    out_ref[anchors : anchors + half] = dot_nt(own_ref[:half], sorted_ref[anchors:])
+    pool = dot_nt(own_ref[anchors:], sorted_ref[:anchors])
+    pool_id = lax.broadcasted_iota(jnp.int32, pool.shape, 0)
+    fanout = list_ref.shape[0]
+    rows = []
+    for ref in (own_ref, sorted_ref):
+        x = ref[...].astype(jnp.float32)
+        squares = as_row(jnp.sum(x * x, axis=1, keepdims=True))
+        rows += [squares[:, :anchors], squares[:, anchors:]]
+    for h in range(fanout):
+        listed = pool_id == list_ref[h : h + 1, :]
+        rows.append(jnp.sum(jnp.where(listed, pool, 0.0), axis=0, keepdims=True))
+    rows.append(jnp.zeros((out_ref.shape[0] - anchors - half - len(rows), anchors), jnp.float32))
+    out_ref[anchors + half :] = jnp.concatenate([x for x in rows if x.shape[0]], axis=0)
 
 
 def pool_kernel(squares_count, chunks, width, *refs):
@@ -150,59 +147,71 @@
     docs = pooled_ref.shape[0]
     half = docs // 2
     anchors = blocks * half
-    rows = blocks * docs
     fanout = list_o.shape[1]
     sums = sums_refs[0][...]
     if sums_count == 2:
         sums = sums + sums_refs[1][...]
-    inner_c = sums[:rows]
-    inner_o = sums[rows : rows + half]
-    scales = lax.rsqrt(sums[rows + half :] + 1e-06)
-    own_scale = as_column(jnp.concatenate([scales[0:1], scales[1:2]], axis=1))
+    inner_a = sums[:anchors]
+    inner_o = sums[anchors : anchors + half]
+    last = sums[anchors + half :]
+    scales = lax.rsqrt(last[:4] + 1e-06)
+    own_scale = as_column(scales[0:1])
+    own_pool_scale = as_column(scales[1:2])
     oth_scale = scales[2:3]
     pool_scale = scales[3:4]
 
-    row_id = lax.broadcasted_iota(jnp.int32, (rows, anchors), 0)
-    col_id = lax.broadcasted_iota(jnp.int32, (rows, anchors), 1)
-    mask_c = (row_id % docs) < half
+    row_id = lax.broadcasted_iota(jnp.int32, (anchors, anchors), 0)
+    col_id = lax.broadcasted_iota(jnp.int32, (anchors, anchors), 1)
+    target = row_id == col_id
+    logits_a = inverse_temp * (inner_a * own_scale * oth_scale)
+    exp_a = jnp.exp(logits_a)
+    total_c = jnp.sum(exp_a, axis=0, keepdims=True)
+    listed, exp_n = [], []
     for h in range(fanout):
-        mask_c = mask_c | (row_id == list_c[h : h + 1, :])
-    target_c = row_id == (col_id // half) * docs + col_id % half
-    logits_c = inverse_temp * (inner_c * own_scale * oth_scale)
-    exp_all = jnp.exp(logits_c)
-    exp_c = jnp.where(mask_c, exp_all, 0.0)
-    total_c = jnp.sum(exp_c, axis=0, keepdims=True)
+        listed.append(row_id == list_c[h : h + 1, :])
+        scale_n = jnp.sum(jnp.where(listed[h], own_pool_scale, 0.0), axis=0, keepdims=True)
+        exp_n.append(jnp.exp(inverse_temp * (last[4 + h : 5 + h] * scale_n * oth_scale)))
+        total_c = total_c + exp_n[h]
     losses_ref[...] = jnp.log(total_c) - jnp.sum(
-        jnp.where(target_c, logits_c, 0.0), axis=0, keepdims=True
-    )
-    target_own = target_c[:docs].astype(jnp.float32)
-    grad_c = inverse_temp * (exp_c[:docs] / total_c - target_own)
+        jnp.where(target, logits_a, 0.0), axis=0, keepdims=True
+    )
+    target_own = target[:half].astype(jnp.float32)
+    grad_c = inverse_temp * (exp_a[:half] / total_c - target_own)
+    grad_p = jnp.zeros((half, anchors), jnp.float32)
+    inner_p = jnp.zeros((half, anchors), jnp.float32)
+    for h in range(fanout):
+        mine = listed[h][:half]
+        grad_p = grad_p + jnp.where(mine, inverse_temp * (exp_n[h] / total_c), 0.0)
+        inner_p = inner_p + jnp.where(mine, last[4 + h : 5 + h], 0.0)
 
     logits_o = inverse_temp * (inner_o * own_scale[:half] * pool_scale)
-    pool_id = lax.broadcasted_iota(jnp.int32, (half, anchors), 1)
+    pool_id = col_id[:half]
     mask_o = pool_id == list_o[:, 0:1]
     for h in range(1, fanout):
         mask_o = mask_o | (pool_id == list_o[:, h : h + 1])
     exp_o = jnp.where(mask_o, jnp.exp(logits_o), 0.0)
-    exp_a = exp_all[:half]
-    total_o = jnp.sum(exp_a, axis=1, keepdims=True) + jnp.sum(exp_o, axis=1, keepdims=True)
-    grad_a = inverse_temp * (exp_a / total_o - target_own[:half])
+    total_o = jnp.sum(exp_a[:half], axis=1, keepdims=True) + jnp.sum(exp_o, axis=1, keepdims=True)
+    grad_a = inverse_temp * (exp_a[:half] / total_o - target_own)
     grad_o = inverse_temp * (exp_o / total_o)
 
     zeros = jnp.zeros((docs - half, anchors), jnp.float32)
     coef = jnp.concatenate(
         [
-            (grad_c + jnp.concatenate([grad_a, zeros], axis=0)) * oth_scale,
+            jnp.concatenate([grad_c + grad_a, grad_p], axis=0) * oth_scale,
             jnp.concatenate([grad_o * pool_scale, zeros], axis=0),
         ],
         axis=1,
     ).astype(jnp.bfloat16)
     inner = jnp.concatenate(
-        [inner_c[:docs], jnp.concatenate([inner_o, zeros], axis=0)], axis=1
+        [
+            jnp.concatenate([inner_a[:half], inner_p], axis=0),
+            jnp.concatenate([inner_o, zeros], axis=0),
+        ],
+        axis=1,
     )
     doc_grad = dot_nn(coef, oth_ref[...])
     doc_grad_ref[...] = doc_grad
-    scale = own_scale[:docs]
+    scale = jnp.concatenate([own_scale[:half], own_pool_scale[:half]], axis=0)
     unit_dots = jnp.sum(coef.astype(jnp.float32) * inner, axis=1, keepdims=True) * scale
     pooled = pooled_ref[...].astype(jnp.float32)
     per_doc = (doc_grad - pooled * (scale * unit_dots)) * (scale / counts_ref[...])
@@ -265,11 +274,10 @@
 
     block_shard = shard_at((place - jnp.arange(dp, dtype=jnp.int32)) % dp)
     owner_block = (place - place_of(negative_owner[0])) % dp
-    rel_list = (owner_block * docs + per_shard + negative_pool_row[0]).reshape(dp, per_shard, -1)
-    list_c = rel_list[block_shard].reshape(anchors, -1).T
-    pool_col = owner_block * per_shard + negative_pool_row[0]
+    pool_place = owner_block * per_shard + negative_pool_row[0]
+    list_c = pool_place.reshape(dp, per_shard, -1)[block_shard].reshape(anchors, -1).T
     list_o = swap(
-        lax.dynamic_slice_in_dim(pool_col, shard * per_shard, per_shard, 0), "pair"
+        lax.dynamic_slice_in_dim(pool_place, shard * per_shard, per_shard, 0), "pair"
     )
 
     group = lax.axis_index("groups")
@@ -359,13 +367,14 @@
             )
     other_blocks = [swap(block, "pair") for block in own_blocks]
     rows = dp * docs
+    last_rows = -(-(4 + list_c.shape[0]) // 8) * 8
     sums, sorted_oth = call(
         functools.partial(gram_kernel, dp),
         (
-            jax.ShapeDtypeStruct((rows + per_shard + 8, anchors), jnp.float32),
+            jax.ShapeDtypeStruct((anchors + per_shard + last_rows, anchors), jnp.float32),
             jax.ShapeDtypeStruct((rows, cols), jnp.bfloat16),
         ),
-        own_blocks + other_blocks,
+        own_blocks + other_blocks + [list_c],
         [pltpu.VMEM((rows, cols), jnp.bfloat16)],
         vmem=16 if dp <= 4 else 48,
     )

time: 155 us -> 153 us (0.987)
  no operation moved by 1% of the time
where the time goes in v11:
time: 153 us
  waiting for transfers between devices  63.9 us (42%)
  starting transfers between devices  44.5 us (29%)
  matrix products  26.4 us (17%)
  local copies, waits for them, and re-layouts  9.3 us (6%)
  Pallas kernels  4.87 us (3%)
  other arithmetic  2.44 us (2%)
    ppermute x6, waiting for transfers between devices, body(): lax.ppermute(ringed[-chunk_count] if step > 1 else moving[h], 'dp', hops)  32.9 us
    dot_general x16, matrix products, dot_nn(): jnp.dot(a, b, precision=precision, preferred_element_type=jnp.float32)  25.5 us
    ppermute x28, starting transfers between devices, swap(): return lax.ppermute(x, axis, [(0, 1), (1, 0)])  18.9 us
    ppermute x28, waiting for transfers between devices, swap(): return lax.ppermute(x, axis, [(0, 1), (1, 0)])  17 us
    ppermute x6, starting transfers between devices, body(): lax.ppermute(ringed[-chunk_count] if step > 1 else moving[h], 'dp', hops)  8.85 us
    ppermute x2, starting transfers between devices, body(): own_blocks[j] = lax.ppermute(own_blocks[j - 1], 'dp', hops)  8.07 us
    ppermute x2, waiting for transfers between devices, body(): own_blocks[j] = lax.ppermute(own_blocks[j - 1], 'dp', hops)  7.43 us
    ppermute x3, waiting for transfers between devices, partner(): lax.ppermute(x, axis, [(i, i ^ flip) for i in range(lax.axis_size(axis))])  6.6 us
  transfers between devices with their start and end apart: 40, of which 17 were waited for; matrix products, arithmetic and copies ran while one was open for 19% of the time, Pallas kernels for 1%

profile of v11, /device:TPU:0, one launch (start us, length us, event | category | flops | bytes accessed | tf_op | source)
XLA Modules:
  0.0 152.6 jit_solution(11176585953586274653)
XLA Ops:
  1.8 3.1 %collective-permute-start = (bf16[256,1024]{1,0:T(8,128)(2,1)S(1)}, bf16[256,1024]{1,0:T(8,128)(2,1)}, u32[]{:S(2)}, u32[]{:S(2)}) collective-permute-start(bf16[256,1024]{1,0:T(8,128)(2,1)S(1)} %constant_dynamic-slice_fusion.1), channel_id=1, source_target_pairs={{0,4},{4,12},{12,8},{8,0},{1,5},{5,13},{13,9},{9,1},{2,6},{6,14},{... | collective-permute-start | bytes 1572872 | tf_op jit(solution)/shard_map/ppermute | solution.py:306
  6.0 2.6 %collective-permute-start.12 = (bf16[256,1024]{1,0:T(8,128)(2,1)S(1)}, bf16[256,1024]{1,0:T(8,128)(2,1)}, u32[]{:S(2)}, u32[]{:S(2)}) collective-permute-start(bf16[256,1024]{1,0:T(8,128)(2,1)S(1)} %constant_dynamic-slice_fusion.2), channel_id=1, source_target_pairs={{0,4},{4,12},{12,8},{8,0},{1,5},{5,13},{13,9},{9,1},{2,6},{6,14},{... | collective-permute-start | bytes 1572872 | tf_op jit(solution)/shard_map/ppermute | solution.py:306
  8.7 3.5 %fusion.73 = bf16[512,16]{0,1:T(8,128)(2,1)S(1)} fusion(bf16[4096,16]{0,1:T(8,128)(2,1)S(1)} %copy-done, bf16[1,512,4096]{2,1,0:T(8,128)(2,1)} %param.8), kind=kOutput, calls=%fused_computation.69 | convolution fusion | flops 67117056 | bytes 4341760 | tf_op jit(solution)/shard_map/dot_general | solution.py:22
  15.7 3.0 %collective-permute-done = bf16[256,1024]{1,0:T(8,128)(2,1)} collective-permute-done((bf16[256,1024]{1,0:T(8,128)(2,1)S(1)}, bf16[256,1024]{1,0:T(8,128)(2,1)}, u32[]{:S(2)}, u32[]{:S(2)}) %collective-permute-start) | collective-permute-done | bytes 524320 | tf_op jit(solution)/shard_map/ppermute | solution.py:306
  24.5 5.5 %collective-permute-done.12 = bf16[256,1024]{1,0:T(8,128)(2,1)} collective-permute-done((bf16[256,1024]{1,0:T(8,128)(2,1)S(1)}, bf16[256,1024]{1,0:T(8,128)(2,1)}, u32[]{:S(2)}, u32[]{:S(2)}) %collective-permute-start.12) | collective-permute-done | bytes 524320 | tf_op jit(solution)/shard_map/ppermute | solution.py:306
  35.9 5.3 %collective-permute-done.4 = bf16[256,1024]{1,0:T(8,128)(2,1)} collective-permute-done((bf16[256,1024]{1,0:T(8,128)(2,1)}, bf16[256,1024]{1,0:T(8,128)(2,1)}, u32[]{:S(2)}, u32[]{:S(2)}) %collective-permute-start.4) | collective-permute-done | bytes 524320 | tf_op jit(solution)/shard_map/ppermute | solution.py:306
  43.6 2.8 %fusion.69 = f32[512,1024]{1,0:T(8,128)S(1)} fusion(f32[512,1024]{1,0:T(8,128)S(1)} %copy-done.6, bf16[256,1024]{1,0:T(8,128)(2,1)} %collective-permute-done.3, bf16[256,1024]{1,0:T(8,128)(2,1)} %collective-permute-done.2, bf16[256,1024]{1,0:T(8,128)(2,1)} %collective-permute-done.1, bf16[256,1024]{1,0:T(8,128)(2,1)} %collective-permute-done, ...), kind=kOutput, calls=%fused_computation.66 | convolution fusion | flops 1086849024 | bytes 7340032 | tf_op jit(solution)/shard_map/dot_general | solution.py:22
  47.2 5.1 %collective-permute-done.16 = bf16[256,1024]{1,0:T(8,128)(2,1)S(1)} collective-permute-done((bf16[256,1024]{1,0:T(8,128)(2,1)}, bf16[256,1024]{1,0:T(8,128)(2,1)S(1)}, u32[]{:S(2)}, u32[]{:S(2)}) %collective-permute-start.16) | collective-permute-done | bytes 524320 | tf_op jit(solution)/shard_map/ppermute | solution.py:306
  55.1 2.5 %fusion.60 = f32[512,1024]{1,0:T(8,128)S(1)} fusion(f32[512,1024]{1,0:T(8,128)S(1)} %add_add_fusion, bf16[256,1024]{1,0:T(8,128)(2,1)S(1)} %collective-permute-done.15, bf16[256,1024]{1,0:T(8,128)(2,1)S(1)} %collective-permute-done.14, bf16[256,1024]{1,0:T(8,128)(2,1)} %collective-permute-done.13, bf16[256,1024]{1,0:T(8,128)(2,1)} %collective-permute-done.12, ...), kind=kOutput, calls=%fused_computation.63 | convolution fusion | flops 1086849024 | bytes 7340032 | tf_op jit(solution)/shard_map/dot_general | solution.py:22
  58.2 5.4 %collective-permute-done.8 = bf16[256,1024]{1,0:T(8,128)(2,1)S(1)} collective-permute-done((bf16[256,1024]{1,0:T(8,128)(2,1)}, bf16[256,1024]{1,0:T(8,128)(2,1)S(1)}, u32[]{:S(2)}, u32[]{:S(2)}) %collective-permute-start.8) | collective-permute-done | bytes 524320 | tf_op jit(solution)/shard_map/ppermute | solution.py:306
  65.5 8.6 %collective-permute-done.20 = bf16[256,1024]{1,0:T(8,128)(2,1)} collective-permute-done((bf16[256,1024]{1,0:T(8,128)(2,1)S(1)}, bf16[256,1024]{1,0:T(8,128)(2,1)}, u32[]{:S(2)}, u32[]{:S(2)}) %collective-permute-start.20) | collective-permute-done | bytes 524320 | tf_op jit(solution)/shard_map/ppermute | solution.py:306
  75.6 2.3 %fusion.66 = f32[512,1024]{1,0:T(8,128)S(1)} fusion(f32[512,1024]{1,0:T(8,128)S(1)} %fusion.69, bf16[256,1024]{1,0:T(8,128)(2,1)S(1)} %collective-permute-done.7, bf16[256,1024]{1,0:T(8,128)(2,1)S(1)} %collective-permute-done.6, bf16[256,1024]{1,0:T(8,128)(2,1)S(1)} %collective-permute-done.5, bf16[256,1024]{1,0:T(8,128)(2,1)} %collective-permute-done.4, ...), kind=kOutput, calls=%fused_computation.65 | convolution fusion | flops 1086849024 | bytes 7340032 | tf_op jit(solution)/shard_map/dot_general | solution.py:22
  78.5 2.6 %fusion.57 = f32[512,1024]{1,0:T(8,128)} fusion(f32[512,1024]{1,0:T(8,128)S(1)} %fusion.60, bf16[256,1024]{1,0:T(8,128)(2,1)S(1)} %collective-permute-done.19, bf16[256,1024]{1,0:T(8,128)(2,1)S(1)} %collective-permute-done.18, bf16[256,1024]{1,0:T(8,128)(2,1)S(1)} %collective-permute-done.17, bf16[256,1024]{1,0:T(8,128)(2,1)S(1)} %collective-permute-done.16, ...), kind=kOutput, calls=%fused_computation.62 | convolution fusion | flops 1086849024 | bytes 7340032 | tf_op jit(solution)/shard_map/dot_general | solution.py:22
  81.1 2.6 %fusion.63 = f32[512,1024]{1,0:T(8,128)} fusion(f32[512,1024]{1,0:T(8,128)S(1)} %fusion.66, bf16[256,1024]{1,0:T(8,128)(2,1)S(1)} %collective-permute-done.11, bf16[256,1024]{1,0:T(8,128)(2,1)S(1)} %collective-permute-done.10, bf16[256,1024]{1,0:T(8,128)(2,1)S(1)} %collective-permute-done.9, bf16[256,1024]{1,0:T(8,128)(2,1)S(1)} %collective-permute-done.8, ...), kind=kOutput, calls=%fused_computation.64 | convolution fusion | flops 1086849024 | bytes 7340032 | tf_op jit(solution)/shard_map/dot_general | solution.py:22
  83.8 4.8 %collective-permute-done.21 = bf16[256,1024]{1,0:T(8,128)(2,1)S(1)} collective-permute-done((bf16[256,1024]{1,0:T(8,128)(2,1)}, bf16[256,1024]{1,0:T(8,128)(2,1)S(1)}, u32[]{:S(2)}, u32[]{:S(2)}) %collective-permute-start.21) | collective-permute-done | bytes 524320 | tf_op jit(solution)/shard_map/ppermute | solution.py:26
  90.5 3.0 %fusion.54 = f32[512,1024]{1,0:T(8,128)S(1)} fusion(f32[512,1024]{1,0:T(8,128)} %fusion.57, bf16[256,1024]{1,0:T(8,128)(2,1)S(1)} %collective-permute-done.23, bf16[256,1024]{1,0:T(8,128)(2,1)S(1)} %collective-permute-done.22, bf16[256,1024]{1,0:T(8,128)(2,1)S(1)} %collective-permute-done.21, bf16[256,1024]{1,0:T(8,128)(2,1)} %collective-permute-done.20, ...), kind=kOutput, calls=%fused_computation.61 | convolution fusion | flops 1086849024 | bytes 7340032 | tf_op jit(solution)/shard_map/dot_general | solution.py:22
  99.6 2.2 %collective-permute-start.27 = (bf16[64,2048]{1,0:T(8,128)(2,1)S(1)}, bf16[64,2048]{1,0:T(8,128)(2,1)}, u32[]{:S(2)}, u32[]{:S(2)}) collective-permute-start(bf16[64,2048]{1,0:T(8,128)(2,1)S(1)} %get-tuple-element.19.refs_0_.refs_4_), channel_id=1, source_target_pairs={{4,0},{12,4},{8,12},{0,8},{5,1},{13,5},{9,13},{1,9},{6,2},{14,6},{... | collective-permute-start | bytes 786440 | tf_op jit(solution)/shard_map/ppermute | solution.py:365
  101.9 5.3 %collective-permute-done.25.refs_1_ = bf16[64,2048]{1,0:T(8,128)(2,1)S(1)} collective-permute-done((bf16[64,2048]{1,0:T(8,128)(2,1)S(1)}, bf16[64,2048]{1,0:T(8,128)(2,1)S(1)}, u32[]{:S(2)}, u32[]{:S(2)}) %collective-permute-start.25) | collective-permute-done | bytes 262176 | tf_op jit(solution)/shard_map/ppermute | solution.py:363
  107.2 7.3 %collective-permute-start.26 = (bf16[64,2048]{1,0:T(8,128)(2,1)S(1)}, bf16[64,2048]{1,0:T(8,128)(2,1)}, u32[]{:S(2)}, u32[]{:S(2)}) collective-permute-start(bf16[64,2048]{1,0:T(8,128)(2,1)S(1)} %collective-permute-done.25.refs_1_), channel_id=1, source_target_pairs={{0,4},{4,12},{12,8},{8,0},{1,5},{5,13},{13,9},{9,1},{2,6},{6,14},{... | collective-permute-start | bytes 786440 | tf_op jit(solution)/shard_map/ppermute | solution.py:363
  124.8 2.7 %collective-permute-done.32.refs_1_ = f32[168,128]{1,0:T(8,128)S(1)} collective-permute-done((f32[168,128]{1,0:T(8,128)S(1)}, f32[168,128]{1,0:T(8,128)S(1)}, u32[]{:S(2)}, u32[]{:S(2)}) %collective-permute-start.32) | collective-permute-done | bytes 86048 | tf_op jit(solution)/shard_map/ppermute | solution.py:26
  131.1 2.6 %collective-permute-done.34 = f32[24,640]{1,0:T(8,128)S(1)} collective-permute-done((f32[24,640]{1,0:T(8,128)S(1)}, f32[24,640]{1,0:T(8,128)S(1)}, u32[]{:S(2)}, u32[]{:S(2)}) %collective-permute-start.34) | collective-permute-done | bytes 61472 | tf_op jit(solution)/shard_map/ppermute | solution.py:26
  136.7 3.0 %collective-permute-start.36 = (bf16[33,1024]{1,0:T(8,128)(2,1)S(1)}, bf16[33,1024]{1,0:T(8,128)(2,1)S(1)}, u32[]{:S(2)}, u32[]{:S(2)}) collective-permute-start(bf16[33,1024]{1,0:T(8,128)(2,1)S(1)} %add_convert_fusion), channel_id=1, source_target_pairs={{0,4},{4,0},{8,12},{12,8},{1,5},{5,1},{9,13},{13,9},{2,6},{6,2},{1... | collective-permute-start | bytes 202760 | tf_op jit(solution)/shard_map/ppermute | solution.py:30
  139.7 3.5 %collective-permute-start.37 = (bf16[33,1024]{1,0:T(8,128)(2,1)S(1)}, bf16[33,1024]{1,0:T(8,128)(2,1)S(1)}, u32[]{:S(2)}, u32[]{:S(2)}) collective-permute-start(bf16[33,1024]{1,0:T(8,128)(2,1)S(1)} %add_convert_fusion), channel_id=1, source_target_pairs={{0,8},{4,12},{8,0},{12,4},{1,9},{5,13},{9,1},{13,5},{2,10},{6,14},... | collective-permute-start | bytes 202760 | tf_op jit(solution)/shard_map/ppermute | solution.py:30
  143.1 6.6 %collective-permute-done.37 = bf16[33,1024]{1,0:T(8,128)(2,1)S(1)} collective-permute-done((bf16[33,1024]{1,0:T(8,128)(2,1)S(1)}, bf16[33,1024]{1,0:T(8,128)(2,1)S(1)}, u32[]{:S(2)}, u32[]{:S(2)}) %collective-permute-start.37) | collective-permute-done | bytes 67616 | tf_op jit(solution)/shard_map/ppermute | solution.py:30
  (133 shorter events, 55.5 us)
Async XLA Ops:
  1.8 16.9 %collective-permute-start = (bf16[256,1024]{1,0:T(8,128)(2,1)S(1)}, bf16[256,1024]{1,0:T(8,128)(2,1)}, u32[]{:S(2)}, u32[]{:S(2)}) collective-permute-start(bf16[256,1024]{1,0:T(8,128)(2,1)S(1)} %constant_dynamic-slice_fusion.1), channel_id=1, source_target_pairs={{0,4},{4,12},{12,8},{8,0},{1,5},{5,13},{13,9},{9,1},{2,6},{6,14},{... | collective-permute-start | bytes 1572872 | tf_op jit(solution)/shard_map/ppermute | solution.py:306
  6.0 23.9 %collective-permute-start.12 = (bf16[256,1024]{1,0:T(8,128)(2,1)S(1)}, bf16[256,1024]{1,0:T(8,128)(2,1)}, u32[]{:S(2)}, u32[]{:S(2)}) collective-permute-start(bf16[256,1024]{1,0:T(8,128)(2,1)S(1)} %constant_dynamic-slice_fusion.2), channel_id=1, source_target_pairs={{0,4},{4,12},{12,8},{8,0},{1,5},{5,13},{13,9},{9,1},{2,6},{6,14},{... | collective-permute-start | bytes 1572872 | tf_op jit(solution)/shard_map/ppermute | solution.py:306
  18.7 13.1 %collective-permute-start.1 = (bf16[256,1024]{1,0:T(8,128)(2,1)}, bf16[256,1024]{1,0:T(8,128)(2,1)}, u32[]{:S(2)}, u32[]{:S(2)}) collective-permute-start(bf16[256,1024]{1,0:T(8,128)(2,1)} %collective-permute-done), channel_id=1, source_target_pairs={{0,16},{16,0},{1,17},{17,1},{2,18},{18,2},{3,19},{19,3},{4,20},{20... | collective-permute-start | bytes 1572872 | tf_op jit(solution)/shard_map/ppermute | solution.py:26
  23.7 11.6 %collective-permute-start.2 = (bf16[256,1024]{1,0:T(8,128)(2,1)}, bf16[256,1024]{1,0:T(8,128)(2,1)}, u32[]{:S(2)}, u32[]{:S(2)}) collective-permute-start(bf16[256,1024]{1,0:T(8,128)(2,1)} %collective-permute-done), channel_id=1, source_target_pairs={{0,1},{1,0},{2,3},{3,2},{4,5},{5,4},{6,7},{7,6},{8,9},{9,8},{10,11... | collective-permute-start | bytes 1572872 | tf_op jit(solution)/shard_map/ppermute | solution.py:26
  23.8 17.4 %collective-permute-start.4 = (bf16[256,1024]{1,0:T(8,128)(2,1)}, bf16[256,1024]{1,0:T(8,128)(2,1)}, u32[]{:S(2)}, u32[]{:S(2)}) collective-permute-start(bf16[256,1024]{1,0:T(8,128)(2,1)} %collective-permute-done), channel_id=1, source_target_pairs={{0,4},{4,12},{12,8},{8,0},{1,5},{5,13},{13,9},{9,1},{2,6},{6,14},{... | collective-permute-start | bytes 1572872 | tf_op jit(solution)/shard_map/ppermute | solution.py:306
  30.0 13.1 %collective-permute-start.13 = (bf16[256,1024]{1,0:T(8,128)(2,1)}, bf16[256,1024]{1,0:T(8,128)(2,1)}, u32[]{:S(2)}, u32[]{:S(2)}) collective-permute-start(bf16[256,1024]{1,0:T(8,128)(2,1)} %collective-permute-done.12), channel_id=1, source_target_pairs={{0,16},{16,0},{1,17},{17,1},{2,18},{18,2},{3,19},{19,3},{4,20},{20... | collective-permute-start | bytes 1572872 | tf_op jit(solution)/shard_map/ppermute | solution.py:26
  31.8 11.2 %collective-permute-start.3 = (bf16[256,1024]{1,0:T(8,128)(2,1)}, bf16[256,1024]{1,0:T(8,128)(2,1)}, u32[]{:S(2)}, u32[]{:S(2)}) collective-permute-start(bf16[256,1024]{1,0:T(8,128)(2,1)} %collective-permute-done.1), channel_id=1, source_target_pairs={{0,1},{1,0},{2,3},{3,2},{4,5},{5,4},{6,7},{7,6},{8,9},{9,8},{10,11... | collective-permute-start | bytes 1572872 | tf_op jit(solution)/shard_map/ppermute | solution.py:26
  34.6 11.8 %collective-permute-start.14 = (bf16[256,1024]{1,0:T(8,128)(2,1)}, bf16[256,1024]{1,0:T(8,128)(2,1)S(1)}, u32[]{:S(2)}, u32[]{:S(2)}) collective-permute-start(bf16[256,1024]{1,0:T(8,128)(2,1)} %collective-permute-done.12), channel_id=1, source_target_pairs={{0,1},{1,0},{2,3},{3,2},{4,5},{5,4},{6,7},{7,6},{8,9},{9,8},{10,11... | collective-permute-start | bytes 1572872 | tf_op jit(solution)/shard_map/ppermute | solution.py:26
  35.2 17.1 %collective-permute-start.16 = (bf16[256,1024]{1,0:T(8,128)(2,1)}, bf16[256,1024]{1,0:T(8,128)(2,1)S(1)}, u32[]{:S(2)}, u32[]{:S(2)}) collective-permute-start(bf16[256,1024]{1,0:T(8,128)(2,1)} %collective-permute-done.12), channel_id=1, source_target_pairs={{0,4},{4,12},{12,8},{8,0},{1,5},{5,13},{13,9},{9,1},{2,6},{6,14},{... | collective-permute-start | bytes 1572872 | tf_op jit(solution)/shard_map/ppermute | solution.py:306
  41.2 13.0 %collective-permute-start.5 = (bf16[256,1024]{1,0:T(8,128)(2,1)}, bf16[256,1024]{1,0:T(8,128)(2,1)S(1)}, u32[]{:S(2)}, u32[]{:S(2)}) collective-permute-start(bf16[256,1024]{1,0:T(8,128)(2,1)} %collective-permute-done.4), channel_id=1, source_target_pairs={{0,16},{16,0},{1,17},{17,1},{2,18},{18,2},{3,19},{19,3},{4,20},{20... | collective-permute-start | bytes 1572872 | tf_op jit(solution)/shard_map/ppermute | solution.py:26
  43.1 14.5 %collective-permute-start.6 = (bf16[256,1024]{1,0:T(8,128)(2,1)}, bf16[256,1024]{1,0:T(8,128)(2,1)S(1)}, u32[]{:S(2)}, u32[]{:S(2)}) collective-permute-start(bf16[256,1024]{1,0:T(8,128)(2,1)} %collective-permute-done.4), channel_id=1, source_target_pairs={{0,1},{1,0},{2,3},{3,2},{4,5},{5,4},{6,7},{7,6},{8,9},{9,8},{10,11... | collective-permute-start | bytes 1572872 | tf_op jit(solution)/shard_map/ppermute | solution.py:26
  43.1 12.0 %collective-permute-start.15 = (bf16[256,1024]{1,0:T(8,128)(2,1)}, bf16[256,1024]{1,0:T(8,128)(2,1)S(1)}, u32[]{:S(2)}, u32[]{:S(2)}) collective-permute-start(bf16[256,1024]{1,0:T(8,128)(2,1)} %collective-permute-done.13), channel_id=1, source_target_pairs={{0,1},{1,0},{2,3},{3,2},{4,5},{5,4},{6,7},{7,6},{8,9},{9,8},{10,11... | collective-permute-start | bytes 1572872 | tf_op jit(solution)/shard_map/ppermute | solution.py:26
  46.4 17.1 %collective-permute-start.8 = (bf16[256,1024]{1,0:T(8,128)(2,1)}, bf16[256,1024]{1,0:T(8,128)(2,1)S(1)}, u32[]{:S(2)}, u32[]{:S(2)}) collective-permute-start(bf16[256,1024]{1,0:T(8,128)(2,1)} %collective-permute-done.4), channel_id=1, source_target_pairs={{0,4},{4,12},{12,8},{8,0},{1,5},{5,13},{13,9},{9,1},{2,6},{6,14},{... | collective-permute-start | bytes 1572872 | tf_op jit(solution)/shard_map/ppermute | solution.py:306
  52.3 13.1 %collective-permute-start.17 = (bf16[256,1024]{1,0:T(8,128)(2,1)S(1)}, bf16[256,1024]{1,0:T(8,128)(2,1)S(1)}, u32[]{:S(2)}, u32[]{:S(2)}) collective-permute-start(bf16[256,1024]{1,0:T(8,128)(2,1)S(1)} %collective-permute-done.16), channel_id=1, source_target_pairs={{0,16},{16,0},{1,17},{17,1},{2,18},{18,2},{3,19},{19,3},{4,20},{20... | collective-permute-start | bytes 1572872 | tf_op jit(solution)/shard_map/ppermute | solution.py:26
  54.2 19.9 %collective-permute-start.20 = (bf16[256,1024]{1,0:T(8,128)(2,1)S(1)}, bf16[256,1024]{1,0:T(8,128)(2,1)}, u32[]{:S(2)}, u32[]{:S(2)}) collective-permute-start(bf16[256,1024]{1,0:T(8,128)(2,1)S(1)} %collective-permute-done.16), channel_id=1, source_target_pairs={{0,4},{4,12},{12,8},{8,0},{1,5},{5,13},{13,9},{9,1},{2,6},{6,14},{... | collective-permute-start | bytes 1572872 | tf_op jit(solution)/shard_map/ppermute | solution.py:306
  55.1 19.0 %collective-permute-start.7 = (bf16[256,1024]{1,0:T(8,128)(2,1)S(1)}, bf16[256,1024]{1,0:T(8,128)(2,1)S(1)}, u32[]{:S(2)}, u32[]{:S(2)}) collective-permute-start(bf16[256,1024]{1,0:T(8,128)(2,1)S(1)} %collective-permute-done.5), channel_id=1, source_target_pairs={{0,1},{1,0},{2,3},{3,2},{4,5},{5,4},{6,7},{7,6},{8,9},{9,8},{10,11... | collective-permute-start | bytes 1572872 | tf_op jit(solution)/shard_map/ppermute | solution.py:26
  57.6 20.4 %collective-permute-start.18 = (bf16[256,1024]{1,0:T(8,128)(2,1)S(1)}, bf16[256,1024]{1,0:T(8,128)(2,1)S(1)}, u32[]{:S(2)}, u32[]{:S(2)}) collective-permute-start(bf16[256,1024]{1,0:T(8,128)(2,1)S(1)} %collective-permute-done.16), channel_id=1, source_target_pairs={{0,1},{1,0},{2,3},{3,2},{4,5},{5,4},{6,7},{7,6},{8,9},{9,8},{10,11... | collective-permute-start | bytes 1572872 | tf_op jit(solution)/shard_map/ppermute | solution.py:26
  63.6 14.7 %collective-permute-start.9 = (bf16[256,1024]{1,0:T(8,128)(2,1)S(1)}, bf16[256,1024]{1,0:T(8,128)(2,1)S(1)}, u32[]{:S(2)}, u32[]{:S(2)}) collective-permute-start(bf16[256,1024]{1,0:T(8,128)(2,1)S(1)} %collective-permute-done.8), channel_id=1, source_target_pairs={{0,16},{16,0},{1,17},{17,1},{2,18},{18,2},{3,19},{19,3},{4,20},{20... | collective-permute-start | bytes 1572872 | tf_op jit(solution)/shard_map/ppermute | solution.py:26
  65.4 15.7 %collective-permute-start.10 = (bf16[256,1024]{1,0:T(8,128)(2,1)S(1)}, bf16[256,1024]{1,0:T(8,128)(2,1)S(1)}, u32[]{:S(2)}, u32[]{:S(2)}) collective-permute-start(bf16[256,1024]{1,0:T(8,128)(2,1)S(1)} %collective-permute-done.8), channel_id=1, source_target_pairs={{0,1},{1,0},{2,3},{3,2},{4,5},{5,4},{6,7},{7,6},{8,9},{9,8},{10,11... | collective-permute-start | bytes 1572872 | tf_op jit(solution)/shard_map/ppermute | solution.py:26
  74.1 14.5 %collective-permute-start.21 = (bf16[256,1024]{1,0:T(8,128)(2,1)}, bf16[256,1024]{1,0:T(8,128)(2,1)S(1)}, u32[]{:S(2)}, u32[]{:S(2)}) collective-permute-start(bf16[256,1024]{1,0:T(8,128)(2,1)} %collective-permute-done.20), channel_id=1, source_target_pairs={{0,16},{16,0},{1,17},{17,1},{2,18},{18,2},{3,19},{19,3},{4,20},{20... | collective-permute-start | bytes 1572872 | tf_op jit(solution)/shard_map/ppermute | solution.py:26
  78.0 10.9 %collective-permute-start.22 = (bf16[256,1024]{1,0:T(8,128)(2,1)}, bf16[256,1024]{1,0:T(8,128)(2,1)S(1)}, u32[]{:S(2)}, u32[]{:S(2)}) collective-permute-start(bf16[256,1024]{1,0:T(8,128)(2,1)} %collective-permute-done.20), channel_id=1, source_target_pairs={{0,1},{1,0},{2,3},{3,2},{4,5},{5,4},{6,7},{7,6},{8,9},{9,8},{10,11... | collective-permute-start | bytes 1572872 | tf_op jit(solution)/shard_map/ppermute | solution.py:26
  99.5 25.3 %collective-permute-start.33 = (s32[32,4]{1,0:T(8,128)S(1)}, s32[32,4]{1,0:T(8,128)S(1)}, u32[]{:S(2)}, u32[]{:S(2)}) collective-permute-start(s32[32,4]{1,0:T(8,128)S(1)} %fusion.108), channel_id=1, source_target_pairs={{0,1},{1,0},{2,3},{3,2},{4,5},{5,4},{6,7},{7,6},{8,9},{9,8},{10,11... | collective-permute-start | bytes 1544 | tf_op jit(solution)/shard_map/ppermute | solution.py:26
  99.6 17.1 %collective-permute-start.27 = (bf16[64,2048]{1,0:T(8,128)(2,1)S(1)}, bf16[64,2048]{1,0:T(8,128)(2,1)}, u32[]{:S(2)}, u32[]{:S(2)}) collective-permute-start(bf16[64,2048]{1,0:T(8,128)(2,1)S(1)} %get-tuple-element.19.refs_0_.refs_4_), channel_id=1, source_target_pairs={{4,0},{12,4},{8,12},{0,8},{5,1},{13,5},{9,13},{1,9},{6,2},{14,6},{... | collective-permute-start | bytes 786440 | tf_op jit(solution)/shard_map/ppermute | solution.py:365
  107.2 11.6 %collective-permute-start.26 = (bf16[64,2048]{1,0:T(8,128)(2,1)S(1)}, bf16[64,2048]{1,0:T(8,128)(2,1)}, u32[]{:S(2)}, u32[]{:S(2)}) collective-permute-start(bf16[64,2048]{1,0:T(8,128)(2,1)S(1)} %collective-permute-done.25.refs_1_), channel_id=1, source_target_pairs={{0,4},{4,12},{12,8},{8,0},{1,5},{5,13},{13,9},{9,1},{2,6},{6,14},{... | collective-permute-start | bytes 786440 | tf_op jit(solution)/shard_map/ppermute | solution.py:363
  (28 other events, 142.0 us)

commit v12 on v11

--- a/solution.py
+++ b/solution.py
@@ -106,6 +106,23 @@
         rows.append(jnp.sum(jnp.where(listed, pool, 0.0), axis=0, keepdims=True))
     rows.append(jnp.zeros((out_ref.shape[0] - anchors - half - len(rows), anchors), jnp.float32))
     out_ref[anchors + half :] = jnp.concatenate([x for x in rows if x.shape[0]], axis=0)
+
+
+def finish_kernel(acc_ref, tokens_ref, *refs):
+    rows, (states_ref, squares_ref) = refs[:-2], refs[-2:]
+    width = acc_ref.shape[1]
+    tile = 256 if width % 256 == 0 else 128
+    tokens = tokens_ref[...]
+    lanes = jnp.zeros((acc_ref.shape[0], 128), jnp.float32)
+    for low in range(0, width, tile):
+        part = slice(low, low + tile)
+        block = jnp.concatenate([row[:, part] for row in rows], axis=0)
+        x = acc_ref[:, part] + dot_nn(tokens, block)
+        states_ref[:, part] = x.astype(jnp.bfloat16)
+        for at in range(0, tile, 128):
+            y = x[:, at : at + 128]
+            lanes = lanes + y * y
+    squares_ref[...] = dot_nt(jnp.ones((8, 128), jnp.float32), lanes, highest)[:1]
 
 
 def pool_kernel(squares_count, chunks, width, *refs):
@@ -328,14 +345,25 @@
             lhs = step_tokens
             late = across
             if step == dp - 1 and h == chunk_count - 1:
-                late = after(across, *states)
+                late = after(across, *states[:h])
             rows = [moved, across, swap(moved, "pair"), swap(late, "pair")]
-            states[h] = lax.optimization_barrier(
-                states[h] + dot_nn(lhs, jnp.concatenate(rows, axis=0))
-            )
+            if event < len(ringed) - 1:
+                product = dot_nn(lhs, jnp.concatenate(rows, axis=0))
+                states[h] = lax.optimization_barrier(states[h] + product)
+            else:
+                last_states, last_squares = call(
+                    finish_kernel,
+                    (
+                        jax.ShapeDtypeStruct((token_count, high - low), jnp.bfloat16),
+                        jax.ShapeDtypeStruct((1, token_count), jnp.float32),
+                    ),
+                    [states[h], lhs, *rows],
+                    flops=1<<24,
+                )
             event += 1
-    states_b = [x.astype(jnp.bfloat16) for x in states]
-    squares = sum(jnp.sum(x * x, axis=1) for x in states)
+    states = states[:-1]
+    states_b = [x.astype(jnp.bfloat16) for x in states] + [last_states]
+    squares = sum(jnp.sum(x * x, axis=1) for x in states)[None] + last_squares
 
     gain = norm_gain_vector.astype(jnp.float32)
     labels = document_labels[0, 0]
@@ -353,7 +381,7 @@
             jax.ShapeDtypeStruct((docs, cols), jnp.bfloat16),
             jax.ShapeDtypeStruct((1, token_count), jnp.float32),
         ),
-        [x[None] for x in squares] + states_b + [labels[None], gain[None], counts[:, None]],
+        squares + states_b + [labels[None], gain[None], counts[:, None]],
     )
     inv_rms = inv_rms[0]
 

time: 153 us -> 154 us (level)
  Pallas kernels: 4.87 us -> 6.44 us
    ppermute x28, waiting for transfers between devices: 17 us -> 22.7 us  [swap(): return lax.ppermute(x, axis, [(0, 1), (1, 0)])]
    ppermute x6, waiting for transfers between devices: 32.9 us -> 29.5 us  [body(): lax.ppermute(ringed[-chunk_count] if step > 1 else moving[h], 'dp', hops)]
    ppermute x28, starting transfers between devices: 18.9 us -> 16.6 us  [swap(): return lax.ppermute(x, axis, [(0, 1), (1, 0)])]
    dynamic_slice x1, local copies, waits for them, and re-layouts: 0.25 us -> 1.89 us  [body(): lax.dynamic_slice_in_dim(tokens, lax.axis_index('mp') * cols, cols, 1)]
    pallas_call x3 -> x4, Pallas kernels: 4.87 us -> 6.44 us  [call(): pl.pallas_call(kernel, out_shape=outs, scratch_shapes=list(scratch), comp...]
    unnamed x26 -> x28, local copies, waits for them, and re-layouts: 2.22 us -> 0.65 us
    dot_general x16 -> x15, matrix products: 25.5 us -> 24.9 us  [dot_nn(): jnp.dot(a, b, precision=precision, preferred_element_type=jnp.float32)]
  transfers between devices with their start and end apart: 40 -> 40, of which waited for: 17 -> 21; matrix products, arithmetic and copies ran while one was open for 19% -> 22% of each run, Pallas kernels for 1% -> 1%
where the time goes in v12:
time: 154 us
  waiting for transfers between devices  64.7 us (42%)
  starting transfers between devices  43.4 us (28%)
  matrix products  25.8 us (17%)
  local copies, waits for them, and re-layouts  9.25 us (6%)
  Pallas kernels  6.44 us (4%)
  other arithmetic  2.86 us (2%)
    ppermute x6, waiting for transfers between devices, body(): lax.ppermute(ringed[-chunk_count] if step > 1 else moving[h], 'dp', hops)  29.5 us
    dot_general x15, matrix products, dot_nn(): jnp.dot(a, b, precision=precision, preferred_element_type=jnp.float32)  24.9 us
    ppermute x28, waiting for transfers between devices, swap(): return lax.ppermute(x, axis, [(0, 1), (1, 0)])  22.7 us
    ppermute x28, starting transfers between devices, swap(): return lax.ppermute(x, axis, [(0, 1), (1, 0)])  16.6 us
    ppermute x6, starting transfers between devices, body(): lax.ppermute(ringed[-chunk_count] if step > 1 else moving[h], 'dp', hops)  9.35 us
    ppermute x2, starting transfers between devices, body(): own_blocks[j] = lax.ppermute(own_blocks[j - 1], 'dp', hops)  8.63 us
    ppermute x2, waiting for transfers between devices, body(): own_blocks[j] = lax.ppermute(own_blocks[j - 1], 'dp', hops)  6.8 us
    ppermute x3, starting transfers between devices, partner(): lax.ppermute(x, axis, [(i, i ^ flip) for i in range(lax.axis_size(axis))])  6.59 us
  transfers between devices with their start and end apart: 40, of which 21 were waited for; matrix products, arithmetic and copies ran while one was open for 22% of the time, Pallas kernels for 1%

profile of v12, /device:TPU:0, one launch (start us, length us, event | category | flops | bytes accessed | tf_op | source)
XLA Modules:
  0.0 153.5 jit_solution(12595304167811217835)
XLA Ops:
  1.8 3.1 %collective-permute-start = (bf16[256,1024]{1,0:T(8,128)(2,1)S(1)}, bf16[256,1024]{1,0:T(8,128)(2,1)}, u32[]{:S(2)}, u32[]{:S(2)}) collective-permute-start(bf16[256,1024]{1,0:T(8,128)(2,1)S(1)} %constant_dynamic-slice_fusion.1), channel_id=1, source_target_pairs={{0,4},{4,12},{12,8},{8,0},{1,5},{5,13},{13,9},{9,1},{2,6},{6,14},{... | collective-permute-start | bytes 1572872 | tf_op jit(solution)/shard_map/ppermute | solution.py:323
  6.0 2.6 %collective-permute-start.12 = (bf16[256,1024]{1,0:T(8,128)(2,1)S(1)}, bf16[256,1024]{1,0:T(8,128)(2,1)}, u32[]{:S(2)}, u32[]{:S(2)}) collective-permute-start(bf16[256,1024]{1,0:T(8,128)(2,1)S(1)} %constant_dynamic-slice_fusion.2), channel_id=1, source_target_pairs={{0,4},{4,12},{12,8},{8,0},{1,5},{5,13},{13,9},{9,1},{2,6},{6,14},{... | collective-permute-start | bytes 1572872 | tf_op jit(solution)/shard_map/ppermute | solution.py:323
  8.7 4.7 %fusion.44 = f32[512,1024]{1,0:T(8,128)} fusion(bf16[1024,2048]{1,0:T(8,128)(2,1)} %param.10, bf16[1,512,4096]{2,1,0:T(8,128)(2,1)} %param.8, s32[]{:T(128)S(6)} %select_n.210), kind=kOutput, calls=%fused_computation.49 | convolution fusion | flops 1073741824 | bytes 5242884 | tf_op jit(solution)/shard_map/dot_general | solution.py:22
  20.6 3.9 %fusion.42 = f32[512,1024]{1,0:T(8,128)} fusion(bf16[1024,2048]{1,0:T(8,128)(2,1)S(1)} %copy-done.9, bf16[1,512,4096]{2,1,0:T(8,128)(2,1)} %param.8, s32[]{:T(128)S(6)} %select_n.210), kind=kOutput, calls=%fused_computation.45 | convolution fusion | flops 1073741824 | bytes 5242884 | tf_op jit(solution)/shard_map/dot_general | solution.py:22
  24.5 3.4 %add_add_fusion = f32[512,1024]{1,0:T(8,128)} fusion(f32[512,1024]{1,0:T(8,128)} %fusion.42, bf16[512,16]{0,1:T(8,128)(2,1)S(1)} %fusion.62, bf16[512,2048]{1,0:T(8,128)(2,1)S(1)} %dynamic-slice_bitcast_fusion, bf16[16,2048]{1,0:T(8,128)(2,1)S(1)} %copy-done.1), kind=kOutput, calls=%fused_computation.44 | convolution fusion | flops 18350080 | bytes 5292032 | tf_op jit(solution)/shard_map/dot_general | solution.py:22
  32.0 2.1 %dynamic-slice_bitcast_fusion.4 = (bf16[512,256]{1,0:T(8,128)(2,1)S(1)}, bf16[512,256]{1,0:T(8,128)(2,1)S(1)}, bf16[512,256]{1,0:T(8,128)(2,1)S(1)}, bf16[512,25...) fusion(bf16[1,512,4096]{2,1,0:T(8,128)(2,1)} %param.8, ...), kind=kLoop, calls=%fused_computation.75 | loop fusion | bytes 6291504 | tf_op jit(solution)/shard_map/dynamic_slice | solution.py:329
  35.9 8.2 %collective-permute-done.4 = bf16[256,1024]{1,0:T(8,128)(2,1)S(1)} collective-permute-done((bf16[256,1024]{1,0:T(8,128)(2,1)}, bf16[256,1024]{1,0:T(8,128)(2,1)S(1)}, u32[]{:S(2)}, u32[]{:S(2)}) %collective-permute-start.4) | collective-permute-done | bytes 524320 | tf_op jit(solution)/shard_map/ppermute | solution.py:323
  46.6 2.4 %fusion.58 = f32[512,1024]{1,0:T(8,128)S(1)} fusion(f32[512,1024]{1,0:T(8,128)S(1)} %copy-done.6, bf16[256,1024]{1,0:T(8,128)(2,1)S(1)} %collective-permute-done.3, bf16[256,1024]{1,0:T(8,128)(2,1)S(1)} %collective-permute-done.2, bf16[256,1024]{1,0:T(8,128)(2,1)S(1)} %collective-permute-done.1, bf16[256,1024]{1,0:T(8,128)(2,1)} %collective-permute-done, ...), kind=kOutput, calls=%fused_computation.56 | convolution fusion | flops 1086849024 | bytes 7340032 | tf_op jit(solution)/shard_map/dot_general | solution.py:22
  49.6 5.7 %collective-permute-done.16 = bf16[256,1024]{1,0:T(8,128)(2,1)S(1)} collective-permute-done((bf16[256,1024]{1,0:T(8,128)(2,1)}, bf16[256,1024]{1,0:T(8,128)(2,1)S(1)}, u32[]{:S(2)}, u32[]{:S(2)}) %collective-permute-start.16) | collective-permute-done | bytes 524320 | tf_op jit(solution)/shard_map/ppermute | solution.py:323
  58.0 8.5 %collective-permute-done.8 = bf16[256,1024]{1,0:T(8,128)(2,1)S(1)} collective-permute-done((bf16[256,1024]{1,0:T(8,128)(2,1)S(1)}, bf16[256,1024]{1,0:T(8,128)(2,1)S(1)}, u32[]{:S(2)}, u32[]{:S(2)}) %collective-permute-start.8) | collective-permute-done | bytes 524320 | tf_op jit(solution)/shard_map/ppermute | solution.py:323
  67.9 2.3 %fusion.49 = f32[512,1024]{1,0:T(8,128)S(1)} fusion(f32[512,1024]{1,0:T(8,128)S(1)} %copy-done.7, bf16[256,1024]{1,0:T(8,128)(2,1)S(1)} %collective-permute-done.15, bf16[256,1024]{1,0:T(8,128)(2,1)S(1)} %collective-permute-done.14, bf16[256,1024]{1,0:T(8,128)(2,1)S(1)} %collective-permute-done.13, bf16[256,1024]{1,0:T(8,128)(2,1)} %collective-permute-done.12, ...), kind=kOutput, calls=%fused_computation.53 | convolution fusion | flops 1086849024 | bytes 7340032 | tf_op jit(solution)/shard_map/dot_general | solution.py:22
  70.5 6.8 %collective-permute-done.20.refs_0_ = bf16[256,1024]{1,0:T(8,128)(2,1)S(1)} collective-permute-done((bf16[256,1024]{1,0:T(8,128)(2,1)S(1)}, bf16[256,1024]{1,0:T(8,128)(2,1)S(1)}, u32[]{:S(2)}, u32[]{:S(2)}) %collective-permute-start.20) | collective-permute-done | bytes 524320 | tf_op jit(solution)/shard_map/ppermute | solution.py:323
  78.7 2.5 %collective-permute-done.9 = bf16[256,1024]{1,0:T(8,128)(2,1)S(1)} collective-permute-done((bf16[256,1024]{1,0:T(8,128)(2,1)S(1)}, bf16[256,1024]{1,0:T(8,128)(2,1)S(1)}, u32[]{:S(2)}, u32[]{:S(2)}) %collective-permute-start.9) | collective-permute-done | bytes 524320 | tf_op jit(solution)/shard_map/ppermute | solution.py:26
  84.5 7.6 %collective-permute-done.21.refs_1_ = bf16[256,1024]{1,0:T(8,128)(2,1)S(1)} collective-permute-done((bf16[256,1024]{1,0:T(8,128)(2,1)S(1)}, bf16[256,1024]{1,0:T(8,128)(2,1)S(1)}, u32[]{:S(2)}, u32[]{:S(2)}) %collective-permute-start.21) | collective-permute-done | bytes 524320 | tf_op jit(solution)/shard_map/ppermute | solution.py:26
  101.5 2.1 %collective-permute-start.27 = (bf16[64,2048]{1,0:T(8,128)(2,1)S(1)}, bf16[64,2048]{1,0:T(8,128)(2,1)}, u32[]{:S(2)}, u32[]{:S(2)}) collective-permute-start(bf16[64,2048]{1,0:T(8,128)(2,1)S(1)} %get-tuple-element.23.refs_0_.refs_4_), channel_id=1, source_target_pairs={{4,0},{12,4},{8,12},{0,8},{5,1},{13,5},{9,13},{1,9},{6,2},{14,6},{... | collective-permute-start | bytes 786440 | tf_op jit(solution)/shard_map/ppermute | solution.py:393
  103.6 4.7 %collective-permute-done.25.refs_1_ = bf16[64,2048]{1,0:T(8,128)(2,1)S(1)} collective-permute-done((bf16[64,2048]{1,0:T(8,128)(2,1)S(1)}, bf16[64,2048]{1,0:T(8,128)(2,1)S(1)}, u32[]{:S(2)}, u32[]{:S(2)}) %collective-permute-start.25) | collective-permute-done | bytes 262176 | tf_op jit(solution)/shard_map/ppermute | solution.py:391
  108.4 7.8 %collective-permute-start.26 = (bf16[64,2048]{1,0:T(8,128)(2,1)S(1)}, bf16[64,2048]{1,0:T(8,128)(2,1)}, u32[]{:S(2)}, u32[]{:S(2)}) collective-permute-start(bf16[64,2048]{1,0:T(8,128)(2,1)S(1)} %collective-permute-done.25.refs_1_), channel_id=1, source_target_pairs={{0,4},{4,12},{12,8},{8,0},{1,5},{5,13},{13,9},{9,1},{2,6},{6,14},{... | collective-permute-start | bytes 786440 | tf_op jit(solution)/shard_map/ppermute | solution.py:391
  118.4 2.1 %collective-permute-done.26.refs_2_ = bf16[64,2048]{1,0:T(8,128)(2,1)} collective-permute-done((bf16[64,2048]{1,0:T(8,128)(2,1)S(1)}, bf16[64,2048]{1,0:T(8,128)(2,1)}, u32[]{:S(2)}, u32[]{:S(2)}) %collective-permute-start.26) | collective-permute-done | bytes 262176 | tf_op jit(solution)/shard_map/ppermute | solution.py:391
  122.4 2.1 %shard_map.121 = (f32[168,128]{1,0:T(8,128)S(1)}, bf16[256,2048]{1,0:T(8,128)(2,1)S(1)}) custom-call(bf16[64,2048]{1,0:T(8,128)(2,1)S(1)} %get-tuple-element.23.refs_0_.refs_4_, bf16[64,2048]{1,0:T(8,128)(2,1)S(1)} %collective-permute-done.25.refs_1_, bf16[64,2048]{1,0:T(8,128)(2,1)} %collective-permute-done.26.refs_2_, ...), custom_call_target="tpu_custom_call" | custom-call | flops 16777216 | bytes 2099200 | tf_op jit(solution)/shard_map/pallas_call | solution.py:59
  126.4 2.7 %collective-permute-done.32.refs_1_ = f32[168,128]{1,0:T(8,128)S(1)} collective-permute-done((f32[168,128]{1,0:T(8,128)S(1)}, f32[168,128]{1,0:T(8,128)S(1)}, u32[]{:S(2)}, u32[]{:S(2)}) %collective-permute-start.32) | collective-permute-done | bytes 86048 | tf_op jit(solution)/shard_map/ppermute | solution.py:26
  132.7 2.6 %collective-permute-done.34 = f32[24,640]{1,0:T(8,128)S(1)} collective-permute-done((f32[24,640]{1,0:T(8,128)S(1)}, f32[24,640]{1,0:T(8,128)S(1)}, u32[]{:S(2)}, u32[]{:S(2)}) %collective-permute-start.34) | collective-permute-done | bytes 61472 | tf_op jit(solution)/shard_map/ppermute | solution.py:26
  138.3 5.9 %collective-permute-start.38 = (bf16[33,1024]{1,0:T(8,128)(2,1)S(1)}, bf16[33,1024]{1,0:T(8,128)(2,1)S(1)}, u32[]{:S(2)}, u32[]{:S(2)}) collective-permute-start(bf16[33,1024]{1,0:T(8,128)(2,1)S(1)} %add_convert_fusion), channel_id=1, source_target_pairs={{0,12},{4,8},{8,4},{12,0},{1,13},{5,9},{9,5},{13,1},{2,14},{6,10},... | collective-permute-start | bytes 202760 | tf_op jit(solution)/shard_map/ppermute | solution.py:30
  144.9 2.6 %collective-permute-done.38 = bf16[33,1024]{1,0:T(8,128)(2,1)S(1)} collective-permute-done((bf16[33,1024]{1,0:T(8,128)(2,1)S(1)}, bf16[33,1024]{1,0:T(8,128)(2,1)S(1)}, u32[]{:S(2)}, u32[]{:S(2)}) %collective-permute-start.38) | collective-permute-done | bytes 67616 | tf_op jit(solution)/shard_map/ppermute | solution.py:30
  147.5 3.1 %collective-permute-done.37 = bf16[33,1024]{1,0:T(8,128)(2,1)S(1)} collective-permute-done((bf16[33,1024]{1,0:T(8,128)(2,1)S(1)}, bf16[33,1024]{1,0:T(8,128)(2,1)S(1)}, u32[]{:S(2)}, u32[]{:S(2)}) %collective-permute-start.37) | collective-permute-done | bytes 67616 | tf_op jit(solution)/shard_map/ppermute | solution.py:30
  (136 shorter events, 52.9 us)
Async XLA Ops:
  1.8 16.9 %collective-permute-start = (bf16[256,1024]{1,0:T(8,128)(2,1)S(1)}, bf16[256,1024]{1,0:T(8,128)(2,1)}, u32[]{:S(2)}, u32[]{:S(2)}) collective-permute-start(bf16[256,1024]{1,0:T(8,128)(2,1)S(1)} %constant_dynamic-slice_fusion.1), channel_id=1, source_target_pairs={{0,4},{4,12},{12,8},{8,0},{1,5},{5,13},{13,9},{9,1},{2,6},{6,14},{... | collective-permute-start | bytes 1572872 | tf_op jit(solution)/shard_map/ppermute | solution.py:323
  6.0 23.1 %collective-permute-start.12 = (bf16[256,1024]{1,0:T(8,128)(2,1)S(1)}, bf16[256,1024]{1,0:T(8,128)(2,1)}, u32[]{:S(2)}, u32[]{:S(2)}) collective-permute-start(bf16[256,1024]{1,0:T(8,128)(2,1)S(1)} %constant_dynamic-slice_fusion.2), channel_id=1, source_target_pairs={{0,4},{4,12},{12,8},{8,0},{1,5},{5,13},{13,9},{9,1},{2,6},{6,14},{... | collective-permute-start | bytes 1572872 | tf_op jit(solution)/shard_map/ppermute | solution.py:323
  18.7 13.3 %collective-permute-start.1 = (bf16[256,1024]{1,0:T(8,128)(2,1)}, bf16[256,1024]{1,0:T(8,128)(2,1)S(1)}, u32[]{:S(2)}, u32[]{:S(2)}) collective-permute-start(bf16[256,1024]{1,0:T(8,128)(2,1)} %collective-permute-done), channel_id=1, source_target_pairs={{0,16},{16,0},{1,17},{17,1},{2,18},{18,2},{3,19},{19,3},{4,20},{20... | collective-permute-start | bytes 1572872 | tf_op jit(solution)/shard_map/ppermute | solution.py:26
  28.2 15.9 %collective-permute-start.4 = (bf16[256,1024]{1,0:T(8,128)(2,1)}, bf16[256,1024]{1,0:T(8,128)(2,1)S(1)}, u32[]{:S(2)}, u32[]{:S(2)}) collective-permute-start(bf16[256,1024]{1,0:T(8,128)(2,1)} %collective-permute-done), channel_id=1, source_target_pairs={{0,4},{4,12},{12,8},{8,0},{1,5},{5,13},{13,9},{9,1},{2,6},{6,14},{... | collective-permute-start | bytes 1572872 | tf_op jit(solution)/shard_map/ppermute | solution.py:323
  29.1 16.3 %collective-permute-start.13 = (bf16[256,1024]{1,0:T(8,128)(2,1)}, bf16[256,1024]{1,0:T(8,128)(2,1)S(1)}, u32[]{:S(2)}, u32[]{:S(2)}) collective-permute-start(bf16[256,1024]{1,0:T(8,128)(2,1)} %collective-permute-done.12), channel_id=1, source_target_pairs={{0,16},{16,0},{1,17},{17,1},{2,18},{18,2},{3,19},{19,3},{4,20},{20... | collective-permute-start | bytes 1572872 | tf_op jit(solution)/shard_map/ppermute | solution.py:26
  32.0 14.6 %collective-permute-start.3 = (bf16[256,1024]{1,0:T(8,128)(2,1)S(1)}, bf16[256,1024]{1,0:T(8,128)(2,1)S(1)}, u32[]{:S(2)}, u32[]{:S(2)}) collective-permute-start(bf16[256,1024]{1,0:T(8,128)(2,1)S(1)} %collective-permute-done.1), channel_id=1, source_target_pairs={{0,1},{1,0},{2,3},{3,2},{4,5},{5,4},{6,7},{7,6},{8,9},{9,8},{10,11... | collective-permute-start | bytes 1572872 | tf_op jit(solution)/shard_map/ppermute | solution.py:26
  34.4 14.7 %collective-permute-start.14 = (bf16[256,1024]{1,0:T(8,128)(2,1)}, bf16[256,1024]{1,0:T(8,128)(2,1)S(1)}, u32[]{:S(2)}, u32[]{:S(2)}) collective-permute-start(bf16[256,1024]{1,0:T(8,128)(2,1)} %collective-permute-done.12), channel_id=1, source_target_pairs={{0,1},{1,0},{2,3},{3,2},{4,5},{5,4},{6,7},{7,6},{8,9},{9,8},{10,11... | collective-permute-start | bytes 1572872 | tf_op jit(solution)/shard_map/ppermute | solution.py:26
  35.0 20.3 %collective-permute-start.16 = (bf16[256,1024]{1,0:T(8,128)(2,1)}, bf16[256,1024]{1,0:T(8,128)(2,1)S(1)}, u32[]{:S(2)}, u32[]{:S(2)}) collective-permute-start(bf16[256,1024]{1,0:T(8,128)(2,1)} %collective-permute-done.12), channel_id=1, source_target_pairs={{0,4},{4,12},{12,8},{8,0},{1,5},{5,13},{13,9},{9,1},{2,6},{6,14},{... | collective-permute-start | bytes 1572872 | tf_op jit(solution)/shard_map/ppermute | solution.py:323
  44.0 13.0 %collective-permute-start.5 = (bf16[256,1024]{1,0:T(8,128)(2,1)S(1)}, bf16[256,1024]{1,0:T(8,128)(2,1)S(1)}, u32[]{:S(2)}, u32[]{:S(2)}) collective-permute-start(bf16[256,1024]{1,0:T(8,128)(2,1)S(1)} %collective-permute-done.4), channel_id=1, source_target_pairs={{0,16},{16,0},{1,17},{17,1},{2,18},{18,2},{3,19},{19,3},{4,20},{20... | collective-permute-start | bytes 1572872 | tf_op jit(solution)/shard_map/ppermute | solution.py:26
  45.4 21.1 %collective-permute-start.8 = (bf16[256,1024]{1,0:T(8,128)(2,1)S(1)}, bf16[256,1024]{1,0:T(8,128)(2,1)S(1)}, u32[]{:S(2)}, u32[]{:S(2)}) collective-permute-start(bf16[256,1024]{1,0:T(8,128)(2,1)S(1)} %collective-permute-done.4), channel_id=1, source_target_pairs={{0,4},{4,12},{12,8},{8,0},{1,5},{5,13},{13,9},{9,1},{2,6},{6,14},{... | collective-permute-start | bytes 1572872 | tf_op jit(solution)/shard_map/ppermute | solution.py:323
  46.6 19.9 %collective-permute-start.15 = (bf16[256,1024]{1,0:T(8,128)(2,1)S(1)}, bf16[256,1024]{1,0:T(8,128)(2,1)S(1)}, u32[]{:S(2)}, u32[]{:S(2)}) collective-permute-start(bf16[256,1024]{1,0:T(8,128)(2,1)S(1)} %collective-permute-done.13), channel_id=1, source_target_pairs={{0,1},{1,0},{2,3},{3,2},{4,5},{5,4},{6,7},{7,6},{8,9},{9,8},{10,11... | collective-permute-start | bytes 1572872 | tf_op jit(solution)/shard_map/ppermute | solution.py:26
  49.1 21.2 %collective-permute-start.6 = (bf16[256,1024]{1,0:T(8,128)(2,1)S(1)}, bf16[256,1024]{1,0:T(8,128)(2,1)S(1)}, u32[]{:S(2)}, u32[]{:S(2)}) collective-permute-start(bf16[256,1024]{1,0:T(8,128)(2,1)S(1)} %collective-permute-done.4), channel_id=1, source_target_pairs={{0,1},{1,0},{2,3},{3,2},{4,5},{5,4},{6,7},{7,6},{8,9},{9,8},{10,11... | collective-permute-start | bytes 1572872 | tf_op jit(solution)/shard_map/ppermute | solution.py:26
  55.3 27.2 %collective-permute-start.17 = (bf16[256,1024]{1,0:T(8,128)(2,1)S(1)}, bf16[256,1024]{1,0:T(8,128)(2,1)S(1)}, u32[]{:S(2)}, u32[]{:S(2)}) collective-permute-start(bf16[256,1024]{1,0:T(8,128)(2,1)S(1)} %collective-permute-done.16), channel_id=1, source_target_pairs={{0,16},{16,0},{1,17},{17,1},{2,18},{18,2},{3,19},{19,3},{4,20},{20... | collective-permute-start | bytes 1572872 | tf_op jit(solution)/shard_map/ppermute | solution.py:26
  57.1 20.2 %collective-permute-start.20 = (bf16[256,1024]{1,0:T(8,128)(2,1)S(1)}, bf16[256,1024]{1,0:T(8,128)(2,1)S(1)}, u32[]{:S(2)}, u32[]{:S(2)}) collective-permute-start(bf16[256,1024]{1,0:T(8,128)(2,1)S(1)} %collective-permute-done.16), channel_id=1, source_target_pairs={{0,4},{4,12},{12,8},{8,0},{1,5},{5,13},{13,9},{9,1},{2,6},{6,14},{... | collective-permute-start | bytes 1572872 | tf_op jit(solution)/shard_map/ppermute | solution.py:323
  66.5 10.8 %collective-permute-start.7 = (bf16[256,1024]{1,0:T(8,128)(2,1)S(1)}, bf16[256,1024]{1,0:T(8,128)(2,1)S(1)}, u32[]{:S(2)}, u32[]{:S(2)}) collective-permute-start(bf16[256,1024]{1,0:T(8,128)(2,1)S(1)} %collective-permute-done.5), channel_id=1, source_target_pairs={{0,1},{1,0},{2,3},{3,2},{4,5},{5,4},{6,7},{7,6},{8,9},{9,8},{10,11... | collective-permute-start | bytes 1572872 | tf_op jit(solution)/shard_map/ppermute | solution.py:26
  66.5 14.7 %collective-permute-start.9 = (bf16[256,1024]{1,0:T(8,128)(2,1)S(1)}, bf16[256,1024]{1,0:T(8,128)(2,1)S(1)}, u32[]{:S(2)}, u32[]{:S(2)}) collective-permute-start(bf16[256,1024]{1,0:T(8,128)(2,1)S(1)} %collective-permute-done.8), channel_id=1, source_target_pairs={{0,16},{16,0},{1,17},{17,1},{2,18},{18,2},{3,19},{19,3},{4,20},{20... | collective-permute-start | bytes 1572872 | tf_op jit(solution)/shard_map/ppermute | solution.py:26
  70.2 21.9 %collective-permute-start.18 = (bf16[256,1024]{1,0:T(8,128)(2,1)S(1)}, bf16[256,1024]{1,0:T(8,128)(2,1)S(1)}, u32[]{:S(2)}, u32[]{:S(2)}) collective-permute-start(bf16[256,1024]{1,0:T(8,128)(2,1)S(1)} %collective-permute-done.16), channel_id=1, source_target_pairs={{0,1},{1,0},{2,3},{3,2},{4,5},{5,4},{6,7},{7,6},{8,9},{9,8},{10,11... | collective-permute-start | bytes 1572872 | tf_op jit(solution)/shard_map/ppermute | solution.py:26
  77.3 14.8 %collective-permute-start.21 = (bf16[256,1024]{1,0:T(8,128)(2,1)S(1)}, bf16[256,1024]{1,0:T(8,128)(2,1)S(1)}, u32[]{:S(2)}, u32[]{:S(2)}) collective-permute-start(bf16[256,1024]{1,0:T(8,128)(2,1)S(1)} %collective-permute-done.20.refs_0_), channel_id=1, source_target_pairs={{0,16},{16,0},{1,17},{17,1},{2,18},{18,2},{3,19},{19,3},{4,20},{20... | collective-permute-start | bytes 1572872 | tf_op jit(solution)/shard_map/ppermute | solution.py:26
  82.5 11.2 %collective-permute-start.22 = (bf16[256,1024]{1,0:T(8,128)(2,1)S(1)}, bf16[256,1024]{1,0:T(8,128)(2,1)S(1)}, u32[]{:S(2)}, u32[]{:S(2)}) collective-permute-start(bf16[256,1024]{1,0:T(8,128)(2,1)S(1)} %collective-permute-done.20.refs_0_), channel_id=1, source_target_pairs={{0,1},{1,0},{2,3},{3,2},{4,5},{5,4},{6,7},{7,6},{8,9},{9,8},{10,11... | collective-permute-start | bytes 1572872 | tf_op jit(solution)/shard_map/ppermute | solution.py:26
  83.1 9.0 %collective-permute-start.19 = (bf16[256,1024]{1,0:T(8,128)(2,1)S(1)}, bf16[256,1024]{1,0:T(8,128)(2,1)S(1)}, u32[]{:S(2)}, u32[]{:S(2)}) collective-permute-start(bf16[256,1024]{1,0:T(8,128)(2,1)S(1)} %collective-permute-done.17), channel_id=1, source_target_pairs={{0,1},{1,0},{2,3},{3,2},{4,5},{5,4},{6,7},{7,6},{8,9},{9,8},{10,11... | collective-permute-start | bytes 1572872 | tf_op jit(solution)/shard_map/ppermute | solution.py:26
  101.5 24.9 %collective-permute-start.33 = (s32[32,4]{1,0:T(8,128)}, s32[32,4]{1,0:T(8,128)S(1)}, u32[]{:S(2)}, u32[]{:S(2)}) collective-permute-start(s32[32,4]{1,0:T(8,128)} %fusion.97), channel_id=1, source_target_pairs={{0,1},{1,0},{2,3},{3,2},{4,5},{5,4},{6,7},{7,6},{8,9},{9,8},{10,11... | collective-permute-start | bytes 1544 | tf_op jit(solution)/shard_map/ppermute | solution.py:26
  101.5 16.9 %collective-permute-start.27 = (bf16[64,2048]{1,0:T(8,128)(2,1)S(1)}, bf16[64,2048]{1,0:T(8,128)(2,1)}, u32[]{:S(2)}, u32[]{:S(2)}) collective-permute-start(bf16[64,2048]{1,0:T(8,128)(2,1)S(1)} %get-tuple-element.23.refs_0_.refs_4_), channel_id=1, source_target_pairs={{4,0},{12,4},{8,12},{0,8},{5,1},{13,5},{9,13},{1,9},{6,2},{14,6},{... | collective-permute-start | bytes 786440 | tf_op jit(solution)/shard_map/ppermute | solution.py:393
  108.4 12.1 %collective-permute-start.26 = (bf16[64,2048]{1,0:T(8,128)(2,1)S(1)}, bf16[64,2048]{1,0:T(8,128)(2,1)}, u32[]{:S(2)}, u32[]{:S(2)}) collective-permute-start(bf16[64,2048]{1,0:T(8,128)(2,1)S(1)} %collective-permute-done.25.refs_1_), channel_id=1, source_target_pairs={{0,4},{4,12},{12,8},{8,0},{1,5},{5,13},{13,9},{9,1},{2,6},{6,14},{... | collective-permute-start | bytes 786440 | tf_op jit(solution)/shard_map/ppermute | solution.py:391
  138.3 9.2 %collective-permute-start.38 = (bf16[33,1024]{1,0:T(8,128)(2,1)S(1)}, bf16[33,1024]{1,0:T(8,128)(2,1)S(1)}, u32[]{:S(2)}, u32[]{:S(2)}) collective-permute-start(bf16[33,1024]{1,0:T(8,128)(2,1)S(1)} %add_convert_fusion), channel_id=1, source_target_pairs={{0,12},{4,8},{8,4},{12,0},{1,13},{5,9},{9,5},{13,1},{2,14},{6,10},... | collective-permute-start | bytes 202760 | tf_op jit(solution)/shard_map/ppermute | solution.py:30
  (29 other events, 151.5 us)

commit v13 on v12

--- a/solution.py
+++ b/solution.py
@@ -54,12 +54,16 @@
     return lax.optimization_barrier((x, *deps))[0]
 
 
-def call(kernel, outs, args, scratch=(), flops=1 << 24, vmem=16):
+def call(kernel, outs, args, scratch=(), flops=1 << 24, vmem=16, scalar=None):
     size = sum(a.size * a.dtype.itemsize for a in args)
     return pl.pallas_call(
         kernel,
         out_shape=outs,
         scratch_shapes=list(scratch),
+        in_specs=[
+            pl.BlockSpec(memory_space=pltpu.SMEM if i == scalar else pltpu.VMEM)
+            for i in range(len(args))
+        ],
         compiler_params=pltpu.CompilerParams(vmem_limit_bytes=vmem << 20),
         cost_estimate=pl.CostEstimate(flops=flops, bytes_accessed=size, transcendentals=0),
     )(*args)
@@ -252,6 +256,52 @@
     small_ref[:rank, :tokens] = up_states_ref[...]
     small_ref[:rank, tokens : tokens + docs] = up_gained
     small_ref[rank : rank + 1, :tokens] = tok_dots
+
+
+def grads_kernel(small_count, chunks, rank, width, *refs):
+    small = refs[0][...]
+    for ref in refs[1:small_count]:
+        small = small + ref[...]
+    side_ref, inv_rms_ref, mid_ref, labels_ref, own_cols_ref, gained_ref, gain_grad_ref = refs[
+        small_count : small_count + 7
+    ]
+    state_refs = refs[small_count + 7 : small_count + 7 + chunks]
+    kept_ref, sent_ref, grads_ref = refs[small_count + 7 + chunks :]
+    tokens = inv_rms_ref.shape[1]
+    docs = gained_ref.shape[0]
+    doc_id = lax.broadcasted_iota(jnp.int32, (docs, tokens), 0)
+    member = jnp.where(doc_id == labels_ref[...], 1.0, 0.0)
+    inv_rms = inv_rms_ref[...]
+    alpha = inv_rms * inv_rms * inv_rms * small[rank : rank + 1, :tokens] / width
+    up_states = small[:rank, :tokens]
+    up_gained = small[:rank, tokens : tokens + docs]
+    mid_grad = (inv_rms * dot_nn(up_gained, member, highest) - alpha * up_states).astype(
+        jnp.bfloat16
+    )
+    mid = mid_ref[...]
+    mid_alpha = (mid * alpha).astype(jnp.bfloat16)
+    mid_docs = dot_nt(mid * inv_rms, member, highest)
+    grads_ref[:rank] = dot_nn(mid_grad, own_cols_ref[...])
+    from_docs = dot_nn(mid_docs, gained_ref[...], highest)
+    for (low, high), state_ref in zip(spans(own_cols_ref.shape[1]), state_refs):
+        grads_ref[rank : 2 * rank, low:high] = from_docs[:, low:high] - dot_nn(
+            mid_alpha, state_ref[...]
+        )
+    grads_ref[2 * rank :] = jnp.concatenate(
+        [gain_grad_ref[...], jnp.zeros((7, own_cols_ref.shape[1]), jnp.float32)], axis=0
+    )
+    half = kept_ref.shape[1]
+    side = side_ref[0]
+
+    @pl.when(side == 0)
+    def _():
+        kept_ref[...] = grads_ref[:, :half]
+        sent_ref[...] = grads_ref[:, half:]
+
+    @pl.when(side != 0)
+    def _():
+        kept_ref[...] = grads_ref[:, half:]
+        sent_ref[...] = grads_ref[:, :half]
 
 
 def body(
@@ -335,6 +385,8 @@
             moved = ringed[event]
             if step == 1:
                 own_first, mid_first = own_tokens, lora_mid
+                if h > 0:
+                    own_first = after(own_first, ringed[0])
                 states[h] = (
                     own_cols[:, low:high].astype(jnp.float32)
                     + dot_nn(own_first, frozen_weight[:, low:high])
@@ -383,7 +435,6 @@
         ),
         squares + states_b + [labels[None], gain[None], counts[:, None]],
     )
-    inv_rms = inv_rms[0]
 
     own_blocks = [pooled] * dp
     for j in range(1, dp):
@@ -438,24 +489,28 @@
         vmem=16 if dp <= 4 else 48,
     )
     losses = losses[:, :per_shard]
-    small = sum_over(small, "mp")
-    alpha = inv_rms * inv_rms * inv_rms * small[rank, :token_count] / width
-    up_states = small[:rank, :token_count]
-    up_gained = small[:rank, token_count : token_count + docs]
-    mid_grad = (
-        inv_rms * dot_nn(up_gained, member_f, highest) - alpha * up_states
-    ).astype(jnp.bfloat16)
-    mid_t = lora_mid.astype(jnp.float32).T
-    a_grad = dot_nn(mid_grad, own_cols)
-    mid_alpha = (mid_t * alpha).astype(jnp.bfloat16)
-    b_grad = dot_nn(dot_nt(mid_t * inv_rms, member_f, highest), gained, highest) - jnp.concatenate(
-        [dot_nn(mid_alpha, x) for x in states_b], axis=1
-    )
-
-    grads = jnp.concatenate([a_grad, b_grad, gain_grad], axis=0)
+    if lax.axis_size("mp") == 2:
+        small = [small, swap(small, "mp")]
+    else:
+        small = [lax.psum(small, "mp")]
     half = cols // 2
-    kept = lax.dynamic_slice_in_dim(grads, side * half, half, 1)
-    sent = lax.dynamic_slice_in_dim(grads, (1 - side) * half, half, 1)
+    kept, sent = call(
+        functools.partial(grads_kernel, len(small), chunk_count, rank, width),
+        (jax.ShapeDtypeStruct((2 * rank + 8, half), jnp.float32),) * 2,
+        small
+        + [
+            side[None],
+            inv_rms,
+            lora_mid.astype(jnp.float32).T,
+            labels[None],
+            own_cols,
+            gained,
+            gain_grad,
+        ]
+        + states_b,
+        [pltpu.VMEM((2 * rank + 8, cols), jnp.float32)],
+        scalar=len(small),
+    )
     kept = kept + swap(sent, "pair")
     kept = kept.astype(jnp.bfloat16)
     level = [kept] + [partner(kept, "dp", j) for j in range(1, dp)]

time: 154 us -> 151 us (0.981)
  matrix products: 25.8 us -> 19.1 us
  waiting for transfers between devices: 64.7 us -> 71.1 us
  starting transfers between devices: 43.4 us -> 40.4 us
    ppermute x28, waiting for transfers between devices: 22.7 us -> 33.3 us  [swap(): return lax.ppermute(x, axis, [(0, 1), (1, 0)])]
    dot_general x15 -> x10, matrix products: 24.9 us -> 18.3 us  [dot_nn(): jnp.dot(a, b, precision=precision, preferred_element_type=jnp.float32)]
    ppermute x6, waiting for transfers between devices: 29.5 us -> 24.4 us  [body(): lax.ppermute(ringed[-chunk_count] if step > 1 else moving[h], 'dp', hops)]
    ppermute x2, starting transfers between devices: 8.63 us -> 6.37 us  [body(): own_blocks[j] = lax.ppermute(own_blocks[j - 1], 'dp', hops)]
    ppermute x6, starting transfers between devices: 9.35 us -> 7.59 us  [body(): lax.ppermute(ringed[-chunk_count] if step > 1 else moving[h], 'dp', hops)]
    dynamic_slice x1, local copies, waits for them, and re-layouts: 2.11 us -> 0.41 us  [body(): lax.dynamic_slice_in_dim(tokens, origin * shard_rows + q * quarter, quart...]
    pallas_call x4 -> x5, Pallas kernels: 6.44 us -> 7.62 us  [call(): pl.pallas_call(kernel, out_shape=outs, scratch_shapes=list(scratch), in_s...]
  transfers between devices with their start and end apart: 40 -> 40, of which waited for: 21 -> 21; matrix products, arithmetic and copies ran while one was open for 22% -> 18% of each run, Pallas kernels for 1% -> 1%
where the time goes in v13:
time: 151 us; the launch traced here: 150 us
  waiting for transfers between devices  71.1 us (47%)
  starting transfers between devices  40.4 us (27%)
  matrix products  19.1 us (13%)
  local copies, waits for them, and re-layouts  8.34 us (6%)
  Pallas kernels  7.62 us (5%)
  other arithmetic  2.81 us (2%)
    ppermute x28, waiting for transfers between devices, swap(): return lax.ppermute(x, axis, [(0, 1), (1, 0)])  33.3 us
    ppermute x6, waiting for transfers between devices, body(): lax.ppermute(ringed[-chunk_count] if step > 1 else moving[h], 'dp', hops)  24.4 us
    dot_general x10, matrix products, dot_nn(): jnp.dot(a, b, precision=precision, preferred_element_type=jnp.float32)  18.3 us
    ppermute x28, starting transfers between devices, swap(): return lax.ppermute(x, axis, [(0, 1), (1, 0)])  17.1 us
    pallas_call x5, Pallas kernels, call(): pl.pallas_call(kernel, out_shape=outs, scratch_shapes=list(scratch), in_s...  7.62 us
    ppermute x6, starting transfers between devices, body(): lax.ppermute(ringed[-chunk_count] if step > 1 else moving[h], 'dp', hops)  7.59 us
    ppermute x2, waiting for transfers between devices, body(): own_blocks[j] = lax.ppermute(own_blocks[j - 1], 'dp', hops)  7.59 us
    ppermute x3, starting transfers between devices, partner(): lax.ppermute(x, axis, [(i, i ^ flip) for i in range(lax.axis_size(axis))])  6.49 us
  transfers between devices with their start and end apart: 40, of which 21 were waited for; matrix products, arithmetic and copies ran while one was open for 18% of the time, Pallas kernels for 1%

profile of v13, /device:TPU:0, one launch (start us, length us, event | category | flops | bytes accessed | tf_op | source)
XLA Modules:
  0.0 150.5 jit_solution(6936241821507805729)
XLA Ops:
  1.8 3.1 %collective-permute-start = (bf16[256,1024]{1,0:T(8,128)(2,1)S(1)}, bf16[256,1024]{1,0:T(8,128)(2,1)}, u32[]{:S(2)}, u32[]{:S(2)}) collective-permute-start(bf16[256,1024]{1,0:T(8,128)(2,1)S(1)} %constant_dynamic-slice_fusion), channel_id=1, source_target_pairs={{0,4},{4,12},{12,8},{8,0},{1,5},{5,13},{13,9},{9,1},{2,6},{6,14},{... | collective-permute-start | bytes 1572872 | tf_op jit(solution)/shard_map/ppermute | solution.py:373
  6.0 2.6 %collective-permute-start.12 = (bf16[256,1024]{1,0:T(8,128)(2,1)S(1)}, bf16[256,1024]{1,0:T(8,128)(2,1)}, u32[]{:S(2)}, u32[]{:S(2)}) collective-permute-start(bf16[256,1024]{1,0:T(8,128)(2,1)S(1)} %constant_dynamic-slice_fusion.1), channel_id=1, source_target_pairs={{0,4},{4,12},{12,8},{8,0},{1,5},{5,13},{13,9},{9,1},{2,6},{6,14},{... | collective-permute-start | bytes 1572872 | tf_op jit(solution)/shard_map/ppermute | solution.py:373
  8.7 3.4 %fusion.64 = bf16[512,16]{0,1:T(8,128)(2,1)S(1)} fusion(bf16[4096,16]{0,1:T(8,128)(2,1)S(1)} %copy-done, bf16[1,512,4096]{2,1,0:T(8,128)(2,1)} %param.8), kind=kOutput, calls=%fused_computation.58 | convolution fusion | flops 67117056 | bytes 4341760 | tf_op jit(solution)/shard_map/dot_general | solution.py:22
  17.4 3.0 %fusion.44 = f32[512,1024]{1,0:T(8,128)S(1)} fusion(bf16[512,1024]{1,0:T(8,128)(2,1)S(1)} %dynamic-slice_bitcast_fusion.1, bf16[1024,2048]{1,0:T(8,128)(2,1)} %param.10), kind=kOutput, calls=%fused_computation.48 | convolution fusion | flops 1073741824 | bytes 5242880 | tf_op jit(solution)/shard_map/dot_general | solution.py:22
  23.5 6.4 %collective-permute-done.12 = bf16[256,1024]{1,0:T(8,128)(2,1)} collective-permute-done((bf16[256,1024]{1,0:T(8,128)(2,1)S(1)}, bf16[256,1024]{1,0:T(8,128)(2,1)}, u32[]{:S(2)}, u32[]{:S(2)}) %collective-permute-start.12) | collective-permute-done | bytes 524320 | tf_op jit(solution)/shard_map/ppermute | solution.py:373
  31.8 3.7 %collective-permute-done.1 = bf16[256,1024]{1,0:T(8,128)(2,1)S(1)} collective-permute-done((bf16[256,1024]{1,0:T(8,128)(2,1)}, bf16[256,1024]{1,0:T(8,128)(2,1)S(1)}, u32[]{:S(2)}, u32[]{:S(2)}) %collective-permute-start.1) | collective-permute-done | bytes 524320 | tf_op jit(solution)/shard_map/ppermute | solution.py:26
  41.8 5.0 %collective-permute-done.13 = bf16[256,1024]{1,0:T(8,128)(2,1)S(1)} collective-permute-done((bf16[256,1024]{1,0:T(8,128)(2,1)}, bf16[256,1024]{1,0:T(8,128)(2,1)S(1)}, u32[]{:S(2)}, u32[]{:S(2)}) %collective-permute-start.13) | collective-permute-done | bytes 524320 | tf_op jit(solution)/shard_map/ppermute | solution.py:26
  47.3 2.3 %fusion.58 = f32[512,1024]{1,0:T(8,128)S(1)} fusion(f32[512,1024]{1,0:T(8,128)S(1)} %add_add_fusion.1, bf16[256,1024]{1,0:T(8,128)(2,1)S(1)} %collective-permute-done.3, bf16[256,1024]{1,0:T(8,128)(2,1)S(1)} %collective-permute-done.2, bf16[256,1024]{1,0:T(8,128)(2,1)S(1)} %collective-permute-done.1, bf16[256,1024]{1,0:T(8,128)(2,1)} %collective-permute-done, ...), kind=kOutput, calls=%fused_computation.55 | convolution fusion | flops 1086849024 | bytes 7340032 | tf_op jit(solution)/shard_map/dot_general | solution.py:22
  50.2 3.4 %collective-permute-done.16 = bf16[256,1024]{1,0:T(8,128)(2,1)S(1)} collective-permute-done((bf16[256,1024]{1,0:T(8,128)(2,1)}, bf16[256,1024]{1,0:T(8,128)(2,1)S(1)}, u32[]{:S(2)}, u32[]{:S(2)}) %collective-permute-start.16) | collective-permute-done | bytes 524320 | tf_op jit(solution)/shard_map/ppermute | solution.py:373
  55.1 3.0 %collective-permute-done.5 = bf16[256,1024]{1,0:T(8,128)(2,1)S(1)} collective-permute-done((bf16[256,1024]{1,0:T(8,128)(2,1)S(1)}, bf16[256,1024]{1,0:T(8,128)(2,1)S(1)}, u32[]{:S(2)}, u32[]{:S(2)}) %collective-permute-start.5) | collective-permute-done | bytes 524320 | tf_op jit(solution)/shard_map/ppermute | solution.py:26
  58.5 6.3 %collective-permute-done.8 = bf16[256,1024]{1,0:T(8,128)(2,1)S(1)} collective-permute-done((bf16[256,1024]{1,0:T(8,128)(2,1)S(1)}, bf16[256,1024]{1,0:T(8,128)(2,1)S(1)}, u32[]{:S(2)}, u32[]{:S(2)}) %collective-permute-start.8) | collective-permute-done | bytes 524320 | tf_op jit(solution)/shard_map/ppermute | solution.py:373
  66.3 2.3 %fusion.49 = f32[512,1024]{1,0:T(8,128)S(1)} fusion(f32[512,1024]{1,0:T(8,128)S(1)} %add_add_fusion, bf16[256,1024]{1,0:T(8,128)(2,1)S(1)} %collective-permute-done.15, bf16[256,1024]{1,0:T(8,128)(2,1)S(1)} %collective-permute-done.14, bf16[256,1024]{1,0:T(8,128)(2,1)S(1)} %collective-permute-done.13, bf16[256,1024]{1,0:T(8,128)(2,1)} %collective-permute-done.12, ...), kind=kOutput, calls=%fused_computation.52 | convolution fusion | flops 1086849024 | bytes 7340032 | tf_op jit(solution)/shard_map/dot_general | solution.py:22
  68.9 6.2 %collective-permute-done.20.refs_0_ = bf16[256,1024]{1,0:T(8,128)(2,1)S(1)} collective-permute-done((bf16[256,1024]{1,0:T(8,128)(2,1)S(1)}, bf16[256,1024]{1,0:T(8,128)(2,1)S(1)}, u32[]{:S(2)}, u32[]{:S(2)}) %collective-permute-start.20) | collective-permute-done | bytes 524320 | tf_op jit(solution)/shard_map/ppermute | solution.py:373
  76.7 2.8 %collective-permute-done.9 = bf16[256,1024]{1,0:T(8,128)(2,1)S(1)} collective-permute-done((bf16[256,1024]{1,0:T(8,128)(2,1)S(1)}, bf16[256,1024]{1,0:T(8,128)(2,1)S(1)}, u32[]{:S(2)}, u32[]{:S(2)}) %collective-permute-start.9) | collective-permute-done | bytes 524320 | tf_op jit(solution)/shard_map/ppermute | solution.py:26
  82.7 7.6 %collective-permute-done.21.refs_1_ = bf16[256,1024]{1,0:T(8,128)(2,1)S(1)} collective-permute-done((bf16[256,1024]{1,0:T(8,128)(2,1)S(1)}, bf16[256,1024]{1,0:T(8,128)(2,1)S(1)}, u32[]{:S(2)}, u32[]{:S(2)}) %collective-permute-start.21) | collective-permute-done | bytes 524320 | tf_op jit(solution)/shard_map/ppermute | solution.py:26
  99.1 2.8 %collective-permute-start.27 = (bf16[64,2048]{1,0:T(8,128)(2,1)S(1)}, bf16[64,2048]{1,0:T(8,128)(2,1)}, u32[]{:S(2)}, u32[]{:S(2)}) collective-permute-start(bf16[64,2048]{1,0:T(8,128)(2,1)S(1)} %get-tuple-element.27.refs_0_.refs_4_), channel_id=1, source_target_pairs={{4,0},{12,4},{8,12},{0,8},{5,1},{13,5},{9,13},{1,9},{6,2},{14,6},{... | collective-permute-start | bytes 786440 | tf_op jit(solution)/shard_map/ppermute | solution.py:444
  101.9 5.4 %collective-permute-done.25.refs_1_ = bf16[64,2048]{1,0:T(8,128)(2,1)S(1)} collective-permute-done((bf16[64,2048]{1,0:T(8,128)(2,1)S(1)}, bf16[64,2048]{1,0:T(8,128)(2,1)S(1)}, u32[]{:S(2)}, u32[]{:S(2)}) %collective-permute-start.25) | collective-permute-done | bytes 262176 | tf_op jit(solution)/shard_map/ppermute | solution.py:442
  107.3 6.2 %collective-permute-start.26 = (bf16[64,2048]{1,0:T(8,128)(2,1)S(1)}, bf16[64,2048]{1,0:T(8,128)(2,1)}, u32[]{:S(2)}, u32[]{:S(2)}) collective-permute-start(bf16[64,2048]{1,0:T(8,128)(2,1)S(1)} %collective-permute-done.25.refs_1_), channel_id=1, source_target_pairs={{0,4},{4,12},{12,8},{8,0},{1,5},{5,13},{13,9},{9,1},{2,6},{6,14},{... | collective-permute-start | bytes 786440 | tf_op jit(solution)/shard_map/ppermute | solution.py:442
  115.8 2.2 %collective-permute-done.26.refs_2_ = bf16[64,2048]{1,0:T(8,128)(2,1)} collective-permute-done((bf16[64,2048]{1,0:T(8,128)(2,1)S(1)}, bf16[64,2048]{1,0:T(8,128)(2,1)}, u32[]{:S(2)}, u32[]{:S(2)}) %collective-permute-start.26) | collective-permute-done | bytes 262176 | tf_op jit(solution)/shard_map/ppermute | solution.py:442
  123.9 2.7 %collective-permute-done.32.refs_1_ = f32[168,128]{1,0:T(8,128)S(1)} collective-permute-done((f32[168,128]{1,0:T(8,128)S(1)}, f32[168,128]{1,0:T(8,128)S(1)}, u32[]{:S(2)}, u32[]{:S(2)}) %collective-permute-start.32) | collective-permute-done | bytes 86048 | tf_op jit(solution)/shard_map/ppermute | solution.py:26
  130.1 2.7 %collective-permute-done.34.refs_1_ = f32[24,640]{1,0:T(8,128)S(1)} collective-permute-done((f32[24,640]{1,0:T(8,128)S(1)}, f32[24,640]{1,0:T(8,128)S(1)}, u32[]{:S(2)}, u32[]{:S(2)}) %collective-permute-start.34) | collective-permute-done | bytes 61472 | tf_op jit(solution)/shard_map/ppermute | solution.py:26
  135.4 5.8 %collective-permute-start.38 = (bf16[40,1024]{1,0:T(8,128)(2,1)S(1)}, bf16[40,1024]{1,0:T(8,128)(2,1)S(1)}, u32[]{:S(2)}, u32[]{:S(2)}) collective-permute-start(bf16[40,1024]{1,0:T(8,128)(2,1)S(1)} %add_convert_fusion), channel_id=1, source_target_pairs={{0,12},{4,8},{8,4},{12,0},{1,13},{5,9},{9,5},{13,1},{2,14},{6,10},... | collective-permute-start | bytes 245768 | tf_op jit(solution)/shard_map/ppermute | solution.py:30
  141.9 2.6 %collective-permute-done.38 = bf16[40,1024]{1,0:T(8,128)(2,1)S(1)} collective-permute-done((bf16[40,1024]{1,0:T(8,128)(2,1)S(1)}, bf16[40,1024]{1,0:T(8,128)(2,1)S(1)}, u32[]{:S(2)}, u32[]{:S(2)}) %collective-permute-start.38) | collective-permute-done | bytes 81952 | tf_op jit(solution)/shard_map/ppermute | solution.py:30
  144.5 3.1 %collective-permute-done.37 = bf16[40,1024]{1,0:T(8,128)(2,1)S(1)} collective-permute-done((bf16[40,1024]{1,0:T(8,128)(2,1)S(1)}, bf16[40,1024]{1,0:T(8,128)(2,1)S(1)}, u32[]{:S(2)}, u32[]{:S(2)}) %collective-permute-start.37) | collective-permute-done | bytes 81952 | tf_op jit(solution)/shard_map/ppermute | solution.py:30
  (125 shorter events, 54.5 us)
Async XLA Ops:
  1.8 18.7 %collective-permute-start = (bf16[256,1024]{1,0:T(8,128)(2,1)S(1)}, bf16[256,1024]{1,0:T(8,128)(2,1)}, u32[]{:S(2)}, u32[]{:S(2)}) collective-permute-start(bf16[256,1024]{1,0:T(8,128)(2,1)S(1)} %constant_dynamic-slice_fusion), channel_id=1, source_target_pairs={{0,4},{4,12},{12,8},{8,0},{1,5},{5,13},{13,9},{9,1},{2,6},{6,14},{... | collective-permute-start | bytes 1572872 | tf_op jit(solution)/shard_map/ppermute | solution.py:373
  6.0 23.9 %collective-permute-start.12 = (bf16[256,1024]{1,0:T(8,128)(2,1)S(1)}, bf16[256,1024]{1,0:T(8,128)(2,1)}, u32[]{:S(2)}, u32[]{:S(2)}) collective-permute-start(bf16[256,1024]{1,0:T(8,128)(2,1)S(1)} %constant_dynamic-slice_fusion.1), channel_id=1, source_target_pairs={{0,4},{4,12},{12,8},{8,0},{1,5},{5,13},{13,9},{9,1},{2,6},{6,14},{... | collective-permute-start | bytes 1572872 | tf_op jit(solution)/shard_map/ppermute | solution.py:373
  20.4 15.1 %collective-permute-start.1 = (bf16[256,1024]{1,0:T(8,128)(2,1)}, bf16[256,1024]{1,0:T(8,128)(2,1)S(1)}, u32[]{:S(2)}, u32[]{:S(2)}) collective-permute-start(bf16[256,1024]{1,0:T(8,128)(2,1)} %collective-permute-done), channel_id=1, source_target_pairs={{0,16},{16,0},{1,17},{17,1},{2,18},{18,2},{3,19},{19,3},{4,20},{20... | collective-permute-start | bytes 1572872 | tf_op jit(solution)/shard_map/ppermute | solution.py:26
  22.9 14.7 %collective-permute-start.2 = (bf16[256,1024]{1,0:T(8,128)(2,1)}, bf16[256,1024]{1,0:T(8,128)(2,1)S(1)}, u32[]{:S(2)}, u32[]{:S(2)}) collective-permute-start(bf16[256,1024]{1,0:T(8,128)(2,1)} %collective-permute-done), channel_id=1, source_target_pairs={{0,1},{1,0},{2,3},{3,2},{4,5},{5,4},{6,7},{7,6},{8,9},{9,8},{10,11... | collective-permute-start | bytes 1572872 | tf_op jit(solution)/shard_map/ppermute | solution.py:26
  23.0 17.2 %collective-permute-start.4 = (bf16[256,1024]{1,0:T(8,128)(2,1)}, bf16[256,1024]{1,0:T(8,128)(2,1)S(1)}, u32[]{:S(2)}, u32[]{:S(2)}) collective-permute-start(bf16[256,1024]{1,0:T(8,128)(2,1)} %collective-permute-done), channel_id=1, source_target_pairs={{0,4},{4,12},{12,8},{8,0},{1,5},{5,13},{13,9},{9,1},{2,6},{6,14},{... | collective-permute-start | bytes 1572872 | tf_op jit(solution)/shard_map/ppermute | solution.py:373
  30.0 16.9 %collective-permute-start.13 = (bf16[256,1024]{1,0:T(8,128)(2,1)}, bf16[256,1024]{1,0:T(8,128)(2,1)S(1)}, u32[]{:S(2)}, u32[]{:S(2)}) collective-permute-start(bf16[256,1024]{1,0:T(8,128)(2,1)} %collective-permute-done.12), channel_id=1, source_target_pairs={{0,16},{16,0},{1,17},{17,1},{2,18},{18,2},{3,19},{19,3},{4,20},{20... | collective-permute-start | bytes 1572872 | tf_op jit(solution)/shard_map/ppermute | solution.py:26
  35.6 11.7 %collective-permute-start.3 = (bf16[256,1024]{1,0:T(8,128)(2,1)S(1)}, bf16[256,1024]{1,0:T(8,128)(2,1)S(1)}, u32[]{:S(2)}, u32[]{:S(2)}) collective-permute-start(bf16[256,1024]{1,0:T(8,128)(2,1)S(1)} %collective-permute-done.1), channel_id=1, source_target_pairs={{0,1},{1,0},{2,3},{3,2},{4,5},{5,4},{6,7},{7,6},{8,9},{9,8},{10,11... | collective-permute-start | bytes 1572872 | tf_op jit(solution)/shard_map/ppermute | solution.py:26
  37.1 12.5 %collective-permute-start.14 = (bf16[256,1024]{1,0:T(8,128)(2,1)}, bf16[256,1024]{1,0:T(8,128)(2,1)S(1)}, u32[]{:S(2)}, u32[]{:S(2)}) collective-permute-start(bf16[256,1024]{1,0:T(8,128)(2,1)} %collective-permute-done.12), channel_id=1, source_target_pairs={{0,1},{1,0},{2,3},{3,2},{4,5},{5,4},{6,7},{7,6},{8,9},{9,8},{10,11... | collective-permute-start | bytes 1572872 | tf_op jit(solution)/shard_map/ppermute | solution.py:26
  37.7 15.9 %collective-permute-start.16 = (bf16[256,1024]{1,0:T(8,128)(2,1)}, bf16[256,1024]{1,0:T(8,128)(2,1)S(1)}, u32[]{:S(2)}, u32[]{:S(2)}) collective-permute-start(bf16[256,1024]{1,0:T(8,128)(2,1)} %collective-permute-done.12), channel_id=1, source_target_pairs={{0,4},{4,12},{12,8},{8,0},{1,5},{5,13},{13,9},{9,1},{2,6},{6,14},{... | collective-permute-start | bytes 1572872 | tf_op jit(solution)/shard_map/ppermute | solution.py:373
  40.3 17.8 %collective-permute-start.5 = (bf16[256,1024]{1,0:T(8,128)(2,1)S(1)}, bf16[256,1024]{1,0:T(8,128)(2,1)S(1)}, u32[]{:S(2)}, u32[]{:S(2)}) collective-permute-start(bf16[256,1024]{1,0:T(8,128)(2,1)S(1)} %collective-permute-done.4), channel_id=1, source_target_pairs={{0,16},{16,0},{1,17},{17,1},{2,18},{18,2},{3,19},{19,3},{4,20},{20... | collective-permute-start | bytes 1572872 | tf_op jit(solution)/shard_map/ppermute | solution.py:26
  46.8 18.0 %collective-permute-start.8 = (bf16[256,1024]{1,0:T(8,128)(2,1)S(1)}, bf16[256,1024]{1,0:T(8,128)(2,1)S(1)}, u32[]{:S(2)}, u32[]{:S(2)}) collective-permute-start(bf16[256,1024]{1,0:T(8,128)(2,1)S(1)} %collective-permute-done.4), channel_id=1, source_target_pairs={{0,4},{4,12},{12,8},{8,0},{1,5},{5,13},{13,9},{9,1},{2,6},{6,14},{... | collective-permute-start | bytes 1572872 | tf_op jit(solution)/shard_map/ppermute | solution.py:373
  47.3 17.5 %collective-permute-start.15 = (bf16[256,1024]{1,0:T(8,128)(2,1)S(1)}, bf16[256,1024]{1,0:T(8,128)(2,1)S(1)}, u32[]{:S(2)}, u32[]{:S(2)}) collective-permute-start(bf16[256,1024]{1,0:T(8,128)(2,1)S(1)} %collective-permute-done.13), channel_id=1, source_target_pairs={{0,1},{1,0},{2,3},{3,2},{4,5},{5,4},{6,7},{7,6},{8,9},{9,8},{10,11... | collective-permute-start | bytes 1572872 | tf_op jit(solution)/shard_map/ppermute | solution.py:26
  49.6 19.0 %collective-permute-start.6 = (bf16[256,1024]{1,0:T(8,128)(2,1)S(1)}, bf16[256,1024]{1,0:T(8,128)(2,1)S(1)}, u32[]{:S(2)}, u32[]{:S(2)}) collective-permute-start(bf16[256,1024]{1,0:T(8,128)(2,1)S(1)} %collective-permute-done.4), channel_id=1, source_target_pairs={{0,1},{1,0},{2,3},{3,2},{4,5},{5,4},{6,7},{7,6},{8,9},{9,8},{10,11... | collective-permute-start | bytes 1572872 | tf_op jit(solution)/shard_map/ppermute | solution.py:26
  53.5 27.2 %collective-permute-start.17 = (bf16[256,1024]{1,0:T(8,128)(2,1)S(1)}, bf16[256,1024]{1,0:T(8,128)(2,1)S(1)}, u32[]{:S(2)}, u32[]{:S(2)}) collective-permute-start(bf16[256,1024]{1,0:T(8,128)(2,1)S(1)} %collective-permute-done.16), channel_id=1, source_target_pairs={{0,16},{16,0},{1,17},{17,1},{2,18},{18,2},{3,19},{19,3},{4,20},{20... | collective-permute-start | bytes 1572872 | tf_op jit(solution)/shard_map/ppermute | solution.py:26
  58.1 17.1 %collective-permute-start.20 = (bf16[256,1024]{1,0:T(8,128)(2,1)S(1)}, bf16[256,1024]{1,0:T(8,128)(2,1)S(1)}, u32[]{:S(2)}, u32[]{:S(2)}) collective-permute-start(bf16[256,1024]{1,0:T(8,128)(2,1)S(1)} %collective-permute-done.16), channel_id=1, source_target_pairs={{0,4},{4,12},{12,8},{8,0},{1,5},{5,13},{13,9},{9,1},{2,6},{6,14},{... | collective-permute-start | bytes 1572872 | tf_op jit(solution)/shard_map/ppermute | solution.py:373
  64.8 10.4 %collective-permute-start.7 = (bf16[256,1024]{1,0:T(8,128)(2,1)S(1)}, bf16[256,1024]{1,0:T(8,128)(2,1)S(1)}, u32[]{:S(2)}, u32[]{:S(2)}) collective-permute-start(bf16[256,1024]{1,0:T(8,128)(2,1)S(1)} %collective-permute-done.5), channel_id=1, source_target_pairs={{0,1},{1,0},{2,3},{3,2},{4,5},{5,4},{6,7},{7,6},{8,9},{9,8},{10,11... | collective-permute-start | bytes 1572872 | tf_op jit(solution)/shard_map/ppermute | solution.py:26
  64.8 14.7 %collective-permute-start.9 = (bf16[256,1024]{1,0:T(8,128)(2,1)S(1)}, bf16[256,1024]{1,0:T(8,128)(2,1)S(1)}, u32[]{:S(2)}, u32[]{:S(2)}) collective-permute-start(bf16[256,1024]{1,0:T(8,128)(2,1)S(1)} %collective-permute-done.8), channel_id=1, source_target_pairs={{0,16},{16,0},{1,17},{17,1},{2,18},{18,2},{3,19},{19,3},{4,20},{20... | collective-permute-start | bytes 1572872 | tf_op jit(solution)/shard_map/ppermute | solution.py:26
  68.6 21.8 %collective-permute-start.18 = (bf16[256,1024]{1,0:T(8,128)(2,1)S(1)}, bf16[256,1024]{1,0:T(8,128)(2,1)S(1)}, u32[]{:S(2)}, u32[]{:S(2)}) collective-permute-start(bf16[256,1024]{1,0:T(8,128)(2,1)S(1)} %collective-permute-done.16), channel_id=1, source_target_pairs={{0,1},{1,0},{2,3},{3,2},{4,5},{5,4},{6,7},{7,6},{8,9},{9,8},{10,11... | collective-permute-start | bytes 1572872 | tf_op jit(solution)/shard_map/ppermute | solution.py:26
  75.1 15.2 %collective-permute-start.21 = (bf16[256,1024]{1,0:T(8,128)(2,1)S(1)}, bf16[256,1024]{1,0:T(8,128)(2,1)S(1)}, u32[]{:S(2)}, u32[]{:S(2)}) collective-permute-start(bf16[256,1024]{1,0:T(8,128)(2,1)S(1)} %collective-permute-done.20.refs_0_), channel_id=1, source_target_pairs={{0,16},{16,0},{1,17},{17,1},{2,18},{18,2},{3,19},{19,3},{4,20},{20... | collective-permute-start | bytes 1572872 | tf_op jit(solution)/shard_map/ppermute | solution.py:26
  80.8 11.2 %collective-permute-start.22 = (bf16[256,1024]{1,0:T(8,128)(2,1)S(1)}, bf16[256,1024]{1,0:T(8,128)(2,1)S(1)}, u32[]{:S(2)}, u32[]{:S(2)}) collective-permute-start(bf16[256,1024]{1,0:T(8,128)(2,1)S(1)} %collective-permute-done.20.refs_0_), channel_id=1, source_target_pairs={{0,1},{1,0},{2,3},{3,2},{4,5},{5,4},{6,7},{7,6},{8,9},{9,8},{10,11... | collective-permute-start | bytes 1572872 | tf_op jit(solution)/shard_map/ppermute | solution.py:26
  99.1 24.8 %collective-permute-start.33 = (s32[32,4]{1,0:T(8,128)}, s32[32,4]{1,0:T(8,128)S(1)}, u32[]{:S(2)}, u32[]{:S(2)}) collective-permute-start(s32[32,4]{1,0:T(8,128)} %fusion.89), channel_id=1, source_target_pairs={{0,1},{1,0},{2,3},{3,2},{4,5},{5,4},{6,7},{7,6},{8,9},{9,8},{10,11... | collective-permute-start | bytes 1544 | tf_op jit(solution)/shard_map/ppermute | solution.py:26
  99.1 16.7 %collective-permute-start.27 = (bf16[64,2048]{1,0:T(8,128)(2,1)S(1)}, bf16[64,2048]{1,0:T(8,128)(2,1)}, u32[]{:S(2)}, u32[]{:S(2)}) collective-permute-start(bf16[64,2048]{1,0:T(8,128)(2,1)S(1)} %get-tuple-element.27.refs_0_.refs_4_), channel_id=1, source_target_pairs={{4,0},{12,4},{8,12},{0,8},{5,1},{13,5},{9,13},{1,9},{6,2},{14,6},{... | collective-permute-start | bytes 786440 | tf_op jit(solution)/shard_map/ppermute | solution.py:444
  107.3 10.6 %collective-permute-start.26 = (bf16[64,2048]{1,0:T(8,128)(2,1)S(1)}, bf16[64,2048]{1,0:T(8,128)(2,1)}, u32[]{:S(2)}, u32[]{:S(2)}) collective-permute-start(bf16[64,2048]{1,0:T(8,128)(2,1)S(1)} %collective-permute-done.25.refs_1_), channel_id=1, source_target_pairs={{0,4},{4,12},{12,8},{8,0},{1,5},{5,13},{13,9},{9,1},{2,6},{6,14},{... | collective-permute-start | bytes 786440 | tf_op jit(solution)/shard_map/ppermute | solution.py:442
  135.4 9.1 %collective-permute-start.38 = (bf16[40,1024]{1,0:T(8,128)(2,1)S(1)}, bf16[40,1024]{1,0:T(8,128)(2,1)S(1)}, u32[]{:S(2)}, u32[]{:S(2)}) collective-permute-start(bf16[40,1024]{1,0:T(8,128)(2,1)S(1)} %add_convert_fusion), channel_id=1, source_target_pairs={{0,12},{4,8},{8,4},{12,0},{1,13},{5,9},{9,5},{13,1},{2,14},{6,10},... | collective-permute-start | bytes 245768 | tf_op jit(solution)/shard_map/ppermute | solution.py:30
  (27 other events, 150.4 us)

commit v14 on v13

--- a/solution.py
+++ b/solution.py
@@ -436,15 +436,17 @@
         squares + states_b + [labels[None], gain[None], counts[:, None]],
     )
 
+    first_other = swap(pooled, "pair")
+    late_pooled = after(pooled, first_other, list_c)
     own_blocks = [pooled] * dp
     for j in range(1, dp):
         if j <= dp // 2:
             own_blocks[j] = lax.ppermute(own_blocks[j - 1], "dp", hops)
         else:
-            own_blocks[dp + dp // 2 - j] = lax.ppermute(
-                own_blocks[(dp + dp // 2 - j + 1) % dp], "dp", back_hops
-            )
-    other_blocks = [swap(block, "pair") for block in own_blocks]
+            at = dp + dp // 2 - j
+            source = late_pooled if at == dp - 1 else own_blocks[at + 1]
+            own_blocks[at] = lax.ppermute(source, "dp", back_hops)
+    other_blocks = [first_other] + [swap(block, "pair") for block in own_blocks[1:]]
     rows = dp * docs
     last_rows = -(-(4 + list_c.shape[0]) // 8) * 8
     sums, sorted_oth = call(

time: 151 us -> 151 us (level)
  starting transfers between devices: 40.4 us -> 32.7 us
  waiting for transfers between devices: 71.1 us -> 78.1 us
    ppermute x2, waiting for transfers between devices: 7.59 us -> 14.4 us  [body(): own_blocks[j] = lax.ppermute(own_blocks[j - 1], 'dp', hops)]
    ppermute x2, starting transfers between devices: 6.37 us -> 0.76 us  [body(): own_blocks[j] = lax.ppermute(own_blocks[j - 1], 'dp', hops)]
    ppermute x3, starting transfers between devices: 6.49 us -> 4.45 us  [partner(): lax.ppermute(x, axis, [(i, i ^ flip) for i in range(lax.axis_size(axis))])]
  transfers between devices with their start and end apart: 40 -> 40, of which waited for: 21 -> 24; matrix products, arithmetic and copies ran while one was open for 18% -> 19% of each run, Pallas kernels for 1% -> 1%
where the time goes in v14:
time: 151 us; the launch traced here: 150 us
  waiting for transfers between devices  78.1 us (52%)
  starting transfers between devices  32.7 us (22%)
  matrix products  19.2 us (13%)
  local copies, waits for them, and re-layouts  8.26 us (5%)
  Pallas kernels  7.35 us (5%)
  other arithmetic  3.51 us (2%)
    ppermute x28, waiting for transfers between devices, swap(): return lax.ppermute(x, axis, [(0, 1), (1, 0)])  34.6 us
    ppermute x6, waiting for transfers between devices, body(): lax.ppermute(ringed[-chunk_count] if step > 1 else moving[h], 'dp', hops)  23.5 us
    dot_general x10, matrix products, dot_nn(): jnp.dot(a, b, precision=precision, preferred_element_type=jnp.float32)  18.4 us
    ppermute x28, starting transfers between devices, swap(): return lax.ppermute(x, axis, [(0, 1), (1, 0)])  17.1 us
    ppermute x2, waiting for transfers between devices, body(): own_blocks[j] = lax.ppermute(own_blocks[j - 1], 'dp', hops)  14.4 us
    ppermute x6, starting transfers between devices, body(): lax.ppermute(ringed[-chunk_count] if step > 1 else moving[h], 'dp', hops)  7.57 us
    pallas_call x5, Pallas kernels, call(): pl.pallas_call(kernel, out_shape=outs, scratch_shapes=list(scratch), in_s...  7.35 us
    ppermute x3, waiting for transfers between devices, partner(): lax.ppermute(x, axis, [(i, i ^ flip) for i in range(lax.axis_size(axis))])  5.6 us
  transfers between devices with their start and end apart: 40, of which 24 were waited for; matrix products, arithmetic and copies ran while one was open for 19% of the time, Pallas kernels for 1%

profile of v14, /device:TPU:0, one launch (start us, length us, event | category | flops | bytes accessed | tf_op | source)
XLA Modules:
  0.0 150.3 jit_solution(7735634249245867733)
XLA Ops:
  1.8 3.1 %collective-permute-start = (bf16[256,1024]{1,0:T(8,128)(2,1)S(1)}, bf16[256,1024]{1,0:T(8,128)(2,1)}, u32[]{:S(2)}, u32[]{:S(2)}) collective-permute-start(bf16[256,1024]{1,0:T(8,128)(2,1)S(1)} %constant_dynamic-slice_fusion), channel_id=1, source_target_pairs={{0,4},{4,12},{12,8},{8,0},{1,5},{5,13},{13,9},{9,1},{2,6},{6,14},{... | collective-permute-start | bytes 1572872 | tf_op jit(solution)/shard_map/ppermute | solution.py:373
  6.0 2.6 %collective-permute-start.12 = (bf16[256,1024]{1,0:T(8,128)(2,1)S(1)}, bf16[256,1024]{1,0:T(8,128)(2,1)}, u32[]{:S(2)}, u32[]{:S(2)}) collective-permute-start(bf16[256,1024]{1,0:T(8,128)(2,1)S(1)} %constant_dynamic-slice_fusion.1), channel_id=1, source_target_pairs={{0,4},{4,12},{12,8},{8,0},{1,5},{5,13},{13,9},{9,1},{2,6},{6,14},{... | collective-permute-start | bytes 1572872 | tf_op jit(solution)/shard_map/ppermute | solution.py:373
  8.7 3.4 %fusion.64 = bf16[512,16]{0,1:T(8,128)(2,1)S(1)} fusion(bf16[4096,16]{0,1:T(8,128)(2,1)S(1)} %copy-done, bf16[1,512,4096]{2,1,0:T(8,128)(2,1)} %param.8), kind=kOutput, calls=%fused_computation.58 | convolution fusion | flops 67117056 | bytes 4341760 | tf_op jit(solution)/shard_map/dot_general | solution.py:22
  17.8 3.0 %fusion.44 = f32[512,1024]{1,0:T(8,128)S(1)} fusion(bf16[512,1024]{1,0:T(8,128)(2,1)S(1)} %dynamic-slice_bitcast_fusion.1, bf16[1024,2048]{1,0:T(8,128)(2,1)} %param.10), kind=kOutput, calls=%fused_computation.48 | convolution fusion | flops 1073741824 | bytes 5242880 | tf_op jit(solution)/shard_map/dot_general | solution.py:22
  24.1 5.9 %collective-permute-done.12 = bf16[256,1024]{1,0:T(8,128)(2,1)} collective-permute-done((bf16[256,1024]{1,0:T(8,128)(2,1)S(1)}, bf16[256,1024]{1,0:T(8,128)(2,1)}, u32[]{:S(2)}, u32[]{:S(2)}) %collective-permute-start.12) | collective-permute-done | bytes 524320 | tf_op jit(solution)/shard_map/ppermute | solution.py:373
  31.8 4.1 %collective-permute-done.1 = bf16[256,1024]{1,0:T(8,128)(2,1)S(1)} collective-permute-done((bf16[256,1024]{1,0:T(8,128)(2,1)}, bf16[256,1024]{1,0:T(8,128)(2,1)S(1)}, u32[]{:S(2)}, u32[]{:S(2)}) %collective-permute-start.1) | collective-permute-done | bytes 524320 | tf_op jit(solution)/shard_map/ppermute | solution.py:26
  41.8 5.4 %collective-permute-done.13 = bf16[256,1024]{1,0:T(8,128)(2,1)S(1)} collective-permute-done((bf16[256,1024]{1,0:T(8,128)(2,1)}, bf16[256,1024]{1,0:T(8,128)(2,1)S(1)}, u32[]{:S(2)}, u32[]{:S(2)}) %collective-permute-start.13) | collective-permute-done | bytes 524320 | tf_op jit(solution)/shard_map/ppermute | solution.py:26
  47.7 2.3 %fusion.58 = f32[512,1024]{1,0:T(8,128)S(1)} fusion(f32[512,1024]{1,0:T(8,128)S(1)} %add_add_fusion.1, bf16[256,1024]{1,0:T(8,128)(2,1)S(1)} %collective-permute-done.3, bf16[256,1024]{1,0:T(8,128)(2,1)S(1)} %collective-permute-done.2, bf16[256,1024]{1,0:T(8,128)(2,1)S(1)} %collective-permute-done.1, bf16[256,1024]{1,0:T(8,128)(2,1)} %collective-permute-done, ...), kind=kOutput, calls=%fused_computation.55 | convolution fusion | flops 1086849024 | bytes 7340032 | tf_op jit(solution)/shard_map/dot_general | solution.py:22
  50.6 3.4 %collective-permute-done.16 = bf16[256,1024]{1,0:T(8,128)(2,1)S(1)} collective-permute-done((bf16[256,1024]{1,0:T(8,128)(2,1)}, bf16[256,1024]{1,0:T(8,128)(2,1)S(1)}, u32[]{:S(2)}, u32[]{:S(2)}) %collective-permute-start.16) | collective-permute-done | bytes 524320 | tf_op jit(solution)/shard_map/ppermute | solution.py:373
  55.4 3.0 %collective-permute-done.5 = bf16[256,1024]{1,0:T(8,128)(2,1)S(1)} collective-permute-done((bf16[256,1024]{1,0:T(8,128)(2,1)S(1)}, bf16[256,1024]{1,0:T(8,128)(2,1)S(1)}, u32[]{:S(2)}, u32[]{:S(2)}) %collective-permute-start.5) | collective-permute-done | bytes 524320 | tf_op jit(solution)/shard_map/ppermute | solution.py:26
  58.9 6.2 %collective-permute-done.8 = bf16[256,1024]{1,0:T(8,128)(2,1)S(1)} collective-permute-done((bf16[256,1024]{1,0:T(8,128)(2,1)S(1)}, bf16[256,1024]{1,0:T(8,128)(2,1)S(1)}, u32[]{:S(2)}, u32[]{:S(2)}) %collective-permute-start.8) | collective-permute-done | bytes 524320 | tf_op jit(solution)/shard_map/ppermute | solution.py:373
  66.7 2.3 %fusion.49 = f32[512,1024]{1,0:T(8,128)S(1)} fusion(f32[512,1024]{1,0:T(8,128)S(1)} %add_add_fusion, bf16[256,1024]{1,0:T(8,128)(2,1)S(1)} %collective-permute-done.15, bf16[256,1024]{1,0:T(8,128)(2,1)S(1)} %collective-permute-done.14, bf16[256,1024]{1,0:T(8,128)(2,1)S(1)} %collective-permute-done.13, bf16[256,1024]{1,0:T(8,128)(2,1)} %collective-permute-done.12, ...), kind=kOutput, calls=%fused_computation.52 | convolution fusion | flops 1086849024 | bytes 7340032 | tf_op jit(solution)/shard_map/dot_general | solution.py:22
  69.3 6.2 %collective-permute-done.20.refs_0_ = bf16[256,1024]{1,0:T(8,128)(2,1)S(1)} collective-permute-done((bf16[256,1024]{1,0:T(8,128)(2,1)S(1)}, bf16[256,1024]{1,0:T(8,128)(2,1)S(1)}, u32[]{:S(2)}, u32[]{:S(2)}) %collective-permute-start.20) | collective-permute-done | bytes 524320 | tf_op jit(solution)/shard_map/ppermute | solution.py:373
  77.0 2.8 %collective-permute-done.9 = bf16[256,1024]{1,0:T(8,128)(2,1)S(1)} collective-permute-done((bf16[256,1024]{1,0:T(8,128)(2,1)S(1)}, bf16[256,1024]{1,0:T(8,128)(2,1)S(1)}, u32[]{:S(2)}, u32[]{:S(2)}) %collective-permute-start.9) | collective-permute-done | bytes 524320 | tf_op jit(solution)/shard_map/ppermute | solution.py:26
  83.1 7.6 %collective-permute-done.21.refs_1_ = bf16[256,1024]{1,0:T(8,128)(2,1)S(1)} collective-permute-done((bf16[256,1024]{1,0:T(8,128)(2,1)S(1)}, bf16[256,1024]{1,0:T(8,128)(2,1)S(1)}, u32[]{:S(2)}, u32[]{:S(2)}) %collective-permute-start.21) | collective-permute-done | bytes 524320 | tf_op jit(solution)/shard_map/ppermute | solution.py:26
  100.5 2.8 %collective-permute-start.28 = (bf16[64,2048]{1,0:T(8,128)(2,1)S(1)}, bf16[64,2048]{1,0:T(8,128)(2,1)}, u32[]{:S(2)}, u32[]{:S(2)}) collective-permute-start(bf16[64,2048]{1,0:T(8,128)(2,1)S(1)} %get-tuple-element.29.refs_0_.refs_4_), channel_id=1, source_target_pairs={{4,0},{12,4},{8,12},{0,8},{5,1},{13,5},{9,13},{1,9},{6,2},{14,6},{... | collective-permute-start | bytes 786440 | tf_op jit(solution)/shard_map/ppermute | solution.py:448
  103.3 9.3 %collective-permute-done.25.refs_1_ = bf16[64,2048]{1,0:T(8,128)(2,1)S(1)} collective-permute-done((bf16[64,2048]{1,0:T(8,128)(2,1)S(1)}, bf16[64,2048]{1,0:T(8,128)(2,1)S(1)}, u32[]{:S(2)}, u32[]{:S(2)}) %collective-permute-start.25) | collective-permute-done | bytes 262176 | tf_op jit(solution)/shard_map/ppermute | solution.py:444
  114.8 5.1 %collective-permute-done.26.refs_2_ = bf16[64,2048]{1,0:T(8,128)(2,1)} collective-permute-done((bf16[64,2048]{1,0:T(8,128)(2,1)S(1)}, bf16[64,2048]{1,0:T(8,128)(2,1)}, u32[]{:S(2)}, u32[]{:S(2)}) %collective-permute-start.26) | collective-permute-done | bytes 262176 | tf_op jit(solution)/shard_map/ppermute | solution.py:444
  125.9 2.7 %collective-permute-done.32.refs_1_ = f32[168,128]{1,0:T(8,128)S(1)} collective-permute-done((f32[168,128]{1,0:T(8,128)S(1)}, f32[168,128]{1,0:T(8,128)S(1)}, u32[]{:S(2)}, u32[]{:S(2)}) %collective-permute-start.32) | collective-permute-done | bytes 86048 | tf_op jit(solution)/shard_map/ppermute | solution.py:26
  128.6 2.0 %shard_map.122 = (f32[1,128]{1,0:T(1,128)}, f32[64,2048]{1,0:T(8,128)}, f32[24,640]{1,0:T(8,128)S(1)}, f32[64,2048]{1,0:T(8,128)S(1)}, f32[1,2048]{1,0:T(1,128)S(1)}) custom-call(f32[168,128]{1,0:T(8,128)S(1)} %get-tuple-element.30.refs_0_, f32[168,128]{1,0:T(8,128)S(1)} %collective-permute-done.32.refs_1_, s32[4,128]{1,0:T(4,128)S(1)} %bitcast.108, ...), custom_call_target="tpu_custom_call" | custom-call | flops 16777216 | bytes 4215552 | tf_op jit(solution)/shard_map/pallas_call | solution.py:59
  132.1 2.7 %collective-permute-done.34.refs_1_ = f32[24,640]{1,0:T(8,128)S(1)} collective-permute-done((f32[24,640]{1,0:T(8,128)S(1)}, f32[24,640]{1,0:T(8,128)S(1)}, u32[]{:S(2)}, u32[]{:S(2)}) %collective-permute-start.34) | collective-permute-done | bytes 61472 | tf_op jit(solution)/shard_map/ppermute | solution.py:26
  137.4 3.5 %collective-permute-start.38 = (bf16[40,1024]{1,0:T(8,128)(2,1)S(1)}, bf16[40,1024]{1,0:T(8,128)(2,1)S(1)}, u32[]{:S(2)}, u32[]{:S(2)}) collective-permute-start(bf16[40,1024]{1,0:T(8,128)(2,1)S(1)} %add_convert_fusion), channel_id=1, source_target_pairs={{0,12},{4,8},{8,4},{12,0},{1,13},{5,9},{9,5},{13,1},{2,14},{6,10},... | collective-permute-start | bytes 245768 | tf_op jit(solution)/shard_map/ppermute | solution.py:30
  141.9 2.7 %collective-permute-done.38 = bf16[40,1024]{1,0:T(8,128)(2,1)S(1)} collective-permute-done((bf16[40,1024]{1,0:T(8,128)(2,1)S(1)}, bf16[40,1024]{1,0:T(8,128)(2,1)S(1)}, u32[]{:S(2)}, u32[]{:S(2)}) %collective-permute-start.38) | collective-permute-done | bytes 81952 | tf_op jit(solution)/shard_map/ppermute | solution.py:30
  144.6 2.7 %collective-permute-done.37 = bf16[40,1024]{1,0:T(8,128)(2,1)S(1)} collective-permute-done((bf16[40,1024]{1,0:T(8,128)(2,1)S(1)}, bf16[40,1024]{1,0:T(8,128)(2,1)S(1)}, u32[]{:S(2)}, u32[]{:S(2)}) %collective-permute-start.37) | collective-permute-done | bytes 81952 | tf_op jit(solution)/shard_map/ppermute | solution.py:30
  (125 shorter events, 54.1 us)
Async XLA Ops:
  1.8 19.1 %collective-permute-start = (bf16[256,1024]{1,0:T(8,128)(2,1)S(1)}, bf16[256,1024]{1,0:T(8,128)(2,1)}, u32[]{:S(2)}, u32[]{:S(2)}) collective-permute-start(bf16[256,1024]{1,0:T(8,128)(2,1)S(1)} %constant_dynamic-slice_fusion), channel_id=1, source_target_pairs={{0,4},{4,12},{12,8},{8,0},{1,5},{5,13},{13,9},{9,1},{2,6},{6,14},{... | collective-permute-start | bytes 1572872 | tf_op jit(solution)/shard_map/ppermute | solution.py:373
  6.0 23.9 %collective-permute-start.12 = (bf16[256,1024]{1,0:T(8,128)(2,1)S(1)}, bf16[256,1024]{1,0:T(8,128)(2,1)}, u32[]{:S(2)}, u32[]{:S(2)}) collective-permute-start(bf16[256,1024]{1,0:T(8,128)(2,1)S(1)} %constant_dynamic-slice_fusion.1), channel_id=1, source_target_pairs={{0,4},{4,12},{12,8},{8,0},{1,5},{5,13},{13,9},{9,1},{2,6},{6,14},{... | collective-permute-start | bytes 1572872 | tf_op jit(solution)/shard_map/ppermute | solution.py:373
  20.8 15.1 %collective-permute-start.1 = (bf16[256,1024]{1,0:T(8,128)(2,1)}, bf16[256,1024]{1,0:T(8,128)(2,1)S(1)}, u32[]{:S(2)}, u32[]{:S(2)}) collective-permute-start(bf16[256,1024]{1,0:T(8,128)(2,1)} %collective-permute-done), channel_id=1, source_target_pairs={{0,16},{16,0},{1,17},{17,1},{2,18},{18,2},{3,19},{19,3},{4,20},{20... | collective-permute-start | bytes 1572872 | tf_op jit(solution)/shard_map/ppermute | solution.py:26
  23.5 14.5 %collective-permute-start.2 = (bf16[256,1024]{1,0:T(8,128)(2,1)}, bf16[256,1024]{1,0:T(8,128)(2,1)S(1)}, u32[]{:S(2)}, u32[]{:S(2)}) collective-permute-start(bf16[256,1024]{1,0:T(8,128)(2,1)} %collective-permute-done), channel_id=1, source_target_pairs={{0,1},{1,0},{2,3},{3,2},{4,5},{5,4},{6,7},{7,6},{8,9},{9,8},{10,11... | collective-permute-start | bytes 1572872 | tf_op jit(solution)/shard_map/ppermute | solution.py:26
  23.6 16.7 %collective-permute-start.4 = (bf16[256,1024]{1,0:T(8,128)(2,1)}, bf16[256,1024]{1,0:T(8,128)(2,1)S(1)}, u32[]{:S(2)}, u32[]{:S(2)}) collective-permute-start(bf16[256,1024]{1,0:T(8,128)(2,1)} %collective-permute-done), channel_id=1, source_target_pairs={{0,4},{4,12},{12,8},{8,0},{1,5},{5,13},{13,9},{9,1},{2,6},{6,14},{... | collective-permute-start | bytes 1572872 | tf_op jit(solution)/shard_map/ppermute | solution.py:373
  30.0 17.3 %collective-permute-start.13 = (bf16[256,1024]{1,0:T(8,128)(2,1)}, bf16[256,1024]{1,0:T(8,128)(2,1)S(1)}, u32[]{:S(2)}, u32[]{:S(2)}) collective-permute-start(bf16[256,1024]{1,0:T(8,128)(2,1)} %collective-permute-done.12), channel_id=1, source_target_pairs={{0,16},{16,0},{1,17},{17,1},{2,18},{18,2},{3,19},{19,3},{4,20},{20... | collective-permute-start | bytes 1572872 | tf_op jit(solution)/shard_map/ppermute | solution.py:26
  36.0 11.7 %collective-permute-start.3 = (bf16[256,1024]{1,0:T(8,128)(2,1)S(1)}, bf16[256,1024]{1,0:T(8,128)(2,1)S(1)}, u32[]{:S(2)}, u32[]{:S(2)}) collective-permute-start(bf16[256,1024]{1,0:T(8,128)(2,1)S(1)} %collective-permute-done.1), channel_id=1, source_target_pairs={{0,1},{1,0},{2,3},{3,2},{4,5},{5,4},{6,7},{7,6},{8,9},{9,8},{10,11... | collective-permute-start | bytes 1572872 | tf_op jit(solution)/shard_map/ppermute | solution.py:26
  37.5 12.5 %collective-permute-start.14 = (bf16[256,1024]{1,0:T(8,128)(2,1)}, bf16[256,1024]{1,0:T(8,128)(2,1)S(1)}, u32[]{:S(2)}, u32[]{:S(2)}) collective-permute-start(bf16[256,1024]{1,0:T(8,128)(2,1)} %collective-permute-done.12), channel_id=1, source_target_pairs={{0,1},{1,0},{2,3},{3,2},{4,5},{5,4},{6,7},{7,6},{8,9},{9,8},{10,11... | collective-permute-start | bytes 1572872 | tf_op jit(solution)/shard_map/ppermute | solution.py:26
  38.0 15.9 %collective-permute-start.16 = (bf16[256,1024]{1,0:T(8,128)(2,1)}, bf16[256,1024]{1,0:T(8,128)(2,1)S(1)}, u32[]{:S(2)}, u32[]{:S(2)}) collective-permute-start(bf16[256,1024]{1,0:T(8,128)(2,1)} %collective-permute-done.12), channel_id=1, source_target_pairs={{0,4},{4,12},{12,8},{8,0},{1,5},{5,13},{13,9},{9,1},{2,6},{6,14},{... | collective-permute-start | bytes 1572872 | tf_op jit(solution)/shard_map/ppermute | solution.py:373
  40.3 18.2 %collective-permute-start.5 = (bf16[256,1024]{1,0:T(8,128)(2,1)S(1)}, bf16[256,1024]{1,0:T(8,128)(2,1)S(1)}, u32[]{:S(2)}, u32[]{:S(2)}) collective-permute-start(bf16[256,1024]{1,0:T(8,128)(2,1)S(1)} %collective-permute-done.4), channel_id=1, source_target_pairs={{0,16},{16,0},{1,17},{17,1},{2,18},{18,2},{3,19},{19,3},{4,20},{20... | collective-permute-start | bytes 1572872 | tf_op jit(solution)/shard_map/ppermute | solution.py:26
  47.2 17.9 %collective-permute-start.8 = (bf16[256,1024]{1,0:T(8,128)(2,1)S(1)}, bf16[256,1024]{1,0:T(8,128)(2,1)S(1)}, u32[]{:S(2)}, u32[]{:S(2)}) collective-permute-start(bf16[256,1024]{1,0:T(8,128)(2,1)S(1)} %collective-permute-done.4), channel_id=1, source_target_pairs={{0,4},{4,12},{12,8},{8,0},{1,5},{5,13},{13,9},{9,1},{2,6},{6,14},{... | collective-permute-start | bytes 1572872 | tf_op jit(solution)/shard_map/ppermute | solution.py:373
  47.7 17.5 %collective-permute-start.15 = (bf16[256,1024]{1,0:T(8,128)(2,1)S(1)}, bf16[256,1024]{1,0:T(8,128)(2,1)S(1)}, u32[]{:S(2)}, u32[]{:S(2)}) collective-permute-start(bf16[256,1024]{1,0:T(8,128)(2,1)S(1)} %collective-permute-done.13), channel_id=1, source_target_pairs={{0,1},{1,0},{2,3},{3,2},{4,5},{5,4},{6,7},{7,6},{8,9},{9,8},{10,11... | collective-permute-start | bytes 1572872 | tf_op jit(solution)/shard_map/ppermute | solution.py:26
  50.0 19.0 %collective-permute-start.6 = (bf16[256,1024]{1,0:T(8,128)(2,1)S(1)}, bf16[256,1024]{1,0:T(8,128)(2,1)S(1)}, u32[]{:S(2)}, u32[]{:S(2)}) collective-permute-start(bf16[256,1024]{1,0:T(8,128)(2,1)S(1)} %collective-permute-done.4), channel_id=1, source_target_pairs={{0,1},{1,0},{2,3},{3,2},{4,5},{5,4},{6,7},{7,6},{8,9},{9,8},{10,11... | collective-permute-start | bytes 1572872 | tf_op jit(solution)/shard_map/ppermute | solution.py:26
  53.9 27.2 %collective-permute-start.17 = (bf16[256,1024]{1,0:T(8,128)(2,1)S(1)}, bf16[256,1024]{1,0:T(8,128)(2,1)S(1)}, u32[]{:S(2)}, u32[]{:S(2)}) collective-permute-start(bf16[256,1024]{1,0:T(8,128)(2,1)S(1)} %collective-permute-done.16), channel_id=1, source_target_pairs={{0,16},{16,0},{1,17},{17,1},{2,18},{18,2},{3,19},{19,3},{4,20},{20... | collective-permute-start | bytes 1572872 | tf_op jit(solution)/shard_map/ppermute | solution.py:26
  58.5 17.1 %collective-permute-start.20 = (bf16[256,1024]{1,0:T(8,128)(2,1)S(1)}, bf16[256,1024]{1,0:T(8,128)(2,1)S(1)}, u32[]{:S(2)}, u32[]{:S(2)}) collective-permute-start(bf16[256,1024]{1,0:T(8,128)(2,1)S(1)} %collective-permute-done.16), channel_id=1, source_target_pairs={{0,4},{4,12},{12,8},{8,0},{1,5},{5,13},{13,9},{9,1},{2,6},{6,14},{... | collective-permute-start | bytes 1572872 | tf_op jit(solution)/shard_map/ppermute | solution.py:373
  65.2 10.4 %collective-permute-start.7 = (bf16[256,1024]{1,0:T(8,128)(2,1)S(1)}, bf16[256,1024]{1,0:T(8,128)(2,1)S(1)}, u32[]{:S(2)}, u32[]{:S(2)}) collective-permute-start(bf16[256,1024]{1,0:T(8,128)(2,1)S(1)} %collective-permute-done.5), channel_id=1, source_target_pairs={{0,1},{1,0},{2,3},{3,2},{4,5},{5,4},{6,7},{7,6},{8,9},{9,8},{10,11... | collective-permute-start | bytes 1572872 | tf_op jit(solution)/shard_map/ppermute | solution.py:26
  65.2 14.7 %collective-permute-start.9 = (bf16[256,1024]{1,0:T(8,128)(2,1)S(1)}, bf16[256,1024]{1,0:T(8,128)(2,1)S(1)}, u32[]{:S(2)}, u32[]{:S(2)}) collective-permute-start(bf16[256,1024]{1,0:T(8,128)(2,1)S(1)} %collective-permute-done.8), channel_id=1, source_target_pairs={{0,16},{16,0},{1,17},{17,1},{2,18},{18,2},{3,19},{19,3},{4,20},{20... | collective-permute-start | bytes 1572872 | tf_op jit(solution)/shard_map/ppermute | solution.py:26
  69.0 21.7 %collective-permute-start.18 = (bf16[256,1024]{1,0:T(8,128)(2,1)S(1)}, bf16[256,1024]{1,0:T(8,128)(2,1)S(1)}, u32[]{:S(2)}, u32[]{:S(2)}) collective-permute-start(bf16[256,1024]{1,0:T(8,128)(2,1)S(1)} %collective-permute-done.16), channel_id=1, source_target_pairs={{0,1},{1,0},{2,3},{3,2},{4,5},{5,4},{6,7},{7,6},{8,9},{9,8},{10,11... | collective-permute-start | bytes 1572872 | tf_op jit(solution)/shard_map/ppermute | solution.py:26
  75.5 15.2 %collective-permute-start.21 = (bf16[256,1024]{1,0:T(8,128)(2,1)S(1)}, bf16[256,1024]{1,0:T(8,128)(2,1)S(1)}, u32[]{:S(2)}, u32[]{:S(2)}) collective-permute-start(bf16[256,1024]{1,0:T(8,128)(2,1)S(1)} %collective-permute-done.20.refs_0_), channel_id=1, source_target_pairs={{0,16},{16,0},{1,17},{17,1},{2,18},{18,2},{3,19},{19,3},{4,20},{20... | collective-permute-start | bytes 1572872 | tf_op jit(solution)/shard_map/ppermute | solution.py:26
  81.2 11.2 %collective-permute-start.22 = (bf16[256,1024]{1,0:T(8,128)(2,1)S(1)}, bf16[256,1024]{1,0:T(8,128)(2,1)S(1)}, u32[]{:S(2)}, u32[]{:S(2)}) collective-permute-start(bf16[256,1024]{1,0:T(8,128)(2,1)S(1)} %collective-permute-done.20.refs_0_), channel_id=1, source_target_pairs={{0,1},{1,0},{2,3},{3,2},{4,5},{5,4},{6,7},{7,6},{8,9},{9,8},{10,11... | collective-permute-start | bytes 1572872 | tf_op jit(solution)/shard_map/ppermute | solution.py:26
  81.8 9.0 %collective-permute-start.19 = (bf16[256,1024]{1,0:T(8,128)(2,1)S(1)}, bf16[256,1024]{1,0:T(8,128)(2,1)S(1)}, u32[]{:S(2)}, u32[]{:S(2)}) collective-permute-start(bf16[256,1024]{1,0:T(8,128)(2,1)S(1)} %collective-permute-done.17), channel_id=1, source_target_pairs={{0,1},{1,0},{2,3},{3,2},{4,5},{5,4},{6,7},{7,6},{8,9},{9,8},{10,11... | collective-permute-start | bytes 1572872 | tf_op jit(solution)/shard_map/ppermute | solution.py:26
  98.7 13.9 %collective-permute-start.25 = (bf16[64,2048]{1,0:T(8,128)(2,1)S(1)}, bf16[64,2048]{1,0:T(8,128)(2,1)S(1)}, u32[]{:S(2)}, u32[]{:S(2)}) collective-permute-start(bf16[64,2048]{1,0:T(8,128)(2,1)S(1)} %get-tuple-element.29.refs_0_.refs_4_), channel_id=1, source_target_pairs={{0,4},{4,12},{12,8},{8,0},{1,5},{5,13},{13,9},{9,1},{2,6},{6,14},{... | collective-permute-start | bytes 786440 | tf_op jit(solution)/shard_map/ppermute | solution.py:444
  100.5 19.5 %collective-permute-start.28 = (bf16[64,2048]{1,0:T(8,128)(2,1)S(1)}, bf16[64,2048]{1,0:T(8,128)(2,1)}, u32[]{:S(2)}, u32[]{:S(2)}) collective-permute-start(bf16[64,2048]{1,0:T(8,128)(2,1)S(1)} %get-tuple-element.29.refs_0_.refs_4_), channel_id=1, source_target_pairs={{4,0},{12,4},{8,12},{0,8},{5,1},{13,5},{9,13},{1,9},{6,2},{14,6},{... | collective-permute-start | bytes 786440 | tf_op jit(solution)/shard_map/ppermute | solution.py:448
  112.6 7.4 %collective-permute-start.26 = (bf16[64,2048]{1,0:T(8,128)(2,1)S(1)}, bf16[64,2048]{1,0:T(8,128)(2,1)}, u32[]{:S(2)}, u32[]{:S(2)}) collective-permute-start(bf16[64,2048]{1,0:T(8,128)(2,1)S(1)} %collective-permute-done.25.refs_1_), channel_id=1, source_target_pairs={{0,4},{4,12},{12,8},{8,0},{1,5},{5,13},{13,9},{9,1},{2,6},{6,14},{... | collective-permute-start | bytes 786440 | tf_op jit(solution)/shard_map/ppermute | solution.py:444
  (27 other events, 157.9 us)

commit v15 on v14

--- a/solution.py
+++ b/solution.py
@@ -160,10 +160,10 @@
     list_c, list_o, pooled_ref, oth_ref, counts_ref, gain_ref, doc_sums_ref, up_ref = refs[
         sums_count : sums_count + 8
     ]
-    up_states_ref, labels_ref = refs[sums_count + 8 : sums_count + 10]
-    state_refs = refs[sums_count + 10 : sums_count + 10 + chunks]
+    labels_ref = refs[sums_count + 8]
+    state_refs = refs[sums_count + 9 : sums_count + 9 + chunks]
     losses_ref, doc_grad_ref, small_ref, gained_ref, gain_grad_ref = refs[
-        sums_count + 10 + chunks :
+        sums_count + 9 + chunks :
     ]
     docs = pooled_ref.shape[0]
     half = docs // 2
@@ -253,9 +253,9 @@
     )
     up_gained = dot_nt(up_ref[...].astype(jnp.float32), gained, highest)
     small_ref[...] = jnp.zeros_like(small_ref)
-    small_ref[:rank, :tokens] = up_states_ref[...]
-    small_ref[:rank, tokens : tokens + docs] = up_gained
-    small_ref[rank : rank + 1, :tokens] = tok_dots
+    small_ref[:rank, :docs] = up_gained
+    for i in range(tokens // 128):
+        small_ref[rank + i : rank + i + 1] = tok_dots[:, i * 128 : (i + 1) * 128]
 
 
 def grads_kernel(small_count, chunks, rank, width, *refs):
@@ -265,16 +265,20 @@
     side_ref, inv_rms_ref, mid_ref, labels_ref, own_cols_ref, gained_ref, gain_grad_ref = refs[
         small_count : small_count + 7
     ]
-    state_refs = refs[small_count + 7 : small_count + 7 + chunks]
-    kept_ref, sent_ref, grads_ref = refs[small_count + 7 + chunks :]
+    up_states_ref = refs[small_count + 7]
+    state_refs = refs[small_count + 8 : small_count + 8 + chunks]
+    kept_ref, sent_ref, grads_ref = refs[small_count + 8 + chunks :]
     tokens = inv_rms_ref.shape[1]
     docs = gained_ref.shape[0]
     doc_id = lax.broadcasted_iota(jnp.int32, (docs, tokens), 0)
     member = jnp.where(doc_id == labels_ref[...], 1.0, 0.0)
     inv_rms = inv_rms_ref[...]
-    alpha = inv_rms * inv_rms * inv_rms * small[rank : rank + 1, :tokens] / width
-    up_states = small[:rank, :tokens]
-    up_gained = small[:rank, tokens : tokens + docs]
+    tok_dots = jnp.concatenate(
+        [small[rank + i : rank + i + 1] for i in range(tokens // 128)], axis=1
+    )
+    alpha = inv_rms * inv_rms * inv_rms * tok_dots / width
+    up_states = up_states_ref[...]
+    up_gained = small[:rank, :docs]
     mid_grad = (inv_rms * dot_nn(up_gained, member, highest) - alpha * up_states).astype(
         jnp.bfloat16
     )
@@ -436,6 +440,9 @@
         squares + states_b + [labels[None], gain[None], counts[:, None]],
     )
 
+    up_parts = [adapter_up[:, low:high] for low, high in parts]
+    up_states = sum(dot_nt(u, x) for u, x in zip(up_parts, states_b))
+    up_states = sum_over(up_states, "mp")
     first_other = swap(pooled, "pair")
     late_pooled = after(pooled, first_other, list_c)
     own_blocks = [pooled] * dp
@@ -459,8 +466,6 @@
         [pltpu.VMEM((rows, cols), jnp.bfloat16)],
         vmem=16 if dp <= 4 else 48,
     )
-    up_parts = [adapter_up[:, low:high] for low, high in parts]
-    up_states = sum(dot_nt(u, x) for u, x in zip(up_parts, states_b))
     if lax.axis_size("mp") == 2:
         sums = [sums, swap(sums, "mp")]
     else:
@@ -470,7 +475,7 @@
         (
             jax.ShapeDtypeStruct((1, anchors), jnp.float32),
             jax.ShapeDtypeStruct((docs, cols), jnp.float32),
-            jax.ShapeDtypeStruct((rank + 8, token_count + 128), jnp.float32),
+            jax.ShapeDtypeStruct((rank + -(-token_count // 1024) * 8, 128), jnp.float32),
             jax.ShapeDtypeStruct((docs, cols), jnp.float32),
             jax.ShapeDtypeStruct((1, cols), jnp.float32),
         ),
@@ -484,7 +489,6 @@
             gain[None],
             doc_sums,
             adapter_up,
-            up_states,
             labels[None],
         ]
         + states_b,
@@ -508,6 +512,7 @@
             own_cols,
             gained,
             gain_grad,
+            up_states,
         ]
         + states_b,
         [pltpu.VMEM((2 * rank + 8, cols), jnp.float32)],

time: 151 us -> 151 us (level)
    ppermute x28 -> x29, waiting for transfers between devices: 34.6 us -> 33.6 us  [swap(): return lax.ppermute(x, axis, [(0, 1), (1, 0)])]
    ppermute x28 -> x29, starting transfers between devices: 17.1 us -> 17.9 us  [swap(): return lax.ppermute(x, axis, [(0, 1), (1, 0)])]
  transfers between devices with their start and end apart: 40 -> 41, of which waited for: 24 -> 24; matrix products, arithmetic and copies ran while one was open for 19% -> 19% of each run, Pallas kernels for 1% -> 3%
where the time goes in v15:
time: 151 us; the launch traced here: 150 us
  waiting for transfers between devices  77.1 us (51%)
  starting transfers between devices  33.4 us (22%)
  matrix products  19.2 us (13%)
  local copies, waits for them, and re-layouts  8.26 us (5%)
  Pallas kernels  7.36 us (5%)
  other arithmetic  3.52 us (2%)
    ppermute x29, waiting for transfers between devices, swap(): return lax.ppermute(x, axis, [(0, 1), (1, 0)])  33.6 us
    ppermute x6, waiting for transfers between devices, body(): lax.ppermute(ringed[-chunk_count] if step > 1 else moving[h], 'dp', hops)  23.4 us
    dot_general x10, matrix products, dot_nn(): jnp.dot(a, b, precision=precision, preferred_element_type=jnp.float32)  18.4 us
    ppermute x29, starting transfers between devices, swap(): return lax.ppermute(x, axis, [(0, 1), (1, 0)])  17.9 us
    ppermute x2, waiting for transfers between devices, body(): own_blocks[j] = lax.ppermute(own_blocks[j - 1], 'dp', hops)  14.5 us
    ppermute x6, starting transfers between devices, body(): lax.ppermute(ringed[-chunk_count] if step > 1 else moving[h], 'dp', hops)  7.58 us
    pallas_call x5, Pallas kernels, call(): pl.pallas_call(kernel, out_shape=outs, scratch_shapes=list(scratch), in_s...  7.36 us
    ppermute x3, waiting for transfers between devices, partner(): lax.ppermute(x, axis, [(i, i ^ flip) for i in range(lax.axis_size(axis))])  5.59 us
  transfers between devices with their start and end apart: 41, of which 24 were waited for; matrix products, arithmetic and copies ran while one was open for 19% of the time, Pallas kernels for 3%

profile of v15, /device:TPU:0, one launch (start us, length us, event | category | flops | bytes accessed | tf_op | source)
XLA Modules:
  0.0 150.1 jit_solution(11001730979146746266)
XLA Ops:
  1.8 3.1 %collective-permute-start = (bf16[256,1024]{1,0:T(8,128)(2,1)S(1)}, bf16[256,1024]{1,0:T(8,128)(2,1)}, u32[]{:S(2)}, u32[]{:S(2)}) collective-permute-start(bf16[256,1024]{1,0:T(8,128)(2,1)S(1)} %constant_dynamic-slice_fusion), channel_id=1, source_target_pairs={{0,4},{4,12},{12,8},{8,0},{1,5},{5,13},{13,9},{9,1},{2,6},{6,14},{... | collective-permute-start | bytes 1572872 | tf_op jit(solution)/shard_map/ppermute | solution.py:377
  6.0 2.6 %collective-permute-start.12 = (bf16[256,1024]{1,0:T(8,128)(2,1)S(1)}, bf16[256,1024]{1,0:T(8,128)(2,1)}, u32[]{:S(2)}, u32[]{:S(2)}) collective-permute-start(bf16[256,1024]{1,0:T(8,128)(2,1)S(1)} %constant_dynamic-slice_fusion.1), channel_id=1, source_target_pairs={{0,4},{4,12},{12,8},{8,0},{1,5},{5,13},{13,9},{9,1},{2,6},{6,14},{... | collective-permute-start | bytes 1572872 | tf_op jit(solution)/shard_map/ppermute | solution.py:377
  8.7 3.4 %fusion.64 = bf16[512,16]{0,1:T(8,128)(2,1)S(1)} fusion(bf16[4096,16]{0,1:T(8,128)(2,1)S(1)} %copy-done, bf16[1,512,4096]{2,1,0:T(8,128)(2,1)} %param.8), kind=kOutput, calls=%fused_computation.58 | convolution fusion | flops 67117056 | bytes 4341760 | tf_op jit(solution)/shard_map/dot_general | solution.py:22
  17.8 3.0 %fusion.44 = f32[512,1024]{1,0:T(8,128)S(1)} fusion(bf16[512,1024]{1,0:T(8,128)(2,1)S(1)} %dynamic-slice_bitcast_fusion.1, bf16[1024,2048]{1,0:T(8,128)(2,1)} %param.10), kind=kOutput, calls=%fused_computation.48 | convolution fusion | flops 1073741824 | bytes 5242880 | tf_op jit(solution)/shard_map/dot_general | solution.py:22
  24.1 5.9 %collective-permute-done.12 = bf16[256,1024]{1,0:T(8,128)(2,1)} collective-permute-done((bf16[256,1024]{1,0:T(8,128)(2,1)S(1)}, bf16[256,1024]{1,0:T(8,128)(2,1)}, u32[]{:S(2)}, u32[]{:S(2)}) %collective-permute-start.12) | collective-permute-done | bytes 524320 | tf_op jit(solution)/shard_map/ppermute | solution.py:377
  31.8 4.2 %collective-permute-done.1 = bf16[256,1024]{1,0:T(8,128)(2,1)S(1)} collective-permute-done((bf16[256,1024]{1,0:T(8,128)(2,1)}, bf16[256,1024]{1,0:T(8,128)(2,1)S(1)}, u32[]{:S(2)}, u32[]{:S(2)}) %collective-permute-start.1) | collective-permute-done | bytes 524320 | tf_op jit(solution)/shard_map/ppermute | solution.py:26
  41.8 5.4 %collective-permute-done.13 = bf16[256,1024]{1,0:T(8,128)(2,1)S(1)} collective-permute-done((bf16[256,1024]{1,0:T(8,128)(2,1)}, bf16[256,1024]{1,0:T(8,128)(2,1)S(1)}, u32[]{:S(2)}, u32[]{:S(2)}) %collective-permute-start.13) | collective-permute-done | bytes 524320 | tf_op jit(solution)/shard_map/ppermute | solution.py:26
  47.7 2.3 %fusion.58 = f32[512,1024]{1,0:T(8,128)S(1)} fusion(f32[512,1024]{1,0:T(8,128)S(1)} %add_add_fusion.1, bf16[256,1024]{1,0:T(8,128)(2,1)S(1)} %collective-permute-done.3, bf16[256,1024]{1,0:T(8,128)(2,1)S(1)} %collective-permute-done.2, bf16[256,1024]{1,0:T(8,128)(2,1)S(1)} %collective-permute-done.1, bf16[256,1024]{1,0:T(8,128)(2,1)} %collective-permute-done, ...), kind=kOutput, calls=%fused_computation.55 | convolution fusion | flops 1086849024 | bytes 7340032 | tf_op jit(solution)/shard_map/dot_general | solution.py:22
  50.6 3.4 %collective-permute-done.16 = bf16[256,1024]{1,0:T(8,128)(2,1)S(1)} collective-permute-done((bf16[256,1024]{1,0:T(8,128)(2,1)}, bf16[256,1024]{1,0:T(8,128)(2,1)S(1)}, u32[]{:S(2)}, u32[]{:S(2)}) %collective-permute-start.16) | collective-permute-done | bytes 524320 | tf_op jit(solution)/shard_map/ppermute | solution.py:377
  55.5 3.0 %collective-permute-done.5 = bf16[256,1024]{1,0:T(8,128)(2,1)S(1)} collective-permute-done((bf16[256,1024]{1,0:T(8,128)(2,1)S(1)}, bf16[256,1024]{1,0:T(8,128)(2,1)S(1)}, u32[]{:S(2)}, u32[]{:S(2)}) %collective-permute-start.5) | collective-permute-done | bytes 524320 | tf_op jit(solution)/shard_map/ppermute | solution.py:26
  58.9 6.2 %collective-permute-done.8 = bf16[256,1024]{1,0:T(8,128)(2,1)S(1)} collective-permute-done((bf16[256,1024]{1,0:T(8,128)(2,1)S(1)}, bf16[256,1024]{1,0:T(8,128)(2,1)S(1)}, u32[]{:S(2)}, u32[]{:S(2)}) %collective-permute-start.8) | collective-permute-done | bytes 524320 | tf_op jit(solution)/shard_map/ppermute | solution.py:377
  66.7 2.3 %fusion.49 = f32[512,1024]{1,0:T(8,128)S(1)} fusion(f32[512,1024]{1,0:T(8,128)S(1)} %add_add_fusion, bf16[256,1024]{1,0:T(8,128)(2,1)S(1)} %collective-permute-done.15, bf16[256,1024]{1,0:T(8,128)(2,1)S(1)} %collective-permute-done.14, bf16[256,1024]{1,0:T(8,128)(2,1)S(1)} %collective-permute-done.13, bf16[256,1024]{1,0:T(8,128)(2,1)} %collective-permute-done.12, ...), kind=kOutput, calls=%fused_computation.52 | convolution fusion | flops 1086849024 | bytes 7340032 | tf_op jit(solution)/shard_map/dot_general | solution.py:22
  69.3 6.2 %collective-permute-done.20.refs_0_ = bf16[256,1024]{1,0:T(8,128)(2,1)S(1)} collective-permute-done((bf16[256,1024]{1,0:T(8,128)(2,1)S(1)}, bf16[256,1024]{1,0:T(8,128)(2,1)S(1)}, u32[]{:S(2)}, u32[]{:S(2)}) %collective-permute-start.20) | collective-permute-done | bytes 524320 | tf_op jit(solution)/shard_map/ppermute | solution.py:377
  77.1 2.8 %collective-permute-done.9 = bf16[256,1024]{1,0:T(8,128)(2,1)S(1)} collective-permute-done((bf16[256,1024]{1,0:T(8,128)(2,1)S(1)}, bf16[256,1024]{1,0:T(8,128)(2,1)S(1)}, u32[]{:S(2)}, u32[]{:S(2)}) %collective-permute-start.9) | collective-permute-done | bytes 524320 | tf_op jit(solution)/shard_map/ppermute | solution.py:26
  83.1 7.6 %collective-permute-done.21.refs_1_ = bf16[256,1024]{1,0:T(8,128)(2,1)S(1)} collective-permute-done((bf16[256,1024]{1,0:T(8,128)(2,1)S(1)}, bf16[256,1024]{1,0:T(8,128)(2,1)S(1)}, u32[]{:S(2)}, u32[]{:S(2)}) %collective-permute-start.21) | collective-permute-done | bytes 524320 | tf_op jit(solution)/shard_map/ppermute | solution.py:26
  100.6 2.8 %collective-permute-start.28 = (bf16[64,2048]{1,0:T(8,128)(2,1)S(1)}, bf16[64,2048]{1,0:T(8,128)(2,1)}, u32[]{:S(2)}, u32[]{:S(2)}) collective-permute-start(bf16[64,2048]{1,0:T(8,128)(2,1)S(1)} %get-tuple-element.29.refs_0_.refs_4_), channel_id=1, source_target_pairs={{4,0},{12,4},{8,12},{0,8},{5,1},{13,5},{9,13},{1,9},{6,2},{14,6},{... | collective-permute-start | bytes 786440 | tf_op jit(solution)/shard_map/ppermute | solution.py:455
  103.4 9.3 %collective-permute-done.25.refs_1_ = bf16[64,2048]{1,0:T(8,128)(2,1)S(1)} collective-permute-done((bf16[64,2048]{1,0:T(8,128)(2,1)S(1)}, bf16[64,2048]{1,0:T(8,128)(2,1)S(1)}, u32[]{:S(2)}, u32[]{:S(2)}) %collective-permute-start.25) | collective-permute-done | bytes 262176 | tf_op jit(solution)/shard_map/ppermute | solution.py:451
  114.8 5.2 %collective-permute-done.26.refs_2_ = bf16[64,2048]{1,0:T(8,128)(2,1)} collective-permute-done((bf16[64,2048]{1,0:T(8,128)(2,1)S(1)}, bf16[64,2048]{1,0:T(8,128)(2,1)}, u32[]{:S(2)}, u32[]{:S(2)}) %collective-permute-start.26) | collective-permute-done | bytes 262176 | tf_op jit(solution)/shard_map/ppermute | solution.py:451
  126.5 2.4 %collective-permute-done.32.refs_1_ = f32[168,128]{1,0:T(8,128)S(1)} collective-permute-done((f32[168,128]{1,0:T(8,128)S(1)}, f32[168,128]{1,0:T(8,128)S(1)}, u32[]{:S(2)}, u32[]{:S(2)}) %collective-permute-start.32) | collective-permute-done | bytes 86048 | tf_op jit(solution)/shard_map/ppermute | solution.py:26
  128.9 2.0 %shard_map.122 = (f32[1,128]{1,0:T(1,128)}, f32[64,2048]{1,0:T(8,128)}, f32[24,128]{1,0:T(8,128)S(1)}, f32[64,2048]{1,0:T(8,128)S(1)}, f32[1,2048]{1,0:T(1,128)S(1)}) custom-call(f32[168,128]{1,0:T(8,128)S(1)} %get-tuple-element.30.refs_0_, f32[168,128]{1,0:T(8,128)S(1)} %collective-permute-done.32.refs_1_, s32[4,128]{1,0:T(4,128)S(1)} %bitcast.108, ...), custom_call_target="tpu_custom_call" | custom-call | flops 16777216 | bytes 4182784 | tf_op jit(solution)/shard_map/pallas_call | solution.py:59
  132.5 2.1 %collective-permute-done.34.refs_1_ = f32[24,128]{1,0:T(8,128)S(1)} collective-permute-done((f32[24,128]{1,0:T(8,128)S(1)}, f32[24,128]{1,0:T(8,128)S(1)}, u32[]{:S(2)}, u32[]{:S(2)}) %collective-permute-start.34) | collective-permute-done | bytes 12320 | tf_op jit(solution)/shard_map/ppermute | solution.py:26
  137.2 3.5 %collective-permute-start.39 = (bf16[40,1024]{1,0:T(8,128)(2,1)S(1)}, bf16[40,1024]{1,0:T(8,128)(2,1)S(1)}, u32[]{:S(2)}, u32[]{:S(2)}) collective-permute-start(bf16[40,1024]{1,0:T(8,128)(2,1)S(1)} %add_convert_fusion), channel_id=1, source_target_pairs={{0,12},{4,8},{8,4},{12,0},{1,13},{5,9},{9,5},{13,1},{2,14},{6,10},... | collective-permute-start | bytes 245768 | tf_op jit(solution)/shard_map/ppermute | solution.py:30
  141.6 2.7 %collective-permute-done.39 = bf16[40,1024]{1,0:T(8,128)(2,1)S(1)} collective-permute-done((bf16[40,1024]{1,0:T(8,128)(2,1)S(1)}, bf16[40,1024]{1,0:T(8,128)(2,1)S(1)}, u32[]{:S(2)}, u32[]{:S(2)}) %collective-permute-start.39) | collective-permute-done | bytes 81952 | tf_op jit(solution)/shard_map/ppermute | solution.py:30
  144.4 2.7 %collective-permute-done.38 = bf16[40,1024]{1,0:T(8,128)(2,1)S(1)} collective-permute-done((bf16[40,1024]{1,0:T(8,128)(2,1)S(1)}, bf16[40,1024]{1,0:T(8,128)(2,1)S(1)}, u32[]{:S(2)}, u32[]{:S(2)}) %collective-permute-start.38) | collective-permute-done | bytes 81952 | tf_op jit(solution)/shard_map/ppermute | solution.py:30
  (128 shorter events, 54.8 us)
Async XLA Ops:
  1.8 19.1 %collective-permute-start = (bf16[256,1024]{1,0:T(8,128)(2,1)S(1)}, bf16[256,1024]{1,0:T(8,128)(2,1)}, u32[]{:S(2)}, u32[]{:S(2)}) collective-permute-start(bf16[256,1024]{1,0:T(8,128)(2,1)S(1)} %constant_dynamic-slice_fusion), channel_id=1, source_target_pairs={{0,4},{4,12},{12,8},{8,0},{1,5},{5,13},{13,9},{9,1},{2,6},{6,14},{... | collective-permute-start | bytes 1572872 | tf_op jit(solution)/shard_map/ppermute | solution.py:377
  6.0 23.9 %collective-permute-start.12 = (bf16[256,1024]{1,0:T(8,128)(2,1)S(1)}, bf16[256,1024]{1,0:T(8,128)(2,1)}, u32[]{:S(2)}, u32[]{:S(2)}) collective-permute-start(bf16[256,1024]{1,0:T(8,128)(2,1)S(1)} %constant_dynamic-slice_fusion.1), channel_id=1, source_target_pairs={{0,4},{4,12},{12,8},{8,0},{1,5},{5,13},{13,9},{9,1},{2,6},{6,14},{... | collective-permute-start | bytes 1572872 | tf_op jit(solution)/shard_map/ppermute | solution.py:377
  20.9 15.1 %collective-permute-start.1 = (bf16[256,1024]{1,0:T(8,128)(2,1)}, bf16[256,1024]{1,0:T(8,128)(2,1)S(1)}, u32[]{:S(2)}, u32[]{:S(2)}) collective-permute-start(bf16[256,1024]{1,0:T(8,128)(2,1)} %collective-permute-done), channel_id=1, source_target_pairs={{0,16},{16,0},{1,17},{17,1},{2,18},{18,2},{3,19},{19,3},{4,20},{20... | collective-permute-start | bytes 1572872 | tf_op jit(solution)/shard_map/ppermute | solution.py:26
  23.5 14.5 %collective-permute-start.2 = (bf16[256,1024]{1,0:T(8,128)(2,1)}, bf16[256,1024]{1,0:T(8,128)(2,1)S(1)}, u32[]{:S(2)}, u32[]{:S(2)}) collective-permute-start(bf16[256,1024]{1,0:T(8,128)(2,1)} %collective-permute-done), channel_id=1, source_target_pairs={{0,1},{1,0},{2,3},{3,2},{4,5},{5,4},{6,7},{7,6},{8,9},{9,8},{10,11... | collective-permute-start | bytes 1572872 | tf_op jit(solution)/shard_map/ppermute | solution.py:26
  23.6 16.7 %collective-permute-start.4 = (bf16[256,1024]{1,0:T(8,128)(2,1)}, bf16[256,1024]{1,0:T(8,128)(2,1)S(1)}, u32[]{:S(2)}, u32[]{:S(2)}) collective-permute-start(bf16[256,1024]{1,0:T(8,128)(2,1)} %collective-permute-done), channel_id=1, source_target_pairs={{0,4},{4,12},{12,8},{8,0},{1,5},{5,13},{13,9},{9,1},{2,6},{6,14},{... | collective-permute-start | bytes 1572872 | tf_op jit(solution)/shard_map/ppermute | solution.py:377
  30.0 17.3 %collective-permute-start.13 = (bf16[256,1024]{1,0:T(8,128)(2,1)}, bf16[256,1024]{1,0:T(8,128)(2,1)S(1)}, u32[]{:S(2)}, u32[]{:S(2)}) collective-permute-start(bf16[256,1024]{1,0:T(8,128)(2,1)} %collective-permute-done.12), channel_id=1, source_target_pairs={{0,16},{16,0},{1,17},{17,1},{2,18},{18,2},{3,19},{19,3},{4,20},{20... | collective-permute-start | bytes 1572872 | tf_op jit(solution)/shard_map/ppermute | solution.py:26
  36.0 11.7 %collective-permute-start.3 = (bf16[256,1024]{1,0:T(8,128)(2,1)S(1)}, bf16[256,1024]{1,0:T(8,128)(2,1)S(1)}, u32[]{:S(2)}, u32[]{:S(2)}) collective-permute-start(bf16[256,1024]{1,0:T(8,128)(2,1)S(1)} %collective-permute-done.1), channel_id=1, source_target_pairs={{0,1},{1,0},{2,3},{3,2},{4,5},{5,4},{6,7},{7,6},{8,9},{9,8},{10,11... | collective-permute-start | bytes 1572872 | tf_op jit(solution)/shard_map/ppermute | solution.py:26
  37.5 12.5 %collective-permute-start.14 = (bf16[256,1024]{1,0:T(8,128)(2,1)}, bf16[256,1024]{1,0:T(8,128)(2,1)S(1)}, u32[]{:S(2)}, u32[]{:S(2)}) collective-permute-start(bf16[256,1024]{1,0:T(8,128)(2,1)} %collective-permute-done.12), channel_id=1, source_target_pairs={{0,1},{1,0},{2,3},{3,2},{4,5},{5,4},{6,7},{7,6},{8,9},{9,8},{10,11... | collective-permute-start | bytes 1572872 | tf_op jit(solution)/shard_map/ppermute | solution.py:26
  38.0 15.9 %collective-permute-start.16 = (bf16[256,1024]{1,0:T(8,128)(2,1)}, bf16[256,1024]{1,0:T(8,128)(2,1)S(1)}, u32[]{:S(2)}, u32[]{:S(2)}) collective-permute-start(bf16[256,1024]{1,0:T(8,128)(2,1)} %collective-permute-done.12), channel_id=1, source_target_pairs={{0,4},{4,12},{12,8},{8,0},{1,5},{5,13},{13,9},{9,1},{2,6},{6,14},{... | collective-permute-start | bytes 1572872 | tf_op jit(solution)/shard_map/ppermute | solution.py:377
  40.3 18.2 %collective-permute-start.5 = (bf16[256,1024]{1,0:T(8,128)(2,1)S(1)}, bf16[256,1024]{1,0:T(8,128)(2,1)S(1)}, u32[]{:S(2)}, u32[]{:S(2)}) collective-permute-start(bf16[256,1024]{1,0:T(8,128)(2,1)S(1)} %collective-permute-done.4), channel_id=1, source_target_pairs={{0,16},{16,0},{1,17},{17,1},{2,18},{18,2},{3,19},{19,3},{4,20},{20... | collective-permute-start | bytes 1572872 | tf_op jit(solution)/shard_map/ppermute | solution.py:26
  47.2 17.9 %collective-permute-start.8 = (bf16[256,1024]{1,0:T(8,128)(2,1)S(1)}, bf16[256,1024]{1,0:T(8,128)(2,1)S(1)}, u32[]{:S(2)}, u32[]{:S(2)}) collective-permute-start(bf16[256,1024]{1,0:T(8,128)(2,1)S(1)} %collective-permute-done.4), channel_id=1, source_target_pairs={{0,4},{4,12},{12,8},{8,0},{1,5},{5,13},{13,9},{9,1},{2,6},{6,14},{... | collective-permute-start | bytes 1572872 | tf_op jit(solution)/shard_map/ppermute | solution.py:377
  47.7 17.5 %collective-permute-start.15 = (bf16[256,1024]{1,0:T(8,128)(2,1)S(1)}, bf16[256,1024]{1,0:T(8,128)(2,1)S(1)}, u32[]{:S(2)}, u32[]{:S(2)}) collective-permute-start(bf16[256,1024]{1,0:T(8,128)(2,1)S(1)} %collective-permute-done.13), channel_id=1, source_target_pairs={{0,1},{1,0},{2,3},{3,2},{4,5},{5,4},{6,7},{7,6},{8,9},{9,8},{10,11... | collective-permute-start | bytes 1572872 | tf_op jit(solution)/shard_map/ppermute | solution.py:26
  50.0 19.0 %collective-permute-start.6 = (bf16[256,1024]{1,0:T(8,128)(2,1)S(1)}, bf16[256,1024]{1,0:T(8,128)(2,1)S(1)}, u32[]{:S(2)}, u32[]{:S(2)}) collective-permute-start(bf16[256,1024]{1,0:T(8,128)(2,1)S(1)} %collective-permute-done.4), channel_id=1, source_target_pairs={{0,1},{1,0},{2,3},{3,2},{4,5},{5,4},{6,7},{7,6},{8,9},{9,8},{10,11... | collective-permute-start | bytes 1572872 | tf_op jit(solution)/shard_map/ppermute | solution.py:26
  53.9 27.2 %collective-permute-start.17 = (bf16[256,1024]{1,0:T(8,128)(2,1)S(1)}, bf16[256,1024]{1,0:T(8,128)(2,1)S(1)}, u32[]{:S(2)}, u32[]{:S(2)}) collective-permute-start(bf16[256,1024]{1,0:T(8,128)(2,1)S(1)} %collective-permute-done.16), channel_id=1, source_target_pairs={{0,16},{16,0},{1,17},{17,1},{2,18},{18,2},{3,19},{19,3},{4,20},{20... | collective-permute-start | bytes 1572872 | tf_op jit(solution)/shard_map/ppermute | solution.py:26
  58.5 17.1 %collective-permute-start.20 = (bf16[256,1024]{1,0:T(8,128)(2,1)S(1)}, bf16[256,1024]{1,0:T(8,128)(2,1)S(1)}, u32[]{:S(2)}, u32[]{:S(2)}) collective-permute-start(bf16[256,1024]{1,0:T(8,128)(2,1)S(1)} %collective-permute-done.16), channel_id=1, source_target_pairs={{0,4},{4,12},{12,8},{8,0},{1,5},{5,13},{13,9},{9,1},{2,6},{6,14},{... | collective-permute-start | bytes 1572872 | tf_op jit(solution)/shard_map/ppermute | solution.py:377
  65.2 10.4 %collective-permute-start.7 = (bf16[256,1024]{1,0:T(8,128)(2,1)S(1)}, bf16[256,1024]{1,0:T(8,128)(2,1)S(1)}, u32[]{:S(2)}, u32[]{:S(2)}) collective-permute-start(bf16[256,1024]{1,0:T(8,128)(2,1)S(1)} %collective-permute-done.5), channel_id=1, source_target_pairs={{0,1},{1,0},{2,3},{3,2},{4,5},{5,4},{6,7},{7,6},{8,9},{9,8},{10,11... | collective-permute-start | bytes 1572872 | tf_op jit(solution)/shard_map/ppermute | solution.py:26
  65.2 14.7 %collective-permute-start.9 = (bf16[256,1024]{1,0:T(8,128)(2,1)S(1)}, bf16[256,1024]{1,0:T(8,128)(2,1)S(1)}, u32[]{:S(2)}, u32[]{:S(2)}) collective-permute-start(bf16[256,1024]{1,0:T(8,128)(2,1)S(1)} %collective-permute-done.8), channel_id=1, source_target_pairs={{0,16},{16,0},{1,17},{17,1},{2,18},{18,2},{3,19},{19,3},{4,20},{20... | collective-permute-start | bytes 1572872 | tf_op jit(solution)/shard_map/ppermute | solution.py:26
  69.0 21.7 %collective-permute-start.18 = (bf16[256,1024]{1,0:T(8,128)(2,1)S(1)}, bf16[256,1024]{1,0:T(8,128)(2,1)S(1)}, u32[]{:S(2)}, u32[]{:S(2)}) collective-permute-start(bf16[256,1024]{1,0:T(8,128)(2,1)S(1)} %collective-permute-done.16), channel_id=1, source_target_pairs={{0,1},{1,0},{2,3},{3,2},{4,5},{5,4},{6,7},{7,6},{8,9},{9,8},{10,11... | collective-permute-start | bytes 1572872 | tf_op jit(solution)/shard_map/ppermute | solution.py:26
  75.5 15.2 %collective-permute-start.21 = (bf16[256,1024]{1,0:T(8,128)(2,1)S(1)}, bf16[256,1024]{1,0:T(8,128)(2,1)S(1)}, u32[]{:S(2)}, u32[]{:S(2)}) collective-permute-start(bf16[256,1024]{1,0:T(8,128)(2,1)S(1)} %collective-permute-done.20.refs_0_), channel_id=1, source_target_pairs={{0,16},{16,0},{1,17},{17,1},{2,18},{18,2},{3,19},{19,3},{4,20},{20... | collective-permute-start | bytes 1572872 | tf_op jit(solution)/shard_map/ppermute | solution.py:26
  81.2 11.2 %collective-permute-start.22 = (bf16[256,1024]{1,0:T(8,128)(2,1)S(1)}, bf16[256,1024]{1,0:T(8,128)(2,1)S(1)}, u32[]{:S(2)}, u32[]{:S(2)}) collective-permute-start(bf16[256,1024]{1,0:T(8,128)(2,1)S(1)} %collective-permute-done.20.refs_0_), channel_id=1, source_target_pairs={{0,1},{1,0},{2,3},{3,2},{4,5},{5,4},{6,7},{7,6},{8,9},{9,8},{10,11... | collective-permute-start | bytes 1572872 | tf_op jit(solution)/shard_map/ppermute | solution.py:26
  81.8 9.0 %collective-permute-start.19 = (bf16[256,1024]{1,0:T(8,128)(2,1)S(1)}, bf16[256,1024]{1,0:T(8,128)(2,1)S(1)}, u32[]{:S(2)}, u32[]{:S(2)}) collective-permute-start(bf16[256,1024]{1,0:T(8,128)(2,1)S(1)} %collective-permute-done.17), channel_id=1, source_target_pairs={{0,1},{1,0},{2,3},{3,2},{4,5},{5,4},{6,7},{7,6},{8,9},{9,8},{10,11... | collective-permute-start | bytes 1572872 | tf_op jit(solution)/shard_map/ppermute | solution.py:26
  98.7 13.9 %collective-permute-start.25 = (bf16[64,2048]{1,0:T(8,128)(2,1)S(1)}, bf16[64,2048]{1,0:T(8,128)(2,1)S(1)}, u32[]{:S(2)}, u32[]{:S(2)}) collective-permute-start(bf16[64,2048]{1,0:T(8,128)(2,1)S(1)} %get-tuple-element.29.refs_0_.refs_4_), channel_id=1, source_target_pairs={{0,4},{4,12},{12,8},{8,0},{1,5},{5,13},{13,9},{9,1},{2,6},{6,14},{... | collective-permute-start | bytes 786440 | tf_op jit(solution)/shard_map/ppermute | solution.py:451
  100.6 19.5 %collective-permute-start.28 = (bf16[64,2048]{1,0:T(8,128)(2,1)S(1)}, bf16[64,2048]{1,0:T(8,128)(2,1)}, u32[]{:S(2)}, u32[]{:S(2)}) collective-permute-start(bf16[64,2048]{1,0:T(8,128)(2,1)S(1)} %get-tuple-element.29.refs_0_.refs_4_), channel_id=1, source_target_pairs={{4,0},{12,4},{8,12},{0,8},{5,1},{13,5},{9,13},{1,9},{6,2},{14,6},{... | collective-permute-start | bytes 786440 | tf_op jit(solution)/shard_map/ppermute | solution.py:455
  112.6 7.4 %collective-permute-start.26 = (bf16[64,2048]{1,0:T(8,128)(2,1)S(1)}, bf16[64,2048]{1,0:T(8,128)(2,1)}, u32[]{:S(2)}, u32[]{:S(2)}) collective-permute-start(bf16[64,2048]{1,0:T(8,128)(2,1)S(1)} %collective-permute-done.25.refs_1_), channel_id=1, source_target_pairs={{0,4},{4,12},{12,8},{8,0},{1,5},{5,13},{13,9},{9,1},{2,6},{6,14},{... | collective-permute-start | bytes 786440 | tf_op jit(solution)/shard_map/ppermute | solution.py:451
  (28 other events, 164.3 us)
